TPU v7x, 32 devices: a whole 2x2x4 slice. The times are simulated.
32 devices in a mesh: parts: 2 (over x), row: 16 (over z, y, core).
Axes of the slice: x: 2, y: 2, z: 4, core: 2. Of those that a mesh axis runs over, the one named last changes fastest.
Arguments:
- features: bfloat16 [768, 32, 512], P(('parts', 'row')), parts along dimension 0, may hold values from -40 to 40
- row_bands: int32 [32], P('parts'), parts along dimension 0, may hold values from 1 to 3, as said below
- w_expand: bfloat16 [512, 2048], replicated, may hold values from -0.25 to 0.25
- kernel: bfloat16 [9, 2048], replicated, may hold values from -2 to 2
- w_project: bfloat16 [2048, 512], replicated, may hold values from -0.125 to 0.125
- w_qkv: bfloat16 [512, 1536], replicated, may hold values from -0.25 to 0.25
- w_out: bfloat16 [512, 512], replicated, may hold values from -0.25 to 0.25
- cotangent: bfloat16 [768, 32, 512], P(('parts', 'row')), parts along dimension 0, may hold values from -6 to 6
Outputs:
- block_out: bfloat16 [768, 32, 512], P(('parts', 'row')), parts along dimension 0
- input_grad: bfloat16 [768, 32, 512], P(('parts', 'row')), parts along dimension 0
There are 2 independent parts, one for each index of `parts`. A program takes and returns all parts, laid end to end along the dimension named above; an argument that names none is the same for every part. Nothing has to cross between parts.
Inputs may be any that keep to these rules, and one draw needn't show every extreme that they name: `row_bands`: devices 2k and 2k + 1 together hold 32 rows of the slab.
All inputs are finite; a program needn't handle non-finite values.
Results may differ from a plain program's by a relative error of at most 0.007.
Values may be sent and summed in bfloat16 or wider, within the bound.
No kernel may reach another device: no remote copies, remote signals or barrier semaphores. Data moves between devices by JAX's collectives and lax.ppermute only.
A program may use at most 256 MiB of HBM per device.

v0:
```python
import math

import jax
import jax.numpy as jnp
from jax import lax
from jax.experimental import pallas as pl
from jax.experimental.pallas import tpu as pltpu
from jax.sharding import PartitionSpec as P

HEADS = 16
GRID_ROWS = 16
BAND = 8
RIM = 2
EPSILON = 1e-06
CHUNK = 256
ROOT = math.sqrt(2.0 / math.pi)
CUBIC = 0.044715
F32 = jnp.float32
BF16 = jnp.bfloat16
VMEM_LIMIT = 56 * 1024 * 1024


def nt_dot(left, right):
    return lax.dot_general(left, right, (((1,), (1,)), ((), ())), preferred_element_type=F32)


def tn_dot(left, right):
    return lax.dot_general(left, right, (((0,), (0,)), ((), ())), preferred_element_type=F32)


def nn_dot(left, right):
    return jnp.dot(left, right, preferred_element_type=F32)


def rms_scale(values):
    return lax.rsqrt(jnp.mean(values * values, -1, keepdims=True) + EPSILON)


def gelu_and_slope(v):
    square = v * v
    cdf = 0.5 + 0.5 * jnp.tanh(v * (ROOT + (ROOT * CUBIC) * square))
    value = v * cdf
    slope = cdf + (value - value * cdf) * (2.0 * ROOT + (6.0 * ROOT * CUBIC) * square)
    return value, slope


def whole(shape, space=None):
    zeros = (0,) * len(shape)
    return pl.BlockSpec(shape, lambda *_: zeros)


def params():
    return pltpu.CompilerParams(vmem_limit_bytes=VMEM_LIMIT)


def assemble_body(index_ref, features_ref, cotangent_ref, pair_ref, edge_ref, slab_ref, grad_ref, both):
    capacity = features_ref.shape[0]
    sent = GRID_ROWS - BAND + RIM
    both[0:capacity] = features_ref[...]
    both[capacity : capacity + sent] = pair_ref[0:sent]
    both[capacity + sent : capacity + sent + RIM] = edge_ref[...]
    for row in range(GRID_ROWS + 2 * RIM):
        slab_ref[row] = both[index_ref[row]]
    both[0:capacity] = cotangent_ref[...]
    both[capacity : capacity + BAND] = pair_ref[sent : sent + BAND]
    for row in range(GRID_ROWS):
        grad_ref[row] = both[index_ref[GRID_ROWS + 2 * RIM + row]]


def assemble(index, features, cotangent, pair_rows, edge_rows):
    capacity, cols, width = features.shape
    sent = GRID_ROWS - BAND + RIM
    return pl.pallas_call(
        assemble_body,
        in_specs=[
            pl.BlockSpec(memory_space=pltpu.SMEM),
            whole(features.shape),
            whole(cotangent.shape),
            whole(pair_rows.shape),
            whole(edge_rows.shape),
        ],
        out_specs=[whole((GRID_ROWS + 2 * RIM, cols, width)), whole((GRID_ROWS, cols, width))],
        out_shape=[
            jax.ShapeDtypeStruct((GRID_ROWS + 2 * RIM, cols, width), BF16),
            jax.ShapeDtypeStruct((GRID_ROWS, cols, width), BF16),
        ],
        grid=(1,),
        scratch_shapes=[pltpu.VMEM((capacity + sent + RIM, cols, width), BF16)],
        compiler_params=params(),
        name="assemble",
    )(index, features, cotangent, pair_rows, edge_rows)


def column_sums(total_left, total_mid, total_right, column, last):
    from_left = pltpu.roll(total_left, 1, 0)
    from_right = pltpu.roll(total_right, last, 0)
    return (
        total_mid
        + jnp.where(column == 0, 0.0, from_left)
        + jnp.where(column == last, 0.0, from_right)
    )


def forward_body(slab_ref, expand_ref, taps_ref, project_ref, first_ref, normed_ref, slope_one_ref,
                 slope_two_ref, normed_one, hidden, hidden_two, total):
    step = pl.program_id(0)
    rows, cols, width = slab_ref.shape
    own = rows - 2 * RIM
    chunk = expand_ref.shape[1]

    @pl.when(step == 0)
    def _():
        values = slab_ref[...].astype(F32).reshape(rows * cols, width)
        normed_one[...] = (values * rms_scale(values)).astype(BF16)
        total[...] = values[RIM * cols : (RIM + own) * cols]

    def expand(row, carry):
        start = pl.multiple_of(row * (2 * cols), 2 * cols)
        expanded = nn_dot(normed_one[pl.ds(start, 2 * cols), :], expand_ref[...])
        value, slope = gelu_and_slope(expanded)
        hidden[pl.ds(2 * row, 2)] = value.astype(BF16).astype(F32).reshape(2, cols, chunk)
        slope_one_ref[pl.ds(2 * row, 2)] = slope.astype(BF16).reshape(2, cols, chunk)
        return carry

    lax.fori_loop(0, rows // 2, expand, 0, unroll=2)

    taps = taps_ref[...].astype(F32)
    column = lax.broadcasted_iota(jnp.int32, (cols, chunk), 0)

    def mix(row, carry):
        above, here, below = hidden[row], hidden[row + 1], hidden[row + 2]
        sums = [
            taps[b : b + 1] * above + taps[3 + b : 4 + b] * here + taps[6 + b : 7 + b] * below
            for b in range(3)
        ]
        mixed = column_sums(sums[0], sums[1], sums[2], column, cols - 1)
        value, slope = gelu_and_slope(mixed)
        hidden_two[pl.ds(pl.multiple_of(row * cols, cols), cols), :] = value.astype(BF16)
        slope_two_ref[row] = slope.astype(BF16)
        return carry

    lax.fori_loop(0, rows - 2, mix, 0, unroll=2)
    total[...] += nn_dot(hidden_two[cols : cols + own * cols, :], project_ref[...])

    @pl.when(step == pl.num_programs(0) - 1)
    def _():
        first = total[...]
        first_ref[...] = first.reshape(own, cols, width)
        normed_ref[...] = (first * rms_scale(first)).astype(BF16).reshape(own, cols, width)


def forward(slab, w_expand, kernel, w_project):
    rows, cols, width = slab.shape
    own = rows - 2 * RIM
    hidden_width = w_expand.shape[1]
    steps = hidden_width // CHUNK
    return pl.pallas_call(
        forward_body,
        grid=(steps,),
        in_specs=[
            whole(slab.shape),
            pl.BlockSpec((width, CHUNK), lambda j: (0, j)),
            pl.BlockSpec((9, CHUNK), lambda j: (0, j)),
            pl.BlockSpec((CHUNK, width), lambda j: (j, 0)),
        ],
        out_specs=[
            whole((own, cols, width)),
            whole((own, cols, width)),
            pl.BlockSpec((rows, cols, CHUNK), lambda j: (0, 0, j)),
            pl.BlockSpec((rows - 2, cols, CHUNK), lambda j: (0, 0, j)),
        ],
        out_shape=[
            jax.ShapeDtypeStruct((own, cols, width), F32),
            jax.ShapeDtypeStruct((own, cols, width), BF16),
            jax.ShapeDtypeStruct((rows, cols, hidden_width), BF16),
            jax.ShapeDtypeStruct((rows - 2, cols, hidden_width), BF16),
        ],
        scratch_shapes=[
            pltpu.VMEM((rows * cols, width), BF16),
            pltpu.VMEM((rows, cols, CHUNK), F32),
            pltpu.VMEM(((rows - 2) * cols, CHUNK), BF16),
            pltpu.VMEM((own * cols, width), F32),
        ],
        compiler_params=params(),
        cost_estimate=pl.CostEstimate(
            flops=4 * rows * cols * width * hidden_width,
            bytes_accessed=12 * 1024 * 1024,
            transcendentals=2 * rows * cols * hidden_width,
        ),
        name="bottleneck_forward",
    )(slab, w_expand, kernel, w_project)


def attention_body(normed_ref, cotangent_ref, qkv_ref, out_ref, attended_ref, grad_ref,
                   projected, grad_attended, grad_projected, attended):
    groups, _, cols, width = normed_ref.shape
    tokens = groups * cols
    windows = cols // 8
    span = groups * 8
    head_dim = width // HEADS
    lanes = 128
    heads = lanes // head_dim
    scale = 1.0 / math.sqrt(head_dim)

    inner = lax.broadcasted_iota(jnp.int32, (tokens, tokens), 0)
    outer = lax.broadcasted_iota(jnp.int32, (tokens, tokens), 1)

    def window_place(order):
        return (order // 8) % groups * cols + order % 8 * windows + order // span

    to_windows = (window_place(inner) == outer).astype(BF16)
    to_rows = (window_place(outer) == inner).astype(BF16)

    normed = nn_dot(to_windows, normed_ref[...].reshape(tokens, width)).astype(BF16)
    projected[...] = nn_dot(normed, qkv_ref[...]).astype(BF16)
    grad_rows = nn_dot(to_windows, cotangent_ref[...].reshape(tokens, width)).astype(BF16)
    grad_attended[...] = nt_dot(grad_rows, out_ref[...]).astype(BF16)

    lane_head = lax.broadcasted_iota(jnp.int32, (heads, span, lanes), 2) // head_dim
    own_head = lane_head == lax.broadcasted_iota(jnp.int32, (heads, span, lanes), 0)

    def spread(values):
        zeros = jnp.zeros((heads, span, lanes), F32)
        wide = jnp.where(own_head, values.astype(F32)[None], zeros)
        return wide.astype(BF16).reshape(heads * span, lanes)

    def collect(values):
        return jnp.sum(jnp.where(own_head, values.reshape(heads, span, lanes), 0.0), axis=0)

    def window(index, carry):
        rows = pl.ds(pl.multiple_of(index * span, span), span)
        for part in range(width // lanes):
            at = part * lanes
            q = projected[rows, at : at + lanes]
            k = projected[rows, width + at : width + at + lanes]
            v = projected[rows, 2 * width + at : 2 * width + at + lanes]
            g = grad_attended[rows, at : at + lanes]
            q_wide = spread(q)
            g_wide = spread(g)
            scores = nt_dot(k, q_wide) * scale
            powers = jnp.exp(scores - jnp.max(scores, axis=0, keepdims=True))
            weights = powers / jnp.sum(powers, axis=0, keepdims=True)
            half = weights.astype(BF16)
            grad_weights = nt_dot(v, g_wide)
            row_dot = jnp.sum(weights * grad_weights, axis=0, keepdims=True)
            grad_scores = (weights * (grad_weights - row_dot)).astype(BF16)
            attended[rows, at : at + lanes] = collect(tn_dot(half, v)).astype(BF16)
            grad_projected[rows, at : at + lanes] = (
                collect(tn_dot(grad_scores, k)) * scale
            ).astype(BF16)
            grad_projected[rows, width + at : width + at + lanes] = (
                nn_dot(grad_scores, q_wide) * scale
            ).astype(BF16)
            grad_projected[rows, 2 * width + at : 2 * width + at + lanes] = nn_dot(
                half, g_wide
            ).astype(BF16)
        return carry

    lax.fori_loop(0, windows, window, 0)

    grad_normed = nt_dot(grad_projected[...], qkv_ref[...]).astype(BF16)
    shape = (groups, 1, cols, width)
    grad_ref[...] = nn_dot(to_rows, grad_normed).astype(BF16).reshape(shape)
    attended_ref[...] = nn_dot(to_rows, attended[...]).astype(BF16).reshape(shape)


def attention(normed, cotangent, w_qkv, w_out):
    groups, own, cols, width = normed.shape
    tokens = groups * cols
    block = pl.BlockSpec((groups, 1, cols, width), lambda r: (0, r, 0, 0))
    out = jax.ShapeDtypeStruct(normed.shape, BF16)
    return pl.pallas_call(
        attention_body,
        grid=(own,),
        in_specs=[block, block, whole(w_qkv.shape), whole(w_out.shape)],
        out_specs=[block, block],
        out_shape=[out, out],
        scratch_shapes=[
            pltpu.VMEM((tokens, 3 * width), BF16),
            pltpu.VMEM((tokens, width), BF16),
            pltpu.VMEM((tokens, 3 * width), BF16),
            pltpu.VMEM((tokens, width), BF16),
        ],
        compiler_params=params(),
        cost_estimate=pl.CostEstimate(
            flops=20 * own * tokens * width * width,
            bytes_accessed=4 * 1024 * 1024,
            transcendentals=own * tokens * 64 * HEADS,
        ),
        name="window_attention",
    )(normed, cotangent, w_qkv, w_out)


def norm_grad_body(first_ref, grad_ref, cotangent_ref, grad_first_ref, grad_half_ref):
    rows, cols, width = first_ref.shape
    first = first_ref[...]
    rms = rms_scale(first)
    normed = first * rms
    grad = grad_ref[...].astype(F32)
    inner = jnp.mean(grad * normed, -1, keepdims=True)
    result = cotangent_ref[...].astype(F32) + rms * (grad - normed * inner)
    grad_first_ref[...] = result
    grad_half_ref[...] = result.astype(BF16)


def norm_grad(first, grad, cotangent):
    rows, cols, width = first.shape
    block = pl.BlockSpec((4, cols, width), lambda r: (r, 0, 0))
    return pl.pallas_call(
        norm_grad_body,
        grid=(rows // 4,),
        in_specs=[block, block, block],
        out_specs=[block, block],
        out_shape=[
            jax.ShapeDtypeStruct(first.shape, F32),
            jax.ShapeDtypeStruct(first.shape, BF16),
        ],
        compiler_params=params(),
        name="norm_grad",
    )(first, grad, cotangent)


def backward_body(slab_ref, grad_first_ref, half_ref, above_ref, below_ref, slope_one_ref, slope_two_ref,
                  expand_ref, taps_ref, project_ref, out_ref, grad_rows, mixed, expanded, total):
    step = pl.program_id(0)
    own, cols, width = half_ref.shape
    chunk = expand_ref.shape[1]

    @pl.when(step == 0)
    def _():
        grad_rows[0:cols] = above_ref[...].reshape(cols, width)
        grad_rows[cols : cols + own * cols] = half_ref[...].reshape(own * cols, width)
        grad_rows[cols + own * cols :] = below_ref[...].reshape(cols, width)
        total[...] = jnp.zeros_like(total)

    def spread(row, carry):
        start = pl.multiple_of(row * (2 * cols), 2 * cols)
        grad = nt_dot(grad_rows[pl.ds(start, 2 * cols), :], project_ref[...])
        slope = slope_two_ref[pl.ds(2 * row, 2)].astype(F32).reshape(2 * cols, chunk)
        mixed[pl.ds(2 * row, 2)] = (grad * slope).astype(BF16).astype(F32).reshape(2, cols, chunk)
        return carry

    lax.fori_loop(0, (own + 2) // 2, spread, 0, unroll=2)

    taps = taps_ref[...].astype(F32)
    column = lax.broadcasted_iota(jnp.int32, (cols, chunk), 0)

    def unmix(row, carry):
        above, here, below = mixed[row], mixed[row + 1], mixed[row + 2]
        sums = [
            taps[8 - b : 9 - b] * above + taps[5 - b : 6 - b] * here + taps[2 - b : 3 - b] * below
            for b in range(3)
        ]
        grad = column_sums(sums[0], sums[1], sums[2], column, cols - 1)
        slope = slope_one_ref[row + RIM].astype(F32)
        expanded[pl.ds(pl.multiple_of(row * cols, cols), cols), :] = (grad * slope).astype(BF16)
        return carry

    lax.fori_loop(0, own, unmix, 0, unroll=2)
    total[...] += nt_dot(expanded[...], expand_ref[...])

    @pl.when(step == pl.num_programs(0) - 1)
    def _():
        values = slab_ref[RIM : RIM + own].astype(F32).reshape(own * cols, width)
        rms = rms_scale(values)
        normed = values * rms
        grad = total[...]
        inner = jnp.mean(grad * normed, -1, keepdims=True)
        result = grad_first_ref[...].reshape(own * cols, width) + rms * (grad - normed * inner)
        out_ref[...] = result.astype(BF16).reshape(own, cols, width)


def backward(slab, grad_first, grad_half, above, below, slope_one, slope_two, w_expand, kernel, w_project):
    own, cols, width = grad_half.shape
    hidden_width = w_expand.shape[1]
    rows = slab.shape[0]
    return pl.pallas_call(
        backward_body,
        grid=(hidden_width // CHUNK,),
        in_specs=[
            whole(slab.shape),
            whole(grad_first.shape),
            whole(grad_half.shape),
            whole(above.shape),
            whole(below.shape),
            pl.BlockSpec((rows, cols, CHUNK), lambda j: (0, 0, j)),
            pl.BlockSpec((rows - 2, cols, CHUNK), lambda j: (0, 0, j)),
            pl.BlockSpec((width, CHUNK), lambda j: (0, j)),
            pl.BlockSpec((9, CHUNK), lambda j: (0, j)),
            pl.BlockSpec((CHUNK, width), lambda j: (j, 0)),
        ],
        out_specs=whole((own, cols, width)),
        out_shape=jax.ShapeDtypeStruct((own, cols, width), BF16),
        scratch_shapes=[
            pltpu.VMEM(((own + 2) * cols, width), BF16),
            pltpu.VMEM((own + 2, cols, CHUNK), F32),
            pltpu.VMEM((own * cols, CHUNK), BF16),
            pltpu.VMEM((own * cols, width), F32),
        ],
        compiler_params=params(),
        cost_estimate=pl.CostEstimate(
            flops=4 * rows * cols * width * hidden_width,
            bytes_accessed=12 * 1024 * 1024,
            transcendentals=0,
        ),
        name="bottleneck_backward",
    )(slab, grad_first, grad_half, above, below, slope_one, slope_two, w_expand, kernel, w_project)


def project_body(first_ref, attended_ref, out_ref, final_ref):
    rows, cols, width = first_ref.shape
    added = nn_dot(attended_ref[...].reshape(rows * cols, width), out_ref[...])
    final_ref[...] = (first_ref[...] + added.reshape(rows, cols, width)).astype(BF16)


def project(first, attended, w_out):
    rows, cols, width = first.shape
    block = pl.BlockSpec((4, cols, width), lambda r: (r, 0, 0))
    return pl.pallas_call(
        project_body,
        grid=(rows // 4,),
        in_specs=[block, block, whole(w_out.shape)],
        out_specs=block,
        out_shape=jax.ShapeDtypeStruct(first.shape, BF16),
        compiler_params=params(),
        name="output_projection",
    )(first, attended, w_out)


def window_groups(size):
    stride = size // 8
    return [[first + stride * k for k in range(8)] for first in range(stride)]


def exchange_windows(rows):
    return lax.all_to_all(
        rows, "row", split_axis=0, concat_axis=0, tiled=True, axis_index_groups=window_groups(lax.axis_size("row"))
    )


def swap_pair(rows):
    size = lax.axis_size("row")
    return lax.ppermute(rows, "row", [(i, i ^ 1) for i in range(size)])


def place_rows(even, parity, leader_share):
    size = GRID_ROWS
    first, second = even[:BAND], even[BAND:]
    other = swap_pair(jnp.where(parity == 0, second, first))
    share = jnp.where(parity == 0, leader_share, 2 * size - leader_share)
    zeros = jnp.zeros_like(first)
    leads = parity == 0
    low = jnp.where(leads | (share == size), first, jnp.where(share < size, second, other))
    mid = jnp.where(share < size, zeros, jnp.where(leads | (share == size), second, first))
    high = jnp.where(share > size, jnp.where(leads, other, second), zeros)
    return jnp.concatenate([low, mid, high], 0)


def on_device(features, row_bands, w_expand, kernel, w_project, w_qkv, w_out, cotangent):
    capacity, cols, width = features.shape
    size = lax.axis_size("row")
    device = lax.axis_index("row")
    parity = device % 2
    leads = parity == 0
    leader_share = BAND * row_bands[device - parity]
    own_share = BAND * row_bands[device]
    sent = GRID_ROWS - BAND + RIM

    payload = jnp.concatenate(
        [
            lax.dynamic_slice_in_dim(features, jnp.where(leads, capacity - sent, 0), sent, 0),
            lax.dynamic_slice_in_dim(cotangent, jnp.where(leads, capacity - BAND, 0), BAND, 0),
        ],
        0,
    )
    pair_rows = swap_pair(payload)
    rim = lax.dynamic_slice_in_dim(features, jnp.where(leads, 0, own_share - RIM), RIM, 0)
    pairs = [(i, i + 1) for i in range(1, size - 1, 2)]
    edge_rows = lax.ppermute(rim, "row", pairs + [(j, i) for i, j in pairs])

    place = jnp.arange(GRID_ROWS + 2 * RIM) - RIM + GRID_ROWS * parity
    in_own = jnp.where(leads, place < leader_share, place >= leader_share)
    own_index = jnp.where(leads, place, place - leader_share)
    pair_index = jnp.where(leads, place - leader_share, place - (GRID_ROWS - RIM))
    slab_index = jnp.where(in_own, own_index, capacity + pair_index)
    slab_index = jnp.where(leads & (place < 0), capacity + sent + RIM + place, slab_index)
    beyond = place - 2 * GRID_ROWS
    slab_index = jnp.where(~leads & (beyond >= 0), capacity + sent + beyond, slab_index)
    pair_index = jnp.where(leads, place - leader_share, place - GRID_ROWS)
    grad_index = jnp.where(in_own, own_index, capacity + pair_index)[RIM : RIM + GRID_ROWS]
    index = jnp.concatenate([slab_index, grad_index]).astype(jnp.int32)

    slab, grad_slab = assemble(index, features, cotangent, pair_rows, edge_rows)
    grad_windows = exchange_windows(grad_slab)
    first, normed, slope_one, slope_two = forward(slab, w_expand, kernel, w_project)
    normed_windows = exchange_windows(normed)
    shape = (8, GRID_ROWS // 8, cols, width)
    attended, grad_normed = attention(
        normed_windows.reshape(shape), grad_windows.reshape(shape), w_qkv, w_out
    )
    grad_normed_rows = exchange_windows(grad_normed.reshape(GRID_ROWS, cols, width))
    attended_rows = exchange_windows(attended.reshape(GRID_ROWS, cols, width))
    grad_first, grad_half = norm_grad(first, grad_normed_rows, grad_slab)
    up = [(i, i + 1) for i in range(size - 1)]
    above = lax.ppermute(grad_half[GRID_ROWS - 1 :], "row", up)
    below = lax.ppermute(grad_half[:1], "row", [(j, i) for i, j in up])
    grad_input = backward(
        slab, grad_first, grad_half, above, below, slope_one, slope_two, w_expand, kernel, w_project
    )
    final = project(first, attended_rows, w_out)
    return (
        place_rows(final, parity, leader_share),
        place_rows(grad_input, parity, leader_share),
    )


def solution(mesh):
    return jax.shard_map(
        on_device,
        mesh=mesh,
        in_specs=(
            P(("parts", "row"), None, None),
            P("parts"),
            P(),
            P(),
            P(),
            P(),
            P(),
            P(("parts", "row"), None, None),
        ),
        out_specs=(P(("parts", "row"), None, None), P(("parts", "row"), None, None)),
        check_vma=False,
    )
```

profile of v0, /device:TPU:0, one launch (start us, length us, event | category | flops | bytes accessed | tf_op | source)
XLA Modules:
  0.0 162.4 jit_solution(14989693371909080493)
XLA Ops:
  0.7 1.0 constant_dynamic-slice_fusion.2
  1.7 1.0 constant_dynamic-slice_fusion.1
  4.5 0.8 constant_dynamic-slice_fusion
  6.7 0.7 pad_add_fusion.index_ref
  8.0 0.8 copy-done.4
  8.8 2.7 %assemble.1 = (bf16[20,32,512]{2,1,0:T(8,128)(2,1)}, bf16[16,32,512]{2,1,0:T(8,128)(2,1)}) custom-call(s32[36]{0:T(128)} %pad_add_fusion.index_ref, bf16[24,32,512]{2,1,0:T(8,128)(2,1)} %features_ref.1, bf16[24,32,512]{2,1,0:T(8,128)(2,1)} %cotangent_ref.1, bf16[18,32,512]{2,1,0:T(8,128)(2,1)} %copy-done.4, bf16[2,32,512]{2,1,0:T(8,128)(2,1)} %copy-done.5), custom_call_target="tpu_custom_call" | custom-call | tf_op jit(solution)/shard_map/assemble/pallas_call | solution.py:73
  11.5 23.1 %bottleneck_forward.1 = (f32[16,32,512]{2,1,0:T(8,128)}, bf16[16,32,512]{2,1,0:T(8,128)(2,1)}, bf16[20,32,2048]{2,1,0:T(8,128)(2,1)}, bf16[18,32,2048]{2,1,0:T(8,128)(2,1)}) custom-call(bf16[20,32,512]{2,1,0:T(8,128)(2,1)} %get-tuple-element.12.slab_ref, bf16[512,2048]{1,0:T(8,128)(2,1)} %expand_ref.3, bf16[9,2048]{1,0:T(8,128)(2,1)} %taps_ref.3, ...), custom_call_target="tpu_custom_call" | custom-call | flops 2684354560 | bytes 12582912 | tf_op jit(solution)/shard_map/bottleneck_forward/pallas_call | solution.py:157
  34.6 25.5 %all_to_all.20 = bf16[16,32,512]{2,1,0:T(8,128)(2,1)} all-to-all(bf16[16,32,512]{2,1,0:T(8,128)(2,1)} %get-tuple-element.14), channel_id=1, replica_groups={{0,2,4,6,8,10,12,14},{1,3,5,7,9,11,13,15},{16,18,20,22,24,26,28,30},{17..., dimensions={0} | all-to-all | bytes 1048576 | tf_op jit(solution)/shard_map/all_to_all | solution.py:436
  60.1 18.1 %all_to_all.21 = bf16[16,32,512]{2,1,0:T(8,128)(2,1)} all-to-all(bf16[16,32,512]{2,1,0:T(8,128)(2,1)S(1)} %copy-done.3), channel_id=1, replica_groups={{0,2,4,6,8,10,12,14},{1,3,5,7,9,11,13,15},{16,18,20,22,24,26,28,30},{17..., dimensions={0} | all-to-all | bytes 1048576 | tf_op jit(solution)/shard_map/all_to_all | solution.py:436
  78.2 17.3 %window_attention.1 = (bf16[8,2,32,512]{3,2,1,0:T(8,128)(2,1)}, bf16[8,2,32,512]{3,2,1,0:T(8,128)(2,1)}) custom-call(bf16[8,2,32,512]{3,2,1,0:T(8,128)(2,1)} %bitcast.7, bf16[8,2,32,512]{3,2,1,0:T(8,128)(2,1)} %bitcast.9, bf16[512,1536]{1,0:T(8,128)(2,1)} %qkv_ref.1, bf16[512,512]{1,0:T(8,128)(2,1)} %out_ref.3), custom_call_target="tpu_custom_call" | custom-call | flops 2684354560 | bytes 4194304 | tf_op jit(solution)/shard_map/window_attention/pallas_call | solution.py:272
  95.4 17.8 %all_to_all.22.grad_ref = bf16[16,32,512]{2,1,0:T(8,128)(2,1)} all-to-all(bf16[16,32,512]{2,1,0:T(8,128)(2,1)} %bitcast.8), channel_id=1, replica_groups={{0,2,4,6,8,10,12,14},{1,3,5,7,9,11,13,15},{16,18,20,22,24,26,28,30},{17..., dimensions={0} | all-to-all | bytes 1048576 | tf_op jit(solution)/shard_map/all_to_all | solution.py:436
  113.3 3.6 %all-to-all-start.2 = ((bf16[16,32,512]{2,1,0:T(8,128)(2,1)}), bf16[16,32,512]{2,1,0:T(8,128)(2,1)S(1)}, u32[]{:S(2)}, u32[]{:S(2)}) async-start(bf16[16,32,512]{2,1,0:T(8,128)(2,1)} %bitcast.6), calls=%async_computation.2 | async-start | bytes 1048576 | tf_op jit(solution)/shard_map/all_to_all | solution.py:436
  116.9 4.1 %norm_grad.1 = (f32[16,32,512]{2,1,0:T(8,128)}, bf16[16,32,512]{2,1,0:T(8,128)(2,1)}) custom-call(f32[16,32,512]{2,1,0:T(8,128)} %get-tuple-element.13.first_ref, bf16[16,32,512]{2,1,0:T(8,128)(2,1)} %all_to_all.22.grad_ref, bf16[16,32,512]{2,1,0:T(8,128)(2,1)} %get-tuple-element.15.cotangent_ref), custom_call_target="tpu_custom_call" | custom-call | tf_op jit(solution)/shard_map/norm_grad/pallas_call | solution.py:309
  121.0 0.8 fusion.4
  121.8 1.3 collective-permute-start.3
  123.1 1.3 collective-permute-start.4
  124.4 6.6 %all-to-all-done.2.attended_ref = bf16[16,32,512]{2,1,0:T(8,128)(2,1)S(1)} async-done(((bf16[16,32,512]{2,1,0:T(8,128)(2,1)}), bf16[16,32,512]{2,1,0:T(8,128)(2,1)S(1)}, u32[]{:S(2)}, u32[]{:S(2)}) %all-to-all-start.2) | async-done | bytes 524320 | tf_op jit(solution)/shard_map/all_to_all | solution.py:436
  131.0 0.8 copy-done.2
  131.7 4.0 %output_projection.1 = bf16[16,32,512]{2,1,0:T(8,128)(2,1)} custom-call(f32[16,32,512]{2,1,0:T(8,128)} %get-tuple-element.13.first_ref, bf16[16,32,512]{2,1,0:T(8,128)(2,1)} %copy-done.2, bf16[512,512]{1,0:T(8,128)(2,1)} %out_ref.3), custom_call_target="tpu_custom_call" | custom-call | tf_op jit(solution)/shard_map/output_projection/pallas_call | solution.py:419
  135.7 1.1 broadcast_select_fusion.1
  137.5 21.0 %bottleneck_backward.1 = bf16[16,32,512]{2,1,0:T(8,128)(2,1)} custom-call(bf16[20,32,512]{2,1,0:T(8,128)(2,1)} %get-tuple-element.12.slab_ref, f32[16,32,512]{2,1,0:T(8,128)} %get-tuple-element.18.grad_first_ref, bf16[16,32,512]{2,1,0:T(8,128)(2,1)} %get-tuple-element.19.half_ref, bf16[1,32,512]{2,1,0:T(8,128)(2,1)} %copy-done.6, ...), custom_call_target="tpu_custom_call" | custom-call | flops 2684354560 | bytes 12582912 | tf_op jit(solution)/shard_map/bottleneck_backward/pallas_call | solution.py:377
  158.5 1.1 broadcast_select_fusion
  160.2 1.0 pad_maximum_fusion
  161.4 1.0 pad_maximum_fusion.1
  (33 shorter events, 4.0 us)
Async XLA Ops:
  0.6 2.6 %copy-start.8 = (s32[16]{0:T(128)S(1)}, s32[16]{0:T(128)}, u32[]{:S(2)}) copy-start(s32[16]{0:T(128)} %param.9) | copy-start | bytes 196
  2.7 4.7 %collective-permute-start = (bf16[18,32,512]{2,1,0:T(8,128)(2,1)S(1)}, bf16[18,32,512]{2,1,0:T(8,128)(2,1)S(1)}, u32[]{:S(2)}, u32[]{:S(2)}) collective-permute-start(bf16[18,32,512]{2,1,0:T(8,128)(2,1)S(1)} %pad_maximum_fusion.2), channel_id=1, source_target_pairs={{0,1},{1,0},{2,3},{3,2},{4,5},{5,4},{6,7},{7,6},{8,9},{9,8},{10,11... | collective-permute-start | bytes 1769480 | tf_op jit(solution)/shard_map/ppermute | solution.py:443
  5.3 2.1 %collective-permute-start.1 = (bf16[2,32,512]{2,1,0:T(8,128)(2,1)S(1)}, bf16[2,32,512]{2,1,0:T(8,128)(2,1)S(1)}, u32[]{:S(2)}, u32[]{:S(2)}) collective-permute-start(bf16[2,32,512]{2,1,0:T(8,128)(2,1)S(1)} %constant_dynamic-slice_fusion), channel_id=1, source_target_pairs={{1,2},{3,4},{5,6},{7,8},{9,10},{11,12},{13,14},{2,1},{4,3},{6,5},{... | collective-permute-start | bytes 196616 | tf_op jit(solution)/shard_map/ppermute | solution.py:479
  7.4 0.6 copy-start.5
  8.0 0.8 copy-start.4
  11.5 48.5 %copy-start.3 = (bf16[16,32,512]{2,1,0:T(8,128)(2,1)S(1)}, bf16[16,32,512]{2,1,0:T(8,128)(2,1)}, u32[]{:S(2)}) copy-start(bf16[16,32,512]{2,1,0:T(8,128)(2,1)} %get-tuple-element.15.cotangent_ref) | copy-start | bytes 1572868
  113.3 17.7 %all-to-all-start.2 = ((bf16[16,32,512]{2,1,0:T(8,128)(2,1)}), bf16[16,32,512]{2,1,0:T(8,128)(2,1)S(1)}, u32[]{:S(2)}, u32[]{:S(2)}) async-start(bf16[16,32,512]{2,1,0:T(8,128)(2,1)} %bitcast.6), calls=%async_computation.2 | async-start | bytes 1048576 | tf_op jit(solution)/shard_map/all_to_all | solution.py:436
  121.8 15.1 %collective-permute-start.3 = (bf16[1,32,512]{2,1,0:T(8,128)(2,1)S(1)}, bf16[1,32,512]{2,1,0:T(8,128)(2,1)S(1)}, u32[]{:S(2)}, u32[]{:S(2)}) collective-permute-start(bf16[1,32,512]{2,1,0:T(8,128)(2,1)S(1)} %get-tuple-element.28), channel_id=1, source_target_pairs={{0,1},{1,2},{2,3},{3,4},{4,5},{5,6},{6,7},{7,8},{8,9},{9,10},{10,1... | collective-permute-start | bytes 98312 | tf_op jit(solution)/shard_map/ppermute | solution.py:505
  123.1 13.8 %collective-permute-start.4 = (bf16[1,32,512]{2,1,0:T(8,128)(2,1)S(1)}, bf16[1,32,512]{2,1,0:T(8,128)(2,1)S(1)}, u32[]{:S(2)}, u32[]{:S(2)}) collective-permute-start(bf16[1,32,512]{2,1,0:T(8,128)(2,1)S(1)} %get-tuple-element.27), channel_id=1, source_target_pairs={{1,0},{2,1},{3,2},{4,3},{5,4},{6,5},{7,6},{8,7},{9,8},{10,9},{11,1... | collective-permute-start | bytes 98312 | tf_op jit(solution)/shard_map/ppermute | solution.py:506
  131.0 0.8 copy-start.2
  136.8 23.4 %collective-permute-start.2 = (bf16[8,32,512]{2,1,0:T(8,128)(2,1)S(1)}, bf16[8,32,512]{2,1,0:T(8,128)(2,1)S(1)}, u32[]{:S(2)}, u32[]{:S(2)}) collective-permute-start(bf16[8,32,512]{2,1,0:T(8,128)(2,1)S(1)} %broadcast_select_fusion.1), channel_id=1, source_target_pairs={{0,1},{1,0},{2,3},{3,2},{4,5},{5,4},{6,7},{7,6},{8,9},{9,8},{10,11... | collective-permute-start | bytes 786440 | tf_op jit(solution)/shard_map/ppermute | solution.py:443
  136.9 0.6 copy-start.6
  136.9 0.6 copy-start.7
  137.5 22.6 %copy-start.1 = (bf16[16,32,512]{2,1,0:T(8,128)(2,1)S(1)}, bf16[16,32,512]{2,1,0:T(8,128)(2,1)}, u32[]{:S(2)}) copy-start(bf16[16,32,512]{2,1,0:T(8,128)(2,1)} %output_projection.1) | copy-start | bytes 1572868
  158.5 2.8 %copy-start = (bf16[16,32,512]{2,1,0:T(8,128)(2,1)S(1)}, bf16[16,32,512]{2,1,0:T(8,128)(2,1)}, u32[]{:S(2)}) copy-start(bf16[16,32,512]{2,1,0:T(8,128)(2,1)} %bottleneck_backward.1) | copy-start | bytes 1572868
  159.6 1.7 %collective-permute-start.5 = (bf16[8,32,512]{2,1,0:T(8,128)(2,1)S(1)}, bf16[8,32,512]{2,1,0:T(8,128)(2,1)S(1)}, u32[]{:S(2)}, u32[]{:S(2)}) collective-permute-start(bf16[8,32,512]{2,1,0:T(8,128)(2,1)S(1)} %broadcast_select_fusion), channel_id=1, source_target_pairs={{0,1},{1,0},{2,3},{3,2},{4,5},{5,4},{6,7},{7,6},{8,9},{9,8},{10,11... | collective-permute-start | bytes 786440 | tf_op jit(solution)/shard_map/ppermute | solution.py:443
where the time goes:
time: 163 us; the launch traced here: 162 us
  Pallas kernels  72.1 us (44%)
  blocking collectives  61.4 us (38%)
  starting transfers between devices  8 us (5%)
  local copies, waits for them, and re-layouts  7.11 us (4%)
  waiting for transfers between devices  6.72 us (4%)
  other arithmetic  4.96 us (3%)
  between operations  2.1 us (1%)
    all_to_all x3, blocking collectives, exchange_windows(): lax.all_to_all(rows, 'row', split_axis=0, concat_axis=0, tiled=True, axis...  61.4 us
    pallas_call x1, Pallas kernels, forward(): pl.pallas_call(forward_body, grid=(steps,), in_specs=[whole(slab.shape),...  23.1 us
    pallas_call x1, Pallas kernels, backward(): pl.pallas_call(backward_body, grid=(hidden_width // CHUNK,), in_specs=[wh...  21 us
    pallas_call x1, Pallas kernels, attention(): pl.pallas_call(attention_body, grid=(own,), in_specs=[block, block, whole...  17.3 us
    all_to_all x1, waiting for transfers between devices, exchange_windows(): lax.all_to_all(rows, 'row', split_axis=0, concat_axis=0, tiled=True, axis...  6.58 us
    pallas_call x1, Pallas kernels, norm_grad(): pl.pallas_call(norm_grad_body, grid=(rows // 4,), in_specs=[block, block,...  4.1 us
    pallas_call x1, Pallas kernels, project(): pl.pallas_call(project_body, grid=(rows // 4,), in_specs=[block, block, w...  4 us
    all_to_all x1, starting transfers between devices, exchange_windows(): lax.all_to_all(rows, 'row', split_axis=0, concat_axis=0, tiled=True, axis...  3.64 us
  transfers between devices with their start and end apart: 7, of which 2 were waited for; matrix products, arithmetic and copies ran while one was open for 4% of the time, Pallas kernels for 18%

commit v1 on v0

v1 whole, which is shorter than its diff:
```python
import math

import jax
import jax.numpy as jnp
import numpy as np
from jax import lax
from jax.experimental import pallas as pl
from jax.experimental.pallas import tpu as pltpu
from jax.sharding import PartitionSpec as P

HEADS = 16
GRID_ROWS = 16
BAND = 8
RIM = 2
EPSILON = 1e-06
CHUNK = 256
LANES = 128
ROOT = math.sqrt(2.0 / math.pi)
CUBIC = 0.044715
F32 = jnp.float32
BF16 = jnp.bfloat16
VMEM_LIMIT = 56 * 1024 * 1024


def nt_dot(left, right):
    return lax.dot_general(left, right, (((1,), (1,)), ((), ())), preferred_element_type=F32)


def tn_dot(left, right):
    return lax.dot_general(left, right, (((0,), (0,)), ((), ())), preferred_element_type=F32)


def nn_dot(left, right):
    return jnp.dot(left, right, preferred_element_type=F32)


def rms_scale(values):
    return lax.rsqrt(jnp.mean(values * values, -1, keepdims=True) + EPSILON)


def gelu_and_slope(v):
    square = v * v
    cdf = 0.5 + 0.5 * jnp.tanh(v * (ROOT + (ROOT * CUBIC) * square))
    value = v * cdf
    slope = cdf + (value - value * cdf) * (2.0 * ROOT + (6.0 * ROOT * CUBIC) * square)
    return value, slope


def whole(shape, space=None):
    zeros = (0,) * len(shape)
    return pl.BlockSpec(shape, lambda *_: zeros)


def params():
    return pltpu.CompilerParams(vmem_limit_bytes=VMEM_LIMIT)


def start_pull(place_ref, index, sources, rows, target, sem):
    first = place_ref[2 * index + 1]
    for number, source in enumerate(sources):

        @pl.when(place_ref[2 * index] == number)
        def _():
            pltpu.make_async_copy(source.at[pl.ds(first, rows)], target, sem).start()


def wait_pull(sources, rows, target, sem):
    pltpu.make_async_copy(sources[0].at[pl.ds(0, rows)], target, sem).wait()


def even_body(place_ref, own_ref, other_ref, out_ref, sems):
    sources = (own_ref, other_ref)
    targets = [out_ref.at[pl.ds(BAND * half, BAND)] for half in range(2)]
    for half in range(2):
        start_pull(place_ref, half, sources, BAND, targets[half], sems.at[half])
    for half in range(2):
        wait_pull(sources, BAND, targets[half], sems.at[half])


def even_rows(places, own, other):
    capacity, cols, width = own.shape
    anywhere = pl.BlockSpec(memory_space=pl.ANY)
    return pl.pallas_call(
        even_body,
        in_specs=[pl.BlockSpec(memory_space=pltpu.SMEM), anywhere, anywhere],
        out_specs=anywhere,
        out_shape=jax.ShapeDtypeStruct((GRID_ROWS, cols, width), own.dtype),
        scratch_shapes=[pltpu.SemaphoreType.DMA((2,))],
        name="even_rows",
    )(places, own, other)


def column_sums(left, mid, right, column, last):
    from_left = jnp.where(column == 0, 0.0, pltpu.roll(left, 1, 0))
    from_right = jnp.where(column == last, 0.0, pltpu.roll(right, last, 0))
    return mid + from_left + from_right


def spread_taps(taps_ref, lanes, cols):
    taps = taps_ref[...].astype(F32)
    return [jnp.broadcast_to(taps[i : i + 1, lanes], (cols, LANES)) for i in range(9)]


def forward_body(place_ref, features_ref, other_ref, rim_ref, expand_ref, taps_ref, project_ref, first_ref,
                 normed_ref, slab_ref, slope_one_ref, slope_two_ref, slab, normed_one, hidden, hidden_two,
                 total, sems):
    step = pl.program_id(0)
    rows, cols, width = slab.shape
    own = rows - 2 * RIM
    chunk = expand_ref.shape[1]

    @pl.when(step == 0)
    def _():
        sources = (features_ref, other_ref, rim_ref)
        pieces = [(0, RIM), (RIM, BAND), (RIM + BAND, BAND), (RIM + 2 * BAND, RIM)]
        for index, (first, count) in enumerate(pieces):
            start_pull(place_ref, index, sources, count, slab.at[pl.ds(first, count)], sems.at[index])
        for index, (first, count) in enumerate(pieces):
            wait_pull(sources, count, slab.at[pl.ds(first, count)], sems.at[index])
        slab_ref[...] = slab[RIM : RIM + own]
        for row in range(0, rows, 2):
            at = slice(row * cols, (row + 2) * cols)
            values = slab[row : row + 2].astype(F32).reshape(2 * cols, width)
            normed_one[at] = (values * rms_scale(values)).astype(BF16)
        total[...] = slab[1 : rows - 1].astype(F32).reshape((rows - 2) * cols, width)

    for row in range(0, rows, 4):
        expanded = nn_dot(normed_one[row * cols : (row + 4) * cols, :], expand_ref[...])
        for inner in range(4):
            for lane in range(0, chunk, LANES):
                lanes = slice(lane, lane + LANES)
                value, slope = gelu_and_slope(expanded[inner * cols : (inner + 1) * cols, lanes])
                hidden[row + inner, :, lanes] = value.astype(BF16).astype(F32)
                if RIM <= row + inner < RIM + own:
                    slope_one_ref[row + inner - RIM, :, lanes] = slope.astype(BF16)

    column = lax.broadcasted_iota(jnp.int32, (cols, LANES), 0)
    for lane in range(0, chunk, LANES):
        lanes = slice(lane, lane + LANES)
        taps = spread_taps(taps_ref, lanes, cols)
        for row in range(rows - 2):
            near = [hidden[row + a, :, lanes] for a in range(3)]
            sums = [
                taps[b] * near[0] + taps[3 + b] * near[1] + taps[6 + b] * near[2] for b in range(3)
            ]
            mixed = column_sums(sums[0], sums[1], sums[2], column, cols - 1)
            value, slope = gelu_and_slope(mixed)
            hidden_two[row * cols : (row + 1) * cols, lanes] = value.astype(BF16)
            slope_two_ref[row, :, lanes] = slope.astype(BF16)
    total[...] += nn_dot(hidden_two[...], project_ref[...])

    @pl.when(step == pl.num_programs(0) - 1)
    def _():
        for row in range(rows - 2):
            first = total[row * cols : (row + 1) * cols]
            first_ref[row] = first
            if 1 <= row <= own:
                normed_ref[row - 1] = (first * rms_scale(first)).astype(BF16)


def forward(places, features, other, rim, w_expand, kernel, w_project):
    capacity, cols, width = features.shape
    own, rows = GRID_ROWS, GRID_ROWS + 2 * RIM
    hidden_width = w_expand.shape[1]
    anywhere = pl.BlockSpec(memory_space=pl.ANY)
    return pl.pallas_call(
        forward_body,
        grid=(hidden_width // CHUNK,),
        in_specs=[
            pl.BlockSpec(memory_space=pltpu.SMEM),
            anywhere,
            anywhere,
            anywhere,
            pl.BlockSpec((width, CHUNK), lambda j: (0, j)),
            pl.BlockSpec((9, CHUNK), lambda j: (0, j)),
            pl.BlockSpec((CHUNK, width), lambda j: (j, 0)),
        ],
        out_specs=[
            whole((rows - 2, cols, width)),
            whole((own, cols, width)),
            whole((own, cols, width)),
            pl.BlockSpec((own, cols, CHUNK), lambda j: (0, 0, j)),
            pl.BlockSpec((rows - 2, cols, CHUNK), lambda j: (0, 0, j)),
        ],
        out_shape=[
            jax.ShapeDtypeStruct((rows - 2, cols, width), F32),
            jax.ShapeDtypeStruct((own, cols, width), BF16),
            jax.ShapeDtypeStruct((own, cols, width), BF16),
            jax.ShapeDtypeStruct((own, cols, hidden_width), BF16),
            jax.ShapeDtypeStruct((rows - 2, cols, hidden_width), BF16),
        ],
        scratch_shapes=[
            pltpu.VMEM((rows, cols, width), BF16),
            pltpu.VMEM((rows * cols, width), BF16),
            pltpu.VMEM((rows, cols, CHUNK), F32),
            pltpu.VMEM(((rows - 2) * cols, CHUNK), BF16),
            pltpu.VMEM(((rows - 2) * cols, width), F32),
            pltpu.SemaphoreType.DMA((4,)),
        ],
        compiler_params=params(),
        cost_estimate=pl.CostEstimate(
            flops=4 * rows * cols * width * hidden_width,
            bytes_accessed=12 * 1024 * 1024,
            transcendentals=2 * rows * cols * hidden_width,
        ),
        name="bottleneck_forward",
    )(places, features, other, rim, w_expand, kernel, w_project)


def window_order(groups, cols):
    order = np.arange(groups * cols)
    span = groups * 8
    place = (order // 8) % groups * cols + order % 8 * (cols // 8) + order // span
    return (place[:, None] == order[None, :]).astype(np.float32)


def head_mask(span, head_dim):
    heads = LANES // head_dim
    row_head = np.arange(heads * span)[:, None] // span
    return (row_head == np.arange(LANES)[None, :] // head_dim).astype(np.float32)


def attention_body(normed_ref, cotangent_ref, order_ref, back_ref, mask_ref, qkv_ref, out_ref, added_ref,
                   grad_ref, projected, grad_attended, grad_projected, attended):
    groups, _, cols, width = normed_ref.shape
    tokens = groups * cols
    span = groups * 8
    head_dim = width // HEADS
    heads = LANES // head_dim
    scale = 1.0 / math.sqrt(head_dim)
    steepness = scale * math.log2(math.e)

    normed = nn_dot(order_ref[...], normed_ref[...].reshape(tokens, width)).astype(BF16)
    projected[...] = nn_dot(normed, qkv_ref[...]).astype(BF16)
    grad_rows = nn_dot(order_ref[...], cotangent_ref[...].reshape(tokens, width)).astype(BF16)
    grad_attended[...] = nt_dot(grad_rows, out_ref[...]).astype(BF16)

    lane_head = lax.broadcasted_iota(jnp.int32, (span, LANES), 1) // head_dim

    def spread(values):
        return jnp.concatenate([values] * heads, axis=0) * mask_ref[...]

    def collect(values):
        result = values[0:span]
        for head in range(1, heads):
            result = jnp.where(lane_head == head, values[head * span : (head + 1) * span], result)
        return result

    for index in range(cols // 8):
        rows = slice(index * span, (index + 1) * span)
        for part in range(width // LANES):
            q_at, k_at, v_at = (
                slice(t * width + part * LANES, t * width + (part + 1) * LANES) for t in range(3)
            )
            q, k, v = projected[rows, q_at], projected[rows, k_at], projected[rows, v_at]
            q_wide = spread(q)
            g_wide = spread(grad_attended[rows, q_at])
            scores = nt_dot(k, q_wide)
            powers = jnp.exp2((scores - jnp.max(scores, axis=0, keepdims=True)) * steepness)
            weights = powers * (1.0 / jnp.sum(powers, axis=0, keepdims=True))
            half = weights.astype(BF16)
            grad_weights = nt_dot(v, g_wide)
            row_dot = jnp.sum(weights * grad_weights, axis=0, keepdims=True)
            grad_scores = (weights * (grad_weights - row_dot)).astype(BF16)
            attended[rows, q_at] = collect(tn_dot(half, v)).astype(BF16)
            grad_projected[rows, q_at] = (collect(tn_dot(grad_scores, k)) * scale).astype(BF16)
            grad_projected[rows, k_at] = (nn_dot(grad_scores, q_wide) * scale).astype(BF16)
            grad_projected[rows, v_at] = nn_dot(half, g_wide).astype(BF16)

    shape = (groups, 1, cols, width)
    grad_normed = nt_dot(grad_projected[...], qkv_ref[...]).astype(BF16)
    grad_ref[...] = nn_dot(back_ref[...], grad_normed).astype(BF16).reshape(shape)
    in_rows = nn_dot(back_ref[...], attended[...]).astype(BF16)
    added_ref[...] = nn_dot(in_rows, out_ref[...]).astype(BF16).reshape(shape)


def attention(normed, cotangent, w_qkv, w_out):
    groups, own, cols, width = normed.shape
    tokens = groups * cols
    order = window_order(groups, cols)
    mask = head_mask(groups * 8, width // HEADS)
    block = pl.BlockSpec((groups, 1, cols, width), lambda r: (0, r, 0, 0))
    out = jax.ShapeDtypeStruct(normed.shape, BF16)
    return pl.pallas_call(
        attention_body,
        grid=(own,),
        in_specs=[
            block,
            block,
            whole(order.shape),
            whole(order.shape),
            whole(mask.shape),
            whole(w_qkv.shape),
            whole(w_out.shape),
        ],
        out_specs=[block, block],
        out_shape=[out, out],
        scratch_shapes=[
            pltpu.VMEM((tokens, 3 * width), BF16),
            pltpu.VMEM((tokens, width), BF16),
            pltpu.VMEM((tokens, 3 * width), BF16),
            pltpu.VMEM((tokens, width), BF16),
        ],
        compiler_params=params(),
        cost_estimate=pl.CostEstimate(
            flops=20 * own * tokens * width * width,
            bytes_accessed=4 * 1024 * 1024,
            transcendentals=own * tokens * 64 * HEADS,
        ),
        name="window_attention",
    )(
        normed,
        cotangent,
        jnp.asarray(order, BF16),
        jnp.asarray(order.T, BF16),
        jnp.asarray(mask, BF16),
        w_qkv,
        w_out,
    )


def backward_body(place_ref, cotangent_ref, other_ref, rim_ref, slab_ref, first_ref, grad_slab_ref, grad_ref,
                  pair_ref, next_ref, slope_one_ref, slope_two_ref, expand_ref, taps_ref, project_ref,
                  out_ref, rim_rows, grad_first, grad_rows, mixed, expanded, total, sems):
    step = pl.program_id(0)
    own, cols, width = slab_ref.shape
    chunk = expand_ref.shape[1]

    @pl.when(step == 0)
    def _():
        sources = (cotangent_ref, other_ref, rim_ref)
        for side in range(2):
            start_pull(place_ref, side, sources, 1, rim_rows.at[pl.ds(side, 1)], sems.at[side])
        total[...] = jnp.zeros_like(total)

        def through_norm(cotangent, grad, first):
            rms = rms_scale(first)
            normed = first * rms
            grad = grad.astype(F32)
            inner = jnp.mean(grad * normed, -1, keepdims=True)
            return cotangent.astype(F32) + rms * (grad - normed * inner)

        for row in range(own):
            result = through_norm(grad_slab_ref[row], grad_ref[row], first_ref[row + 1])
            grad_first[row * cols : (row + 1) * cols] = result
            grad_rows[(row + 1) * cols : (row + 2) * cols] = result.astype(BF16)
        for side in range(2):
            wait_pull(sources, 1, rim_rows.at[pl.ds(side, 1)], sems.at[side])
        leads = place_ref[4] == 0
        above = jnp.where(leads, next_ref[0].astype(F32), pair_ref[0].astype(F32))
        below = jnp.where(leads, pair_ref[0].astype(F32), next_ref[0].astype(F32))
        grad_rows[0:cols] = through_norm(rim_rows[0], above, first_ref[0]).astype(BF16)
        grad_rows[(own + 1) * cols :] = through_norm(rim_rows[1], below, first_ref[own + 1]).astype(BF16)

    for row in range(0, own + 2, 6):
        grad = nt_dot(grad_rows[row * cols : (row + 6) * cols, :], project_ref[...])
        for inner in range(6):
            for lane in range(0, chunk, LANES):
                lanes = slice(lane, lane + LANES)
                slope = slope_two_ref[row + inner, :, lanes].astype(F32)
                value = grad[inner * cols : (inner + 1) * cols, lanes] * slope
                mixed[row + inner, :, lanes] = value.astype(BF16).astype(F32)

    column = lax.broadcasted_iota(jnp.int32, (cols, LANES), 0)
    for lane in range(0, chunk, LANES):
        lanes = slice(lane, lane + LANES)
        taps = spread_taps(taps_ref, lanes, cols)
        for row in range(own):
            near = [mixed[row + a, :, lanes] for a in range(3)]
            sums = [
                taps[8 - b] * near[0] + taps[5 - b] * near[1] + taps[2 - b] * near[2] for b in range(3)
            ]
            grad = column_sums(sums[0], sums[1], sums[2], column, cols - 1)
            slope = slope_one_ref[row, :, lanes].astype(F32)
            expanded[row * cols : (row + 1) * cols, lanes] = (grad * slope).astype(BF16)
    total[...] += nt_dot(expanded[...], expand_ref[...])

    @pl.when(step == pl.num_programs(0) - 1)
    def _():
        for row in range(own):
            at = slice(row * cols, (row + 1) * cols)
            values = slab_ref[row].astype(F32)
            rms = rms_scale(values)
            normed = values * rms
            grad = total[at]
            inner = jnp.mean(grad * normed, -1, keepdims=True)
            out_ref[row] = (grad_first[at] + rms * (grad - normed * inner)).astype(BF16)


def backward(places, cotangent, other, rim, slab, first, grad_slab, grad, pair_row, next_row, slope_one,
             slope_two, w_expand, kernel, w_project):
    own, cols, width = slab.shape
    hidden_width = w_expand.shape[1]
    anywhere = pl.BlockSpec(memory_space=pl.ANY)
    return pl.pallas_call(
        backward_body,
        grid=(hidden_width // CHUNK,),
        in_specs=[
            pl.BlockSpec(memory_space=pltpu.SMEM),
            anywhere,
            anywhere,
            anywhere,
            whole(slab.shape),
            whole(first.shape),
            whole(grad_slab.shape),
            whole(grad.shape),
            whole(pair_row.shape),
            whole(next_row.shape),
            pl.BlockSpec((own, cols, CHUNK), lambda j: (0, 0, j)),
            pl.BlockSpec((own + 2, cols, CHUNK), lambda j: (0, 0, j)),
            pl.BlockSpec((width, CHUNK), lambda j: (0, j)),
            pl.BlockSpec((9, CHUNK), lambda j: (0, j)),
            pl.BlockSpec((CHUNK, width), lambda j: (j, 0)),
        ],
        out_specs=whole((own, cols, width)),
        out_shape=jax.ShapeDtypeStruct((own, cols, width), BF16),
        scratch_shapes=[
            pltpu.VMEM((2, cols, width), BF16),
            pltpu.VMEM((own * cols, width), F32),
            pltpu.VMEM(((own + 2) * cols, width), BF16),
            pltpu.VMEM((own + 2, cols, CHUNK), F32),
            pltpu.VMEM((own * cols, CHUNK), BF16),
            pltpu.VMEM((own * cols, width), F32),
            pltpu.SemaphoreType.DMA((2,)),
        ],
        compiler_params=params(),
        cost_estimate=pl.CostEstimate(
            flops=4 * (own + 2) * cols * width * hidden_width,
            bytes_accessed=12 * 1024 * 1024,
            transcendentals=0,
        ),
        name="bottleneck_backward",
    )(places, cotangent, other, rim, slab, first, grad_slab, grad, pair_row, next_row, slope_one,
      slope_two, w_expand, kernel, w_project)


def window_groups(size):
    stride = size // 8
    return [[first + stride * k for k in range(8)] for first in range(stride)]


def exchange_windows(rows):
    groups = window_groups(lax.axis_size("row"))
    return lax.all_to_all(
        rows, "row", split_axis=0, concat_axis=0, tiled=True, axis_index_groups=groups
    )


def swap_pair(rows):
    size = lax.axis_size("row")
    return lax.ppermute(rows, "row", [(i, i ^ 1) for i in range(size)])


def swap_next(rows):
    size = lax.axis_size("row")
    pairs = [(i, i + 1) for i in range(1, size - 1, 2)]
    return lax.ppermute(rows, "row", pairs + [(j, i) for i, j in pairs])


def place_rows(even, other, leads, leader_share):
    size = GRID_ROWS
    first, second = even[:BAND], even[BAND:]
    share = jnp.where(leads, leader_share, 2 * size - leader_share)
    zeros = jnp.zeros_like(first)
    low = jnp.where(leads | (share == size), first, jnp.where(share < size, second, other))
    mid = jnp.where(share < size, zeros, jnp.where(leads | (share == size), second, first))
    high = jnp.where(share > size, jnp.where(leads, other, second), zeros)
    return jnp.concatenate([low, mid, high], 0)


def on_device(features, row_bands, w_expand, kernel, w_project, w_qkv, w_out, cotangent):
    capacity, cols, width = features.shape
    device = lax.axis_index("row")
    parity = device % 2
    leads = parity == 0
    leader_share = BAND * row_bands[device - parity]
    own_share = BAND * row_bands[device]

    def place(first, count):
        row = first + GRID_ROWS * parity
        beyond = (row < 0) | (row >= 2 * GRID_ROWS)
        in_own = jnp.where(leads, row < leader_share, row >= leader_share)
        local = jnp.where(row < leader_share, row, row - leader_share)
        source = jnp.where(beyond, 2, jnp.where(in_own, 0, 1))
        return [source, jnp.where(beyond, 0, local)]

    rim_first = jnp.where(leads, 0, own_share - RIM)
    rim_cotangent = jnp.where(leads, 0, own_share - 1)
    rim = swap_next(
        jnp.concatenate(
            [
                lax.dynamic_slice_in_dim(features, rim_first, RIM, 0),
                lax.dynamic_slice_in_dim(cotangent, rim_cotangent, 1, 0),
            ],
            0,
        )
    )
    other_cotangent = swap_pair(cotangent)
    other_features = swap_pair(features)

    halves = place(0, BAND) + place(BAND, BAND)
    slab_places = jnp.stack(place(-RIM, RIM) + halves + place(GRID_ROWS, RIM))
    above, below = place(-1, 1), place(GRID_ROWS, 1)
    grad_places = jnp.stack(
        [above[0], jnp.where(above[0] == 2, RIM, above[1]), below[0], jnp.where(below[0] == 2, RIM, below[1]), parity]
    )

    grad_slab = even_rows(jnp.stack(halves), cotangent, other_cotangent)
    grad_windows = exchange_windows(grad_slab)
    first, normed, slab, slope_one, slope_two = forward(
        slab_places, features, other_features, rim, w_expand, kernel, w_project
    )
    normed, grad_windows = lax.optimization_barrier((normed, grad_windows))
    normed_windows = exchange_windows(normed)
    shape = (8, GRID_ROWS // 8, cols, width)
    added, grad_normed = attention(
        normed_windows.reshape(shape), grad_windows.reshape(shape), w_qkv, w_out
    )
    grad_rows = exchange_windows(grad_normed.reshape(GRID_ROWS, cols, width))
    added, grad_rows = lax.optimization_barrier((added, grad_rows))
    added_rows = exchange_windows(added.reshape(GRID_ROWS, cols, width))
    top, bottom = grad_rows[:1], grad_rows[GRID_ROWS - 1 :]
    pair_row = swap_pair(jnp.where(leads, bottom, top))
    next_row = swap_next(jnp.where(leads, top, bottom))
    grad_input = backward(
        grad_places, cotangent, other_cotangent, rim, slab, first, grad_slab, grad_rows, pair_row, next_row,
        slope_one, slope_two, w_expand, kernel, w_project,
    )
    grad_input, added_rows = lax.optimization_barrier((grad_input, added_rows))
    final = (first[1 : GRID_ROWS + 1] + added_rows.astype(F32)).astype(BF16)
    sent = [jnp.where(leads, rows[BAND:], rows[:BAND]) for rows in (final, grad_input)]
    swapped = swap_pair(jnp.stack(sent))
    return (
        place_rows(final, swapped[0], leads, leader_share),
        place_rows(grad_input, swapped[1], leads, leader_share),
    )


def solution(mesh):
    return jax.shard_map(
        on_device,
        mesh=mesh,
        in_specs=(
            P(("parts", "row"), None, None),
            P("parts"),
            P(),
            P(),
            P(),
            P(),
            P(),
            P(("parts", "row"), None, None),
        ),
        out_specs=(P(("parts", "row"), None, None), P(("parts", "row"), None, None)),
        check_vma=False,
    )
```

time: 163 us -> 152 us (0.933)
  the two profiles are of different devices: /device:TPU:0 before, /device:TPU:19 now
where the time goes in v1:
time: 152 us; the launch traced here: 151 us
  Pallas kernels  64.8 us (43%)
  blocking collectives  39.3 us (26%)
  starting transfers between devices  28.6 us (19%)
  local copies, waits for them, and re-layouts  8.01 us (5%)
  waiting for transfers between devices  4.74 us (3%)
  other arithmetic  2.95 us (2%)
  between operations  2.23 us (1%)
    all_to_all x2, blocking collectives, exchange_windows(): lax.all_to_all(rows, 'row', split_axis=0, concat_axis=0, tiled=True, axis...  39.3 us
    pallas_call x1, Pallas kernels, even_rows(): pl.pallas_call(even_body, in_specs=[pl.BlockSpec(memory_space=pltpu.SMEM)...  17.7 us
    pallas_call x1, Pallas kernels, forward(): pl.pallas_call(forward_body, grid=(hidden_width // CHUNK,), in_specs=[pl....  17.1 us
    pallas_call x1, Pallas kernels, attention(): pl.pallas_call(attention_body, grid=(own,), in_specs=[block, block, whole...  16.3 us
    pallas_call x1, Pallas kernels, backward(): pl.pallas_call(backward_body, grid=(hidden_width // CHUNK,), in_specs=[pl...  13.7 us
    all_to_all x2, starting transfers between devices, exchange_windows(): lax.all_to_all(rows, 'row', split_axis=0, concat_axis=0, tiled=True, axis...  11.1 us
    ppermute x4, starting transfers between devices, swap_pair(): return lax.ppermute(rows, 'row', [(i, i ^ 1) for i in range(size)])  8.8 us
    ppermute x2, starting transfers between devices, swap_next(): return lax.ppermute(rows, 'row', pairs + [(j, i) for i, j in pairs])  8.67 us
  transfers between devices with their start and end apart: 8, of which 3 were waited for; matrix products, arithmetic and copies ran while one was open for 3% of the time, Pallas kernels for 32%

profile of v1, /device:TPU:19, one launch (start us, length us, event | category | flops | bytes accessed | tf_op | source)
XLA Modules:
  0.0 150.6 jit_solution(9799278287477201807)
XLA Ops:
  0.6 0.7 collective-permute-start.2
  1.5 1.3 fusion
  4.1 0.9 copy-done.2
  5.0 17.7 %even_rows.1.grad_slab_ref = bf16[16,32,512]{2,1,0:T(8,128)(2,1)} custom-call(s32[4]{0:T(128)} %pad_add_fusion.place_ref, bf16[24,32,512]{2,1,0:T(8,128)(2,1)} %cotangent_ref.1, bf16[24,32,512]{2,1,0:T(8,128)(2,1)} %copy-done.2), custom_call_target="tpu_custom_call" | custom-call | tf_op jit(solution)/shard_map/even_rows/pallas_call | solution.py:83
  22.7 5.6 %all-to-all-start = ((bf16[16,32,512]{2,1,0:T(8,128)(2,1)}), bf16[16,32,512]{2,1,0:T(8,128)(2,1)S(1)}, u32[]{:S(2)}, u32[]{:S(2)}) async-start(bf16[16,32,512]{2,1,0:T(8,128)(2,1)} %even_rows.1.grad_slab_ref), calls=%async_computation | async-start | bytes 1048576 | tf_op jit(solution)/shard_map/all_to_all | solution.py:444
  28.9 0.8 constant_dynamic-slice_fusion
  29.7 0.8 constant_dynamic-slice_fusion.1
  30.6 4.0 %collective-permute-start.1 = (bf16[3,32,512]{2,1,0:T(8,128)(2,1)S(1)}, bf16[3,32,512]{2,1,0:T(8,128)(2,1)S(1)}, u32[]{:S(2)}, u32[]{:S(2)}) collective-permute-start(bf16[3,32,512]{2,1,0:T(8,128)(2,1)S(1)} %pad_maximum_fusion.3), channel_id=1, source_target_pairs={{1,2},{3,4},{5,6},{7,8},{9,10},{11,12},{13,14},{2,1},{4,3},{6,5},{... | collective-permute-start | bytes 294920 | tf_op jit(solution)/shard_map/ppermute | solution.py:457
  34.6 0.7 stack.67.place_ref
  35.2 2.0 %collective-permute-done.1.rim_ref = bf16[3,32,512]{2,1,0:T(8,128)(2,1)S(1)} collective-permute-done((bf16[3,32,512]{2,1,0:T(8,128)(2,1)S(1)}, bf16[3,32,512]{2,1,0:T(8,128)(2,1)S(1)}, u32[]{:S(2)}, u32[]{:S(2)}) %collective-permute-start.1) | collective-permute-done | bytes 98336 | tf_op jit(solution)/shard_map/ppermute | solution.py:457
  37.8 0.9 copy-done.8
  38.7 17.1 %bottleneck_forward.1 = (f32[18,32,512]{2,1,0:T(8,128)}, bf16[16,32,512]{2,1,0:T(8,128)(2,1)}, bf16[16,32,512]{2,1,0:T(8,128)(2,1)}, bf16[16,32,2048]{2,1,0:T(8,128)(2,1)}, bf16[18,32,2048]{2,1,0:T(8,128)(2,1)}) custom-call(s32[8]{0:T(128)} %stack.67.place_ref, bf16[24,32,512]{2,1,0:T(8,128)(2,1)} %features_ref.1, bf16[24,32,512]{2,1,0:T(8,128)(2,1)} %copy-done.8, ...), custom_call_target="tpu_custom_call" | custom-call | flops 2684354560 | bytes 12582912 | tf_op jit(solution)/shard_map/bottleneck_forward/pallas_call | solution.py:166
  55.9 21.9 %all_to_all.20 = bf16[16,32,512]{2,1,0:T(8,128)(2,1)} all-to-all(bf16[16,32,512]{2,1,0:T(8,128)(2,1)} %get-tuple-element.18), channel_id=1, replica_groups={{0,2,4,6,8,10,12,14},{1,3,5,7,9,11,13,15},{16,18,20,22,24,26,28,30},{17..., dimensions={0} | all-to-all | bytes 1048576 | tf_op jit(solution)/shard_map/all_to_all | solution.py:444
  77.8 16.3 %window_attention.1 = (bf16[8,2,32,512]{3,2,1,0:T(8,128)(2,1)}, bf16[8,2,32,512]{3,2,1,0:T(8,128)(2,1)}) custom-call(bf16[8,2,32,512]{3,2,1,0:T(8,128)(2,1)} %bitcast.37, bf16[8,2,32,512]{3,2,1,0:T(8,128)(2,1)} %bitcast.35, bf16[256,256]{1,0:T(8,128)(2,1)} %constant.48.clone.order_ref, bf16[256,256]{1,0:T(8,128)(2,1)} %constant.49.clone.back_ref, ...), custom_call_target="tpu_custom_call" | custom-call | flops 2684354560 | bytes 4194304 | tf_op jit(solution)/shard_map/window_attention/pallas_call | solution.py:284
  94.1 17.4 %all_to_all.21.grad_ref = bf16[16,32,512]{2,1,0:T(8,128)(2,1)S(1)} all-to-all(bf16[16,32,512]{2,1,0:T(8,128)(2,1)} %bitcast.38), channel_id=1, replica_groups={{0,2,4,6,8,10,12,14},{1,3,5,7,9,11,13,15},{16,18,20,22,24,26,28,30},{17..., dimensions={0} | all-to-all | bytes 1048576 | tf_op jit(solution)/shard_map/all_to_all | solution.py:444
  111.5 5.5 %all-to-all-start.3 = ((bf16[16,32,512]{2,1,0:T(8,128)(2,1)}), bf16[16,32,512]{2,1,0:T(8,128)(2,1)S(1)}, u32[]{:S(2)}, u32[]{:S(2)}) async-start(bf16[16,32,512]{2,1,0:T(8,128)(2,1)} %bitcast.36), calls=%async_computation.3 | async-start | bytes 1048576 | tf_op jit(solution)/shard_map/all_to_all | solution.py:444
  117.0 4.7 %collective-permute-start.4 = (bf16[1,32,512]{2,1,0:T(8,128)(2,1)S(1)}, bf16[1,32,512]{2,1,0:T(8,128)(2,1)S(1)}, u32[]{:S(2)}, u32[]{:S(2)}) collective-permute-start(bf16[1,32,512]{2,1,0:T(8,128)(2,1)S(1)} %get-tuple-element.36), channel_id=1, source_target_pairs={{1,2},{3,4},{5,6},{7,8},{9,10},{11,12},{13,14},{2,1},{4,3},{6,5},{... | collective-permute-start | bytes 98312 | tf_op jit(solution)/shard_map/ppermute | solution.py:457
  122.4 1.2 collective-permute-done.4.next_ref
  124.3 13.7 %bottleneck_backward.1 = bf16[16,32,512]{2,1,0:T(8,128)(2,1)} custom-call(s32[5]{0:T(128)} %stack.72.place_ref, bf16[24,32,512]{2,1,0:T(8,128)(2,1)} %cotangent_ref.1, bf16[24,32,512]{2,1,0:T(8,128)(2,1)} %copy-done.2, bf16[3,32,512]{2,1,0:T(8,128)(2,1)} %copy-done.5, bf16[16,32,512]{2,1,0:T(8,128)(2,1)} %get-tuple-element.16.slab_ref, ...), custom_call_target="tpu_custom_call" | custom-call | flops 2415919104 | bytes 12582912 | tf_op jit(solution)/shard_map/bottleneck_backward/pallas_call | solution.py:395
  138.2 0.8 copy-done
  139.2 7.9 %collective-permute-start.5 = (bf16[2,8,32,512]{3,2,1,0:T(8,128)(2,1)S(1)}, bf16[2,8,32,512]{3,2,1,0:T(8,128)(2,1)S(1)}, u32[]{:S(2)}, u32[]{:S(2)}) collective-permute-start(bf16[2,8,32,512]{3,2,1,0:T(8,128)(2,1)S(1)} %pad_maximum_fusion.2), channel_id=1, source_target_pairs={{0,1},{1,0},{2,3},{3,2},{4,5},{5,4},{6,7},{7,6},{8,9},{9,8},{10,11... | collective-permute-start | bytes 1572872 | tf_op jit(solution)/shard_map/ppermute | solution.py:451
  147.1 1.5 %collective-permute-done.5 = bf16[2,8,32,512]{3,2,1,0:T(8,128)(2,1)S(1)} collective-permute-done((bf16[2,8,32,512]{3,2,1,0:T(8,128)(2,1)S(1)}, bf16[2,8,32,512]{3,2,1,0:T(8,128)(2,1)S(1)}, u32[]{:S(2)}, u32[]{:S(2)}) %collective-permute-start.5) | collective-permute-done | bytes 524320 | tf_op jit(solution)/shard_map/ppermute | solution.py:451
  148.7 1.0 pad_maximum_fusion.1
  149.7 1.0 pad_maximum_fusion
  (30 shorter events, 3.0 us)
Async XLA Ops:
  0.6 3.5 %collective-permute-start.2 = (bf16[24,32,512]{2,1,0:T(8,128)(2,1)}, bf16[24,32,512]{2,1,0:T(8,128)(2,1)S(1)}, u32[]{:S(2)}, u32[]{:S(2)}) collective-permute-start(bf16[24,32,512]{2,1,0:T(8,128)(2,1)} %cotangent_ref.1), channel_id=1, source_target_pairs={{0,1},{1,0},{2,3},{3,2},{4,5},{5,4},{6,7},{7,6},{8,9},{9,8},{10,11... | collective-permute-start | bytes 2359304 | tf_op jit(solution)/shard_map/ppermute | solution.py:451
  1.4 35.8 %collective-permute-start = (bf16[24,32,512]{2,1,0:T(8,128)(2,1)}, bf16[24,32,512]{2,1,0:T(8,128)(2,1)S(1)}, u32[]{:S(2)}, u32[]{:S(2)}) collective-permute-start(bf16[24,32,512]{2,1,0:T(8,128)(2,1)} %features_ref.1), channel_id=1, source_target_pairs={{0,1},{1,0},{2,3},{3,2},{4,5},{5,4},{6,7},{7,6},{8,9},{9,8},{10,11... | collective-permute-start | bytes 2359304 | tf_op jit(solution)/shard_map/ppermute | solution.py:451
  4.1 0.9 copy-start.2
  22.7 33.2 %all-to-all-start = ((bf16[16,32,512]{2,1,0:T(8,128)(2,1)}), bf16[16,32,512]{2,1,0:T(8,128)(2,1)S(1)}, u32[]{:S(2)}, u32[]{:S(2)}) async-start(bf16[16,32,512]{2,1,0:T(8,128)(2,1)} %even_rows.1.grad_slab_ref), calls=%async_computation | async-start | bytes 1048576 | tf_op jit(solution)/shard_map/all_to_all | solution.py:444
  30.6 6.6 %collective-permute-start.1 = (bf16[3,32,512]{2,1,0:T(8,128)(2,1)S(1)}, bf16[3,32,512]{2,1,0:T(8,128)(2,1)S(1)}, u32[]{:S(2)}, u32[]{:S(2)}) collective-permute-start(bf16[3,32,512]{2,1,0:T(8,128)(2,1)S(1)} %pad_maximum_fusion.3), channel_id=1, source_target_pairs={{1,2},{3,4},{5,6},{7,8},{9,10},{11,12},{13,14},{2,1},{4,3},{6,5},{... | collective-permute-start | bytes 294920 | tf_op jit(solution)/shard_map/ppermute | solution.py:457
  37.2 0.6 copy-start.5
  37.8 0.9 copy-start.8
  55.9 21.9 %copy-start.4 = (bf16[16,32,512]{2,1,0:T(8,128)(2,1)}, bf16[16,32,512]{2,1,0:T(8,128)(2,1)S(1)}, u32[]{:S(2)}) copy-start(bf16[16,32,512]{2,1,0:T(8,128)(2,1)S(1)} %all-to-all-done) | copy-start | bytes 1572868
  111.5 12.2 %copy-start.3 = (bf16[16,32,512]{2,1,0:T(8,128)(2,1)}, bf16[16,32,512]{2,1,0:T(8,128)(2,1)S(1)}, u32[]{:S(2)}) copy-start(bf16[16,32,512]{2,1,0:T(8,128)(2,1)S(1)} %all_to_all.21.grad_ref) | copy-start | bytes 1572868
  111.5 26.5 %all-to-all-start.3 = ((bf16[16,32,512]{2,1,0:T(8,128)(2,1)}), bf16[16,32,512]{2,1,0:T(8,128)(2,1)S(1)}, u32[]{:S(2)}, u32[]{:S(2)}) async-start(bf16[16,32,512]{2,1,0:T(8,128)(2,1)} %bitcast.36), calls=%async_computation.3 | async-start | bytes 1048576 | tf_op jit(solution)/shard_map/all_to_all | solution.py:444
  117.0 6.6 %collective-permute-start.4 = (bf16[1,32,512]{2,1,0:T(8,128)(2,1)S(1)}, bf16[1,32,512]{2,1,0:T(8,128)(2,1)S(1)}, u32[]{:S(2)}, u32[]{:S(2)}) collective-permute-start(bf16[1,32,512]{2,1,0:T(8,128)(2,1)S(1)} %get-tuple-element.36), channel_id=1, source_target_pairs={{1,2},{3,4},{5,6},{7,8},{9,10},{11,12},{13,14},{2,1},{4,3},{6,5},{... | collective-permute-start | bytes 98312 | tf_op jit(solution)/shard_map/ppermute | solution.py:457
  121.8 1.9 %collective-permute-start.3 = (bf16[1,32,512]{2,1,0:T(8,128)(2,1)S(1)}, bf16[1,32,512]{2,1,0:T(8,128)(2,1)S(1)}, u32[]{:S(2)}, u32[]{:S(2)}) collective-permute-start(bf16[1,32,512]{2,1,0:T(8,128)(2,1)S(1)} %get-tuple-element.37), channel_id=1, source_target_pairs={{0,1},{1,0},{2,3},{3,2},{4,5},{5,4},{6,7},{7,6},{8,9},{9,8},{10,11... | collective-permute-start | bytes 98312 | tf_op jit(solution)/shard_map/ppermute | solution.py:451
  123.7 0.6 copy-start.6
  123.7 0.6 copy-start.7
  124.3 13.7 %copy-start.1 = (f32[18,32,512]{2,1,0:T(8,128)S(1)}, f32[18,32,512]{2,1,0:T(8,128)}, u32[]{:S(2)}) copy-start(f32[18,32,512]{2,1,0:T(8,128)} %get-tuple-element.15.first_ref) | copy-start | bytes 3538948
  138.0 1.0 copy-start
  139.2 9.4 %collective-permute-start.5 = (bf16[2,8,32,512]{3,2,1,0:T(8,128)(2,1)S(1)}, bf16[2,8,32,512]{3,2,1,0:T(8,128)(2,1)S(1)}, u32[]{:S(2)}, u32[]{:S(2)}) collective-permute-start(bf16[2,8,32,512]{3,2,1,0:T(8,128)(2,1)S(1)} %pad_maximum_fusion.2), channel_id=1, source_target_pairs={{0,1},{1,0},{2,3},{3,2},{4,5},{5,4},{6,7},{7,6},{8,9},{9,8},{10,11... | collective-permute-start | bytes 1572872 | tf_op jit(solution)/shard_map/ppermute | solution.py:451

commit v2 on v1

--- a/solution.py
+++ b/solution.py
@@ -13,7 +13,7 @@
 BAND = 8
 RIM = 2
 EPSILON = 1e-06
-CHUNK = 256
+CHUNK = 512
 LANES = 128
 ROOT = math.sqrt(2.0 / math.pi)
 CUBIC = 0.044715
@@ -55,39 +55,98 @@
     return pltpu.CompilerParams(vmem_limit_bytes=VMEM_LIMIT)
 
 
-def start_pull(place_ref, index, sources, rows, target, sem):
-    first = place_ref[2 * index + 1]
+def anywhere():
+    return pl.BlockSpec(memory_space=pl.ANY)
+
+
+def in_scalars():
+    return pl.BlockSpec(memory_space=pltpu.SMEM)
+
+
+def shares(bands_ref):
+    device = lax.axis_index("row")
+    parity = lax.rem(device, 2)
+    return parity, BAND * bands_ref[device - parity], BAND * bands_ref[device]
+
+
+def place(bands_ref, first):
+    parity, leader_share, _ = shares(bands_ref)
+    row = first + GRID_ROWS * parity
+    beyond = (row < 0) | (row >= 2 * GRID_ROWS)
+    in_leader = row < leader_share
+    in_own = in_leader == (parity == 0)
+    source = jnp.where(beyond, 2, jnp.where(in_own, 0, 1))
+    return source, jnp.where(beyond, 0, jnp.where(in_leader, row, row - leader_share))
+
+
+def start_pull(bands_ref, first, sources, rows, target, sem, rim_row=0):
+    where, row = place(bands_ref, first)
+    row = jnp.where(where == 2, rim_row, row)
     for number, source in enumerate(sources):
 
-        @pl.when(place_ref[2 * index] == number)
+        @pl.when(where == number)
         def _():
-            pltpu.make_async_copy(source.at[pl.ds(first, rows)], target, sem).start()
+            pltpu.make_async_copy(source.at[pl.ds(row, rows)], target, sem).start()
 
 
 def wait_pull(sources, rows, target, sem):
     pltpu.make_async_copy(sources[0].at[pl.ds(0, rows)], target, sem).wait()
 
 
-def even_body(place_ref, own_ref, other_ref, out_ref, sems):
+def even_body(bands_ref, own_ref, other_ref, out_ref, sems):
     sources = (own_ref, other_ref)
     targets = [out_ref.at[pl.ds(BAND * half, BAND)] for half in range(2)]
     for half in range(2):
-        start_pull(place_ref, half, sources, BAND, targets[half], sems.at[half])
+        start_pull(bands_ref, BAND * half, sources, BAND, targets[half], sems.at[half])
     for half in range(2):
         wait_pull(sources, BAND, targets[half], sems.at[half])
 
 
-def even_rows(places, own, other):
+def even_rows(bands, own, other):
     capacity, cols, width = own.shape
-    anywhere = pl.BlockSpec(memory_space=pl.ANY)
+    shape = (GRID_ROWS, cols, width)
     return pl.pallas_call(
         even_body,
-        in_specs=[pl.BlockSpec(memory_space=pltpu.SMEM), anywhere, anywhere],
-        out_specs=anywhere,
-        out_shape=jax.ShapeDtypeStruct((GRID_ROWS, cols, width), own.dtype),
+        grid=(1,),
+        in_specs=[in_scalars(), anywhere(), anywhere()],
+        out_specs=whole(shape),
+        out_shape=jax.ShapeDtypeStruct(shape, own.dtype),
         scratch_shapes=[pltpu.SemaphoreType.DMA((2,))],
+        compiler_params=params(),
         name="even_rows",
-    )(places, own, other)
+    )(bands, own, other)
+
+
+def rim_body(bands_ref, features_ref, cotangent_ref, out_ref, sems):
+    parity, _, share = shares(bands_ref)
+    leads = parity == 0
+    copies = [
+        pltpu.make_async_copy(
+            features_ref.at[pl.ds(jnp.where(leads, 0, share - RIM), RIM)], out_ref.at[pl.ds(0, RIM)], sems.at[0]
+        ),
+        pltpu.make_async_copy(
+            cotangent_ref.at[pl.ds(jnp.where(leads, 0, share - 1), 1)], out_ref.at[pl.ds(RIM, 1)], sems.at[1]
+        ),
+    ]
+    for copy in copies:
+        copy.start()
+    for copy in copies:
+        copy.wait()
+
+
+def rim_rows(bands, features, cotangent):
+    capacity, cols, width = features.shape
+    shape = (RIM + 1, cols, width)
+    return pl.pallas_call(
+        rim_body,
+        grid=(1,),
+        in_specs=[in_scalars(), anywhere(), anywhere()],
+        out_specs=whole(shape),
+        out_shape=jax.ShapeDtypeStruct(shape, features.dtype),
+        scratch_shapes=[pltpu.SemaphoreType.DMA((2,))],
+        compiler_params=params(),
+        name="rim_rows",
+    )(bands, features, cotangent)
 
 
 def column_sums(left, mid, right, column, last):
@@ -101,7 +160,7 @@
     return [jnp.broadcast_to(taps[i : i + 1, lanes], (cols, LANES)) for i in range(9)]
 
 
-def forward_body(place_ref, features_ref, other_ref, rim_ref, expand_ref, taps_ref, project_ref, first_ref,
+def forward_body(bands_ref, features_ref, other_ref, rim_ref, expand_ref, taps_ref, project_ref, first_ref,
                  normed_ref, slab_ref, slope_one_ref, slope_two_ref, slab, normed_one, hidden, hidden_two,
                  total, sems):
     step = pl.program_id(0)
@@ -114,7 +173,7 @@
         sources = (features_ref, other_ref, rim_ref)
         pieces = [(0, RIM), (RIM, BAND), (RIM + BAND, BAND), (RIM + 2 * BAND, RIM)]
         for index, (first, count) in enumerate(pieces):
-            start_pull(place_ref, index, sources, count, slab.at[pl.ds(first, count)], sems.at[index])
+            start_pull(bands_ref, first - RIM, sources, count, slab.at[pl.ds(first, count)], sems.at[index])
         for index, (first, count) in enumerate(pieces):
             wait_pull(sources, count, slab.at[pl.ds(first, count)], sems.at[index])
         slab_ref[...] = slab[RIM : RIM + own]
@@ -158,19 +217,18 @@
                 normed_ref[row - 1] = (first * rms_scale(first)).astype(BF16)
 
 
-def forward(places, features, other, rim, w_expand, kernel, w_project):
+def forward(bands, features, other, rim, w_expand, kernel, w_project):
     capacity, cols, width = features.shape
     own, rows = GRID_ROWS, GRID_ROWS + 2 * RIM
     hidden_width = w_expand.shape[1]
-    anywhere = pl.BlockSpec(memory_space=pl.ANY)
     return pl.pallas_call(
         forward_body,
         grid=(hidden_width // CHUNK,),
         in_specs=[
-            pl.BlockSpec(memory_space=pltpu.SMEM),
-            anywhere,
-            anywhere,
-            anywhere,
+            in_scalars(),
+            anywhere(),
+            anywhere(),
+            anywhere(),
             pl.BlockSpec((width, CHUNK), lambda j: (0, j)),
             pl.BlockSpec((9, CHUNK), lambda j: (0, j)),
             pl.BlockSpec((CHUNK, width), lambda j: (j, 0)),
@@ -204,7 +262,7 @@
             transcendentals=2 * rows * cols * hidden_width,
         ),
         name="bottleneck_forward",
-    )(places, features, other, rim, w_expand, kernel, w_project)
+    )(bands, features, other, rim, w_expand, kernel, w_project)
 
 
 def window_order(groups, cols):
@@ -240,11 +298,11 @@
     def spread(values):
         return jnp.concatenate([values] * heads, axis=0) * mask_ref[...]
 
-    def collect(values):
-        result = values[0:span]
-        for head in range(1, heads):
-            result = jnp.where(lane_head == head, values[head * span : (head + 1) * span], result)
-        return result
+    def per_query(values, weights):
+        wide = nn_dot(values.T, weights)
+        half = LANES // 2
+        own = jnp.concatenate([wide[:half, :LANES], wide[half:, LANES:]], axis=0).T
+        return jnp.where(lane_head % 2 == 0, own[:span], own[span:])
 
     for index in range(cols // 8):
         rows = slice(index * span, (index + 1) * span)
@@ -262,8 +320,8 @@
             grad_weights = nt_dot(v, g_wide)
             row_dot = jnp.sum(weights * grad_weights, axis=0, keepdims=True)
             grad_scores = (weights * (grad_weights - row_dot)).astype(BF16)
-            attended[rows, q_at] = collect(tn_dot(half, v)).astype(BF16)
-            grad_projected[rows, q_at] = (collect(tn_dot(grad_scores, k)) * scale).astype(BF16)
+            attended[rows, q_at] = per_query(v, half).astype(BF16)
+            grad_projected[rows, q_at] = (per_query(k, grad_scores) * scale).astype(BF16)
             grad_projected[rows, k_at] = (nn_dot(grad_scores, q_wide) * scale).astype(BF16)
             grad_projected[rows, v_at] = nn_dot(half, g_wide).astype(BF16)
 
@@ -319,9 +377,9 @@
     )
 
 
-def backward_body(place_ref, cotangent_ref, other_ref, rim_ref, slab_ref, first_ref, grad_slab_ref, grad_ref,
+def backward_body(bands_ref, cotangent_ref, other_ref, rim_ref, slab_ref, first_ref, grad_slab_ref, grad_ref,
                   pair_ref, next_ref, slope_one_ref, slope_two_ref, expand_ref, taps_ref, project_ref,
-                  out_ref, rim_rows, grad_first, grad_rows, mixed, expanded, total, sems):
+                  out_ref, rims, grad_first, grad_rows, mixed, expanded, total, sems):
     step = pl.program_id(0)
     own, cols, width = slab_ref.shape
     chunk = expand_ref.shape[1]
@@ -329,8 +387,8 @@
     @pl.when(step == 0)
     def _():
         sources = (cotangent_ref, other_ref, rim_ref)
-        for side in range(2):
-            start_pull(place_ref, side, sources, 1, rim_rows.at[pl.ds(side, 1)], sems.at[side])
+        for side, first in enumerate((-1, own)):
+            start_pull(bands_ref, first, sources, 1, rims.at[pl.ds(side, 1)], sems.at[side], RIM)
         total[...] = jnp.zeros_like(total)
 
         def through_norm(cotangent, grad, first):
@@ -345,12 +403,12 @@
             grad_first[row * cols : (row + 1) * cols] = result
             grad_rows[(row + 1) * cols : (row + 2) * cols] = result.astype(BF16)
         for side in range(2):
-            wait_pull(sources, 1, rim_rows.at[pl.ds(side, 1)], sems.at[side])
-        leads = place_ref[4] == 0
+            wait_pull(sources, 1, rims.at[pl.ds(side, 1)], sems.at[side])
+        leads = lax.rem(lax.axis_index("row"), 2) == 0
         above = jnp.where(leads, next_ref[0].astype(F32), pair_ref[0].astype(F32))
         below = jnp.where(leads, pair_ref[0].astype(F32), next_ref[0].astype(F32))
-        grad_rows[0:cols] = through_norm(rim_rows[0], above, first_ref[0]).astype(BF16)
-        grad_rows[(own + 1) * cols :] = through_norm(rim_rows[1], below, first_ref[own + 1]).astype(BF16)
+        grad_rows[0:cols] = through_norm(rims[0], above, first_ref[0]).astype(BF16)
+        grad_rows[(own + 1) * cols :] = through_norm(rims[1], below, first_ref[own + 1]).astype(BF16)
 
     for row in range(0, own + 2, 6):
         grad = nt_dot(grad_rows[row * cols : (row + 6) * cols, :], project_ref[...])
@@ -387,19 +445,18 @@
             out_ref[row] = (grad_first[at] + rms * (grad - normed * inner)).astype(BF16)
 
 
-def backward(places, cotangent, other, rim, slab, first, grad_slab, grad, pair_row, next_row, slope_one,
+def backward(bands, cotangent, other, rim, slab, first, grad_slab, grad, pair_row, next_row, slope_one,
              slope_two, w_expand, kernel, w_project):
     own, cols, width = slab.shape
     hidden_width = w_expand.shape[1]
-    anywhere = pl.BlockSpec(memory_space=pl.ANY)
     return pl.pallas_call(
         backward_body,
         grid=(hidden_width // CHUNK,),
         in_specs=[
-            pl.BlockSpec(memory_space=pltpu.SMEM),
-            anywhere,
-            anywhere,
-            anywhere,
+            in_scalars(),
+            anywhere(),
+            anywhere(),
+            anywhere(),
             whole(slab.shape),
             whole(first.shape),
             whole(grad_slab.shape),
@@ -430,7 +487,7 @@
             transcendentals=0,
         ),
         name="bottleneck_backward",
-    )(places, cotangent, other, rim, slab, first, grad_slab, grad, pair_row, next_row, slope_one,
+    )(bands, cotangent, other, rim, slab, first, grad_slab, grad, pair_row, next_row, slope_one,
       slope_two, w_expand, kernel, w_project)
 
 
@@ -473,42 +530,16 @@
     device = lax.axis_index("row")
     parity = device % 2
     leads = parity == 0
-    leader_share = BAND * row_bands[device - parity]
-    own_share = BAND * row_bands[device]
-
-    def place(first, count):
-        row = first + GRID_ROWS * parity
-        beyond = (row < 0) | (row >= 2 * GRID_ROWS)
-        in_own = jnp.where(leads, row < leader_share, row >= leader_share)
-        local = jnp.where(row < leader_share, row, row - leader_share)
-        source = jnp.where(beyond, 2, jnp.where(in_own, 0, 1))
-        return [source, jnp.where(beyond, 0, local)]
-
-    rim_first = jnp.where(leads, 0, own_share - RIM)
-    rim_cotangent = jnp.where(leads, 0, own_share - 1)
-    rim = swap_next(
-        jnp.concatenate(
-            [
-                lax.dynamic_slice_in_dim(features, rim_first, RIM, 0),
-                lax.dynamic_slice_in_dim(cotangent, rim_cotangent, 1, 0),
-            ],
-            0,
-        )
-    )
+
+    rim = swap_next(rim_rows(row_bands, features, cotangent))
     other_cotangent = swap_pair(cotangent)
     other_features = swap_pair(features)
-
-    halves = place(0, BAND) + place(BAND, BAND)
-    slab_places = jnp.stack(place(-RIM, RIM) + halves + place(GRID_ROWS, RIM))
-    above, below = place(-1, 1), place(GRID_ROWS, 1)
-    grad_places = jnp.stack(
-        [above[0], jnp.where(above[0] == 2, RIM, above[1]), below[0], jnp.where(below[0] == 2, RIM, below[1]), parity]
-    )
-
-    grad_slab = even_rows(jnp.stack(halves), cotangent, other_cotangent)
+    grad_slab = even_rows(row_bands, cotangent, other_cotangent)
+    rim, grad_slab = lax.optimization_barrier((rim, grad_slab))
+
     grad_windows = exchange_windows(grad_slab)
     first, normed, slab, slope_one, slope_two = forward(
-        slab_places, features, other_features, rim, w_expand, kernel, w_project
+        row_bands, features, other_features, rim, w_expand, kernel, w_project
     )
     normed, grad_windows = lax.optimization_barrier((normed, grad_windows))
     normed_windows = exchange_windows(normed)
@@ -517,19 +548,20 @@
         normed_windows.reshape(shape), grad_windows.reshape(shape), w_qkv, w_out
     )
     grad_rows = exchange_windows(grad_normed.reshape(GRID_ROWS, cols, width))
-    added, grad_rows = lax.optimization_barrier((added, grad_rows))
-    added_rows = exchange_windows(added.reshape(GRID_ROWS, cols, width))
     top, bottom = grad_rows[:1], grad_rows[GRID_ROWS - 1 :]
     pair_row = swap_pair(jnp.where(leads, bottom, top))
     next_row = swap_next(jnp.where(leads, top, bottom))
+    added, pair_row, next_row = lax.optimization_barrier((added, pair_row, next_row))
+    added_rows = exchange_windows(added.reshape(GRID_ROWS, cols, width))
     grad_input = backward(
-        grad_places, cotangent, other_cotangent, rim, slab, first, grad_slab, grad_rows, pair_row, next_row,
+        row_bands, cotangent, other_cotangent, rim, slab, first, grad_slab, grad_rows, pair_row, next_row,
         slope_one, slope_two, w_expand, kernel, w_project,
     )
     grad_input, added_rows = lax.optimization_barrier((grad_input, added_rows))
     final = (first[1 : GRID_ROWS + 1] + added_rows.astype(F32)).astype(BF16)
     sent = [jnp.where(leads, rows[BAND:], rows[:BAND]) for rows in (final, grad_input)]
     swapped = swap_pair(jnp.stack(sent))
+    leader_share = BAND * row_bands[device - parity]
     return (
         place_rows(final, swapped[0], leads, leader_share),
         place_rows(grad_input, swapped[1], leads, leader_share),

time: 152 us -> 116 us (0.76)
  the two profiles are of different devices: /device:TPU:19 before, /device:TPU:0 now
where the time goes in v2:
time: 116 us; the launch traced here: 115 us
  Pallas kernels  47.9 us (41%)
  starting transfers between devices  22.7 us (20%)
  blocking collectives  20.3 us (18%)
  waiting for transfers between devices  18 us (16%)
  local copies, waits for them, and re-layouts  2.37 us (2%)
  other arithmetic  2.32 us (2%)
  between operations  1.53 us (1%)
    all_to_all x3, starting transfers between devices, exchange_windows(): lax.all_to_all(rows, 'row', split_axis=0, concat_axis=0, tiled=True, axis...  20.6 us
    all_to_all x1, blocking collectives, exchange_windows(): lax.all_to_all(rows, 'row', split_axis=0, concat_axis=0, tiled=True, axis...  20.3 us
    all_to_all x3, waiting for transfers between devices, exchange_windows(): lax.all_to_all(rows, 'row', split_axis=0, concat_axis=0, tiled=True, axis...  16.8 us
    pallas_call x1, Pallas kernels, forward(): pl.pallas_call(forward_body, grid=(hidden_width // CHUNK,), in_specs=[in_...  15.9 us
    pallas_call x1, Pallas kernels, attention(): pl.pallas_call(attention_body, grid=(own,), in_specs=[block, block, whole...  14.9 us
    pallas_call x1, Pallas kernels, backward(): pl.pallas_call(backward_body, grid=(hidden_width // CHUNK,), in_specs=[in...  12.4 us
    pallas_call x1, Pallas kernels, even_rows(): pl.pallas_call(even_body, grid=(1,), in_specs=[in_scalars(), anywhere(),...  2.54 us
  transfers between devices with their start and end apart: 9, of which 4 were waited for; matrix products, arithmetic and copies ran while one was open for 1% of the time, Pallas kernels for 29%

profile of v2, /device:TPU:0, one launch (start us, length us, event | category | flops | bytes accessed | tf_op | source)
XLA Modules:
  0.0 115.2 jit_solution(3207042819083639399)
XLA Ops:
  0.6 0.5 collective-permute-start.2
  1.1 0.1 collective-permute-start
  1.2 2.2 %rim_rows.1 = bf16[3,32,512]{2,1,0:T(8,128)(2,1)} custom-call(s32[16]{0:T(128)} %bands_ref.7, bf16[24,32,512]{2,1,0:T(8,128)(2,1)} %features_ref.3, bf16[24,32,512]{2,1,0:T(8,128)(2,1)} %cotangent_ref.3), custom_call_target="tpu_custom_call" | custom-call | tf_op jit(solution)/shard_map/rim_rows/pallas_call | solution.py:140
  3.4 0.7 collective-permute-start.1
  4.1 0.9 copy-done.2
  5.0 2.5 %even_rows.1.grad_slab_ref = bf16[16,32,512]{2,1,0:T(8,128)(2,1)} custom-call(s32[16]{0:T(128)} %bands_ref.7, bf16[24,32,512]{2,1,0:T(8,128)(2,1)} %cotangent_ref.3, bf16[24,32,512]{2,1,0:T(8,128)(2,1)} %copy-done.2), custom_call_target="tpu_custom_call" | custom-call | tf_op jit(solution)/shard_map/even_rows/pallas_call | solution.py:108
  7.5 9.3 %all-to-all-start = ((bf16[16,32,512]{2,1,0:T(8,128)(2,1)}), bf16[16,32,512]{2,1,0:T(8,128)(2,1)S(1)}, u32[]{:S(2)}, u32[]{:S(2)}) async-start(bf16[16,32,512]{2,1,0:T(8,128)(2,1)} %even_rows.1.grad_slab_ref), calls=%async_computation | async-start | bytes 1048576 | tf_op jit(solution)/shard_map/all_to_all | solution.py:501
  16.9 0.9 copy-done.9
  17.8 15.9 %bottleneck_forward.1 = (f32[18,32,512]{2,1,0:T(8,128)}, bf16[16,32,512]{2,1,0:T(8,128)(2,1)}, bf16[16,32,512]{2,1,0:T(8,128)(2,1)}, bf16[16,32,2048]{2,1,0:T(8,128)(2,1)}, bf16[18,32,2048]{2,1,0:T(8,128)(2,1)}) custom-call(s32[16]{0:T(128)} %bands_ref.7, bf16[24,32,512]{2,1,0:T(8,128)(2,1)} %features_ref.3, bf16[24,32,512]{2,1,0:T(8,128)(2,1)} %copy-done.9, ...), custom_call_target="tpu_custom_call" | custom-call | flops 2684354560 | bytes 12582912 | tf_op jit(solution)/shard_map/bottleneck_forward/pallas_call | solution.py:224
  33.7 20.3 %all_to_all.20 = bf16[16,32,512]{2,1,0:T(8,128)(2,1)} all-to-all(bf16[16,32,512]{2,1,0:T(8,128)(2,1)} %get-tuple-element.23), channel_id=1, replica_groups={{0,2,4,6,8,10,12,14},{1,3,5,7,9,11,13,15},{16,18,20,22,24,26,28,30},{17..., dimensions={0} | all-to-all | bytes 1048576 | tf_op jit(solution)/shard_map/all_to_all | solution.py:501
  54.0 14.9 %window_attention.1 = (bf16[8,2,32,512]{3,2,1,0:T(8,128)(2,1)}, bf16[8,2,32,512]{3,2,1,0:T(8,128)(2,1)}) custom-call(bf16[8,2,32,512]{3,2,1,0:T(8,128)(2,1)} %bitcast.24, bf16[8,2,32,512]{3,2,1,0:T(8,128)(2,1)} %bitcast.23, bf16[256,256]{1,0:T(8,128)(2,1)} %constant.33.clone.order_ref, bf16[256,256]{1,0:T(8,128)(2,1)} %constant.34.clone.back_ref, ...), custom_call_target="tpu_custom_call" | custom-call | flops 2684354560 | bytes 4194304 | tf_op jit(solution)/shard_map/window_attention/pallas_call | solution.py:342
  68.9 3.6 %all-to-all-start.2 = ((bf16[16,32,512]{2,1,0:T(8,128)(2,1)}), bf16[16,32,512]{2,1,0:T(8,128)(2,1)S(1)}, u32[]{:S(2)}, u32[]{:S(2)}) async-start(bf16[16,32,512]{2,1,0:T(8,128)(2,1)} %bitcast.22), calls=%async_computation.2 | async-start | bytes 1048576 | tf_op jit(solution)/shard_map/all_to_all | solution.py:501
  72.6 14.1 %all-to-all-done.2.grad_ref = bf16[16,32,512]{2,1,0:T(8,128)(2,1)S(1)} async-done(((bf16[16,32,512]{2,1,0:T(8,128)(2,1)}), bf16[16,32,512]{2,1,0:T(8,128)(2,1)S(1)}, u32[]{:S(2)}, u32[]{:S(2)}) %all-to-all-start.2) | async-done | bytes 524320 | tf_op jit(solution)/shard_map/all_to_all | solution.py:501
  86.8 0.7 collective-permute-start.4
  87.4 0.5 collective-permute-done.3.pair_ref
  88.0 7.7 %all-to-all-start.3 = ((bf16[16,32,512]{2,1,0:T(8,128)(2,1)}), bf16[16,32,512]{2,1,0:T(8,128)(2,1)S(1)}, u32[]{:S(2)}, u32[]{:S(2)}) async-start(bf16[16,32,512]{2,1,0:T(8,128)(2,1)} %bitcast.21), calls=%async_computation.3 | async-start | bytes 1048576 | tf_op jit(solution)/shard_map/all_to_all | solution.py:501
  95.7 12.4 %bottleneck_backward.1 = bf16[16,32,512]{2,1,0:T(8,128)(2,1)} custom-call(s32[16]{0:T(128)} %bands_ref.7, bf16[24,32,512]{2,1,0:T(8,128)(2,1)} %cotangent_ref.3, bf16[24,32,512]{2,1,0:T(8,128)(2,1)} %copy-done.2, bf16[3,32,512]{2,1,0:T(8,128)(2,1)} %copy-done.5, bf16[16,32,512]{2,1,0:T(8,128)(2,1)} %get-tuple-element.20.slab_ref, ...), custom_call_target="tpu_custom_call" | custom-call | flops 2415919104 | bytes 12582912 | tf_op jit(solution)/shard_map/bottleneck_backward/pallas_call | solution.py:452
  108.1 2.7 %all-to-all-done.3 = bf16[16,32,512]{2,1,0:T(8,128)(2,1)S(1)} async-done(((bf16[16,32,512]{2,1,0:T(8,128)(2,1)}), bf16[16,32,512]{2,1,0:T(8,128)(2,1)S(1)}, u32[]{:S(2)}, u32[]{:S(2)}) %all-to-all-start.3) | async-done | bytes 524320 | tf_op jit(solution)/shard_map/all_to_all | solution.py:501
  110.8 0.2 add_convert_fusion
  111.2 0.6 dynamic_slice.3
  112.5 0.6 collective-permute-done.5
  113.1 0.1 select_select_fusion.2
  113.2 1.0 pad_maximum_fusion.1
  114.2 1.0 pad_maximum_fusion
  (28 shorter events, 0.3 us)
Async XLA Ops:
  0.6 3.5 %collective-permute-start.2 = (bf16[24,32,512]{2,1,0:T(8,128)(2,1)}, bf16[24,32,512]{2,1,0:T(8,128)(2,1)S(1)}, u32[]{:S(2)}, u32[]{:S(2)}) collective-permute-start(bf16[24,32,512]{2,1,0:T(8,128)(2,1)} %cotangent_ref.3), channel_id=1, source_target_pairs={{0,1},{1,0},{2,3},{3,2},{4,5},{5,4},{6,7},{7,6},{8,9},{9,8},{10,11... | collective-permute-start | bytes 2359304 | tf_op jit(solution)/shard_map/ppermute | solution.py:508
  1.1 15.7 %collective-permute-start = (bf16[24,32,512]{2,1,0:T(8,128)(2,1)}, bf16[24,32,512]{2,1,0:T(8,128)(2,1)S(1)}, u32[]{:S(2)}, u32[]{:S(2)}) collective-permute-start(bf16[24,32,512]{2,1,0:T(8,128)(2,1)} %features_ref.3), channel_id=1, source_target_pairs={{0,1},{1,0},{2,3},{3,2},{4,5},{5,4},{6,7},{7,6},{8,9},{9,8},{10,11... | collective-permute-start | bytes 2359304 | tf_op jit(solution)/shard_map/ppermute | solution.py:508
  3.4 4.1 %collective-permute-start.1 = (bf16[3,32,512]{2,1,0:T(8,128)(2,1)}, bf16[3,32,512]{2,1,0:T(8,128)(2,1)S(1)}, u32[]{:S(2)}, u32[]{:S(2)}) collective-permute-start(bf16[3,32,512]{2,1,0:T(8,128)(2,1)} %rim_rows.1), channel_id=1, source_target_pairs={{1,2},{3,4},{5,6},{7,8},{9,10},{11,12},{13,14},{2,1},{4,3},{6,5},{... | collective-permute-start | bytes 294920 | tf_op jit(solution)/shard_map/ppermute | solution.py:514
  4.1 0.9 copy-start.2
  7.5 9.3 %copy-start.5 = (bf16[3,32,512]{2,1,0:T(8,128)(2,1)}, bf16[3,32,512]{2,1,0:T(8,128)(2,1)S(1)}, u32[]{:S(2)}) copy-start(bf16[3,32,512]{2,1,0:T(8,128)(2,1)S(1)} %collective-permute-done.1.rim_ref) | copy-start | bytes 294916
  7.5 26.1 %all-to-all-start = ((bf16[16,32,512]{2,1,0:T(8,128)(2,1)}), bf16[16,32,512]{2,1,0:T(8,128)(2,1)S(1)}, u32[]{:S(2)}, u32[]{:S(2)}) async-start(bf16[16,32,512]{2,1,0:T(8,128)(2,1)} %even_rows.1.grad_slab_ref), calls=%async_computation | async-start | bytes 1048576 | tf_op jit(solution)/shard_map/all_to_all | solution.py:501
  16.9 0.9 copy-start.9
  33.7 20.3 %copy-start.4 = (bf16[16,32,512]{2,1,0:T(8,128)(2,1)}, bf16[16,32,512]{2,1,0:T(8,128)(2,1)S(1)}, u32[]{:S(2)}) copy-start(bf16[16,32,512]{2,1,0:T(8,128)(2,1)S(1)} %all-to-all-done) | copy-start | bytes 1572868
  68.9 17.7 %all-to-all-start.2 = ((bf16[16,32,512]{2,1,0:T(8,128)(2,1)}), bf16[16,32,512]{2,1,0:T(8,128)(2,1)S(1)}, u32[]{:S(2)}, u32[]{:S(2)}) async-start(bf16[16,32,512]{2,1,0:T(8,128)(2,1)} %bitcast.22), calls=%async_computation.2 | async-start | bytes 1048576 | tf_op jit(solution)/shard_map/all_to_all | solution.py:501
  86.7 9.0 %copy-start.3 = (bf16[16,32,512]{2,1,0:T(8,128)(2,1)}, bf16[16,32,512]{2,1,0:T(8,128)(2,1)S(1)}, u32[]{:S(2)}) copy-start(bf16[16,32,512]{2,1,0:T(8,128)(2,1)S(1)} %all-to-all-done.2.grad_ref) | copy-start | bytes 1572868
  86.7 1.3 %collective-permute-start.3 = (bf16[1,32,512]{2,1,0:T(8,128)(2,1)S(1)}, bf16[1,32,512]{2,1,0:T(8,128)(2,1)S(1)}, u32[]{:S(2)}, u32[]{:S(2)}) collective-permute-start(bf16[1,32,512]{2,1,0:T(8,128)(2,1)S(1)} %get-tuple-element.43), channel_id=1, source_target_pairs={{0,1},{1,0},{2,3},{3,2},{4,5},{5,4},{6,7},{7,6},{8,9},{9,8},{10,11... | collective-permute-start | bytes 98312 | tf_op jit(solution)/shard_map/ppermute | solution.py:508
  86.8 1.2 %collective-permute-start.4 = (bf16[1,32,512]{2,1,0:T(8,128)(2,1)S(1)}, bf16[1,32,512]{2,1,0:T(8,128)(2,1)S(1)}, u32[]{:S(2)}, u32[]{:S(2)}) collective-permute-start(bf16[1,32,512]{2,1,0:T(8,128)(2,1)S(1)} %get-tuple-element.42), channel_id=1, source_target_pairs={{1,2},{3,4},{5,6},{7,8},{9,10},{11,12},{13,14},{2,1},{4,3},{6,5},{... | collective-permute-start | bytes 98312 | tf_op jit(solution)/shard_map/ppermute | solution.py:514
  88.0 7.7 %copy-start.6 = (bf16[1,32,512]{2,1,0:T(8,128)(2,1)}, bf16[1,32,512]{2,1,0:T(8,128)(2,1)S(1)}, u32[]{:S(2)}) copy-start(bf16[1,32,512]{2,1,0:T(8,128)(2,1)S(1)} %collective-permute-done.3.pair_ref) | copy-start | bytes 98308
  88.0 7.7 %copy-start.7 = (bf16[1,32,512]{2,1,0:T(8,128)(2,1)}, bf16[1,32,512]{2,1,0:T(8,128)(2,1)S(1)}, u32[]{:S(2)}) copy-start(bf16[1,32,512]{2,1,0:T(8,128)(2,1)S(1)} %collective-permute-done.4.next_ref) | copy-start | bytes 98308
  88.0 22.9 %all-to-all-start.3 = ((bf16[16,32,512]{2,1,0:T(8,128)(2,1)}), bf16[16,32,512]{2,1,0:T(8,128)(2,1)S(1)}, u32[]{:S(2)}, u32[]{:S(2)}) async-start(bf16[16,32,512]{2,1,0:T(8,128)(2,1)} %bitcast.21), calls=%async_computation.3 | async-start | bytes 1048576 | tf_op jit(solution)/shard_map/all_to_all | solution.py:501
  95.7 15.2 %copy-start.1 = (f32[18,32,512]{2,1,0:T(8,128)S(1)}, f32[18,32,512]{2,1,0:T(8,128)}, u32[]{:S(2)}) copy-start(f32[18,32,512]{2,1,0:T(8,128)} %get-tuple-element.19.first_ref) | copy-start | bytes 3538948
  108.1 2.9 %copy-start = (bf16[16,32,512]{2,1,0:T(8,128)(2,1)S(1)}, bf16[16,32,512]{2,1,0:T(8,128)(2,1)}, u32[]{:S(2)}) copy-start(bf16[16,32,512]{2,1,0:T(8,128)(2,1)} %bottleneck_backward.1) | copy-start | bytes 1572868
  108.1 3.1 %copy-start.8 = (s32[16]{0:T(128)S(1)}, s32[16]{0:T(128)}, u32[]{:S(2)}) copy-start(s32[16]{0:T(128)} %bands_ref.7) | copy-start | bytes 196
  111.1 2.0 %collective-permute-start.5 = (bf16[2,8,32,512]{3,2,1,0:T(8,128)(2,1)S(1)}, bf16[2,8,32,512]{3,2,1,0:T(8,128)(2,1)S(1)}, u32[]{:S(2)}, u32[]{:S(2)}) collective-permute-start(bf16[2,8,32,512]{3,2,1,0:T(8,128)(2,1)S(1)} %pad_maximum_fusion.2), channel_id=1, source_target_pairs={{0,1},{1,0},{2,3},{3,2},{4,5},{5,4},{6,7},{7,6},{8,9},{9,8},{10,11... | collective-permute-start | bytes 1572872 | tf_op jit(solution)/shard_map/ppermute | solution.py:508

commit v3 on v2

--- a/solution.py
+++ b/solution.py
@@ -15,6 +15,7 @@
 EPSILON = 1e-06
 CHUNK = 512
 LANES = 128
+WIDE = 256
 ROOT = math.sqrt(2.0 / math.pi)
 CUBIC = 0.044715
 F32 = jnp.float32
@@ -161,7 +162,7 @@
 
 
 def forward_body(bands_ref, features_ref, other_ref, rim_ref, expand_ref, taps_ref, project_ref, first_ref,
-                 normed_ref, slab_ref, slope_one_ref, slope_two_ref, slab, normed_one, hidden, hidden_two,
+                 normed_ref, slab_ref, slope_one_ref, slope_two_ref, slab, normed_one, expanded, hidden, hidden_two,
                  total, sems):
     step = pl.program_id(0)
     rows, cols, width = slab.shape
@@ -183,19 +184,17 @@
             normed_one[at] = (values * rms_scale(values)).astype(BF16)
         total[...] = slab[1 : rows - 1].astype(F32).reshape((rows - 2) * cols, width)
 
-    for row in range(0, rows, 4):
-        expanded = nn_dot(normed_one[row * cols : (row + 4) * cols, :], expand_ref[...])
-        for inner in range(4):
-            for lane in range(0, chunk, LANES):
-                lanes = slice(lane, lane + LANES)
-                value, slope = gelu_and_slope(expanded[inner * cols : (inner + 1) * cols, lanes])
-                hidden[row + inner, :, lanes] = value.astype(BF16).astype(F32)
-                if RIM <= row + inner < RIM + own:
-                    slope_one_ref[row + inner - RIM, :, lanes] = slope.astype(BF16)
-
     column = lax.broadcasted_iota(jnp.int32, (cols, LANES), 0)
     for lane in range(0, chunk, LANES):
         lanes = slice(lane, lane + LANES)
+        if lane % WIDE == 0:
+            wide = slice(lane, lane + WIDE)
+            expanded[:, :, wide] = nn_dot(normed_one[...], expand_ref[:, wide]).reshape(rows, cols, WIDE)
+        for row in range(rows):
+            value, slope = gelu_and_slope(expanded[row, :, lanes])
+            hidden[row, :, lanes] = value.astype(BF16).astype(F32)
+            if RIM <= row < RIM + own:
+                slope_one_ref[row - RIM, :, lanes] = slope.astype(BF16)
         taps = spread_taps(taps_ref, lanes, cols)
         for row in range(rows - 2):
             near = [hidden[row + a, :, lanes] for a in range(3)]
@@ -251,6 +250,7 @@
             pltpu.VMEM((rows, cols, width), BF16),
             pltpu.VMEM((rows * cols, width), BF16),
             pltpu.VMEM((rows, cols, CHUNK), F32),
+            pltpu.VMEM((rows, cols, CHUNK), F32),
             pltpu.VMEM(((rows - 2) * cols, CHUNK), BF16),
             pltpu.VMEM(((rows - 2) * cols, width), F32),
             pltpu.SemaphoreType.DMA((4,)),
@@ -265,33 +265,49 @@
     )(bands, features, other, rim, w_expand, kernel, w_project)
 
 
-def window_order(groups, cols):
-    order = np.arange(groups * cols)
-    span = groups * 8
-    place = (order // 8) % groups * cols + order % 8 * (cols // 8) + order // span
-    return (place[:, None] == order[None, :]).astype(np.float32)
-
-
 def head_mask(span, head_dim):
     heads = LANES // head_dim
     row_head = np.arange(heads * span)[:, None] // span
     return (row_head == np.arange(LANES)[None, :] // head_dim).astype(np.float32)
 
 
-def attention_body(normed_ref, cotangent_ref, order_ref, back_ref, mask_ref, qkv_ref, out_ref, added_ref,
-                   grad_ref, projected, grad_attended, grad_projected, attended):
-    groups, _, cols, width = normed_ref.shape
-    tokens = groups * cols
+def attention_body(normed_ref, cotangent_ref, mask_ref, qkv_ref, out_ref, added_ref, grad_ref,
+                   rows_wide, in_windows, projected, grad_attended, grad_projected, attended):
+    groups, own, cols, width = normed_ref.shape
+    windows = cols // 8
     span = groups * 8
     head_dim = width // HEADS
     heads = LANES // head_dim
     scale = 1.0 / math.sqrt(head_dim)
     steepness = scale * math.log2(math.e)
-
-    normed = nn_dot(order_ref[...], normed_ref[...].reshape(tokens, width)).astype(BF16)
-    projected[...] = nn_dot(normed, qkv_ref[...]).astype(BF16)
-    grad_rows = nn_dot(order_ref[...], cotangent_ref[...].reshape(tokens, width)).astype(BF16)
-    grad_attended[...] = nt_dot(grad_rows, out_ref[...]).astype(BF16)
+    places = [(r, q) for r in range(own) for q in range(windows)]
+
+    tiles = [slice(at, at + LANES) for at in range(0, width, LANES)]
+
+    def to_windows(source_ref):
+        for tile, lanes in enumerate(tiles):
+            for group in range(groups):
+                rows_wide[tile, group] = source_ref[group, :, :, lanes].astype(F32)
+            for index, (r, q) in enumerate(places):
+                pieces = [
+                    rows_wide[tile, group, r, pl.ds(q, 8, stride=windows), :] for group in range(groups)
+                ]
+                rows = slice(index * span, (index + 1) * span)
+                in_windows[rows, lanes] = jnp.concatenate(pieces, axis=0).astype(BF16)
+
+    def to_rows(values, target_ref):
+        for tile, lanes in enumerate(tiles):
+            for index, (r, q) in enumerate(places):
+                for group in range(groups):
+                    first = index * span + group * 8
+                    rows_wide[tile, group, r, pl.ds(q, 8, stride=windows), :] = values[first : first + 8, lanes]
+            for group in range(groups):
+                target_ref[group, :, :, lanes] = rows_wide[tile, group].astype(BF16)
+
+    to_windows(cotangent_ref)
+    grad_attended[...] = nt_dot(in_windows[...], out_ref[...]).astype(BF16)
+    to_windows(normed_ref)
+    projected[...] = nn_dot(in_windows[...], qkv_ref[...]).astype(BF16)
 
     lane_head = lax.broadcasted_iota(jnp.int32, (span, LANES), 1) // head_dim
 
@@ -304,8 +320,8 @@
         own = jnp.concatenate([wide[:half, :LANES], wide[half:, LANES:]], axis=0).T
         return jnp.where(lane_head % 2 == 0, own[:span], own[span:])
 
-    for index in range(cols // 8):
-        rows = slice(index * span, (index + 1) * span)
+    def window(index, carry):
+        rows = pl.ds(pl.multiple_of(index * span, span), span)
         for part in range(width // LANES):
             q_at, k_at, v_at = (
                 slice(t * width + part * LANES, t * width + (part + 1) * LANES) for t in range(3)
@@ -324,36 +340,34 @@
             grad_projected[rows, q_at] = (per_query(k, grad_scores) * scale).astype(BF16)
             grad_projected[rows, k_at] = (nn_dot(grad_scores, q_wide) * scale).astype(BF16)
             grad_projected[rows, v_at] = nn_dot(half, g_wide).astype(BF16)
-
-    shape = (groups, 1, cols, width)
-    grad_normed = nt_dot(grad_projected[...], qkv_ref[...]).astype(BF16)
-    grad_ref[...] = nn_dot(back_ref[...], grad_normed).astype(BF16).reshape(shape)
-    in_rows = nn_dot(back_ref[...], attended[...]).astype(BF16)
-    added_ref[...] = nn_dot(in_rows, out_ref[...]).astype(BF16).reshape(shape)
+        return carry
+
+    lax.fori_loop(0, len(places), window, 0, unroll=4)
+
+    to_rows(nt_dot(grad_projected[...], qkv_ref[...]), grad_ref)
+    to_rows(nn_dot(attended[...], out_ref[...]), added_ref)
 
 
 def attention(normed, cotangent, w_qkv, w_out):
     groups, own, cols, width = normed.shape
-    tokens = groups * cols
-    order = window_order(groups, cols)
+    tokens = groups * own * cols
     mask = head_mask(groups * 8, width // HEADS)
-    block = pl.BlockSpec((groups, 1, cols, width), lambda r: (0, r, 0, 0))
     out = jax.ShapeDtypeStruct(normed.shape, BF16)
     return pl.pallas_call(
         attention_body,
-        grid=(own,),
+        grid=(1,),
         in_specs=[
-            block,
-            block,
-            whole(order.shape),
-            whole(order.shape),
+            whole(normed.shape),
+            whole(normed.shape),
             whole(mask.shape),
             whole(w_qkv.shape),
             whole(w_out.shape),
         ],
-        out_specs=[block, block],
+        out_specs=[whole(normed.shape)] * 2,
         out_shape=[out, out],
         scratch_shapes=[
+            pltpu.VMEM((width // LANES, groups, own, cols, LANES), F32),
+            pltpu.VMEM((tokens, width), BF16),
             pltpu.VMEM((tokens, 3 * width), BF16),
             pltpu.VMEM((tokens, width), BF16),
             pltpu.VMEM((tokens, 3 * width), BF16),
@@ -361,25 +375,17 @@
         ],
         compiler_params=params(),
         cost_estimate=pl.CostEstimate(
-            flops=20 * own * tokens * width * width,
+            flops=20 * tokens * width * width,
             bytes_accessed=4 * 1024 * 1024,
-            transcendentals=own * tokens * 64 * HEADS,
+            transcendentals=tokens * 64 * HEADS,
         ),
         name="window_attention",
-    )(
-        normed,
-        cotangent,
-        jnp.asarray(order, BF16),
-        jnp.asarray(order.T, BF16),
-        jnp.asarray(mask, BF16),
-        w_qkv,
-        w_out,
-    )
+    )(normed, cotangent, jnp.asarray(mask, BF16), w_qkv, w_out)
 
 
 def backward_body(bands_ref, cotangent_ref, other_ref, rim_ref, slab_ref, first_ref, grad_slab_ref, grad_ref,
                   pair_ref, next_ref, slope_one_ref, slope_two_ref, expand_ref, taps_ref, project_ref,
-                  out_ref, rims, grad_first, grad_rows, mixed, expanded, total, sems):
+                  out_ref, rims, grad_first, grad_rows, grads, mixed, expanded, total, sems):
     step = pl.program_id(0)
     own, cols, width = slab_ref.shape
     chunk = expand_ref.shape[1]
@@ -410,18 +416,15 @@
         grad_rows[0:cols] = through_norm(rims[0], above, first_ref[0]).astype(BF16)
         grad_rows[(own + 1) * cols :] = through_norm(rims[1], below, first_ref[own + 1]).astype(BF16)
 
-    for row in range(0, own + 2, 6):
-        grad = nt_dot(grad_rows[row * cols : (row + 6) * cols, :], project_ref[...])
-        for inner in range(6):
-            for lane in range(0, chunk, LANES):
-                lanes = slice(lane, lane + LANES)
-                slope = slope_two_ref[row + inner, :, lanes].astype(F32)
-                value = grad[inner * cols : (inner + 1) * cols, lanes] * slope
-                mixed[row + inner, :, lanes] = value.astype(BF16).astype(F32)
-
     column = lax.broadcasted_iota(jnp.int32, (cols, LANES), 0)
     for lane in range(0, chunk, LANES):
         lanes = slice(lane, lane + LANES)
+        if lane % WIDE == 0:
+            wide = slice(lane, lane + WIDE)
+            grads[:, :, wide] = nt_dot(grad_rows[...], project_ref[wide, :]).reshape(own + 2, cols, WIDE)
+        for row in range(own + 2):
+            slope = slope_two_ref[row, :, lanes].astype(F32)
+            mixed[row, :, lanes] = (grads[row, :, lanes] * slope).astype(BF16).astype(F32)
         taps = spread_taps(taps_ref, lanes, cols)
         for row in range(own):
             near = [mixed[row + a, :, lanes] for a in range(3)]
@@ -475,6 +478,7 @@
             pltpu.VMEM((2, cols, width), BF16),
             pltpu.VMEM((own * cols, width), F32),
             pltpu.VMEM(((own + 2) * cols, width), BF16),
+            pltpu.VMEM((own + 2, cols, CHUNK), F32),
             pltpu.VMEM((own + 2, cols, CHUNK), F32),
             pltpu.VMEM((own * cols, CHUNK), BF16),
             pltpu.VMEM((own * cols, width), F32),

time: 116 us -> 116 us (level)
  no operation moved by 1% of the time
where the time goes in v3:
time: 116 us; the launch traced here: 115 us
  Pallas kernels  47.9 us (41%)
  starting transfers between devices  22.7 us (20%)
  blocking collectives  20.3 us (18%)
  waiting for transfers between devices  17.7 us (15%)
  local copies, waits for them, and re-layouts  2.37 us (2%)
  other arithmetic  2.32 us (2%)
  between operations  1.53 us (1%)
    all_to_all x3, starting transfers between devices, exchange_windows(): lax.all_to_all(rows, 'row', split_axis=0, concat_axis=0, tiled=True, axis...  20.6 us
    all_to_all x1, blocking collectives, exchange_windows(): lax.all_to_all(rows, 'row', split_axis=0, concat_axis=0, tiled=True, axis...  20.3 us
    all_to_all x3, waiting for transfers between devices, exchange_windows(): lax.all_to_all(rows, 'row', split_axis=0, concat_axis=0, tiled=True, axis...  16.5 us
    pallas_call x1, Pallas kernels, forward(): pl.pallas_call(forward_body, grid=(hidden_width // CHUNK,), in_specs=[in_...  16.1 us
    pallas_call x1, Pallas kernels, attention(): pl.pallas_call(attention_body, grid=(1,), in_specs=[whole(normed.shape),...  14.3 us
    pallas_call x1, Pallas kernels, backward(): pl.pallas_call(backward_body, grid=(hidden_width // CHUNK,), in_specs=[in...  12.7 us
    pallas_call x1, Pallas kernels, even_rows(): pl.pallas_call(even_body, grid=(1,), in_specs=[in_scalars(), anywhere(),...  2.54 us
  transfers between devices with their start and end apart: 9, of which 4 were waited for; matrix products, arithmetic and copies ran while one was open for 1% of the time, Pallas kernels for 29%

profile of v3, /device:TPU:0, one launch (start us, length us, event | category | flops | bytes accessed | tf_op | source)
XLA Modules:
  0.0 114.8 jit_solution(16461864432721680830)
XLA Ops:
  0.6 0.5 collective-permute-start.2
  1.1 0.1 collective-permute-start
  1.2 2.2 %rim_rows.1 = bf16[3,32,512]{2,1,0:T(8,128)(2,1)} custom-call(s32[16]{0:T(128)} %bands_ref.7, bf16[24,32,512]{2,1,0:T(8,128)(2,1)} %features_ref.3, bf16[24,32,512]{2,1,0:T(8,128)(2,1)} %cotangent_ref.3), custom_call_target="tpu_custom_call" | custom-call | tf_op jit(solution)/shard_map/rim_rows/pallas_call | solution.py:141
  3.4 0.7 collective-permute-start.1
  4.1 0.9 copy-done.2
  5.0 2.5 %even_rows.1.grad_slab_ref = bf16[16,32,512]{2,1,0:T(8,128)(2,1)} custom-call(s32[16]{0:T(128)} %bands_ref.7, bf16[24,32,512]{2,1,0:T(8,128)(2,1)} %cotangent_ref.3, bf16[24,32,512]{2,1,0:T(8,128)(2,1)} %copy-done.2), custom_call_target="tpu_custom_call" | custom-call | tf_op jit(solution)/shard_map/even_rows/pallas_call | solution.py:109
  7.5 9.3 %all-to-all-start = ((bf16[16,32,512]{2,1,0:T(8,128)(2,1)}), bf16[16,32,512]{2,1,0:T(8,128)(2,1)S(1)}, u32[]{:S(2)}, u32[]{:S(2)}) async-start(bf16[16,32,512]{2,1,0:T(8,128)(2,1)} %even_rows.1.grad_slab_ref), calls=%async_computation | async-start | bytes 1048576 | tf_op jit(solution)/shard_map/all_to_all | solution.py:505
  16.9 0.9 copy-done.9
  17.8 16.1 %bottleneck_forward.1 = (f32[18,32,512]{2,1,0:T(8,128)}, bf16[16,32,512]{2,1,0:T(8,128)(2,1)}, bf16[16,32,512]{2,1,0:T(8,128)(2,1)}, bf16[16,32,2048]{2,1,0:T(8,128)(2,1)}, bf16[18,32,2048]{2,1,0:T(8,128)(2,1)}) custom-call(s32[16]{0:T(128)} %bands_ref.7, bf16[24,32,512]{2,1,0:T(8,128)(2,1)} %features_ref.3, bf16[24,32,512]{2,1,0:T(8,128)(2,1)} %copy-done.9, ...), custom_call_target="tpu_custom_call" | custom-call | flops 2684354560 | bytes 12582912 | tf_op jit(solution)/shard_map/bottleneck_forward/pallas_call | solution.py:223
  33.9 20.3 %all_to_all.20 = bf16[16,32,512]{2,1,0:T(8,128)(2,1)} all-to-all(bf16[16,32,512]{2,1,0:T(8,128)(2,1)} %get-tuple-element.23), channel_id=1, replica_groups={{0,2,4,6,8,10,12,14},{1,3,5,7,9,11,13,15},{16,18,20,22,24,26,28,30},{17..., dimensions={0} | all-to-all | bytes 1048576 | tf_op jit(solution)/shard_map/all_to_all | solution.py:505
  54.2 14.3 %window_attention.1 = (bf16[8,2,32,512]{3,2,1,0:T(8,128)(2,1)}, bf16[8,2,32,512]{3,2,1,0:T(8,128)(2,1)}) custom-call(bf16[8,2,32,512]{3,2,1,0:T(8,128)(2,1)} %bitcast.24, bf16[8,2,32,512]{3,2,1,0:T(8,128)(2,1)} %bitcast.23, bf16[256,128]{1,0:T(8,128)(2,1)} %constant.29.clone.mask_ref, bf16[512,1536]{1,0:T(8,128)(2,1)} %qkv_ref.1, bf16[512,512]{1,0:T(8,128)(2,1)} %out_ref.1), custom_call_target="tpu_custom_call" | custom-call | flops 2684354560 | bytes 4194304 | tf_op jit(solution)/shard_map/window_attention/pallas_call | solution.py:356
  68.5 3.6 %all-to-all-start.2 = ((bf16[16,32,512]{2,1,0:T(8,128)(2,1)}), bf16[16,32,512]{2,1,0:T(8,128)(2,1)S(1)}, u32[]{:S(2)}, u32[]{:S(2)}) async-start(bf16[16,32,512]{2,1,0:T(8,128)(2,1)} %bitcast.22), calls=%async_computation.2 | async-start | bytes 1048576 | tf_op jit(solution)/shard_map/all_to_all | solution.py:505
  72.2 14.1 %all-to-all-done.2.grad_ref = bf16[16,32,512]{2,1,0:T(8,128)(2,1)S(1)} async-done(((bf16[16,32,512]{2,1,0:T(8,128)(2,1)}), bf16[16,32,512]{2,1,0:T(8,128)(2,1)S(1)}, u32[]{:S(2)}, u32[]{:S(2)}) %all-to-all-start.2) | async-done | bytes 524320 | tf_op jit(solution)/shard_map/all_to_all | solution.py:505
  86.4 0.7 collective-permute-start.4
  87.0 0.5 collective-permute-done.3.pair_ref
  87.6 7.7 %all-to-all-start.3 = ((bf16[16,32,512]{2,1,0:T(8,128)(2,1)}), bf16[16,32,512]{2,1,0:T(8,128)(2,1)S(1)}, u32[]{:S(2)}, u32[]{:S(2)}) async-start(bf16[16,32,512]{2,1,0:T(8,128)(2,1)} %bitcast.21), calls=%async_computation.3 | async-start | bytes 1048576 | tf_op jit(solution)/shard_map/all_to_all | solution.py:505
  95.3 12.7 %bottleneck_backward.1 = bf16[16,32,512]{2,1,0:T(8,128)(2,1)} custom-call(s32[16]{0:T(128)} %bands_ref.7, bf16[24,32,512]{2,1,0:T(8,128)(2,1)} %cotangent_ref.3, bf16[24,32,512]{2,1,0:T(8,128)(2,1)} %copy-done.2, bf16[3,32,512]{2,1,0:T(8,128)(2,1)} %copy-done.5, bf16[16,32,512]{2,1,0:T(8,128)(2,1)} %get-tuple-element.20.slab_ref, ...), custom_call_target="tpu_custom_call" | custom-call | flops 2415919104 | bytes 12582912 | tf_op jit(solution)/shard_map/bottleneck_backward/pallas_call | solution.py:455
  108.1 2.4 %all-to-all-done.3 = bf16[16,32,512]{2,1,0:T(8,128)(2,1)S(1)} async-done(((bf16[16,32,512]{2,1,0:T(8,128)(2,1)}), bf16[16,32,512]{2,1,0:T(8,128)(2,1)S(1)}, u32[]{:S(2)}, u32[]{:S(2)}) %all-to-all-start.3) | async-done | bytes 524320 | tf_op jit(solution)/shard_map/all_to_all | solution.py:505
  110.5 0.2 add_convert_fusion
  110.8 0.6 dynamic_slice.3
  112.1 0.6 collective-permute-done.5
  112.7 0.1 select_select_fusion.2
  112.8 1.0 pad_maximum_fusion.1
  113.8 1.0 pad_maximum_fusion
  (28 shorter events, 0.3 us)
Async XLA Ops:
  0.6 3.5 %collective-permute-start.2 = (bf16[24,32,512]{2,1,0:T(8,128)(2,1)}, bf16[24,32,512]{2,1,0:T(8,128)(2,1)S(1)}, u32[]{:S(2)}, u32[]{:S(2)}) collective-permute-start(bf16[24,32,512]{2,1,0:T(8,128)(2,1)} %cotangent_ref.3), channel_id=1, source_target_pairs={{0,1},{1,0},{2,3},{3,2},{4,5},{5,4},{6,7},{7,6},{8,9},{9,8},{10,11... | collective-permute-start | bytes 2359304 | tf_op jit(solution)/shard_map/ppermute | solution.py:512
  1.1 15.7 %collective-permute-start = (bf16[24,32,512]{2,1,0:T(8,128)(2,1)}, bf16[24,32,512]{2,1,0:T(8,128)(2,1)S(1)}, u32[]{:S(2)}, u32[]{:S(2)}) collective-permute-start(bf16[24,32,512]{2,1,0:T(8,128)(2,1)} %features_ref.3), channel_id=1, source_target_pairs={{0,1},{1,0},{2,3},{3,2},{4,5},{5,4},{6,7},{7,6},{8,9},{9,8},{10,11... | collective-permute-start | bytes 2359304 | tf_op jit(solution)/shard_map/ppermute | solution.py:512
  3.4 4.1 %collective-permute-start.1 = (bf16[3,32,512]{2,1,0:T(8,128)(2,1)}, bf16[3,32,512]{2,1,0:T(8,128)(2,1)S(1)}, u32[]{:S(2)}, u32[]{:S(2)}) collective-permute-start(bf16[3,32,512]{2,1,0:T(8,128)(2,1)} %rim_rows.1), channel_id=1, source_target_pairs={{1,2},{3,4},{5,6},{7,8},{9,10},{11,12},{13,14},{2,1},{4,3},{6,5},{... | collective-permute-start | bytes 294920 | tf_op jit(solution)/shard_map/ppermute | solution.py:518
  4.1 0.9 copy-start.2
  7.5 9.3 %copy-start.5 = (bf16[3,32,512]{2,1,0:T(8,128)(2,1)}, bf16[3,32,512]{2,1,0:T(8,128)(2,1)S(1)}, u32[]{:S(2)}) copy-start(bf16[3,32,512]{2,1,0:T(8,128)(2,1)S(1)} %collective-permute-done.1.rim_ref) | copy-start | bytes 294916
  7.5 26.4 %all-to-all-start = ((bf16[16,32,512]{2,1,0:T(8,128)(2,1)}), bf16[16,32,512]{2,1,0:T(8,128)(2,1)S(1)}, u32[]{:S(2)}, u32[]{:S(2)}) async-start(bf16[16,32,512]{2,1,0:T(8,128)(2,1)} %even_rows.1.grad_slab_ref), calls=%async_computation | async-start | bytes 1048576 | tf_op jit(solution)/shard_map/all_to_all | solution.py:505
  16.9 0.9 copy-start.9
  33.9 20.3 %copy-start.4 = (bf16[16,32,512]{2,1,0:T(8,128)(2,1)}, bf16[16,32,512]{2,1,0:T(8,128)(2,1)S(1)}, u32[]{:S(2)}) copy-start(bf16[16,32,512]{2,1,0:T(8,128)(2,1)S(1)} %all-to-all-done) | copy-start | bytes 1572868
  68.5 17.7 %all-to-all-start.2 = ((bf16[16,32,512]{2,1,0:T(8,128)(2,1)}), bf16[16,32,512]{2,1,0:T(8,128)(2,1)S(1)}, u32[]{:S(2)}, u32[]{:S(2)}) async-start(bf16[16,32,512]{2,1,0:T(8,128)(2,1)} %bitcast.22), calls=%async_computation.2 | async-start | bytes 1048576 | tf_op jit(solution)/shard_map/all_to_all | solution.py:505
  86.3 9.0 %copy-start.3 = (bf16[16,32,512]{2,1,0:T(8,128)(2,1)}, bf16[16,32,512]{2,1,0:T(8,128)(2,1)S(1)}, u32[]{:S(2)}) copy-start(bf16[16,32,512]{2,1,0:T(8,128)(2,1)S(1)} %all-to-all-done.2.grad_ref) | copy-start | bytes 1572868
  86.3 1.3 %collective-permute-start.3 = (bf16[1,32,512]{2,1,0:T(8,128)(2,1)S(1)}, bf16[1,32,512]{2,1,0:T(8,128)(2,1)S(1)}, u32[]{:S(2)}, u32[]{:S(2)}) collective-permute-start(bf16[1,32,512]{2,1,0:T(8,128)(2,1)S(1)} %get-tuple-element.43), channel_id=1, source_target_pairs={{0,1},{1,0},{2,3},{3,2},{4,5},{5,4},{6,7},{7,6},{8,9},{9,8},{10,11... | collective-permute-start | bytes 98312 | tf_op jit(solution)/shard_map/ppermute | solution.py:512
  86.4 1.2 %collective-permute-start.4 = (bf16[1,32,512]{2,1,0:T(8,128)(2,1)S(1)}, bf16[1,32,512]{2,1,0:T(8,128)(2,1)S(1)}, u32[]{:S(2)}, u32[]{:S(2)}) collective-permute-start(bf16[1,32,512]{2,1,0:T(8,128)(2,1)S(1)} %get-tuple-element.42), channel_id=1, source_target_pairs={{1,2},{3,4},{5,6},{7,8},{9,10},{11,12},{13,14},{2,1},{4,3},{6,5},{... | collective-permute-start | bytes 98312 | tf_op jit(solution)/shard_map/ppermute | solution.py:518
  87.6 7.7 %copy-start.6 = (bf16[1,32,512]{2,1,0:T(8,128)(2,1)}, bf16[1,32,512]{2,1,0:T(8,128)(2,1)S(1)}, u32[]{:S(2)}) copy-start(bf16[1,32,512]{2,1,0:T(8,128)(2,1)S(1)} %collective-permute-done.3.pair_ref) | copy-start | bytes 98308
  87.6 7.7 %copy-start.7 = (bf16[1,32,512]{2,1,0:T(8,128)(2,1)}, bf16[1,32,512]{2,1,0:T(8,128)(2,1)S(1)}, u32[]{:S(2)}) copy-start(bf16[1,32,512]{2,1,0:T(8,128)(2,1)S(1)} %collective-permute-done.4.next_ref) | copy-start | bytes 98308
  87.6 22.9 %all-to-all-start.3 = ((bf16[16,32,512]{2,1,0:T(8,128)(2,1)}), bf16[16,32,512]{2,1,0:T(8,128)(2,1)S(1)}, u32[]{:S(2)}, u32[]{:S(2)}) async-start(bf16[16,32,512]{2,1,0:T(8,128)(2,1)} %bitcast.21), calls=%async_computation.3 | async-start | bytes 1048576 | tf_op jit(solution)/shard_map/all_to_all | solution.py:505
  95.3 15.2 %copy-start.1 = (f32[18,32,512]{2,1,0:T(8,128)S(1)}, f32[18,32,512]{2,1,0:T(8,128)}, u32[]{:S(2)}) copy-start(f32[18,32,512]{2,1,0:T(8,128)} %get-tuple-element.19.first_ref) | copy-start | bytes 3538948
  108.0 2.6 %copy-start = (bf16[16,32,512]{2,1,0:T(8,128)(2,1)S(1)}, bf16[16,32,512]{2,1,0:T(8,128)(2,1)}, u32[]{:S(2)}) copy-start(bf16[16,32,512]{2,1,0:T(8,128)(2,1)} %bottleneck_backward.1) | copy-start | bytes 1572868
  108.0 2.8 %copy-start.8 = (s32[16]{0:T(128)S(1)}, s32[16]{0:T(128)}, u32[]{:S(2)}) copy-start(s32[16]{0:T(128)} %bands_ref.7) | copy-start | bytes 196
  110.8 2.0 %collective-permute-start.5 = (bf16[2,8,32,512]{3,2,1,0:T(8,128)(2,1)S(1)}, bf16[2,8,32,512]{3,2,1,0:T(8,128)(2,1)S(1)}, u32[]{:S(2)}, u32[]{:S(2)}) collective-permute-start(bf16[2,8,32,512]{3,2,1,0:T(8,128)(2,1)S(1)} %pad_maximum_fusion.2), channel_id=1, source_target_pairs={{0,1},{1,0},{2,3},{3,2},{4,5},{5,4},{6,7},{7,6},{8,9},{9,8},{10,11... | collective-permute-start | bytes 1572872 | tf_op jit(solution)/shard_map/ppermute | solution.py:512

commit v4 on v3

--- a/solution.py
+++ b/solution.py
@@ -156,6 +156,14 @@
     return mid + from_left + from_right
 
 
+def loop_rows(first, stop, body):
+    def step(row, carry):
+        body(row)
+        return carry
+
+    lax.fori_loop(first, stop, step, 0, unroll=2)
+
+
 def spread_taps(taps_ref, lanes, cols):
     taps = taps_ref[...].astype(F32)
     return [jnp.broadcast_to(taps[i : i + 1, lanes], (cols, LANES)) for i in range(9)]
@@ -185,26 +193,35 @@
         total[...] = slab[1 : rows - 1].astype(F32).reshape((rows - 2) * cols, width)
 
     column = lax.broadcasted_iota(jnp.int32, (cols, LANES), 0)
-    for lane in range(0, chunk, LANES):
-        lanes = slice(lane, lane + LANES)
-        if lane % WIDE == 0:
-            wide = slice(lane, lane + WIDE)
-            expanded[:, :, wide] = nn_dot(normed_one[...], expand_ref[:, wide]).reshape(rows, cols, WIDE)
-        for row in range(rows):
-            value, slope = gelu_and_slope(expanded[row, :, lanes])
-            hidden[row, :, lanes] = value.astype(BF16).astype(F32)
-            if RIM <= row < RIM + own:
-                slope_one_ref[row - RIM, :, lanes] = slope.astype(BF16)
-        taps = spread_taps(taps_ref, lanes, cols)
-        for row in range(rows - 2):
-            near = [hidden[row + a, :, lanes] for a in range(3)]
-            sums = [
-                taps[b] * near[0] + taps[3 + b] * near[1] + taps[6 + b] * near[2] for b in range(3)
-            ]
-            mixed = column_sums(sums[0], sums[1], sums[2], column, cols - 1)
-            value, slope = gelu_and_slope(mixed)
-            hidden_two[row * cols : (row + 1) * cols, lanes] = value.astype(BF16)
-            slope_two_ref[row, :, lanes] = slope.astype(BF16)
+    for start in range(0, chunk, WIDE):
+        wide = slice(start, start + WIDE)
+        pieces = [slice(lane, lane + LANES) for lane in range(start, start + WIDE, LANES)]
+        expanded[:, :, wide] = nn_dot(normed_one[...], expand_ref[:, wide]).reshape(rows, cols, WIDE)
+
+        def activate(row, keep):
+            for lanes in pieces:
+                value, slope = gelu_and_slope(expanded[row, :, lanes])
+                hidden[row, :, lanes] = value.astype(BF16).astype(F32)
+                if keep:
+                    slope_one_ref[row - RIM, :, lanes] = slope.astype(BF16)
+
+        for row in (0, 1, rows - 2, rows - 1):
+            activate(row, False)
+        loop_rows(RIM, RIM + own, lambda row: activate(row, True))
+        taps = [spread_taps(taps_ref, lanes, cols) for lanes in pieces]
+
+        def mix(row):
+            for lanes, tap in zip(pieces, taps):
+                near = [hidden[row + a, :, lanes] for a in range(3)]
+                sums = [
+                    tap[b] * near[0] + tap[3 + b] * near[1] + tap[6 + b] * near[2] for b in range(3)
+                ]
+                mixed = column_sums(sums[0], sums[1], sums[2], column, cols - 1)
+                value, slope = gelu_and_slope(mixed)
+                hidden_two[pl.ds(pl.multiple_of(row * cols, cols), cols), lanes] = value.astype(BF16)
+                slope_two_ref[row, :, lanes] = slope.astype(BF16)
+
+        loop_rows(0, rows - 2, mix)
     total[...] += nn_dot(hidden_two[...], project_ref[...])
 
     @pl.when(step == pl.num_programs(0) - 1)
@@ -342,7 +359,7 @@
             grad_projected[rows, v_at] = nn_dot(half, g_wide).astype(BF16)
         return carry
 
-    lax.fori_loop(0, len(places), window, 0, unroll=4)
+    lax.fori_loop(0, len(places), window, 0, unroll=2)
 
     to_rows(nt_dot(grad_projected[...], qkv_ref[...]), grad_ref)
     to_rows(nn_dot(attended[...], out_ref[...]), added_ref)
@@ -417,23 +434,30 @@
         grad_rows[(own + 1) * cols :] = through_norm(rims[1], below, first_ref[own + 1]).astype(BF16)
 
     column = lax.broadcasted_iota(jnp.int32, (cols, LANES), 0)
-    for lane in range(0, chunk, LANES):
-        lanes = slice(lane, lane + LANES)
-        if lane % WIDE == 0:
-            wide = slice(lane, lane + WIDE)
-            grads[:, :, wide] = nt_dot(grad_rows[...], project_ref[wide, :]).reshape(own + 2, cols, WIDE)
-        for row in range(own + 2):
-            slope = slope_two_ref[row, :, lanes].astype(F32)
-            mixed[row, :, lanes] = (grads[row, :, lanes] * slope).astype(BF16).astype(F32)
-        taps = spread_taps(taps_ref, lanes, cols)
-        for row in range(own):
-            near = [mixed[row + a, :, lanes] for a in range(3)]
-            sums = [
-                taps[8 - b] * near[0] + taps[5 - b] * near[1] + taps[2 - b] * near[2] for b in range(3)
-            ]
-            grad = column_sums(sums[0], sums[1], sums[2], column, cols - 1)
-            slope = slope_one_ref[row, :, lanes].astype(F32)
-            expanded[row * cols : (row + 1) * cols, lanes] = (grad * slope).astype(BF16)
+    for start in range(0, chunk, WIDE):
+        wide = slice(start, start + WIDE)
+        pieces = [slice(lane, lane + LANES) for lane in range(start, start + WIDE, LANES)]
+        grads[:, :, wide] = nt_dot(grad_rows[...], project_ref[wide, :]).reshape(own + 2, cols, WIDE)
+
+        def through_gelu(row):
+            for lanes in pieces:
+                slope = slope_two_ref[row, :, lanes].astype(F32)
+                mixed[row, :, lanes] = (grads[row, :, lanes] * slope).astype(BF16).astype(F32)
+
+        loop_rows(0, own + 2, through_gelu)
+        taps = [spread_taps(taps_ref, lanes, cols) for lanes in pieces]
+
+        def unmix(row):
+            for lanes, tap in zip(pieces, taps):
+                near = [mixed[row + a, :, lanes] for a in range(3)]
+                sums = [
+                    tap[8 - b] * near[0] + tap[5 - b] * near[1] + tap[2 - b] * near[2] for b in range(3)
+                ]
+                grad = column_sums(sums[0], sums[1], sums[2], column, cols - 1)
+                slope = slope_one_ref[row, :, lanes].astype(F32)
+                expanded[pl.ds(pl.multiple_of(row * cols, cols), cols), lanes] = (grad * slope).astype(BF16)
+
+        loop_rows(0, own, unmix)
     total[...] += nt_dot(expanded[...], expand_ref[...])
 
     @pl.when(step == pl.num_programs(0) - 1)

time: 116 us -> 122 us (1.052)
  Pallas kernels: 47.9 us -> 55.5 us
  waiting for transfers between devices: 17.7 us -> 15 us
    pallas_call x1, Pallas kernels: 16.1 us -> 20.3 us  [forward(): pl.pallas_call(forward_body, grid=(hidden_width // CHUNK,), in_specs=[in_...]
    pallas_call x1, Pallas kernels: 12.7 us -> 15.8 us  [backward(): pl.pallas_call(backward_body, grid=(hidden_width // CHUNK,), in_specs=[in...]
    all_to_all x3, waiting for transfers between devices: 16.5 us -> 14.1 us  [exchange_windows(): lax.all_to_all(rows, 'row', split_axis=0, concat_axis=0, tiled=True, axis...]
  transfers between devices with their start and end apart: 9 -> 9, of which waited for: 4 -> 3; matrix products, arithmetic and copies ran while one was open for 1% -> 0% of each run, Pallas kernels for 29% -> 34%
where the time goes in v4:
time: 122 us; the launch traced here: 121 us
  Pallas kernels  55.5 us (45%)
  starting transfers between devices  23.1 us (19%)
  blocking collectives  20.3 us (17%)
  waiting for transfers between devices  15 us (12%)
  local copies, waits for them, and re-layouts  3.19 us (3%)
  other arithmetic  2.32 us (2%)
  between operations  1.51 us (1%)
    all_to_all x3, starting transfers between devices, exchange_windows(): lax.all_to_all(rows, 'row', split_axis=0, concat_axis=0, tiled=True, axis...  20.6 us
    all_to_all x1, blocking collectives, exchange_windows(): lax.all_to_all(rows, 'row', split_axis=0, concat_axis=0, tiled=True, axis...  20.3 us
    pallas_call x1, Pallas kernels, forward(): pl.pallas_call(forward_body, grid=(hidden_width // CHUNK,), in_specs=[in_...  20.3 us
    pallas_call x1, Pallas kernels, backward(): pl.pallas_call(backward_body, grid=(hidden_width // CHUNK,), in_specs=[in...  15.8 us
    pallas_call x1, Pallas kernels, attention(): pl.pallas_call(attention_body, grid=(1,), in_specs=[whole(normed.shape),...  14.7 us
    all_to_all x3, waiting for transfers between devices, exchange_windows(): lax.all_to_all(rows, 'row', split_axis=0, concat_axis=0, tiled=True, axis...  14.1 us
    unnamed x20, local copies, waits for them, and re-layouts  2.61 us
    pallas_call x1, Pallas kernels, even_rows(): pl.pallas_call(even_body, grid=(1,), in_specs=[in_scalars(), anywhere(),...  2.54 us
  transfers between devices with their start and end apart: 9, of which 3 were waited for; matrix products, arithmetic and copies ran while one was open for 0% of the time, Pallas kernels for 34%

profile of v4, /device:TPU:0, one launch (start us, length us, event | category | flops | bytes accessed | tf_op | source)
XLA Modules:
  0.0 120.9 jit_solution(12945173824894172497)
XLA Ops:
  0.6 0.5 collective-permute-start.2
  1.2 2.2 %rim_rows.1 = bf16[3,32,512]{2,1,0:T(8,128)(2,1)} custom-call(s32[16]{0:T(128)} %bands_ref.7, bf16[24,32,512]{2,1,0:T(8,128)(2,1)} %features_ref.3, bf16[24,32,512]{2,1,0:T(8,128)(2,1)} %cotangent_ref.3), custom_call_target="tpu_custom_call" | custom-call | tf_op jit(solution)/shard_map/rim_rows/pallas_call | solution.py:141
  3.4 0.7 collective-permute-start.1
  4.1 0.9 copy-done.2
  5.0 2.5 %even_rows.1.grad_slab_ref = bf16[16,32,512]{2,1,0:T(8,128)(2,1)} custom-call(s32[16]{0:T(128)} %bands_ref.7, bf16[24,32,512]{2,1,0:T(8,128)(2,1)} %cotangent_ref.3, bf16[24,32,512]{2,1,0:T(8,128)(2,1)} %copy-done.2), custom_call_target="tpu_custom_call" | custom-call | tf_op jit(solution)/shard_map/even_rows/pallas_call | solution.py:109
  7.5 9.3 %all-to-all-start = ((bf16[16,32,512]{2,1,0:T(8,128)(2,1)}), bf16[16,32,512]{2,1,0:T(8,128)(2,1)S(1)}, u32[]{:S(2)}, u32[]{:S(2)}) async-start(bf16[16,32,512]{2,1,0:T(8,128)(2,1)} %even_rows.1.grad_slab_ref), calls=%async_computation | async-start | bytes 1048576 | tf_op jit(solution)/shard_map/all_to_all | solution.py:529
  16.9 0.9 copy-done.9
  17.8 20.3 %bottleneck_forward.1 = (f32[18,32,512]{2,1,0:T(8,128)}, bf16[16,32,512]{2,1,0:T(8,128)(2,1)}, bf16[16,32,512]{2,1,0:T(8,128)(2,1)}, bf16[16,32,2048]{2,1,0:T(8,128)(2,1)}, bf16[18,32,2048]{2,1,0:T(8,128)(2,1)}) custom-call(s32[16]{0:T(128)} %bands_ref.7, bf16[24,32,512]{2,1,0:T(8,128)(2,1)} %features_ref.3, bf16[24,32,512]{2,1,0:T(8,128)(2,1)} %copy-done.9, ...), custom_call_target="tpu_custom_call" | custom-call | flops 2684354560 | bytes 12582912 | tf_op jit(solution)/shard_map/bottleneck_forward/pallas_call | solution.py:240
  38.1 20.3 %all_to_all.20 = bf16[16,32,512]{2,1,0:T(8,128)(2,1)} all-to-all(bf16[16,32,512]{2,1,0:T(8,128)(2,1)} %get-tuple-element.23), channel_id=1, replica_groups={{0,2,4,6,8,10,12,14},{1,3,5,7,9,11,13,15},{16,18,20,22,24,26,28,30},{17..., dimensions={0} | all-to-all | bytes 1048576 | tf_op jit(solution)/shard_map/all_to_all | solution.py:529
  58.4 14.7 %window_attention.1 = (bf16[8,2,32,512]{3,2,1,0:T(8,128)(2,1)}, bf16[8,2,32,512]{3,2,1,0:T(8,128)(2,1)}) custom-call(bf16[8,2,32,512]{3,2,1,0:T(8,128)(2,1)} %bitcast.24, bf16[8,2,32,512]{3,2,1,0:T(8,128)(2,1)} %bitcast.23, bf16[256,128]{1,0:T(8,128)(2,1)} %constant.29.clone.mask_ref, bf16[512,1536]{1,0:T(8,128)(2,1)} %qkv_ref.1, bf16[512,512]{1,0:T(8,128)(2,1)} %out_ref.1), custom_call_target="tpu_custom_call" | custom-call | flops 2684354560 | bytes 4194304 | tf_op jit(solution)/shard_map/window_attention/pallas_call | solution.py:373
  73.1 3.6 %all-to-all-start.2 = ((bf16[16,32,512]{2,1,0:T(8,128)(2,1)}), bf16[16,32,512]{2,1,0:T(8,128)(2,1)S(1)}, u32[]{:S(2)}, u32[]{:S(2)}) async-start(bf16[16,32,512]{2,1,0:T(8,128)(2,1)} %bitcast.22), calls=%async_computation.2 | async-start | bytes 1048576 | tf_op jit(solution)/shard_map/all_to_all | solution.py:529
  76.8 14.1 %all-to-all-done.2.grad_ref = bf16[16,32,512]{2,1,0:T(8,128)(2,1)S(1)} async-done(((bf16[16,32,512]{2,1,0:T(8,128)(2,1)}), bf16[16,32,512]{2,1,0:T(8,128)(2,1)S(1)}, u32[]{:S(2)}, u32[]{:S(2)}) %all-to-all-start.2) | async-done | bytes 524320 | tf_op jit(solution)/shard_map/all_to_all | solution.py:529
  91.0 0.7 collective-permute-start.4
  91.6 0.5 collective-permute-done.3.pair_ref
  92.2 7.7 %all-to-all-start.3 = ((bf16[16,32,512]{2,1,0:T(8,128)(2,1)}), bf16[16,32,512]{2,1,0:T(8,128)(2,1)S(1)}, u32[]{:S(2)}, u32[]{:S(2)}) async-start(bf16[16,32,512]{2,1,0:T(8,128)(2,1)} %bitcast.21), calls=%async_computation.3 | async-start | bytes 1048576 | tf_op jit(solution)/shard_map/all_to_all | solution.py:529
  99.9 15.8 %bottleneck_backward.1 = bf16[16,32,512]{2,1,0:T(8,128)(2,1)} custom-call(s32[16]{0:T(128)} %bands_ref.7, bf16[24,32,512]{2,1,0:T(8,128)(2,1)} %cotangent_ref.3, bf16[24,32,512]{2,1,0:T(8,128)(2,1)} %copy-done.2, bf16[3,32,512]{2,1,0:T(8,128)(2,1)} %copy-done.5, bf16[16,32,512]{2,1,0:T(8,128)(2,1)} %get-tuple-element.20.slab_ref, ...), custom_call_target="tpu_custom_call" | custom-call | flops 2415919104 | bytes 12582912 | tf_op jit(solution)/shard_map/bottleneck_backward/pallas_call | solution.py:479
  115.7 0.2 add_convert_fusion
  115.9 0.8 copy-done
  116.8 0.4 collective-permute-start.5
  117.2 0.6 dynamic_slice.3
  118.5 0.3 collective-permute-done.5
  118.8 0.1 select_select_fusion.2
  118.9 1.0 pad_maximum_fusion.1
  119.9 1.0 pad_maximum_fusion
  (28 shorter events, 0.3 us)
Async XLA Ops:
  0.6 3.5 %collective-permute-start.2 = (bf16[24,32,512]{2,1,0:T(8,128)(2,1)}, bf16[24,32,512]{2,1,0:T(8,128)(2,1)S(1)}, u32[]{:S(2)}, u32[]{:S(2)}) collective-permute-start(bf16[24,32,512]{2,1,0:T(8,128)(2,1)} %cotangent_ref.3), channel_id=1, source_target_pairs={{0,1},{1,0},{2,3},{3,2},{4,5},{5,4},{6,7},{7,6},{8,9},{9,8},{10,11... | collective-permute-start | bytes 2359304 | tf_op jit(solution)/shard_map/ppermute | solution.py:536
  1.1 15.7 %collective-permute-start = (bf16[24,32,512]{2,1,0:T(8,128)(2,1)}, bf16[24,32,512]{2,1,0:T(8,128)(2,1)S(1)}, u32[]{:S(2)}, u32[]{:S(2)}) collective-permute-start(bf16[24,32,512]{2,1,0:T(8,128)(2,1)} %features_ref.3), channel_id=1, source_target_pairs={{0,1},{1,0},{2,3},{3,2},{4,5},{5,4},{6,7},{7,6},{8,9},{9,8},{10,11... | collective-permute-start | bytes 2359304 | tf_op jit(solution)/shard_map/ppermute | solution.py:536
  3.4 4.1 %collective-permute-start.1 = (bf16[3,32,512]{2,1,0:T(8,128)(2,1)}, bf16[3,32,512]{2,1,0:T(8,128)(2,1)S(1)}, u32[]{:S(2)}, u32[]{:S(2)}) collective-permute-start(bf16[3,32,512]{2,1,0:T(8,128)(2,1)} %rim_rows.1), channel_id=1, source_target_pairs={{1,2},{3,4},{5,6},{7,8},{9,10},{11,12},{13,14},{2,1},{4,3},{6,5},{... | collective-permute-start | bytes 294920 | tf_op jit(solution)/shard_map/ppermute | solution.py:542
  4.1 0.9 copy-start.2
  7.5 9.3 %copy-start.5 = (bf16[3,32,512]{2,1,0:T(8,128)(2,1)}, bf16[3,32,512]{2,1,0:T(8,128)(2,1)S(1)}, u32[]{:S(2)}) copy-start(bf16[3,32,512]{2,1,0:T(8,128)(2,1)S(1)} %collective-permute-done.1.rim_ref) | copy-start | bytes 294916
  7.5 30.5 %all-to-all-start = ((bf16[16,32,512]{2,1,0:T(8,128)(2,1)}), bf16[16,32,512]{2,1,0:T(8,128)(2,1)S(1)}, u32[]{:S(2)}, u32[]{:S(2)}) async-start(bf16[16,32,512]{2,1,0:T(8,128)(2,1)} %even_rows.1.grad_slab_ref), calls=%async_computation | async-start | bytes 1048576 | tf_op jit(solution)/shard_map/all_to_all | solution.py:529
  16.9 0.9 copy-start.9
  38.1 20.3 %copy-start.4 = (bf16[16,32,512]{2,1,0:T(8,128)(2,1)}, bf16[16,32,512]{2,1,0:T(8,128)(2,1)S(1)}, u32[]{:S(2)}) copy-start(bf16[16,32,512]{2,1,0:T(8,128)(2,1)S(1)} %all-to-all-done) | copy-start | bytes 1572868
  73.1 17.8 %all-to-all-start.2 = ((bf16[16,32,512]{2,1,0:T(8,128)(2,1)}), bf16[16,32,512]{2,1,0:T(8,128)(2,1)S(1)}, u32[]{:S(2)}, u32[]{:S(2)}) async-start(bf16[16,32,512]{2,1,0:T(8,128)(2,1)} %bitcast.22), calls=%async_computation.2 | async-start | bytes 1048576 | tf_op jit(solution)/shard_map/all_to_all | solution.py:529
  90.9 9.0 %copy-start.3 = (bf16[16,32,512]{2,1,0:T(8,128)(2,1)}, bf16[16,32,512]{2,1,0:T(8,128)(2,1)S(1)}, u32[]{:S(2)}) copy-start(bf16[16,32,512]{2,1,0:T(8,128)(2,1)S(1)} %all-to-all-done.2.grad_ref) | copy-start | bytes 1572868
  90.9 1.3 %collective-permute-start.3 = (bf16[1,32,512]{2,1,0:T(8,128)(2,1)S(1)}, bf16[1,32,512]{2,1,0:T(8,128)(2,1)S(1)}, u32[]{:S(2)}, u32[]{:S(2)}) collective-permute-start(bf16[1,32,512]{2,1,0:T(8,128)(2,1)S(1)} %get-tuple-element.43), channel_id=1, source_target_pairs={{0,1},{1,0},{2,3},{3,2},{4,5},{5,4},{6,7},{7,6},{8,9},{9,8},{10,11... | collective-permute-start | bytes 98312 | tf_op jit(solution)/shard_map/ppermute | solution.py:536
  91.0 1.2 collective-permute-start.4
  92.2 7.7 %copy-start.6 = (bf16[1,32,512]{2,1,0:T(8,128)(2,1)}, bf16[1,32,512]{2,1,0:T(8,128)(2,1)S(1)}, u32[]{:S(2)}) copy-start(bf16[1,32,512]{2,1,0:T(8,128)(2,1)S(1)} %collective-permute-done.3.pair_ref) | copy-start | bytes 98308
  92.2 7.7 %copy-start.7 = (bf16[1,32,512]{2,1,0:T(8,128)(2,1)}, bf16[1,32,512]{2,1,0:T(8,128)(2,1)S(1)}, u32[]{:S(2)}) copy-start(bf16[1,32,512]{2,1,0:T(8,128)(2,1)S(1)} %collective-permute-done.4.next_ref) | copy-start | bytes 98308
  92.2 23.5 %all-to-all-start.3 = ((bf16[16,32,512]{2,1,0:T(8,128)(2,1)}), bf16[16,32,512]{2,1,0:T(8,128)(2,1)S(1)}, u32[]{:S(2)}, u32[]{:S(2)}) async-start(bf16[16,32,512]{2,1,0:T(8,128)(2,1)} %bitcast.21), calls=%async_computation.3 | async-start | bytes 1048576 | tf_op jit(solution)/shard_map/all_to_all | solution.py:529
  99.9 15.8 %copy-start.1 = (f32[18,32,512]{2,1,0:T(8,128)S(1)}, f32[18,32,512]{2,1,0:T(8,128)}, u32[]{:S(2)}) copy-start(f32[18,32,512]{2,1,0:T(8,128)} %get-tuple-element.19.first_ref) | copy-start | bytes 3538948
  115.7 1.0 copy-start
  115.7 1.6 %copy-start.8 = (s32[16]{0:T(128)S(1)}, s32[16]{0:T(128)}, u32[]{:S(2)}) copy-start(s32[16]{0:T(128)} %bands_ref.7) | copy-start | bytes 196
  116.8 2.0 %collective-permute-start.5 = (bf16[2,8,32,512]{3,2,1,0:T(8,128)(2,1)S(1)}, bf16[2,8,32,512]{3,2,1,0:T(8,128)(2,1)S(1)}, u32[]{:S(2)}, u32[]{:S(2)}) collective-permute-start(bf16[2,8,32,512]{3,2,1,0:T(8,128)(2,1)S(1)} %pad_maximum_fusion.2), channel_id=1, source_target_pairs={{0,1},{1,0},{2,3},{3,2},{4,5},{5,4},{6,7},{7,6},{8,9},{9,8},{10,11... | collective-permute-start | bytes 1572872 | tf_op jit(solution)/shard_map/ppermute | solution.py:536

commit v5 on v2

--- a/solution.py
+++ b/solution.py
@@ -38,12 +38,19 @@
     return lax.rsqrt(jnp.mean(values * values, -1, keepdims=True) + EPSILON)
 
 
-def gelu_and_slope(v):
+def gelu_parts(v):
     square = v * v
     cdf = 0.5 + 0.5 * jnp.tanh(v * (ROOT + (ROOT * CUBIC) * square))
-    value = v * cdf
-    slope = cdf + (value - value * cdf) * (2.0 * ROOT + (6.0 * ROOT * CUBIC) * square)
-    return value, slope
+    return square, cdf, v * cdf
+
+
+def gelu(v):
+    return gelu_parts(v)[2]
+
+
+def gelu_slope(v):
+    square, cdf, value = gelu_parts(v)
+    return cdf + (value - value * cdf) * (2.0 * ROOT + (6.0 * ROOT * CUBIC) * square)
 
 
 def whole(shape, space=None):
@@ -161,7 +168,7 @@
 
 
 def forward_body(bands_ref, features_ref, other_ref, rim_ref, expand_ref, taps_ref, project_ref, first_ref,
-                 normed_ref, slab_ref, slope_one_ref, slope_two_ref, slab, normed_one, hidden, hidden_two,
+                 normed_ref, slab_ref, expanded_ref, mixed_ref, slab, normed_one, hidden, hidden_two,
                  total, sems):
     step = pl.program_id(0)
     rows, cols, width = slab.shape
@@ -188,10 +195,10 @@
         for inner in range(4):
             for lane in range(0, chunk, LANES):
                 lanes = slice(lane, lane + LANES)
-                value, slope = gelu_and_slope(expanded[inner * cols : (inner + 1) * cols, lanes])
-                hidden[row + inner, :, lanes] = value.astype(BF16).astype(F32)
+                values = expanded[inner * cols : (inner + 1) * cols, lanes]
+                hidden[row + inner, :, lanes] = gelu(values).astype(BF16).astype(F32)
                 if RIM <= row + inner < RIM + own:
-                    slope_one_ref[row + inner - RIM, :, lanes] = slope.astype(BF16)
+                    expanded_ref[row + inner - RIM, :, lanes] = values
 
     column = lax.broadcasted_iota(jnp.int32, (cols, LANES), 0)
     for lane in range(0, chunk, LANES):
@@ -203,9 +210,8 @@
                 taps[b] * near[0] + taps[3 + b] * near[1] + taps[6 + b] * near[2] for b in range(3)
             ]
             mixed = column_sums(sums[0], sums[1], sums[2], column, cols - 1)
-            value, slope = gelu_and_slope(mixed)
-            hidden_two[row * cols : (row + 1) * cols, lanes] = value.astype(BF16)
-            slope_two_ref[row, :, lanes] = slope.astype(BF16)
+            hidden_two[row * cols : (row + 1) * cols, lanes] = gelu(mixed).astype(BF16)
+            mixed_ref[row, :, lanes] = mixed
     total[...] += nn_dot(hidden_two[...], project_ref[...])
 
     @pl.when(step == pl.num_programs(0) - 1)
@@ -244,8 +250,8 @@
             jax.ShapeDtypeStruct((rows - 2, cols, width), F32),
             jax.ShapeDtypeStruct((own, cols, width), BF16),
             jax.ShapeDtypeStruct((own, cols, width), BF16),
-            jax.ShapeDtypeStruct((own, cols, hidden_width), BF16),
-            jax.ShapeDtypeStruct((rows - 2, cols, hidden_width), BF16),
+            jax.ShapeDtypeStruct((own, cols, hidden_width), F32),
+            jax.ShapeDtypeStruct((rows - 2, cols, hidden_width), F32),
         ],
         scratch_shapes=[
             pltpu.VMEM((rows, cols, width), BF16),
@@ -265,11 +271,34 @@
     )(bands, features, other, rim, w_expand, kernel, w_project)
 
 
-def window_order(groups, cols):
-    order = np.arange(groups * cols)
-    span = groups * 8
-    place = (order // 8) % groups * cols + order % 8 * (cols // 8) + order // span
-    return (place[:, None] == order[None, :]).astype(np.float32)
+def slopes_body(expanded_ref, mixed_ref, slope_one_ref, slope_two_ref):
+    for source, target in ((expanded_ref, slope_one_ref), (mixed_ref, slope_two_ref)):
+        rows, _, chunk = source.shape
+        for row in range(rows):
+            for lane in range(0, chunk, LANES):
+                lanes = slice(lane, lane + LANES)
+                target[row, :, lanes] = gelu_slope(source[row, :, lanes]).astype(BF16)
+
+
+def slopes(expanded, mixed):
+    hidden_width = expanded.shape[2]
+    blocks = [
+        pl.BlockSpec(values.shape[:2] + (CHUNK,), lambda j: (0, 0, j)) for values in (expanded, mixed)
+    ]
+    return pl.pallas_call(
+        slopes_body,
+        grid=(hidden_width // CHUNK,),
+        in_specs=blocks,
+        out_specs=blocks,
+        out_shape=[jax.ShapeDtypeStruct(values.shape, BF16) for values in (expanded, mixed)],
+        compiler_params=params(),
+        cost_estimate=pl.CostEstimate(
+            flops=15 * (expanded.size + mixed.size),
+            bytes_accessed=6 * (expanded.size + mixed.size),
+            transcendentals=expanded.size + mixed.size,
+        ),
+        name="gelu_slopes",
+    )(expanded, mixed)
 
 
 def head_mask(span, head_dim):
@@ -278,103 +307,178 @@
     return (row_head == np.arange(LANES)[None, :] // head_dim).astype(np.float32)
 
 
-def attention_body(normed_ref, cotangent_ref, order_ref, back_ref, mask_ref, qkv_ref, out_ref, added_ref,
-                   grad_ref, projected, grad_attended, grad_projected, attended):
-    groups, _, cols, width = normed_ref.shape
-    tokens = groups * cols
+def lane_tiles(width):
+    return [slice(at, at + LANES) for at in range(0, width, LANES)]
+
+
+def window_places(own, cols):
+    return [(r, q) for r in range(own) for q in range(cols // 8)]
+
+
+def to_windows(source_ref, rows_wide, target):
+    groups, own, cols, width = source_ref.shape
+    span = groups * 8
+    for tile, lanes in enumerate(lane_tiles(width)):
+        for group in range(groups):
+            rows_wide[tile, group] = source_ref[group, :, :, lanes].astype(F32)
+        for index, (r, q) in enumerate(window_places(own, cols)):
+            pieces = [
+                rows_wide[tile, group, r, pl.ds(q, 8, stride=cols // 8), :] for group in range(groups)
+            ]
+            rows = slice(index * span, (index + 1) * span)
+            target[rows, lanes] = jnp.concatenate(pieces, axis=0).astype(BF16)
+
+
+def to_rows(values, rows_wide, target_ref):
+    groups, own, cols, width = target_ref.shape
+    span = groups * 8
+    for tile, lanes in enumerate(lane_tiles(width)):
+        for index, (r, q) in enumerate(window_places(own, cols)):
+            for group in range(groups):
+                first = index * span + group * 8
+                rows_wide[tile, group, r, pl.ds(q, 8, stride=cols // 8), :] = values[first : first + 8, lanes]
+        for group in range(groups):
+            target_ref[group, :, :, lanes] = rows_wide[tile, group].astype(BF16)
+
+
+def wide_scratch(shape):
+    groups, own, cols, width = shape
+    return pltpu.VMEM((width // LANES, groups, own, cols, LANES), F32)
+
+
+def grad_attended_body(cotangent_ref, out_ref, grad_ref, rows_wide, in_windows):
+    to_windows(cotangent_ref, rows_wide, in_windows)
+    grad_ref[...] = nt_dot(in_windows[...], out_ref[...]).astype(BF16)
+
+
+def attended_gradient(cotangent, w_out):
+    groups, own, cols, width = cotangent.shape
+    shape = (groups * own * cols, width)
+    return pl.pallas_call(
+        grad_attended_body,
+        grid=(1,),
+        in_specs=[whole(cotangent.shape), whole(w_out.shape)],
+        out_specs=whole(shape),
+        out_shape=jax.ShapeDtypeStruct(shape, BF16),
+        scratch_shapes=[wide_scratch(cotangent.shape), pltpu.VMEM(shape, BF16)],
+        compiler_params=params(),
+        cost_estimate=pl.CostEstimate(
+            flops=2 * shape[0] * width * width, bytes_accessed=2 * 1024 * 1024, transcendentals=0
+        ),
+        name="attended_gradient",
+    )(cotangent, w_out)
+
+
+def per_query(values, weights, span, head_dim):
+    wide = nn_dot(values.T, weights)
+    half = LANES // 2
+    own = jnp.concatenate([wide[:half, :LANES], wide[half:, LANES:]], axis=0).T
+    lane_head = lax.broadcasted_iota(jnp.int32, (span, LANES), 1) // head_dim
+    return jnp.where(lane_head % 2 == 0, own[:span], own[span:])
+
+
+def attention_body(normed_ref, grad_attended_ref, mask_ref, qkv_ref, grad_ref, weights_ref, values_ref,
+                   rows_wide, in_windows, projected, grad_projected):
+    groups, own, cols, width = normed_ref.shape
     span = groups * 8
     head_dim = width // HEADS
     heads = LANES // head_dim
     scale = 1.0 / math.sqrt(head_dim)
     steepness = scale * math.log2(math.e)
 
-    normed = nn_dot(order_ref[...], normed_ref[...].reshape(tokens, width)).astype(BF16)
-    projected[...] = nn_dot(normed, qkv_ref[...]).astype(BF16)
-    grad_rows = nn_dot(order_ref[...], cotangent_ref[...].reshape(tokens, width)).astype(BF16)
-    grad_attended[...] = nt_dot(grad_rows, out_ref[...]).astype(BF16)
-
-    lane_head = lax.broadcasted_iota(jnp.int32, (span, LANES), 1) // head_dim
+    to_windows(normed_ref, rows_wide, in_windows)
+    projected[...] = nn_dot(in_windows[...], qkv_ref[...]).astype(BF16)
+    values_ref[...] = projected[:, 2 * width :]
 
     def spread(values):
         return jnp.concatenate([values] * heads, axis=0) * mask_ref[...]
 
-    def per_query(values, weights):
-        wide = nn_dot(values.T, weights)
-        half = LANES // 2
-        own = jnp.concatenate([wide[:half, :LANES], wide[half:, LANES:]], axis=0).T
-        return jnp.where(lane_head % 2 == 0, own[:span], own[span:])
-
-    for index in range(cols // 8):
-        rows = slice(index * span, (index + 1) * span)
+    def window(index, carry):
+        rows = pl.ds(pl.multiple_of(index * span, span), span)
         for part in range(width // LANES):
             q_at, k_at, v_at = (
                 slice(t * width + part * LANES, t * width + (part + 1) * LANES) for t in range(3)
             )
             q, k, v = projected[rows, q_at], projected[rows, k_at], projected[rows, v_at]
             q_wide = spread(q)
-            g_wide = spread(grad_attended[rows, q_at])
+            g_wide = spread(grad_attended_ref[rows, q_at])
             scores = nt_dot(k, q_wide)
             powers = jnp.exp2((scores - jnp.max(scores, axis=0, keepdims=True)) * steepness)
             weights = powers * (1.0 / jnp.sum(powers, axis=0, keepdims=True))
             half = weights.astype(BF16)
+            weights_ref[index, :, part * heads * span : (part + 1) * heads * span] = half
             grad_weights = nt_dot(v, g_wide)
             row_dot = jnp.sum(weights * grad_weights, axis=0, keepdims=True)
             grad_scores = (weights * (grad_weights - row_dot)).astype(BF16)
-            attended[rows, q_at] = per_query(v, half).astype(BF16)
-            grad_projected[rows, q_at] = (per_query(k, grad_scores) * scale).astype(BF16)
+            grad_projected[rows, q_at] = (per_query(k, grad_scores, span, head_dim) * scale).astype(BF16)
             grad_projected[rows, k_at] = (nn_dot(grad_scores, q_wide) * scale).astype(BF16)
             grad_projected[rows, v_at] = nn_dot(half, g_wide).astype(BF16)
-
-    shape = (groups, 1, cols, width)
-    grad_normed = nt_dot(grad_projected[...], qkv_ref[...]).astype(BF16)
-    grad_ref[...] = nn_dot(back_ref[...], grad_normed).astype(BF16).reshape(shape)
-    in_rows = nn_dot(back_ref[...], attended[...]).astype(BF16)
-    added_ref[...] = nn_dot(in_rows, out_ref[...]).astype(BF16).reshape(shape)
-
-
-def attention(normed, cotangent, w_qkv, w_out):
+        return carry
+
+    lax.fori_loop(0, own * cols // 8, window, 0, unroll=4)
+    to_rows(nt_dot(grad_projected[...], qkv_ref[...]), rows_wide, grad_ref)
+
+
+def attention(normed, grad_attended, w_qkv):
     groups, own, cols, width = normed.shape
-    tokens = groups * cols
-    order = window_order(groups, cols)
-    mask = head_mask(groups * 8, width // HEADS)
-    block = pl.BlockSpec((groups, 1, cols, width), lambda r: (0, r, 0, 0))
-    out = jax.ShapeDtypeStruct(normed.shape, BF16)
+    span = groups * 8
+    tokens = groups * own * cols
+    windows = tokens // span
+    mask = head_mask(span, width // HEADS)
+    out_shapes = [normed.shape, (windows, span, HEADS * span), (tokens, width)]
     return pl.pallas_call(
         attention_body,
-        grid=(own,),
+        grid=(1,),
         in_specs=[
-            block,
-            block,
-            whole(order.shape),
-            whole(order.shape),
+            whole(normed.shape),
+            whole(grad_attended.shape),
             whole(mask.shape),
             whole(w_qkv.shape),
-            whole(w_out.shape),
-        ],
-        out_specs=[block, block],
-        out_shape=[out, out],
+        ],
+        out_specs=[whole(shape) for shape in out_shapes],
+        out_shape=[jax.ShapeDtypeStruct(shape, BF16) for shape in out_shapes],
         scratch_shapes=[
-            pltpu.VMEM((tokens, 3 * width), BF16),
+            wide_scratch(normed.shape),
             pltpu.VMEM((tokens, width), BF16),
             pltpu.VMEM((tokens, 3 * width), BF16),
-            pltpu.VMEM((tokens, width), BF16),
+            pltpu.VMEM((tokens, 3 * width), BF16),
         ],
         compiler_params=params(),
         cost_estimate=pl.CostEstimate(
-            flops=20 * own * tokens * width * width,
+            flops=16 * tokens * width * width,
             bytes_accessed=4 * 1024 * 1024,
-            transcendentals=own * tokens * 64 * HEADS,
+            transcendentals=tokens * span * HEADS,
         ),
         name="window_attention",
-    )(
-        normed,
-        cotangent,
-        jnp.asarray(order, BF16),
-        jnp.asarray(order.T, BF16),
-        jnp.asarray(mask, BF16),
-        w_qkv,
-        w_out,
-    )
+    )(normed, grad_attended, jnp.asarray(mask, BF16), w_qkv)
+
+
+def attended_body(weights_ref, values_ref, out_ref, added_ref, rows_wide, attended):
+    windows, span, wide = weights_ref.shape
+    width = values_ref.shape[1]
+    heads = LANES * HEADS // width
+    for index in range(windows):
+        rows = slice(index * span, (index + 1) * span)
+        for part, lanes in enumerate(lane_tiles(width)):
+            weights = weights_ref[index, :, part * heads * span : (part + 1) * heads * span]
+            attended[rows, lanes] = per_query(values_ref[rows, lanes], weights, span, width // HEADS).astype(BF16)
+    to_rows(nn_dot(attended[...], out_ref[...]), rows_wide, added_ref)
+
+
+def attend(weights, values, w_out, shape):
+    return pl.pallas_call(
+        attended_body,
+        grid=(1,),
+        in_specs=[whole(weights.shape), whole(values.shape), whole(w_out.shape)],
+        out_specs=whole(shape),
+        out_shape=jax.ShapeDtypeStruct(shape, BF16),
+        scratch_shapes=[wide_scratch(shape), pltpu.VMEM(values.shape, BF16)],
+        compiler_params=params(),
+        cost_estimate=pl.CostEstimate(
+            flops=4 * values.size * values.shape[1], bytes_accessed=3 * 1024 * 1024, transcendentals=0
+        ),
+        name="attended_output",
+    )(weights, values, w_out)
 
 
 def backward_body(bands_ref, cotangent_ref, other_ref, rim_ref, slab_ref, first_ref, grad_slab_ref, grad_ref,
@@ -538,16 +642,21 @@
     rim, grad_slab = lax.optimization_barrier((rim, grad_slab))
 
     grad_windows = exchange_windows(grad_slab)
-    first, normed, slab, slope_one, slope_two = forward(
+    first, normed, slab, expanded, mixed = forward(
         row_bands, features, other_features, rim, w_expand, kernel, w_project
     )
     normed, grad_windows = lax.optimization_barrier((normed, grad_windows))
     normed_windows = exchange_windows(normed)
     shape = (8, GRID_ROWS // 8, cols, width)
-    added, grad_normed = attention(
-        normed_windows.reshape(shape), grad_windows.reshape(shape), w_qkv, w_out
+    slope_one, slope_two = slopes(expanded, mixed)
+    grad_attended = attended_gradient(grad_windows.reshape(shape), w_out)
+    normed_windows, slope_one, slope_two, grad_attended = lax.optimization_barrier(
+        (normed_windows, slope_one, slope_two, grad_attended)
     )
+    grad_normed, weights, values = attention(normed_windows.reshape(shape), grad_attended, w_qkv)
     grad_rows = exchange_windows(grad_normed.reshape(GRID_ROWS, cols, width))
+    added = attend(weights, values, w_out, shape)
+    grad_rows, added = lax.optimization_barrier((grad_rows, added))
     top, bottom = grad_rows[:1], grad_rows[GRID_ROWS - 1 :]
     pair_row = swap_pair(jnp.where(leads, bottom, top))
     next_row = swap_next(jnp.where(leads, top, bottom))

time: 116 us -> 114 us (0.983)
  blocking collectives: 20.3 us -> 0 us
  Pallas kernels: 47.9 us -> 58.4 us
  starting transfers between devices: 22.7 us -> 28.7 us
    all_to_all x1 -> x0, blocking collectives: 20.3 us -> none  [exchange_windows(): lax.all_to_all(rows, 'row', split_axis=0, concat_axis=0, tiled=True, axis...]
    pallas_call x1 -> x4, Pallas kernels: 14.9 us -> 27 us  [the longest x1 12.9 us: attention(): pl.pallas_call(attention_body, grid=(1,), in_specs=[whole(normed.shape),...]
    all_to_all x3 -> x4, starting transfers between devices: 20.6 us -> 26.6 us  [exchange_windows(): lax.all_to_all(rows, 'row', split_axis=0, concat_axis=0, tiled=True, axis...]
    pallas_call x1, Pallas kernels: 15.9 us -> 14.3 us  [forward(): pl.pallas_call(forward_body, grid=(hidden_width // CHUNK,), in_specs=[in_...]
    unnamed x20 -> x22, local copies, waits for them, and re-layouts: 1.78 us -> 2.58 us
    all_to_all x3 -> x4, waiting for transfers between devices: 16.8 us -> 17.4 us  [exchange_windows(): lax.all_to_all(rows, 'row', split_axis=0, concat_axis=0, tiled=True, axis...]
  transfers between devices with their start and end apart: 9 -> 10, of which waited for: 4 -> 5; matrix products, arithmetic and copies ran while one was open for 1% -> 1% of each run, Pallas kernels for 29% -> 40%
where the time goes in v5:
time: 114 us; the launch traced here: 113 us
  Pallas kernels  58.4 us (51%)
  starting transfers between devices  28.7 us (25%)
  waiting for transfers between devices  18.6 us (16%)
  local copies, waits for them, and re-layouts  3.16 us (3%)
  other arithmetic  2.32 us (2%)
  between operations  1.53 us (1%)
    all_to_all x4, starting transfers between devices, exchange_windows(): lax.all_to_all(rows, 'row', split_axis=0, concat_axis=0, tiled=True, axis...  26.6 us
    all_to_all x4, waiting for transfers between devices, exchange_windows(): lax.all_to_all(rows, 'row', split_axis=0, concat_axis=0, tiled=True, axis...  17.4 us
    pallas_call x1, Pallas kernels, forward(): pl.pallas_call(forward_body, grid=(hidden_width // CHUNK,), in_specs=[in_...  14.3 us
    pallas_call x1, Pallas kernels, attention(): pl.pallas_call(attention_body, grid=(1,), in_specs=[whole(normed.shape),...  12.9 us
    pallas_call x1, Pallas kernels, backward(): pl.pallas_call(backward_body, grid=(hidden_width // CHUNK,), in_specs=[in...  12.4 us
    pallas_call x1, Pallas kernels, slopes(): pl.pallas_call(slopes_body, grid=(hidden_width // CHUNK,), in_specs=block...  7.75 us
    pallas_call x1, Pallas kernels, attend(): pl.pallas_call(attended_body, grid=(1,), in_specs=[whole(weights.shape),...  3.72 us
    unnamed x22, local copies, waits for them, and re-layouts  2.58 us
  transfers between devices with their start and end apart: 10, of which 5 were waited for; matrix products, arithmetic and copies ran while one was open for 1% of the time, Pallas kernels for 40%

profile of v5, /device:TPU:0, one launch (start us, length us, event | category | flops | bytes accessed | tf_op | source)
XLA Modules:
  0.0 112.7 jit_solution(7338287435955381848)
XLA Ops:
  1.2 2.2 %rim_rows.1 = bf16[3,32,512]{2,1,0:T(8,128)(2,1)} custom-call(s32[16]{0:T(128)} %bands_ref.7, bf16[24,32,512]{2,1,0:T(8,128)(2,1)} %features_ref.3, bf16[24,32,512]{2,1,0:T(8,128)(2,1)} %cotangent_ref.3), custom_call_target="tpu_custom_call" | custom-call | tf_op jit(solution)/shard_map/rim_rows/pallas_call | solution.py:147
  3.4 0.7 collective-permute-start.1
  4.1 0.9 copy-done.2
  5.0 2.5 %even_rows.1.grad_slab_ref = bf16[16,32,512]{2,1,0:T(8,128)(2,1)} custom-call(s32[16]{0:T(128)} %bands_ref.7, bf16[24,32,512]{2,1,0:T(8,128)(2,1)} %cotangent_ref.3, bf16[24,32,512]{2,1,0:T(8,128)(2,1)} %copy-done.2), custom_call_target="tpu_custom_call" | custom-call | tf_op jit(solution)/shard_map/even_rows/pallas_call | solution.py:115
  7.5 9.3 %all-to-all-start = ((bf16[16,32,512]{2,1,0:T(8,128)(2,1)}), bf16[16,32,512]{2,1,0:T(8,128)(2,1)S(1)}, u32[]{:S(2)}, u32[]{:S(2)}) async-start(bf16[16,32,512]{2,1,0:T(8,128)(2,1)} %even_rows.1.grad_slab_ref), calls=%async_computation | async-start | bytes 1048576 | tf_op jit(solution)/shard_map/all_to_all | solution.py:605
  16.9 0.9 copy-done.10
  17.8 14.3 %bottleneck_forward.1 = (f32[18,32,512]{2,1,0:T(8,128)}, bf16[16,32,512]{2,1,0:T(8,128)(2,1)}, bf16[16,32,512]{2,1,0:T(8,128)(2,1)}, f32[16,32,2048]{2,1,0:T(8,128)}, f32[18,32,2048]{2,1,0:T(8,128)}) custom-call(s32[16]{0:T(128)} %bands_ref.7, bf16[24,32,512]{2,1,0:T(8,128)(2,1)} %features_ref.3, bf16[24,32,512]{2,1,0:T(8,128)(2,1)} %copy-done.10, ...), custom_call_target="tpu_custom_call" | custom-call | flops 2684354560 | bytes 12582912 | tf_op jit(solution)/shard_map/bottleneck_forward/pallas_call | solution.py:230
  32.1 6.0 %all-to-all-start.1 = ((bf16[16,32,512]{2,1,0:T(8,128)(2,1)}), bf16[16,32,512]{2,1,0:T(8,128)(2,1)S(1)}, u32[]{:S(2)}, u32[]{:S(2)}) async-start(bf16[16,32,512]{2,1,0:T(8,128)(2,1)} %get-tuple-element.32), calls=%async_computation.1 | async-start | bytes 1048576 | tf_op jit(solution)/shard_map/all_to_all | solution.py:605
  38.1 7.8 %gelu_slopes.1 = (bf16[16,32,2048]{2,1,0:T(8,128)(2,1)}, bf16[18,32,2048]{2,1,0:T(8,128)(2,1)}) custom-call(f32[16,32,2048]{2,1,0:T(8,128)} %get-tuple-element.33.expanded_ref, f32[18,32,2048]{2,1,0:T(8,128)} %get-tuple-element.34.mixed_ref), custom_call_target="tpu_custom_call" | custom-call | flops 33423360 | bytes 13369344 | tf_op jit(solution)/shard_map/gelu_slopes/pallas_call | solution.py:288
  45.9 2.5 %attended_gradient.1.grad_attended_ref = bf16[512,512]{1,0:T(8,128)(2,1)} custom-call(bf16[8,2,32,512]{3,2,1,0:T(8,128)(2,1)} %bitcast.22, bf16[512,512]{1,0:T(8,128)(2,1)} %out_ref.3), custom_call_target="tpu_custom_call" | custom-call | flops 268435456 | bytes 2097152 | tf_op jit(solution)/shard_map/attended_gradient/pallas_call | solution.py:357
  48.4 4.0 %all-to-all-done.1 = bf16[16,32,512]{2,1,0:T(8,128)(2,1)S(1)} async-done(((bf16[16,32,512]{2,1,0:T(8,128)(2,1)}), bf16[16,32,512]{2,1,0:T(8,128)(2,1)S(1)}, u32[]{:S(2)}, u32[]{:S(2)}) %all-to-all-start.1) | async-done | bytes 524320 | tf_op jit(solution)/shard_map/all_to_all | solution.py:605
  52.4 0.8 copy-done.5
  53.2 12.9 %window_attention.1 = (bf16[8,2,32,512]{3,2,1,0:T(8,128)(2,1)}, bf16[8,64,1024]{2,1,0:T(8,128)(2,1)}, bf16[512,512]{1,0:T(8,128)(2,1)}) custom-call(bf16[8,2,32,512]{3,2,1,0:T(8,128)(2,1)} %bitcast.24, bf16[512,512]{1,0:T(8,128)(2,1)} %attended_gradient.1.grad_attended_ref, bf16[256,128]{1,0:T(8,128)(2,1)} %constant.29.clone.mask_ref, bf16[512,1536]{1,0:T(8,128)(2,1)} %qkv_ref.1), custom_call_target="tpu_custom_call" | custom-call | flops 2147483648 | bytes 4194304 | tf_op jit(solution)/shard_map/window_attention/pallas_call | solution.py:429
  66.1 3.6 %all-to-all-start.2 = ((bf16[16,32,512]{2,1,0:T(8,128)(2,1)}), bf16[16,32,512]{2,1,0:T(8,128)(2,1)S(1)}, u32[]{:S(2)}, u32[]{:S(2)}) async-start(bf16[16,32,512]{2,1,0:T(8,128)(2,1)} %bitcast.23), calls=%async_computation.2 | async-start | bytes 1048576 | tf_op jit(solution)/shard_map/all_to_all | solution.py:605
  69.7 3.7 %attended_output.1 = bf16[8,2,32,512]{3,2,1,0:T(8,128)(2,1)} custom-call(bf16[8,64,1024]{2,1,0:T(8,128)(2,1)} %get-tuple-element.41.weights_ref, bf16[512,512]{1,0:T(8,128)(2,1)} %get-tuple-element.42.values_ref, bf16[512,512]{1,0:T(8,128)(2,1)} %out_ref.3), custom_call_target="tpu_custom_call" | custom-call | flops 536870912 | bytes 3145728 | tf_op jit(solution)/shard_map/attended_output/pallas_call | solution.py:469
  73.5 10.8 %all-to-all-done.2.grad_ref = bf16[16,32,512]{2,1,0:T(8,128)(2,1)S(1)} async-done(((bf16[16,32,512]{2,1,0:T(8,128)(2,1)}), bf16[16,32,512]{2,1,0:T(8,128)(2,1)S(1)}, u32[]{:S(2)}, u32[]{:S(2)}) %all-to-all-start.2) | async-done | bytes 524320 | tf_op jit(solution)/shard_map/all_to_all | solution.py:605
  84.3 0.7 collective-permute-start.4
  85.5 7.7 %all-to-all-start.3 = ((bf16[16,32,512]{2,1,0:T(8,128)(2,1)}), bf16[16,32,512]{2,1,0:T(8,128)(2,1)S(1)}, u32[]{:S(2)}, u32[]{:S(2)}) async-start(bf16[16,32,512]{2,1,0:T(8,128)(2,1)} %bitcast.21), calls=%async_computation.3 | async-start | bytes 1048576 | tf_op jit(solution)/shard_map/all_to_all | solution.py:605
  93.2 12.4 %bottleneck_backward.1 = bf16[16,32,512]{2,1,0:T(8,128)(2,1)} custom-call(s32[16]{0:T(128)} %bands_ref.7, bf16[24,32,512]{2,1,0:T(8,128)(2,1)} %cotangent_ref.3, bf16[24,32,512]{2,1,0:T(8,128)(2,1)} %copy-done.2, bf16[3,32,512]{2,1,0:T(8,128)(2,1)} %copy-done.6, bf16[16,32,512]{2,1,0:T(8,128)(2,1)} %get-tuple-element.29.slab_ref, ...), custom_call_target="tpu_custom_call" | custom-call | flops 2415919104 | bytes 12582912 | tf_op jit(solution)/shard_map/bottleneck_backward/pallas_call | solution.py:556
  105.6 2.7 %all-to-all-done.3 = bf16[16,32,512]{2,1,0:T(8,128)(2,1)S(1)} async-done(((bf16[16,32,512]{2,1,0:T(8,128)(2,1)}), bf16[16,32,512]{2,1,0:T(8,128)(2,1)S(1)}, u32[]{:S(2)}, u32[]{:S(2)}) %all-to-all-start.3) | async-done | bytes 524320 | tf_op jit(solution)/shard_map/all_to_all | solution.py:605
  108.8 0.6 dynamic_slice.3
  110.0 0.6 collective-permute-done.5
  110.8 1.0 pad_maximum_fusion.1
  111.7 1.0 pad_maximum_fusion
  (34 shorter events, 1.7 us)
Async XLA Ops:
  0.6 3.5 %collective-permute-start.2 = (bf16[24,32,512]{2,1,0:T(8,128)(2,1)}, bf16[24,32,512]{2,1,0:T(8,128)(2,1)S(1)}, u32[]{:S(2)}, u32[]{:S(2)}) collective-permute-start(bf16[24,32,512]{2,1,0:T(8,128)(2,1)} %cotangent_ref.3), channel_id=1, source_target_pairs={{0,1},{1,0},{2,3},{3,2},{4,5},{5,4},{6,7},{7,6},{8,9},{9,8},{10,11... | collective-permute-start | bytes 2359304 | tf_op jit(solution)/shard_map/ppermute | solution.py:612
  1.1 15.7 %collective-permute-start = (bf16[24,32,512]{2,1,0:T(8,128)(2,1)}, bf16[24,32,512]{2,1,0:T(8,128)(2,1)S(1)}, u32[]{:S(2)}, u32[]{:S(2)}) collective-permute-start(bf16[24,32,512]{2,1,0:T(8,128)(2,1)} %features_ref.3), channel_id=1, source_target_pairs={{0,1},{1,0},{2,3},{3,2},{4,5},{5,4},{6,7},{7,6},{8,9},{9,8},{10,11... | collective-permute-start | bytes 2359304 | tf_op jit(solution)/shard_map/ppermute | solution.py:612
  3.4 4.1 %collective-permute-start.1 = (bf16[3,32,512]{2,1,0:T(8,128)(2,1)}, bf16[3,32,512]{2,1,0:T(8,128)(2,1)S(1)}, u32[]{:S(2)}, u32[]{:S(2)}) collective-permute-start(bf16[3,32,512]{2,1,0:T(8,128)(2,1)} %rim_rows.1), channel_id=1, source_target_pairs={{1,2},{3,4},{5,6},{7,8},{9,10},{11,12},{13,14},{2,1},{4,3},{6,5},{... | collective-permute-start | bytes 294920 | tf_op jit(solution)/shard_map/ppermute | solution.py:618
  4.1 0.9 copy-start.2
  7.5 9.4 %copy-start.6 = (bf16[3,32,512]{2,1,0:T(8,128)(2,1)}, bf16[3,32,512]{2,1,0:T(8,128)(2,1)S(1)}, u32[]{:S(2)}) copy-start(bf16[3,32,512]{2,1,0:T(8,128)(2,1)S(1)} %collective-permute-done.1.rim_ref) | copy-start | bytes 294916
  7.5 24.6 %all-to-all-start = ((bf16[16,32,512]{2,1,0:T(8,128)(2,1)}), bf16[16,32,512]{2,1,0:T(8,128)(2,1)S(1)}, u32[]{:S(2)}, u32[]{:S(2)}) async-start(bf16[16,32,512]{2,1,0:T(8,128)(2,1)} %even_rows.1.grad_slab_ref), calls=%async_computation | async-start | bytes 1048576 | tf_op jit(solution)/shard_map/all_to_all | solution.py:605
  16.9 0.9 copy-start.10
  32.1 13.8 %copy-start.4 = (bf16[16,32,512]{2,1,0:T(8,128)(2,1)}, bf16[16,32,512]{2,1,0:T(8,128)(2,1)S(1)}, u32[]{:S(2)}) copy-start(bf16[16,32,512]{2,1,0:T(8,128)(2,1)S(1)} %all-to-all-done) | copy-start | bytes 1572868
  32.1 20.3 %all-to-all-start.1 = ((bf16[16,32,512]{2,1,0:T(8,128)(2,1)}), bf16[16,32,512]{2,1,0:T(8,128)(2,1)S(1)}, u32[]{:S(2)}, u32[]{:S(2)}) async-start(bf16[16,32,512]{2,1,0:T(8,128)(2,1)} %get-tuple-element.32), calls=%async_computation.1 | async-start | bytes 1048576 | tf_op jit(solution)/shard_map/all_to_all | solution.py:605
  52.4 0.8 copy-start.5
  66.1 18.1 %all-to-all-start.2 = ((bf16[16,32,512]{2,1,0:T(8,128)(2,1)}), bf16[16,32,512]{2,1,0:T(8,128)(2,1)S(1)}, u32[]{:S(2)}, u32[]{:S(2)}) async-start(bf16[16,32,512]{2,1,0:T(8,128)(2,1)} %bitcast.23), calls=%async_computation.2 | async-start | bytes 1048576 | tf_op jit(solution)/shard_map/all_to_all | solution.py:605
  84.2 9.0 %copy-start.3 = (bf16[16,32,512]{2,1,0:T(8,128)(2,1)}, bf16[16,32,512]{2,1,0:T(8,128)(2,1)S(1)}, u32[]{:S(2)}) copy-start(bf16[16,32,512]{2,1,0:T(8,128)(2,1)S(1)} %all-to-all-done.2.grad_ref) | copy-start | bytes 1572868
  84.2 1.3 %collective-permute-start.3 = (bf16[1,32,512]{2,1,0:T(8,128)(2,1)S(1)}, bf16[1,32,512]{2,1,0:T(8,128)(2,1)S(1)}, u32[]{:S(2)}, u32[]{:S(2)}) collective-permute-start(bf16[1,32,512]{2,1,0:T(8,128)(2,1)S(1)} %get-tuple-element.61), channel_id=1, source_target_pairs={{0,1},{1,0},{2,3},{3,2},{4,5},{5,4},{6,7},{7,6},{8,9},{9,8},{10,11... | collective-permute-start | bytes 98312 | tf_op jit(solution)/shard_map/ppermute | solution.py:612
  84.3 1.2 %collective-permute-start.4 = (bf16[1,32,512]{2,1,0:T(8,128)(2,1)S(1)}, bf16[1,32,512]{2,1,0:T(8,128)(2,1)S(1)}, u32[]{:S(2)}, u32[]{:S(2)}) collective-permute-start(bf16[1,32,512]{2,1,0:T(8,128)(2,1)S(1)} %get-tuple-element.60), channel_id=1, source_target_pairs={{1,2},{3,4},{5,6},{7,8},{9,10},{11,12},{13,14},{2,1},{4,3},{6,5},{... | collective-permute-start | bytes 98312 | tf_op jit(solution)/shard_map/ppermute | solution.py:618
  85.5 7.7 %copy-start.7 = (bf16[1,32,512]{2,1,0:T(8,128)(2,1)}, bf16[1,32,512]{2,1,0:T(8,128)(2,1)S(1)}, u32[]{:S(2)}) copy-start(bf16[1,32,512]{2,1,0:T(8,128)(2,1)S(1)} %collective-permute-done.3.pair_ref) | copy-start | bytes 98308
  85.5 7.7 %copy-start.8 = (bf16[1,32,512]{2,1,0:T(8,128)(2,1)}, bf16[1,32,512]{2,1,0:T(8,128)(2,1)S(1)}, u32[]{:S(2)}) copy-start(bf16[1,32,512]{2,1,0:T(8,128)(2,1)S(1)} %collective-permute-done.4.next_ref) | copy-start | bytes 98308
  85.5 22.9 %all-to-all-start.3 = ((bf16[16,32,512]{2,1,0:T(8,128)(2,1)}), bf16[16,32,512]{2,1,0:T(8,128)(2,1)S(1)}, u32[]{:S(2)}, u32[]{:S(2)}) async-start(bf16[16,32,512]{2,1,0:T(8,128)(2,1)} %bitcast.21), calls=%async_computation.3 | async-start | bytes 1048576 | tf_op jit(solution)/shard_map/all_to_all | solution.py:605
  93.2 15.2 %copy-start.1 = (f32[18,32,512]{2,1,0:T(8,128)S(1)}, f32[18,32,512]{2,1,0:T(8,128)}, u32[]{:S(2)}) copy-start(f32[18,32,512]{2,1,0:T(8,128)} %get-tuple-element.28.first_ref) | copy-start | bytes 3538948
  105.6 2.9 %copy-start = (bf16[16,32,512]{2,1,0:T(8,128)(2,1)S(1)}, bf16[16,32,512]{2,1,0:T(8,128)(2,1)}, u32[]{:S(2)}) copy-start(bf16[16,32,512]{2,1,0:T(8,128)(2,1)} %bottleneck_backward.1) | copy-start | bytes 1572868
  105.6 3.1 %copy-start.9 = (s32[16]{0:T(128)S(1)}, s32[16]{0:T(128)}, u32[]{:S(2)}) copy-start(s32[16]{0:T(128)} %bands_ref.7) | copy-start | bytes 196
  108.7 2.0 %collective-permute-start.5 = (bf16[2,8,32,512]{3,2,1,0:T(8,128)(2,1)S(1)}, bf16[2,8,32,512]{3,2,1,0:T(8,128)(2,1)S(1)}, u32[]{:S(2)}, u32[]{:S(2)}) collective-permute-start(bf16[2,8,32,512]{3,2,1,0:T(8,128)(2,1)S(1)} %pad_maximum_fusion.2), channel_id=1, source_target_pairs={{0,1},{1,0},{2,3},{3,2},{4,5},{5,4},{6,7},{7,6},{8,9},{9,8},{10,11... | collective-permute-start | bytes 1572872 | tf_op jit(solution)/shard_map/ppermute | solution.py:612

commit v6 on v5

--- a/solution.py
+++ b/solution.py
@@ -19,7 +19,7 @@
 CUBIC = 0.044715
 F32 = jnp.float32
 BF16 = jnp.bfloat16
-VMEM_LIMIT = 56 * 1024 * 1024
+VMEM_LIMIT = 20 * 1024 * 1024
 
 
 def nt_dot(left, right):
@@ -53,17 +53,12 @@
     return cdf + (value - value * cdf) * (2.0 * ROOT + (6.0 * ROOT * CUBIC) * square)
 
 
-def whole(shape, space=None):
-    zeros = (0,) * len(shape)
-    return pl.BlockSpec(shape, lambda *_: zeros)
+def in_vmem():
+    return pl.BlockSpec(memory_space=pltpu.VMEM)
 
 
 def params():
     return pltpu.CompilerParams(vmem_limit_bytes=VMEM_LIMIT)
-
-
-def anywhere():
-    return pl.BlockSpec(memory_space=pl.ANY)
 
 
 def in_scalars():
@@ -86,71 +81,47 @@
     return source, jnp.where(beyond, 0, jnp.where(in_leader, row, row - leader_share))
 
 
-def start_pull(bands_ref, first, sources, rows, target, sem, rim_row=0):
+def pull(bands_ref, first, sources, rows, target, at, rim_row=0):
     where, row = place(bands_ref, first)
     row = jnp.where(where == 2, rim_row, row)
     for number, source in enumerate(sources):
 
         @pl.when(where == number)
         def _():
-            pltpu.make_async_copy(source.at[pl.ds(row, rows)], target, sem).start()
-
-
-def wait_pull(sources, rows, target, sem):
-    pltpu.make_async_copy(sources[0].at[pl.ds(0, rows)], target, sem).wait()
-
-
-def even_body(bands_ref, own_ref, other_ref, out_ref, sems):
-    sources = (own_ref, other_ref)
-    targets = [out_ref.at[pl.ds(BAND * half, BAND)] for half in range(2)]
+            target[at : at + rows] = source[pl.ds(row, rows)]
+
+
+def even_body(bands_ref, own_ref, other_ref, out_ref):
     for half in range(2):
-        start_pull(bands_ref, BAND * half, sources, BAND, targets[half], sems.at[half])
-    for half in range(2):
-        wait_pull(sources, BAND, targets[half], sems.at[half])
+        pull(bands_ref, BAND * half, (own_ref, other_ref), BAND, out_ref, BAND * half)
 
 
 def even_rows(bands, own, other):
-    capacity, cols, width = own.shape
-    shape = (GRID_ROWS, cols, width)
+    shape = (GRID_ROWS,) + own.shape[1:]
     return pl.pallas_call(
         even_body,
-        grid=(1,),
-        in_specs=[in_scalars(), anywhere(), anywhere()],
-        out_specs=whole(shape),
+        in_specs=[in_scalars(), in_vmem(), in_vmem()],
+        out_specs=in_vmem(),
         out_shape=jax.ShapeDtypeStruct(shape, own.dtype),
-        scratch_shapes=[pltpu.SemaphoreType.DMA((2,))],
         compiler_params=params(),
         name="even_rows",
     )(bands, own, other)
 
 
-def rim_body(bands_ref, features_ref, cotangent_ref, out_ref, sems):
+def rim_body(bands_ref, features_ref, cotangent_ref, out_ref):
     parity, _, share = shares(bands_ref)
     leads = parity == 0
-    copies = [
-        pltpu.make_async_copy(
-            features_ref.at[pl.ds(jnp.where(leads, 0, share - RIM), RIM)], out_ref.at[pl.ds(0, RIM)], sems.at[0]
-        ),
-        pltpu.make_async_copy(
-            cotangent_ref.at[pl.ds(jnp.where(leads, 0, share - 1), 1)], out_ref.at[pl.ds(RIM, 1)], sems.at[1]
-        ),
-    ]
-    for copy in copies:
-        copy.start()
-    for copy in copies:
-        copy.wait()
+    out_ref[0:RIM] = features_ref[pl.ds(jnp.where(leads, 0, share - RIM), RIM)]
+    out_ref[RIM : RIM + 1] = cotangent_ref[pl.ds(jnp.where(leads, 0, share - 1), 1)]
 
 
 def rim_rows(bands, features, cotangent):
-    capacity, cols, width = features.shape
-    shape = (RIM + 1, cols, width)
+    shape = (RIM + 1,) + features.shape[1:]
     return pl.pallas_call(
         rim_body,
-        grid=(1,),
-        in_specs=[in_scalars(), anywhere(), anywhere()],
-        out_specs=whole(shape),
+        in_specs=[in_scalars(), in_vmem(), in_vmem()],
+        out_specs=in_vmem(),
         out_shape=jax.ShapeDtypeStruct(shape, features.dtype),
-        scratch_shapes=[pltpu.SemaphoreType.DMA((2,))],
         compiler_params=params(),
         name="rim_rows",
     )(bands, features, cotangent)
@@ -163,64 +134,62 @@
 
 
 def spread_taps(taps_ref, lanes, cols):
-    taps = taps_ref[...].astype(F32)
-    return [jnp.broadcast_to(taps[i : i + 1, lanes], (cols, LANES)) for i in range(9)]
+    taps = taps_ref[:, lanes].astype(F32)
+    return [jnp.broadcast_to(taps[i : i + 1], (cols, LANES)) for i in range(9)]
+
+
+def hidden_lanes(step, lane=0, count=CHUNK):
+    return pl.ds(pl.multiple_of(step * CHUNK + lane, LANES), count)
 
 
 def forward_body(bands_ref, features_ref, other_ref, rim_ref, expand_ref, taps_ref, project_ref, first_ref,
-                 normed_ref, slab_ref, expanded_ref, mixed_ref, slab, normed_one, hidden, hidden_two,
-                 total, sems):
-    step = pl.program_id(0)
+                 normed_ref, slab_ref, expanded_ref, mixed_ref, slab, normed_one, hidden, hidden_two, total):
     rows, cols, width = slab.shape
     own = rows - 2 * RIM
-    chunk = expand_ref.shape[1]
-
-    @pl.when(step == 0)
-    def _():
-        sources = (features_ref, other_ref, rim_ref)
-        pieces = [(0, RIM), (RIM, BAND), (RIM + BAND, BAND), (RIM + 2 * BAND, RIM)]
-        for index, (first, count) in enumerate(pieces):
-            start_pull(bands_ref, first - RIM, sources, count, slab.at[pl.ds(first, count)], sems.at[index])
-        for index, (first, count) in enumerate(pieces):
-            wait_pull(sources, count, slab.at[pl.ds(first, count)], sems.at[index])
-        slab_ref[...] = slab[RIM : RIM + own]
-        for row in range(0, rows, 2):
-            at = slice(row * cols, (row + 2) * cols)
-            values = slab[row : row + 2].astype(F32).reshape(2 * cols, width)
-            normed_one[at] = (values * rms_scale(values)).astype(BF16)
-        total[...] = slab[1 : rows - 1].astype(F32).reshape((rows - 2) * cols, width)
-
-    for row in range(0, rows, 4):
-        expanded = nn_dot(normed_one[row * cols : (row + 4) * cols, :], expand_ref[...])
-        for inner in range(4):
-            for lane in range(0, chunk, LANES):
-                lanes = slice(lane, lane + LANES)
-                values = expanded[inner * cols : (inner + 1) * cols, lanes]
-                hidden[row + inner, :, lanes] = gelu(values).astype(BF16).astype(F32)
-                if RIM <= row + inner < RIM + own:
-                    expanded_ref[row + inner - RIM, :, lanes] = values
-
+
+    sources = (features_ref, other_ref, rim_ref)
+    for first, count in ((0, RIM), (RIM, BAND), (RIM + BAND, BAND), (RIM + 2 * BAND, RIM)):
+        pull(bands_ref, first - RIM, sources, count, slab, first)
+    slab_ref[...] = slab[RIM : RIM + own]
+    for row in range(0, rows, 2):
+        at = slice(row * cols, (row + 2) * cols)
+        values = slab[row : row + 2].astype(F32).reshape(2 * cols, width)
+        normed_one[at] = (values * rms_scale(values)).astype(BF16)
+    total[...] = slab[1 : rows - 1].astype(F32).reshape((rows - 2) * cols, width)
     column = lax.broadcasted_iota(jnp.int32, (cols, LANES), 0)
-    for lane in range(0, chunk, LANES):
-        lanes = slice(lane, lane + LANES)
-        taps = spread_taps(taps_ref, lanes, cols)
-        for row in range(rows - 2):
-            near = [hidden[row + a, :, lanes] for a in range(3)]
-            sums = [
-                taps[b] * near[0] + taps[3 + b] * near[1] + taps[6 + b] * near[2] for b in range(3)
-            ]
-            mixed = column_sums(sums[0], sums[1], sums[2], column, cols - 1)
-            hidden_two[row * cols : (row + 1) * cols, lanes] = gelu(mixed).astype(BF16)
-            mixed_ref[row, :, lanes] = mixed
-    total[...] += nn_dot(hidden_two[...], project_ref[...])
-
-    @pl.when(step == pl.num_programs(0) - 1)
-    def _():
-        for row in range(rows - 2):
-            first = total[row * cols : (row + 1) * cols]
-            first_ref[row] = first
-            if 1 <= row <= own:
-                normed_ref[row - 1] = (first * rms_scale(first)).astype(BF16)
+
+    def step(index, carry):
+        weights = expand_ref[:, hidden_lanes(index)]
+        for row in range(0, rows, 4):
+            expanded = nn_dot(normed_one[row * cols : (row + 4) * cols, :], weights)
+            for inner in range(4):
+                for lane in range(0, CHUNK, LANES):
+                    lanes = slice(lane, lane + LANES)
+                    values = expanded[inner * cols : (inner + 1) * cols, lanes]
+                    hidden[row + inner, :, lanes] = gelu(values).astype(BF16).astype(F32)
+                    if RIM <= row + inner < RIM + own:
+                        expanded_ref[row + inner - RIM, :, hidden_lanes(index, lane, LANES)] = values
+
+        for lane in range(0, CHUNK, LANES):
+            lanes = slice(lane, lane + LANES)
+            taps = spread_taps(taps_ref, hidden_lanes(index, lane, LANES), cols)
+            for row in range(rows - 2):
+                near = [hidden[row + a, :, lanes] for a in range(3)]
+                sums = [
+                    taps[b] * near[0] + taps[3 + b] * near[1] + taps[6 + b] * near[2] for b in range(3)
+                ]
+                mixed = column_sums(sums[0], sums[1], sums[2], column, cols - 1)
+                hidden_two[row * cols : (row + 1) * cols, lanes] = gelu(mixed).astype(BF16)
+                mixed_ref[row, :, hidden_lanes(index, lane, LANES)] = mixed
+        total[...] += nn_dot(hidden_two[...], project_ref[hidden_lanes(index), :])
+        return carry
+
+    lax.fori_loop(0, expand_ref.shape[1] // CHUNK, step, 0)
+    for row in range(rows - 2):
+        first = total[row * cols : (row + 1) * cols]
+        first_ref[row] = first
+        if 1 <= row <= own:
+            normed_ref[row - 1] = (first * rms_scale(first)).astype(BF16)
 
 
 def forward(bands, features, other, rim, w_expand, kernel, w_project):
@@ -229,23 +198,8 @@
     hidden_width = w_expand.shape[1]
     return pl.pallas_call(
         forward_body,
-        grid=(hidden_width // CHUNK,),
-        in_specs=[
-            in_scalars(),
-            anywhere(),
-            anywhere(),
-            anywhere(),
-            pl.BlockSpec((width, CHUNK), lambda j: (0, j)),
-            pl.BlockSpec((9, CHUNK), lambda j: (0, j)),
-            pl.BlockSpec((CHUNK, width), lambda j: (j, 0)),
-        ],
-        out_specs=[
-            whole((rows - 2, cols, width)),
-            whole((own, cols, width)),
-            whole((own, cols, width)),
-            pl.BlockSpec((own, cols, CHUNK), lambda j: (0, 0, j)),
-            pl.BlockSpec((rows - 2, cols, CHUNK), lambda j: (0, 0, j)),
-        ],
+        in_specs=[in_scalars()] + [in_vmem()] * 6,
+        out_specs=[in_vmem()] * 5,
         out_shape=[
             jax.ShapeDtypeStruct((rows - 2, cols, width), F32),
             jax.ShapeDtypeStruct((own, cols, width), BF16),
@@ -259,7 +213,6 @@
             pltpu.VMEM((rows, cols, CHUNK), F32),
             pltpu.VMEM(((rows - 2) * cols, CHUNK), BF16),
             pltpu.VMEM(((rows - 2) * cols, width), F32),
-            pltpu.SemaphoreType.DMA((4,)),
         ],
         compiler_params=params(),
         cost_estimate=pl.CostEstimate(
@@ -273,23 +226,21 @@
 
 def slopes_body(expanded_ref, mixed_ref, slope_one_ref, slope_two_ref):
     for source, target in ((expanded_ref, slope_one_ref), (mixed_ref, slope_two_ref)):
-        rows, _, chunk = source.shape
-        for row in range(rows):
-            for lane in range(0, chunk, LANES):
+
+        def step(row, carry):
+            for lane in range(0, source.shape[2], LANES):
                 lanes = slice(lane, lane + LANES)
                 target[row, :, lanes] = gelu_slope(source[row, :, lanes]).astype(BF16)
+            return carry
+
+        lax.fori_loop(0, source.shape[0], step, 0)
 
 
 def slopes(expanded, mixed):
-    hidden_width = expanded.shape[2]
-    blocks = [
-        pl.BlockSpec(values.shape[:2] + (CHUNK,), lambda j: (0, 0, j)) for values in (expanded, mixed)
-    ]
     return pl.pallas_call(
         slopes_body,
-        grid=(hidden_width // CHUNK,),
-        in_specs=blocks,
-        out_specs=blocks,
+        in_specs=[in_vmem()] * 2,
+        out_specs=[in_vmem()] * 2,
         out_shape=[jax.ShapeDtypeStruct(values.shape, BF16) for values in (expanded, mixed)],
         compiler_params=params(),
         cost_estimate=pl.CostEstimate(
@@ -356,9 +307,8 @@
     shape = (groups * own * cols, width)
     return pl.pallas_call(
         grad_attended_body,
-        grid=(1,),
-        in_specs=[whole(cotangent.shape), whole(w_out.shape)],
-        out_specs=whole(shape),
+        in_specs=[in_vmem()] * 2,
+        out_specs=in_vmem(),
         out_shape=jax.ShapeDtypeStruct(shape, BF16),
         scratch_shapes=[wide_scratch(cotangent.shape), pltpu.VMEM(shape, BF16)],
         compiler_params=params(),
@@ -428,14 +378,8 @@
     out_shapes = [normed.shape, (windows, span, HEADS * span), (tokens, width)]
     return pl.pallas_call(
         attention_body,
-        grid=(1,),
-        in_specs=[
-            whole(normed.shape),
-            whole(grad_attended.shape),
-            whole(mask.shape),
-            whole(w_qkv.shape),
-        ],
-        out_specs=[whole(shape) for shape in out_shapes],
+        in_specs=[in_vmem()] * 4,
+        out_specs=[in_vmem()] * 3,
         out_shape=[jax.ShapeDtypeStruct(shape, BF16) for shape in out_shapes],
         scratch_shapes=[
             wide_scratch(normed.shape),
@@ -468,9 +412,8 @@
 def attend(weights, values, w_out, shape):
     return pl.pallas_call(
         attended_body,
-        grid=(1,),
-        in_specs=[whole(weights.shape), whole(values.shape), whole(w_out.shape)],
-        out_specs=whole(shape),
+        in_specs=[in_vmem()] * 3,
+        out_specs=in_vmem(),
         out_shape=jax.ShapeDtypeStruct(shape, BF16),
         scratch_shapes=[wide_scratch(shape), pltpu.VMEM(values.shape, BF16)],
         compiler_params=params(),
@@ -483,70 +426,64 @@
 
 def backward_body(bands_ref, cotangent_ref, other_ref, rim_ref, slab_ref, first_ref, grad_slab_ref, grad_ref,
                   pair_ref, next_ref, slope_one_ref, slope_two_ref, expand_ref, taps_ref, project_ref,
-                  out_ref, rims, grad_first, grad_rows, mixed, expanded, total, sems):
-    step = pl.program_id(0)
+                  out_ref, rims, grad_first, grad_rows, mixed, expanded, total):
     own, cols, width = slab_ref.shape
-    chunk = expand_ref.shape[1]
-
-    @pl.when(step == 0)
-    def _():
-        sources = (cotangent_ref, other_ref, rim_ref)
-        for side, first in enumerate((-1, own)):
-            start_pull(bands_ref, first, sources, 1, rims.at[pl.ds(side, 1)], sems.at[side], RIM)
-        total[...] = jnp.zeros_like(total)
-
-        def through_norm(cotangent, grad, first):
-            rms = rms_scale(first)
-            normed = first * rms
-            grad = grad.astype(F32)
-            inner = jnp.mean(grad * normed, -1, keepdims=True)
-            return cotangent.astype(F32) + rms * (grad - normed * inner)
-
-        for row in range(own):
-            result = through_norm(grad_slab_ref[row], grad_ref[row], first_ref[row + 1])
-            grad_first[row * cols : (row + 1) * cols] = result
-            grad_rows[(row + 1) * cols : (row + 2) * cols] = result.astype(BF16)
-        for side in range(2):
-            wait_pull(sources, 1, rims.at[pl.ds(side, 1)], sems.at[side])
-        leads = lax.rem(lax.axis_index("row"), 2) == 0
-        above = jnp.where(leads, next_ref[0].astype(F32), pair_ref[0].astype(F32))
-        below = jnp.where(leads, pair_ref[0].astype(F32), next_ref[0].astype(F32))
-        grad_rows[0:cols] = through_norm(rims[0], above, first_ref[0]).astype(BF16)
-        grad_rows[(own + 1) * cols :] = through_norm(rims[1], below, first_ref[own + 1]).astype(BF16)
-
-    for row in range(0, own + 2, 6):
-        grad = nt_dot(grad_rows[row * cols : (row + 6) * cols, :], project_ref[...])
-        for inner in range(6):
-            for lane in range(0, chunk, LANES):
-                lanes = slice(lane, lane + LANES)
-                slope = slope_two_ref[row + inner, :, lanes].astype(F32)
-                value = grad[inner * cols : (inner + 1) * cols, lanes] * slope
-                mixed[row + inner, :, lanes] = value.astype(BF16).astype(F32)
-
+
+    def through_norm(cotangent, grad, first):
+        rms = rms_scale(first)
+        normed = first * rms
+        grad = grad.astype(F32)
+        inner = jnp.mean(grad * normed, -1, keepdims=True)
+        return cotangent.astype(F32) + rms * (grad - normed * inner)
+
+    for side, first in enumerate((-1, own)):
+        pull(bands_ref, first, (cotangent_ref, other_ref, rim_ref), 1, rims, side, RIM)
+    for row in range(own):
+        result = through_norm(grad_slab_ref[row], grad_ref[row], first_ref[row + 1])
+        grad_first[row * cols : (row + 1) * cols] = result
+        grad_rows[(row + 1) * cols : (row + 2) * cols] = result.astype(BF16)
+    leads = lax.rem(lax.axis_index("row"), 2) == 0
+    above = jnp.where(leads, next_ref[0].astype(F32), pair_ref[0].astype(F32))
+    below = jnp.where(leads, pair_ref[0].astype(F32), next_ref[0].astype(F32))
+    grad_rows[0:cols] = through_norm(rims[0], above, first_ref[0]).astype(BF16)
+    grad_rows[(own + 1) * cols :] = through_norm(rims[1], below, first_ref[own + 1]).astype(BF16)
+    total[...] = jnp.zeros_like(total)
     column = lax.broadcasted_iota(jnp.int32, (cols, LANES), 0)
-    for lane in range(0, chunk, LANES):
-        lanes = slice(lane, lane + LANES)
-        taps = spread_taps(taps_ref, lanes, cols)
-        for row in range(own):
-            near = [mixed[row + a, :, lanes] for a in range(3)]
-            sums = [
-                taps[8 - b] * near[0] + taps[5 - b] * near[1] + taps[2 - b] * near[2] for b in range(3)
-            ]
-            grad = column_sums(sums[0], sums[1], sums[2], column, cols - 1)
-            slope = slope_one_ref[row, :, lanes].astype(F32)
-            expanded[row * cols : (row + 1) * cols, lanes] = (grad * slope).astype(BF16)
-    total[...] += nt_dot(expanded[...], expand_ref[...])
-
-    @pl.when(step == pl.num_programs(0) - 1)
-    def _():
-        for row in range(own):
-            at = slice(row * cols, (row + 1) * cols)
-            values = slab_ref[row].astype(F32)
-            rms = rms_scale(values)
-            normed = values * rms
-            grad = total[at]
-            inner = jnp.mean(grad * normed, -1, keepdims=True)
-            out_ref[row] = (grad_first[at] + rms * (grad - normed * inner)).astype(BF16)
+
+    def step(index, carry):
+        weights = project_ref[hidden_lanes(index), :]
+        for row in range(0, own + 2, 6):
+            grad = nt_dot(grad_rows[row * cols : (row + 6) * cols, :], weights)
+            for inner in range(6):
+                for lane in range(0, CHUNK, LANES):
+                    lanes = slice(lane, lane + LANES)
+                    slope = slope_two_ref[row + inner, :, hidden_lanes(index, lane, LANES)].astype(F32)
+                    value = grad[inner * cols : (inner + 1) * cols, lanes] * slope
+                    mixed[row + inner, :, lanes] = value.astype(BF16).astype(F32)
+
+        for lane in range(0, CHUNK, LANES):
+            lanes = slice(lane, lane + LANES)
+            taps = spread_taps(taps_ref, hidden_lanes(index, lane, LANES), cols)
+            for row in range(own):
+                near = [mixed[row + a, :, lanes] for a in range(3)]
+                sums = [
+                    taps[8 - b] * near[0] + taps[5 - b] * near[1] + taps[2 - b] * near[2] for b in range(3)
+                ]
+                grad = column_sums(sums[0], sums[1], sums[2], column, cols - 1)
+                slope = slope_one_ref[row, :, hidden_lanes(index, lane, LANES)].astype(F32)
+                expanded[row * cols : (row + 1) * cols, lanes] = (grad * slope).astype(BF16)
+        total[...] += nt_dot(expanded[...], expand_ref[:, hidden_lanes(index)])
+        return carry
+
+    lax.fori_loop(0, expand_ref.shape[1] // CHUNK, step, 0)
+    for row in range(own):
+        at = slice(row * cols, (row + 1) * cols)
+        values = slab_ref[row].astype(F32)
+        rms = rms_scale(values)
+        normed = values * rms
+        grad = total[at]
+        inner = jnp.mean(grad * normed, -1, keepdims=True)
+        out_ref[row] = (grad_first[at] + rms * (grad - normed * inner)).astype(BF16)
 
 
 def backward(bands, cotangent, other, rim, slab, first, grad_slab, grad, pair_row, next_row, slope_one,
@@ -555,25 +492,8 @@
     hidden_width = w_expand.shape[1]
     return pl.pallas_call(
         backward_body,
-        grid=(hidden_width // CHUNK,),
-        in_specs=[
-            in_scalars(),
-            anywhere(),
-            anywhere(),
-            anywhere(),
-            whole(slab.shape),
-            whole(first.shape),
-            whole(grad_slab.shape),
-            whole(grad.shape),
-            whole(pair_row.shape),
-            whole(next_row.shape),
-            pl.BlockSpec((own, cols, CHUNK), lambda j: (0, 0, j)),
-            pl.BlockSpec((own + 2, cols, CHUNK), lambda j: (0, 0, j)),
-            pl.BlockSpec((width, CHUNK), lambda j: (0, j)),
-            pl.BlockSpec((9, CHUNK), lambda j: (0, j)),
-            pl.BlockSpec((CHUNK, width), lambda j: (j, 0)),
-        ],
-        out_specs=whole((own, cols, width)),
+        in_specs=[in_scalars()] + [in_vmem()] * 14,
+        out_specs=in_vmem(),
         out_shape=jax.ShapeDtypeStruct((own, cols, width), BF16),
         scratch_shapes=[
             pltpu.VMEM((2, cols, width), BF16),
@@ -582,7 +502,6 @@
             pltpu.VMEM((own + 2, cols, CHUNK), F32),
             pltpu.VMEM((own * cols, CHUNK), BF16),
             pltpu.VMEM((own * cols, width), F32),
-            pltpu.SemaphoreType.DMA((2,)),
         ],
         compiler_params=params(),
         cost_estimate=pl.CostEstimate(

time: 114 us -> 129 us (1.13)
  local copies, waits for them, and re-layouts: 3.16 us -> 39.4 us
  Pallas kernels: 58.4 us -> 40.9 us
  waiting for transfers between devices: 18.6 us -> 10 us
  starting transfers between devices: 28.7 us -> 32.9 us
    unnamed x22 -> x72, local copies, waits for them, and re-layouts: 2.58 us -> 38.8 us
    pallas_call x8, Pallas kernels: 58.4 us -> 40.9 us  [the longest x1 11.4 us: attention(): pl.pallas_call(attention_body, in_specs=[in_vmem()] * 4, out_specs=[in_vm...]
    all_to_all x4, waiting for transfers between devices: 17.4 us -> 9.19 us  [exchange_windows(): lax.all_to_all(rows, 'row', split_axis=0, concat_axis=0, tiled=True, axis...]
    all_to_all x4, starting transfers between devices: 26.6 us -> 29.8 us  [exchange_windows(): lax.all_to_all(rows, 'row', split_axis=0, concat_axis=0, tiled=True, axis...]
  transfers between devices with their start and end apart: 10 -> 10, of which waited for: 5 -> 4; matrix products, arithmetic and copies ran while one was open for 1% -> 0% of each run, Pallas kernels for 40% -> 23%
where the time goes in v6:
time: 129 us; the launch traced here: 128 us
  Pallas kernels  40.9 us (32%)
  local copies, waits for them, and re-layouts  39.4 us (31%)
  starting transfers between devices  32.9 us (26%)
  waiting for transfers between devices  10 us (8%)
  other arithmetic  3.36 us (3%)
  between operations  1.55 us (1%)
    unnamed x72, local copies, waits for them, and re-layouts  38.8 us
    all_to_all x4, starting transfers between devices, exchange_windows(): lax.all_to_all(rows, 'row', split_axis=0, concat_axis=0, tiled=True, axis...  29.8 us
    pallas_call x1, Pallas kernels, attention(): pl.pallas_call(attention_body, in_specs=[in_vmem()] * 4, out_specs=[in_vm...  11.4 us
    pallas_call x1, Pallas kernels, forward(): pl.pallas_call(forward_body, in_specs=[in_scalars()] + [in_vmem()] * 6, o...  11.2 us
    pallas_call x1, Pallas kernels, backward(): pl.pallas_call(backward_body, in_specs=[in_scalars()] + [in_vmem()] * 14,...  9.7 us
    all_to_all x4, waiting for transfers between devices, exchange_windows(): lax.all_to_all(rows, 'row', split_axis=0, concat_axis=0, tiled=True, axis...  9.19 us
    pallas_call x1, Pallas kernels, slopes(): pl.pallas_call(slopes_body, in_specs=[in_vmem()] * 2, out_specs=[in_vmem(...  4.71 us
  transfers between devices with their start and end apart: 10, of which 4 were waited for; matrix products, arithmetic and copies ran while one was open for 0% of the time, Pallas kernels for 23%

profile of v6, /device:TPU:0, one launch (start us, length us, event | category | flops | bytes accessed | tf_op | source)
XLA Modules:
  0.0 128.0 jit_solution(3030008717391872128)
XLA Ops:
  5.4 1.4 %even_rows.1.grad_slab_ref = bf16[16,32,512]{2,1,0:T(8,128)(2,1)} custom-call(s32[16]{0:T(128)S(1)} %copy-done.32, bf16[24,32,512]{2,1,0:T(8,128)(2,1)S(1)} %copy-done.1, bf16[24,32,512]{2,1,0:T(8,128)(2,1)S(1)} %collective-permute-done.2.other_ref), custom_call_target="tpu_custom_call" | custom-call | tf_op jit(solution)/shard_map/even_rows/pallas_call | solution.py:101
  6.8 11.1 %all-to-all-start = ((bf16[16,32,512]{2,1,0:T(8,128)(2,1)}), bf16[16,32,512]{2,1,0:T(8,128)(2,1)S(1)}, u32[]{:S(2)}, u32[]{:S(2)}) async-start(bf16[16,32,512]{2,1,0:T(8,128)(2,1)} %even_rows.1.grad_slab_ref), calls=%async_computation | async-start | bytes 1048576 | tf_op jit(solution)/shard_map/all_to_all | solution.py:524
  18.0 1.6 %copy-done.13 = bf16[512,2048]{1,0:T(8,128)(2,1)S(1)} copy-done((bf16[512,2048]{1,0:T(8,128)(2,1)S(1)}, bf16[512,2048]{1,0:T(8,128)(2,1)}, u32[]{:S(2)}) %copy-start.13) | copy-done | bytes 2097176
  19.6 1.6 %copy-done.15 = bf16[2048,512]{1,0:T(8,128)(2,1)S(1)} copy-done((bf16[2048,512]{1,0:T(8,128)(2,1)S(1)}, bf16[2048,512]{1,0:T(8,128)(2,1)}, u32[]{:S(2)}) %copy-start.15) | copy-done | bytes 2097176
  22.3 11.2 %bottleneck_forward.1 = (f32[18,32,512]{2,1,0:T(8,128)S(1)}, bf16[16,32,512]{2,1,0:T(8,128)(2,1)S(1)}, bf16[16,32,512]{2,1,0:T(8,128)(2,1)S(1)}, f32[16,32,2048]{2,1,0:T(8,128)S(1)}, f32[18,32,2048]{2,1,0:T(8,128)S(1)}) custom-call(s32[16]{0:T(128)S(1)} %copy-done.33, bf16[24,32,512]{2,1,0:T(8,128)(2,1)S(1)} %copy-done.22, ...), custom_call_target="tpu_custom_call" | custom-call | flops 2684354560 | bytes 12582912 | tf_op jit(solution)/shard_map/bottleneck_forward/pallas_call | solution.py:199
  33.5 2.2 %copy-done.2 = f32[18,32,2048]{2,1,0:T(8,128)} copy-done((f32[18,32,2048]{2,1,0:T(8,128)}, f32[18,32,2048]{2,1,0:T(8,128)S(1)}, u32[]{:S(2)}) %copy-start.2) | copy-done | bytes 4718616
  35.6 2.0 %copy-done.4 = f32[16,32,2048]{2,1,0:T(8,128)} copy-done((f32[16,32,2048]{2,1,0:T(8,128)}, f32[16,32,2048]{2,1,0:T(8,128)S(1)}, u32[]{:S(2)}) %copy-start.4) | copy-done | bytes 4194328
  39.3 6.0 %all-to-all-start.1 = ((bf16[16,32,512]{2,1,0:T(8,128)(2,1)}), bf16[16,32,512]{2,1,0:T(8,128)(2,1)}, u32[]{:S(2)}, u32[]{:S(2)}) async-start(bf16[16,32,512]{2,1,0:T(8,128)(2,1)} %copy-done.28), calls=%async_computation.1 | async-start | bytes 1048576 | tf_op jit(solution)/shard_map/all_to_all | solution.py:524
  45.3 2.3 %copy-done.3 = f32[18,32,2048]{2,1,0:T(8,128)S(1)} copy-done((f32[18,32,2048]{2,1,0:T(8,128)S(1)}, f32[18,32,2048]{2,1,0:T(8,128)}, u32[]{:S(2)}) %copy-start.3) | copy-done | bytes 4718616
  47.6 2.2 %copy-done.5 = f32[16,32,2048]{2,1,0:T(8,128)S(1)} copy-done((f32[16,32,2048]{2,1,0:T(8,128)S(1)}, f32[16,32,2048]{2,1,0:T(8,128)}, u32[]{:S(2)}) %copy-start.5) | copy-done | bytes 4194328
  49.8 4.7 %gelu_slopes.1 = (bf16[16,32,2048]{2,1,0:T(8,128)(2,1)S(1)}, bf16[18,32,2048]{2,1,0:T(8,128)(2,1)S(1)}) custom-call(f32[16,32,2048]{2,1,0:T(8,128)S(1)} %copy-done.5, f32[18,32,2048]{2,1,0:T(8,128)S(1)} %copy-done.3), custom_call_target="tpu_custom_call" | custom-call | flops 33423360 | bytes 13369344 | tf_op jit(solution)/shard_map/gelu_slopes/pallas_call | solution.py:240
  54.6 1.4 %copy-done.8 = bf16[18,32,2048]{2,1,0:T(8,128)(2,1)} copy-done((bf16[18,32,2048]{2,1,0:T(8,128)(2,1)}, bf16[18,32,2048]{2,1,0:T(8,128)(2,1)S(1)}, u32[]{:S(2)}) %copy-start.8) | copy-done | bytes 2359320
  56.0 1.3 %copy-done.17 = bf16[16,32,2048]{2,1,0:T(8,128)(2,1)} copy-done((bf16[16,32,2048]{2,1,0:T(8,128)(2,1)}, bf16[16,32,2048]{2,1,0:T(8,128)(2,1)S(1)}, u32[]{:S(2)}) %copy-start.17) | copy-done | bytes 2097176
  60.7 1.4 %copy-done.34 = bf16[512,1536]{1,0:T(8,128)(2,1)S(1)} copy-done((bf16[512,1536]{1,0:T(8,128)(2,1)S(1)}, bf16[512,1536]{1,0:T(8,128)(2,1)}, u32[]{:S(2)}) %copy-start.34) | copy-done | bytes 1572888
  62.1 11.4 %window_attention.1 = (bf16[8,2,32,512]{3,2,1,0:T(8,128)(2,1)S(1)}, bf16[8,64,1024]{2,1,0:T(8,128)(2,1)S(1)}, bf16[512,512]{1,0:T(8,128)(2,1)S(1)}) custom-call(bf16[8,2,32,512]{3,2,1,0:T(8,128)(2,1)} %bitcast.2.normed_ref, bf16[512,512]{1,0:T(8,128)(2,1)S(1)} %copy-done.26, bf16[256,128]{1,0:T(8,128)(2,1)S(1)} %copy-done.35, bf16[512,1536]{1,0:T(8,128)(2,1)S(1)} %copy-done.34), custom_call_target="tpu_custom_call" | custom-call | flops 2147483648 | bytes 4194304 | tf_op jit(solution)/shard_map/window_attention/pallas_call | solution.py:379
  76.2 5.0 %all-to-all-start.2 = ((bf16[16,32,512]{2,1,0:T(8,128)(2,1)}), bf16[16,32,512]{2,1,0:T(8,128)(2,1)S(1)}, u32[]{:S(2)}, u32[]{:S(2)}) async-start(bf16[16,32,512]{2,1,0:T(8,128)(2,1)} %bitcast.23), calls=%async_computation.2 | async-start | bytes 1048576 | tf_op jit(solution)/shard_map/all_to_all | solution.py:524
  84.5 1.4 %attended_output.1 = bf16[8,2,32,512]{3,2,1,0:T(8,128)(2,1)S(1)} custom-call(bf16[8,64,1024]{2,1,0:T(8,128)(2,1)S(1)} %copy-done.20, bf16[512,512]{1,0:T(8,128)(2,1)S(1)} %copy-done.24, bf16[512,512]{1,0:T(8,128)(2,1)S(1)} %copy-done.11), custom_call_target="tpu_custom_call" | custom-call | flops 536870912 | bytes 3145728 | tf_op jit(solution)/shard_map/attended_output/pallas_call | solution.py:413
  86.7 8.2 %all-to-all-done.2.grad_ref = bf16[16,32,512]{2,1,0:T(8,128)(2,1)S(1)} async-done(((bf16[16,32,512]{2,1,0:T(8,128)(2,1)}), bf16[16,32,512]{2,1,0:T(8,128)(2,1)S(1)}, u32[]{:S(2)}, u32[]{:S(2)}) %all-to-all-start.2) | async-done | bytes 524320 | tf_op jit(solution)/shard_map/all_to_all | solution.py:524
  96.2 7.7 %all-to-all-start.3 = ((bf16[16,32,512]{2,1,0:T(8,128)(2,1)}), bf16[16,32,512]{2,1,0:T(8,128)(2,1)}, u32[]{:S(2)}, u32[]{:S(2)}) async-start(bf16[16,32,512]{2,1,0:T(8,128)(2,1)} %bitcast.21), calls=%async_computation.3 | async-start | bytes 1048576 | tf_op jit(solution)/shard_map/all_to_all | solution.py:524
  104.9 1.7 %copy-done.9 = bf16[18,32,2048]{2,1,0:T(8,128)(2,1)S(1)} copy-done((bf16[18,32,2048]{2,1,0:T(8,128)(2,1)S(1)}, bf16[18,32,2048]{2,1,0:T(8,128)(2,1)}, u32[]{:S(2)}) %copy-start.9) | copy-done | bytes 2359320
  106.5 1.6 %copy-done.14 = bf16[512,2048]{1,0:T(8,128)(2,1)S(1)} copy-done((bf16[512,2048]{1,0:T(8,128)(2,1)S(1)}, bf16[512,2048]{1,0:T(8,128)(2,1)}, u32[]{:S(2)}) %copy-start.14) | copy-done | bytes 2097176
  108.1 1.6 %copy-done.16 = bf16[2048,512]{1,0:T(8,128)(2,1)S(1)} copy-done((bf16[2048,512]{1,0:T(8,128)(2,1)S(1)}, bf16[2048,512]{1,0:T(8,128)(2,1)}, u32[]{:S(2)}) %copy-start.16) | copy-done | bytes 2097176
  109.7 1.6 %copy-done.18 = bf16[16,32,2048]{2,1,0:T(8,128)(2,1)S(1)} copy-done((bf16[16,32,2048]{2,1,0:T(8,128)(2,1)S(1)}, bf16[16,32,2048]{2,1,0:T(8,128)(2,1)}, u32[]{:S(2)}) %copy-start.18) | copy-done | bytes 2097176
  112.4 9.7 %bottleneck_backward.1 = bf16[16,32,512]{2,1,0:T(8,128)(2,1)S(1)} custom-call(s32[16]{0:T(128)S(1)} %copy-done.33, bf16[24,32,512]{2,1,0:T(8,128)(2,1)S(1)} %copy-done.1, bf16[24,32,512]{2,1,0:T(8,128)(2,1)S(1)} %collective-permute-done.2.other_ref, bf16[3,32,512]{2,1,0:T(8,128)(2,1)S(1)} %collective-permute-done.1.rim_ref, ...), custom_call_target="tpu_custom_call" | custom-call | flops 2415919104 | bytes 12582912 | tf_op jit(solution)/shard_map/bottleneck_backward/pallas_call | solution.py:493
  (84 shorter events, 26.3 us)
Async XLA Ops:
  0.6 4.8 %collective-permute-start.2 = (bf16[24,32,512]{2,1,0:T(8,128)(2,1)}, bf16[24,32,512]{2,1,0:T(8,128)(2,1)S(1)}, u32[]{:S(2)}, u32[]{:S(2)}) collective-permute-start(bf16[24,32,512]{2,1,0:T(8,128)(2,1)} %cotangent_ref.3), channel_id=1, source_target_pairs={{0,1},{1,0},{2,3},{3,2},{4,5},{5,4},{6,7},{7,6},{8,9},{9,8},{10,11... | collective-permute-start | bytes 2359304 | tf_op jit(solution)/shard_map/ppermute | solution.py:531
  1.1 16.8 %collective-permute-start = (bf16[24,32,512]{2,1,0:T(8,128)(2,1)}, bf16[24,32,512]{2,1,0:T(8,128)(2,1)}, u32[]{:S(2)}, u32[]{:S(2)}) collective-permute-start(bf16[24,32,512]{2,1,0:T(8,128)(2,1)} %features_ref.3), channel_id=1, source_target_pairs={{0,1},{1,0},{2,3},{3,2},{4,5},{5,4},{6,7},{7,6},{8,9},{9,8},{10,11... | collective-permute-start | bytes 2359304 | tf_op jit(solution)/shard_map/ppermute | solution.py:531
  4.2 13.8 %copy-start.31 = (bf16[9,2048]{1,0:T(8,128)(2,1)S(1)}, bf16[9,2048]{1,0:T(8,128)(2,1)}, u32[]{:S(2)}) copy-start(bf16[9,2048]{1,0:T(8,128)(2,1)} %taps_ref.3) | copy-start | bytes 110596
  4.2 13.8 %copy-start.33 = (s32[16]{0:T(128)S(1)}, s32[16]{0:T(128)}, u32[]{:S(2)}) copy-start(s32[16]{0:T(128)} %bands_ref.7) | copy-start | bytes 196
  4.7 2.1 %collective-permute-start.1 = (bf16[3,32,512]{2,1,0:T(8,128)(2,1)S(1)}, bf16[3,32,512]{2,1,0:T(8,128)(2,1)S(1)}, u32[]{:S(2)}, u32[]{:S(2)}) collective-permute-start(bf16[3,32,512]{2,1,0:T(8,128)(2,1)S(1)} %rim_rows.1), channel_id=1, source_target_pairs={{1,2},{3,4},{5,6},{7,8},{9,10},{11,12},{13,14},{2,1},{4,3},{6,5},{... | collective-permute-start | bytes 294920 | tf_op jit(solution)/shard_map/ppermute | solution.py:537
  6.8 32.5 %all-to-all-start = ((bf16[16,32,512]{2,1,0:T(8,128)(2,1)}), bf16[16,32,512]{2,1,0:T(8,128)(2,1)S(1)}, u32[]{:S(2)}, u32[]{:S(2)}) async-start(bf16[16,32,512]{2,1,0:T(8,128)(2,1)} %even_rows.1.grad_slab_ref), calls=%async_computation | async-start | bytes 1048576 | tf_op jit(solution)/shard_map/all_to_all | solution.py:524
  18.0 1.6 %copy-start.13 = (bf16[512,2048]{1,0:T(8,128)(2,1)S(1)}, bf16[512,2048]{1,0:T(8,128)(2,1)}, u32[]{:S(2)}) copy-start(bf16[512,2048]{1,0:T(8,128)(2,1)} %expand_ref.3) | copy-start | bytes 6291460
  19.6 1.6 %copy-start.15 = (bf16[2048,512]{1,0:T(8,128)(2,1)S(1)}, bf16[2048,512]{1,0:T(8,128)(2,1)}, u32[]{:S(2)}) copy-start(bf16[2048,512]{1,0:T(8,128)(2,1)} %project_ref.3) | copy-start | bytes 6291460
  33.5 2.2 %copy-start.2 = (f32[18,32,2048]{2,1,0:T(8,128)}, f32[18,32,2048]{2,1,0:T(8,128)S(1)}, u32[]{:S(2)}) copy-start(f32[18,32,2048]{2,1,0:T(8,128)S(1)} %get-tuple-element.34.mixed_ref) | copy-start | bytes 14155780
  35.6 2.0 %copy-start.4 = (f32[16,32,2048]{2,1,0:T(8,128)}, f32[16,32,2048]{2,1,0:T(8,128)S(1)}, u32[]{:S(2)}) copy-start(f32[16,32,2048]{2,1,0:T(8,128)S(1)} %get-tuple-element.33.expanded_ref) | copy-start | bytes 12582916
  39.3 20.4 %all-to-all-start.1 = ((bf16[16,32,512]{2,1,0:T(8,128)(2,1)}), bf16[16,32,512]{2,1,0:T(8,128)(2,1)}, u32[]{:S(2)}, u32[]{:S(2)}) async-start(bf16[16,32,512]{2,1,0:T(8,128)(2,1)} %copy-done.28), calls=%async_computation.1 | async-start | bytes 1048576 | tf_op jit(solution)/shard_map/all_to_all | solution.py:524
  45.3 2.3 %copy-start.3 = (f32[18,32,2048]{2,1,0:T(8,128)S(1)}, f32[18,32,2048]{2,1,0:T(8,128)}, u32[]{:S(2)}) copy-start(f32[18,32,2048]{2,1,0:T(8,128)} %copy-done.2) | copy-start | bytes 14155780
  47.6 2.2 %copy-start.5 = (f32[16,32,2048]{2,1,0:T(8,128)S(1)}, f32[16,32,2048]{2,1,0:T(8,128)}, u32[]{:S(2)}) copy-start(f32[16,32,2048]{2,1,0:T(8,128)} %copy-done.4) | copy-start | bytes 12582916
  49.8 7.5 %copy-start.10 = (bf16[512,512]{1,0:T(8,128)(2,1)S(1)}, bf16[512,512]{1,0:T(8,128)(2,1)}, u32[]{:S(2)}) copy-start(bf16[512,512]{1,0:T(8,128)(2,1)} %out_ref.3) | copy-start | bytes 1572868
  49.8 9.8 %copy-start.35 = (bf16[256,128]{1,0:T(8,128)(2,1)S(1)}, bf16[256,128]{1,0:T(8,128)(2,1)}, u32[]{:S(2)}) copy-start(bf16[256,128]{1,0:T(8,128)(2,1)} %constant.29.clone.mask_ref) | copy-start | bytes 196612
  76.2 18.7 %all-to-all-start.2 = ((bf16[16,32,512]{2,1,0:T(8,128)(2,1)}), bf16[16,32,512]{2,1,0:T(8,128)(2,1)S(1)}, u32[]{:S(2)}, u32[]{:S(2)}) async-start(bf16[16,32,512]{2,1,0:T(8,128)(2,1)} %bitcast.23), calls=%async_computation.2 | async-start | bytes 1048576 | tf_op jit(solution)/shard_map/all_to_all | solution.py:524
  94.9 9.0 %copy-start.6 = (bf16[16,32,512]{2,1,0:T(8,128)(2,1)}, bf16[16,32,512]{2,1,0:T(8,128)(2,1)S(1)}, u32[]{:S(2)}) copy-start(bf16[16,32,512]{2,1,0:T(8,128)(2,1)S(1)} %all-to-all-done.2.grad_ref) | copy-start | bytes 1572868
  94.9 1.3 collective-permute-start.3
  95.0 1.2 collective-permute-start.4
  96.2 25.9 %all-to-all-start.3 = ((bf16[16,32,512]{2,1,0:T(8,128)(2,1)}), bf16[16,32,512]{2,1,0:T(8,128)(2,1)}, u32[]{:S(2)}, u32[]{:S(2)}) async-start(bf16[16,32,512]{2,1,0:T(8,128)(2,1)} %bitcast.21), calls=%async_computation.3 | async-start | bytes 1048576 | tf_op jit(solution)/shard_map/all_to_all | solution.py:524
  104.9 1.7 %copy-start.9 = (bf16[18,32,2048]{2,1,0:T(8,128)(2,1)S(1)}, bf16[18,32,2048]{2,1,0:T(8,128)(2,1)}, u32[]{:S(2)}) copy-start(bf16[18,32,2048]{2,1,0:T(8,128)(2,1)} %copy-done.8) | copy-start | bytes 7077892
  106.5 1.6 %copy-start.14 = (bf16[512,2048]{1,0:T(8,128)(2,1)S(1)}, bf16[512,2048]{1,0:T(8,128)(2,1)}, u32[]{:S(2)}) copy-start(bf16[512,2048]{1,0:T(8,128)(2,1)} %expand_ref.3) | copy-start | bytes 6291460
  108.1 1.6 %copy-start.16 = (bf16[2048,512]{1,0:T(8,128)(2,1)S(1)}, bf16[2048,512]{1,0:T(8,128)(2,1)}, u32[]{:S(2)}) copy-start(bf16[2048,512]{1,0:T(8,128)(2,1)} %project_ref.3) | copy-start | bytes 6291460
  123.4 2.6 %collective-permute-start.5 = (bf16[2,8,32,512]{3,2,1,0:T(8,128)(2,1)S(1)}, bf16[2,8,32,512]{3,2,1,0:T(8,128)(2,1)S(1)}, u32[]{:S(2)}, u32[]{:S(2)}) collective-permute-start(bf16[2,8,32,512]{3,2,1,0:T(8,128)(2,1)S(1)} %pad_maximum_fusion.2), channel_id=1, source_target_pairs={{0,1},{1,0},{2,3},{3,2},{4,5},{5,4},{6,7},{7,6},{8,9},{9,8},{10,11... | collective-permute-start | bytes 1572872 | tf_op jit(solution)/shard_map/ppermute | solution.py:531
  (22 other events, 23.4 us)

commit v7 on v6

--- a/solution.py
+++ b/solution.py
@@ -15,11 +15,12 @@
 EPSILON = 1e-06
 CHUNK = 512
 LANES = 128
+WIDE = 256
 ROOT = math.sqrt(2.0 / math.pi)
 CUBIC = 0.044715
 F32 = jnp.float32
 BF16 = jnp.bfloat16
-VMEM_LIMIT = 20 * 1024 * 1024
+VMEM_LIMIT = 56 * 1024 * 1024
 
 
 def nt_dot(left, right):
@@ -53,12 +54,21 @@
     return cdf + (value - value * cdf) * (2.0 * ROOT + (6.0 * ROOT * CUBIC) * square)
 
 
+def whole(shape, space=None):
+    zeros = (0,) * len(shape)
+    return pl.BlockSpec(shape, lambda *_: zeros)
+
+
+def params():
+    return pltpu.CompilerParams(vmem_limit_bytes=VMEM_LIMIT)
+
+
 def in_vmem():
     return pl.BlockSpec(memory_space=pltpu.VMEM)
 
 
-def params():
-    return pltpu.CompilerParams(vmem_limit_bytes=VMEM_LIMIT)
+def in_hbm():
+    return pl.BlockSpec(memory_space=pltpu.HBM)
 
 
 def in_scalars():
@@ -81,47 +91,86 @@
     return source, jnp.where(beyond, 0, jnp.where(in_leader, row, row - leader_share))
 
 
-def pull(bands_ref, first, sources, rows, target, at, rim_row=0):
+def start_pull(bands_ref, first, sources, rows, target, sem, rim_row=0):
     where, row = place(bands_ref, first)
     row = jnp.where(where == 2, rim_row, row)
     for number, source in enumerate(sources):
 
         @pl.when(where == number)
         def _():
-            target[at : at + rows] = source[pl.ds(row, rows)]
-
-
-def even_body(bands_ref, own_ref, other_ref, out_ref):
+            pltpu.make_async_copy(source.at[pl.ds(row, rows)], target, sem).start()
+
+
+def wait_pull(sources, rows, target, sem):
+    pltpu.make_async_copy(sources[0].at[pl.ds(0, rows)], target, sem).wait()
+
+
+def even_body(bands_ref, own_ref, other_ref, out_ref, held, sems):
+    halves = [pl.ds(BAND * half, BAND) for half in range(2)]
+    places = [place(bands_ref, BAND * half) for half in range(2)]
+
+    def copies(half):
+        row = places[half][1]
+        return (
+            pltpu.make_async_copy(own_ref.at[pl.ds(row, BAND)], held.at[halves[half]], sems.at[half]),
+            pltpu.make_async_copy(other_ref.at[pl.ds(row, BAND)], out_ref.at[halves[half]], sems.at[2 + half]),
+            pltpu.make_async_copy(held.at[halves[half]], out_ref.at[halves[half]], sems.at[2 + half]),
+        )
+
     for half in range(2):
-        pull(bands_ref, BAND * half, (own_ref, other_ref), BAND, out_ref, BAND * half)
+        fetch, direct, store = copies(half)
+        pl.when(places[half][0] == 0)(fetch.start)
+        pl.when(places[half][0] == 1)(direct.start)
+    for half in range(2):
+        fetch, direct, store = copies(half)
+
+        @pl.when(places[half][0] == 0)
+        def _():
+            fetch.wait()
+            store.start()
+
+    for half in range(2):
+        copies(half)[2].wait()
 
 
 def even_rows(bands, own, other):
     shape = (GRID_ROWS,) + own.shape[1:]
     return pl.pallas_call(
         even_body,
-        in_specs=[in_scalars(), in_vmem(), in_vmem()],
-        out_specs=in_vmem(),
+        in_specs=[in_scalars(), in_hbm(), in_vmem()],
+        out_specs=in_hbm(),
         out_shape=jax.ShapeDtypeStruct(shape, own.dtype),
+        scratch_shapes=[pltpu.VMEM(shape, own.dtype), pltpu.SemaphoreType.DMA((4,))],
         compiler_params=params(),
         name="even_rows",
     )(bands, own, other)
 
 
-def rim_body(bands_ref, features_ref, cotangent_ref, out_ref):
+def rim_body(bands_ref, features_ref, cotangent_ref, out_ref, sems):
     parity, _, share = shares(bands_ref)
     leads = parity == 0
-    out_ref[0:RIM] = features_ref[pl.ds(jnp.where(leads, 0, share - RIM), RIM)]
-    out_ref[RIM : RIM + 1] = cotangent_ref[pl.ds(jnp.where(leads, 0, share - 1), 1)]
+    copies = [
+        pltpu.make_async_copy(
+            features_ref.at[pl.ds(jnp.where(leads, 0, share - RIM), RIM)], out_ref.at[pl.ds(0, RIM)], sems.at[0]
+        ),
+        pltpu.make_async_copy(
+            cotangent_ref.at[pl.ds(jnp.where(leads, 0, share - 1), 1)], out_ref.at[pl.ds(RIM, 1)], sems.at[1]
+        ),
+    ]
+    for copy in copies:
+        copy.start()
+    for copy in copies:
+        copy.wait()
 
 
 def rim_rows(bands, features, cotangent):
     shape = (RIM + 1,) + features.shape[1:]
     return pl.pallas_call(
         rim_body,
-        in_specs=[in_scalars(), in_vmem(), in_vmem()],
+        in_specs=[in_scalars(), in_hbm(), in_hbm()],
         out_specs=in_vmem(),
         out_shape=jax.ShapeDtypeStruct(shape, features.dtype),
+        scratch_shapes=[pltpu.SemaphoreType.DMA((2,))],
         compiler_params=params(),
         name="rim_rows",
     )(bands, features, cotangent)
@@ -138,19 +187,37 @@
     return [jnp.broadcast_to(taps[i : i + 1], (cols, LANES)) for i in range(9)]
 
 
-def hidden_lanes(step, lane=0, count=CHUNK):
-    return pl.ds(pl.multiple_of(step * CHUNK + lane, LANES), count)
+def chunk_lanes(index):
+    return pl.ds(index * CHUNK, CHUNK)
+
+
+def lane_pieces(first, count):
+    return [slice(at, at + LANES) for at in range(first, first + count, LANES)]
 
 
 def forward_body(bands_ref, features_ref, other_ref, rim_ref, expand_ref, taps_ref, project_ref, first_ref,
-                 normed_ref, slab_ref, expanded_ref, mixed_ref, slab, normed_one, hidden, hidden_two, total):
+                 normed_ref, slab_ref, expanded_ref, mixed_ref, slab, normed_one, expand, project, expanded,
+                 hidden, mixed, hidden_two, total, normed, row_sems, weight_sems, out_sems):
     rows, cols, width = slab.shape
     own = rows - 2 * RIM
+    chunks = expand_ref.shape[1] // CHUNK
 
     sources = (features_ref, other_ref, rim_ref)
-    for first, count in ((0, RIM), (RIM, BAND), (RIM + BAND, BAND), (RIM + 2 * BAND, RIM)):
-        pull(bands_ref, first - RIM, sources, count, slab, first)
-    slab_ref[...] = slab[RIM : RIM + own]
+    pieces = [(0, RIM), (RIM, BAND), (RIM + BAND, BAND), (RIM + 2 * BAND, RIM)]
+    for index, (first, count) in enumerate(pieces):
+        start_pull(bands_ref, first - RIM, sources, count, slab.at[pl.ds(first, count)], row_sems.at[index])
+    fetches = []
+    for index in range(chunks):
+        lanes = chunk_lanes(index)
+        fetches.append(pltpu.make_async_copy(expand_ref.at[:, lanes], expand.at[index], weight_sems.at[2 * index]))
+        fetches.append(pltpu.make_async_copy(project_ref.at[lanes], project.at[index], weight_sems.at[2 * index + 1]))
+    for fetch in fetches:
+        fetch.start()
+    for index, (first, count) in enumerate(pieces):
+        wait_pull(sources, count, slab.at[pl.ds(first, count)], row_sems.at[index])
+
+    stores = [pltpu.make_async_copy(slab.at[pl.ds(RIM, own)], slab_ref, out_sems.at[0])]
+    stores[0].start()
     for row in range(0, rows, 2):
         at = slice(row * cols, (row + 2) * cols)
         values = slab[row : row + 2].astype(F32).reshape(2 * cols, width)
@@ -158,50 +225,70 @@
     total[...] = slab[1 : rows - 1].astype(F32).reshape((rows - 2) * cols, width)
     column = lax.broadcasted_iota(jnp.int32, (cols, LANES), 0)
 
-    def step(index, carry):
-        weights = expand_ref[:, hidden_lanes(index)]
-        for row in range(0, rows, 4):
-            expanded = nn_dot(normed_one[row * cols : (row + 4) * cols, :], weights)
-            for inner in range(4):
-                for lane in range(0, CHUNK, LANES):
-                    lanes = slice(lane, lane + LANES)
-                    values = expanded[inner * cols : (inner + 1) * cols, lanes]
-                    hidden[row + inner, :, lanes] = gelu(values).astype(BF16).astype(F32)
-                    if RIM <= row + inner < RIM + own:
-                        expanded_ref[row + inner - RIM, :, hidden_lanes(index, lane, LANES)] = values
-
-        for lane in range(0, CHUNK, LANES):
-            lanes = slice(lane, lane + LANES)
-            taps = spread_taps(taps_ref, hidden_lanes(index, lane, LANES), cols)
+    def expand_chunk(index):
+        fetches[2 * index].wait()
+        for lane in range(0, CHUNK, WIDE):
+            product = nn_dot(normed_one[...], expand[index, :, lane : lane + WIDE])
+            expanded[:, :, index * CHUNK + lane : index * CHUNK + lane + WIDE] = product.reshape(rows, cols, WIDE)
+
+    def project_chunk(index):
+        fetches[2 * index + 1].wait()
+        total[...] += nn_dot(hidden_two[index % 2], project[index])
+
+    expand_chunk(0)
+    for index in range(chunks):
+        if index + 1 < chunks:
+            expand_chunk(index + 1)
+        if index > 0:
+            project_chunk(index - 1)
+        for lanes in lane_pieces(0, CHUNK):
+            at = slice(index * CHUNK + lanes.start, index * CHUNK + lanes.stop)
+            for row in range(rows):
+                hidden[row, :, lanes] = gelu(expanded[row, :, at]).astype(BF16).astype(F32)
+            taps = spread_taps(taps_ref, at, cols)
             for row in range(rows - 2):
                 near = [hidden[row + a, :, lanes] for a in range(3)]
                 sums = [
                     taps[b] * near[0] + taps[3 + b] * near[1] + taps[6 + b] * near[2] for b in range(3)
                 ]
-                mixed = column_sums(sums[0], sums[1], sums[2], column, cols - 1)
-                hidden_two[row * cols : (row + 1) * cols, lanes] = gelu(mixed).astype(BF16)
-                mixed_ref[row, :, hidden_lanes(index, lane, LANES)] = mixed
-        total[...] += nn_dot(hidden_two[...], project_ref[hidden_lanes(index), :])
-        return carry
-
-    lax.fori_loop(0, expand_ref.shape[1] // CHUNK, step, 0)
-    for row in range(rows - 2):
+                values = column_sums(sums[0], sums[1], sums[2], column, cols - 1)
+                hidden_two[index % 2, row * cols : (row + 1) * cols, lanes] = gelu(values).astype(BF16)
+                mixed[row, :, at] = values
+        lanes = chunk_lanes(index)
+        stores.append(
+            pltpu.make_async_copy(
+                expanded.at[pl.ds(RIM, own), :, lanes], expanded_ref.at[:, :, lanes], out_sems.at[1 + 2 * index]
+            )
+        )
+        stores.append(
+            pltpu.make_async_copy(mixed.at[:, :, lanes], mixed_ref.at[:, :, lanes], out_sems.at[2 + 2 * index])
+        )
+        for store in stores[-2:]:
+            store.start()
+    project_chunk(chunks - 1)
+
+    for row in range(1, own + 1):
         first = total[row * cols : (row + 1) * cols]
-        first_ref[row] = first
-        if 1 <= row <= own:
-            normed_ref[row - 1] = (first * rms_scale(first)).astype(BF16)
+        normed[row - 1] = (first * rms_scale(first)).astype(BF16)
+    stores.append(pltpu.make_async_copy(normed, normed_ref, out_sems.at[1 + 2 * chunks]))
+    stores.append(pltpu.make_async_copy(total, first_ref, out_sems.at[2 + 2 * chunks]))
+    for store in stores[-2:]:
+        store.start()
+    for store in stores:
+        store.wait()
 
 
 def forward(bands, features, other, rim, w_expand, kernel, w_project):
     capacity, cols, width = features.shape
     own, rows = GRID_ROWS, GRID_ROWS + 2 * RIM
     hidden_width = w_expand.shape[1]
+    chunks = hidden_width // CHUNK
     return pl.pallas_call(
         forward_body,
-        in_specs=[in_scalars()] + [in_vmem()] * 6,
-        out_specs=[in_vmem()] * 5,
+        in_specs=[in_scalars()] + [in_hbm()] * 4 + [in_vmem(), in_hbm()],
+        out_specs=[in_hbm()] * 5,
         out_shape=[
-            jax.ShapeDtypeStruct((rows - 2, cols, width), F32),
+            jax.ShapeDtypeStruct(((rows - 2) * cols, width), F32),
             jax.ShapeDtypeStruct((own, cols, width), BF16),
             jax.ShapeDtypeStruct((own, cols, width), BF16),
             jax.ShapeDtypeStruct((own, cols, hidden_width), F32),
@@ -210,9 +297,17 @@
         scratch_shapes=[
             pltpu.VMEM((rows, cols, width), BF16),
             pltpu.VMEM((rows * cols, width), BF16),
+            pltpu.VMEM((chunks, width, CHUNK), BF16),
+            pltpu.VMEM((chunks, CHUNK, width), BF16),
+            pltpu.VMEM((rows, cols, hidden_width), F32),
             pltpu.VMEM((rows, cols, CHUNK), F32),
-            pltpu.VMEM(((rows - 2) * cols, CHUNK), BF16),
+            pltpu.VMEM((rows - 2, cols, hidden_width), F32),
+            pltpu.VMEM((2, (rows - 2) * cols, CHUNK), BF16),
             pltpu.VMEM(((rows - 2) * cols, width), F32),
+            pltpu.VMEM((own, cols, width), BF16),
+            pltpu.SemaphoreType.DMA((4,)),
+            pltpu.SemaphoreType.DMA((2 * chunks,)),
+            pltpu.SemaphoreType.DMA((2 * chunks + 3,)),
         ],
         compiler_params=params(),
         cost_estimate=pl.CostEstimate(
@@ -226,21 +321,23 @@
 
 def slopes_body(expanded_ref, mixed_ref, slope_one_ref, slope_two_ref):
     for source, target in ((expanded_ref, slope_one_ref), (mixed_ref, slope_two_ref)):
-
-        def step(row, carry):
-            for lane in range(0, source.shape[2], LANES):
+        rows, _, chunk = source.shape
+        for row in range(rows):
+            for lane in range(0, chunk, LANES):
                 lanes = slice(lane, lane + LANES)
                 target[row, :, lanes] = gelu_slope(source[row, :, lanes]).astype(BF16)
-            return carry
-
-        lax.fori_loop(0, source.shape[0], step, 0)
 
 
 def slopes(expanded, mixed):
+    hidden_width = expanded.shape[2]
+    blocks = [
+        pl.BlockSpec(values.shape[:2] + (CHUNK,), lambda j: (0, 0, j)) for values in (expanded, mixed)
+    ]
     return pl.pallas_call(
         slopes_body,
-        in_specs=[in_vmem()] * 2,
-        out_specs=[in_vmem()] * 2,
+        grid=(hidden_width // CHUNK,),
+        in_specs=blocks,
+        out_specs=blocks,
         out_shape=[jax.ShapeDtypeStruct(values.shape, BF16) for values in (expanded, mixed)],
         compiler_params=params(),
         cost_estimate=pl.CostEstimate(
@@ -307,8 +404,9 @@
     shape = (groups * own * cols, width)
     return pl.pallas_call(
         grad_attended_body,
-        in_specs=[in_vmem()] * 2,
-        out_specs=in_vmem(),
+        grid=(1,),
+        in_specs=[whole(cotangent.shape), whole(w_out.shape)],
+        out_specs=whole(shape),
         out_shape=jax.ShapeDtypeStruct(shape, BF16),
         scratch_shapes=[wide_scratch(cotangent.shape), pltpu.VMEM(shape, BF16)],
         compiler_params=params(),
@@ -378,8 +476,14 @@
     out_shapes = [normed.shape, (windows, span, HEADS * span), (tokens, width)]
     return pl.pallas_call(
         attention_body,
-        in_specs=[in_vmem()] * 4,
-        out_specs=[in_vmem()] * 3,
+        grid=(1,),
+        in_specs=[
+            whole(normed.shape),
+            whole(grad_attended.shape),
+            whole(mask.shape),
+            whole(w_qkv.shape),
+        ],
+        out_specs=[whole(shape) for shape in out_shapes],
         out_shape=[jax.ShapeDtypeStruct(shape, BF16) for shape in out_shapes],
         scratch_shapes=[
             wide_scratch(normed.shape),
@@ -412,8 +516,9 @@
 def attend(weights, values, w_out, shape):
     return pl.pallas_call(
         attended_body,
-        in_specs=[in_vmem()] * 3,
-        out_specs=in_vmem(),
+        grid=(1,),
+        in_specs=[whole(weights.shape), whole(values.shape), whole(w_out.shape)],
+        out_specs=whole(shape),
         out_shape=jax.ShapeDtypeStruct(shape, BF16),
         scratch_shapes=[wide_scratch(shape), pltpu.VMEM(values.shape, BF16)],
         compiler_params=params(),
@@ -426,8 +531,40 @@
 
 def backward_body(bands_ref, cotangent_ref, other_ref, rim_ref, slab_ref, first_ref, grad_slab_ref, grad_ref,
                   pair_ref, next_ref, slope_one_ref, slope_two_ref, expand_ref, taps_ref, project_ref,
-                  out_ref, rims, grad_first, grad_rows, mixed, expanded, total):
-    own, cols, width = slab_ref.shape
+                  out_ref, rims, slab, first, grad_slab, grad_in, slope_one, slope_two, expand, project,
+                  grad_first, grad_rows, grads, mixed, expanded, total, row_sems, in_sems, chunk_sems):
+    own, cols, width = slab.shape
+    chunks = expand_ref.shape[1] // CHUNK
+
+    sources = (cotangent_ref, other_ref, rim_ref)
+    sides = list(enumerate((-1, own)))
+    for side, place_first in sides:
+        start_pull(bands_ref, place_first, sources, 1, rims.at[pl.ds(side, 1)], row_sems.at[side], RIM)
+    inputs = [
+        pltpu.make_async_copy(source, target, in_sems.at[index])
+        for index, (source, target) in enumerate(
+            ((first_ref, first), (grad_ref, grad_in), (grad_slab_ref, grad_slab), (slab_ref, slab))
+        )
+    ]
+    for copy in inputs:
+        copy.start()
+    fetches = []
+    for index in range(chunks):
+        lanes = chunk_lanes(index)
+        pairs = (
+            (project_ref.at[lanes], project.at[index]),
+            (slope_two_ref.at[:, :, lanes], slope_two.at[:, :, lanes]),
+            (slope_one_ref.at[:, :, lanes], slope_one.at[:, :, lanes]),
+            (expand_ref.at[:, lanes], expand.at[index]),
+        )
+        fetches.append(
+            [
+                pltpu.make_async_copy(source, target, chunk_sems.at[4 * index + number])
+                for number, (source, target) in enumerate(pairs)
+            ]
+        )
+        for copy in fetches[-1]:
+            copy.start()
 
     def through_norm(cotangent, grad, first):
         rms = rms_scale(first)
@@ -436,49 +573,63 @@
         inner = jnp.mean(grad * normed, -1, keepdims=True)
         return cotangent.astype(F32) + rms * (grad - normed * inner)
 
-    for side, first in enumerate((-1, own)):
-        pull(bands_ref, first, (cotangent_ref, other_ref, rim_ref), 1, rims, side, RIM)
+    for copy in inputs[:3]:
+        copy.wait()
     for row in range(own):
-        result = through_norm(grad_slab_ref[row], grad_ref[row], first_ref[row + 1])
+        below = first[(row + 1) * cols : (row + 2) * cols]
+        result = through_norm(grad_slab[row], grad_in[row], below)
         grad_first[row * cols : (row + 1) * cols] = result
         grad_rows[(row + 1) * cols : (row + 2) * cols] = result.astype(BF16)
+    for side, place_first in sides:
+        wait_pull(sources, 1, rims.at[pl.ds(side, 1)], row_sems.at[side])
     leads = lax.rem(lax.axis_index("row"), 2) == 0
     above = jnp.where(leads, next_ref[0].astype(F32), pair_ref[0].astype(F32))
     below = jnp.where(leads, pair_ref[0].astype(F32), next_ref[0].astype(F32))
-    grad_rows[0:cols] = through_norm(rims[0], above, first_ref[0]).astype(BF16)
-    grad_rows[(own + 1) * cols :] = through_norm(rims[1], below, first_ref[own + 1]).astype(BF16)
-    total[...] = jnp.zeros_like(total)
+    last = (own + 1) * cols
+    grad_rows[0:cols] = through_norm(rims[0], above, first[0:cols]).astype(BF16)
+    grad_rows[last:] = through_norm(rims[1], below, first[last:]).astype(BF16)
     column = lax.broadcasted_iota(jnp.int32, (cols, LANES), 0)
 
-    def step(index, carry):
-        weights = project_ref[hidden_lanes(index), :]
-        for row in range(0, own + 2, 6):
-            grad = nt_dot(grad_rows[row * cols : (row + 6) * cols, :], weights)
-            for inner in range(6):
-                for lane in range(0, CHUNK, LANES):
-                    lanes = slice(lane, lane + LANES)
-                    slope = slope_two_ref[row + inner, :, hidden_lanes(index, lane, LANES)].astype(F32)
-                    value = grad[inner * cols : (inner + 1) * cols, lanes] * slope
-                    mixed[row + inner, :, lanes] = value.astype(BF16).astype(F32)
-
-        for lane in range(0, CHUNK, LANES):
-            lanes = slice(lane, lane + LANES)
-            taps = spread_taps(taps_ref, hidden_lanes(index, lane, LANES), cols)
+    def project_chunk(index):
+        fetches[index][0].wait()
+        for lane in range(0, CHUNK, WIDE):
+            wide = slice(lane, lane + WIDE)
+            product = nt_dot(grad_rows[...], project[index, wide, :])
+            grads[index % 2, :, :, wide] = product.reshape(own + 2, cols, WIDE)
+
+    def expand_chunk(index):
+        fetches[index][3].wait()
+        product = nt_dot(expanded[index % 2], expand[index])
+        total[...] = product if index == 0 else total[...] + product
+
+    project_chunk(0)
+    for index in range(chunks):
+        if index + 1 < chunks:
+            project_chunk(index + 1)
+        if index > 0:
+            expand_chunk(index - 1)
+        for copy in fetches[index][1:3]:
+            copy.wait()
+        for lanes in lane_pieces(0, CHUNK):
+            at = slice(index * CHUNK + lanes.start, index * CHUNK + lanes.stop)
+            for row in range(own + 2):
+                value = grads[index % 2, row, :, lanes] * slope_two[row, :, at].astype(F32)
+                mixed[row, :, lanes] = value.astype(BF16).astype(F32)
+            taps = spread_taps(taps_ref, at, cols)
             for row in range(own):
                 near = [mixed[row + a, :, lanes] for a in range(3)]
                 sums = [
                     taps[8 - b] * near[0] + taps[5 - b] * near[1] + taps[2 - b] * near[2] for b in range(3)
                 ]
-                grad = column_sums(sums[0], sums[1], sums[2], column, cols - 1)
-                slope = slope_one_ref[row, :, hidden_lanes(index, lane, LANES)].astype(F32)
-                expanded[row * cols : (row + 1) * cols, lanes] = (grad * slope).astype(BF16)
-        total[...] += nt_dot(expanded[...], expand_ref[:, hidden_lanes(index)])
-        return carry
-
-    lax.fori_loop(0, expand_ref.shape[1] // CHUNK, step, 0)
+                value = column_sums(sums[0], sums[1], sums[2], column, cols - 1)
+                value = value * slope_one[row, :, at].astype(F32)
+                expanded[index % 2, row * cols : (row + 1) * cols, lanes] = value.astype(BF16)
+    expand_chunk(chunks - 1)
+
+    inputs[3].wait()
     for row in range(own):
         at = slice(row * cols, (row + 1) * cols)
-        values = slab_ref[row].astype(F32)
+        values = slab[row].astype(F32)
         rms = rms_scale(values)
         normed = values * rms
         grad = total[at]
@@ -490,18 +641,31 @@
              slope_two, w_expand, kernel, w_project):
     own, cols, width = slab.shape
     hidden_width = w_expand.shape[1]
+    chunks = hidden_width // CHUNK
     return pl.pallas_call(
         backward_body,
-        in_specs=[in_scalars()] + [in_vmem()] * 14,
+        in_specs=[in_scalars()] + [in_hbm()] * 7 + [in_vmem()] * 2 + [in_hbm()] * 3 + [in_vmem(), in_hbm()],
         out_specs=in_vmem(),
         out_shape=jax.ShapeDtypeStruct((own, cols, width), BF16),
         scratch_shapes=[
             pltpu.VMEM((2, cols, width), BF16),
+            pltpu.VMEM((own, cols, width), BF16),
+            pltpu.VMEM(((own + 2) * cols, width), F32),
+            pltpu.VMEM((own, cols, width), BF16),
+            pltpu.VMEM((own, cols, width), BF16),
+            pltpu.VMEM((own, cols, hidden_width), BF16),
+            pltpu.VMEM((own + 2, cols, hidden_width), BF16),
+            pltpu.VMEM((chunks, width, CHUNK), BF16),
+            pltpu.VMEM((chunks, CHUNK, width), BF16),
             pltpu.VMEM((own * cols, width), F32),
             pltpu.VMEM(((own + 2) * cols, width), BF16),
+            pltpu.VMEM((2, own + 2, cols, CHUNK), F32),
             pltpu.VMEM((own + 2, cols, CHUNK), F32),
-            pltpu.VMEM((own * cols, CHUNK), BF16),
+            pltpu.VMEM((2, own * cols, CHUNK), BF16),
             pltpu.VMEM((own * cols, width), F32),
+            pltpu.SemaphoreType.DMA((2,)),
+            pltpu.SemaphoreType.DMA((4,)),
+            pltpu.SemaphoreType.DMA((4 * chunks,)),
         ],
         compiler_params=params(),
         cost_estimate=pl.CostEstimate(
@@ -586,7 +750,8 @@
         slope_one, slope_two, w_expand, kernel, w_project,
     )
     grad_input, added_rows = lax.optimization_barrier((grad_input, added_rows))
-    final = (first[1 : GRID_ROWS + 1] + added_rows.astype(F32)).astype(BF16)
+    first = first.reshape(GRID_ROWS + 2, cols, width)[1 : GRID_ROWS + 1]
+    final = (first + added_rows.astype(F32)).astype(BF16)
     sent = [jnp.where(leads, rows[BAND:], rows[:BAND]) for rows in (final, grad_input)]
     swapped = swap_pair(jnp.stack(sent))
     leader_share = BAND * row_bands[device - parity]

time: 129 us -> 114 us (0.88)
  local copies, waits for them, and re-layouts: 39.4 us -> 3.44 us
  Pallas kernels: 40.9 us -> 61.1 us
  waiting for transfers between devices: 10 us -> 16.4 us
  starting transfers between devices: 32.9 us -> 28.9 us
    unnamed x72 -> x22, local copies, waits for them, and re-layouts: 38.8 us -> 2.78 us
    pallas_call x8, Pallas kernels: 40.9 us -> 61.1 us  [the longest x1 14.5 us: forward(): pl.pallas_call(forward_body, in_specs=[in_scalars()] + [in_hbm()] * 4 + [...]
    all_to_all x4, waiting for transfers between devices: 9.19 us -> 15.5 us  [exchange_windows(): lax.all_to_all(rows, 'row', split_axis=0, concat_axis=0, tiled=True, axis...]
    all_to_all x4, starting transfers between devices: 29.8 us -> 26.2 us  [exchange_windows(): lax.all_to_all(rows, 'row', split_axis=0, concat_axis=0, tiled=True, axis...]
  transfers between devices with their start and end apart: 10 -> 10, of which waited for: 4 -> 5; matrix products, arithmetic and copies ran while one was open for 0% -> 1% of each run, Pallas kernels for 23% -> 42%
where the time goes in v7:
time: 114 us
  Pallas kernels  61.1 us (54%)
  starting transfers between devices  28.9 us (25%)
  waiting for transfers between devices  16.4 us (14%)
  local copies, waits for them, and re-layouts  3.44 us (3%)
  other arithmetic  2.32 us (2%)
  between operations  1.51 us (1%)
    all_to_all x4, starting transfers between devices, exchange_windows(): lax.all_to_all(rows, 'row', split_axis=0, concat_axis=0, tiled=True, axis...  26.2 us
    all_to_all x4, waiting for transfers between devices, exchange_windows(): lax.all_to_all(rows, 'row', split_axis=0, concat_axis=0, tiled=True, axis...  15.5 us
    pallas_call x1, Pallas kernels, forward(): pl.pallas_call(forward_body, in_specs=[in_scalars()] + [in_hbm()] * 4 + [...  14.5 us
    pallas_call x1, Pallas kernels, backward(): pl.pallas_call(backward_body, in_specs=[in_scalars()] + [in_hbm()] * 7 +...  14.4 us
    pallas_call x1, Pallas kernels, attention(): pl.pallas_call(attention_body, grid=(1,), in_specs=[whole(normed.shape),...  12.9 us
    pallas_call x1, Pallas kernels, slopes(): pl.pallas_call(slopes_body, grid=(hidden_width // CHUNK,), in_specs=block...  7.75 us
    pallas_call x1, Pallas kernels, attend(): pl.pallas_call(attended_body, grid=(1,), in_specs=[whole(weights.shape),...  3.82 us
    pallas_call x1, Pallas kernels, even_rows(): pl.pallas_call(even_body, in_specs=[in_scalars(), in_hbm(), in_vmem()], o...  2.94 us
  transfers between devices with their start and end apart: 10, of which 5 were waited for; matrix products, arithmetic and copies ran while one was open for 1% of the time, Pallas kernels for 42%

profile of v7, /device:TPU:0, one launch (start us, length us, event | category | flops | bytes accessed | tf_op | source)
XLA Modules:
  0.0 113.6 jit_solution(8236874575543888261)
XLA Ops:
  1.2 2.2 %rim_rows.1 = bf16[3,32,512]{2,1,0:T(8,128)(2,1)} custom-call(s32[16]{0:T(128)} %bands_ref.7, bf16[24,32,512]{2,1,0:T(8,128)(2,1)} %features_ref.3, bf16[24,32,512]{2,1,0:T(8,128)(2,1)} %cotangent_ref.3), custom_call_target="tpu_custom_call" | custom-call | tf_op jit(solution)/shard_map/rim_rows/pallas_call | solution.py:168
  3.4 0.7 collective-permute-start.1
  4.1 0.9 copy-done.2
  5.0 2.9 %even_rows.1.grad_slab_ref = bf16[16,32,512]{2,1,0:T(8,128)(2,1)} custom-call(s32[16]{0:T(128)} %bands_ref.7, bf16[24,32,512]{2,1,0:T(8,128)(2,1)} %cotangent_ref.3, bf16[24,32,512]{2,1,0:T(8,128)(2,1)} %copy-done.2), custom_call_target="tpu_custom_call" | custom-call | tf_op jit(solution)/shard_map/even_rows/pallas_call | solution.py:138
  7.9 8.9 %all-to-all-start = ((bf16[16,32,512]{2,1,0:T(8,128)(2,1)}), bf16[16,32,512]{2,1,0:T(8,128)(2,1)S(1)}, u32[]{:S(2)}, u32[]{:S(2)}) async-start(bf16[16,32,512]{2,1,0:T(8,128)(2,1)} %even_rows.1.grad_slab_ref), calls=%async_computation | async-start | bytes 1048576 | tf_op jit(solution)/shard_map/all_to_all | solution.py:688
  16.9 0.9 copy-done.10
  17.8 14.5 %bottleneck_forward.1 = (f32[576,512]{1,0:T(8,128)}, bf16[16,32,512]{2,1,0:T(8,128)(2,1)}, bf16[16,32,512]{2,1,0:T(8,128)(2,1)}, f32[16,32,2048]{2,1,0:T(8,128)}, f32[18,32,2048]{2,1,0:T(8,128)}) custom-call(s32[16]{0:T(128)} %bands_ref.7, bf16[24,32,512]{2,1,0:T(8,128)(2,1)} %features_ref.3, bf16[24,32,512]{2,1,0:T(8,128)(2,1)} %copy-done.10, ...), custom_call_target="tpu_custom_call" | custom-call | flops 2684354560 | bytes 12582912 | tf_op jit(solution)/shard_map/bottleneck_forward/pallas_call | solution.py:286
  32.3 6.0 %all-to-all-start.1 = ((bf16[16,32,512]{2,1,0:T(8,128)(2,1)}), bf16[16,32,512]{2,1,0:T(8,128)(2,1)S(1)}, u32[]{:S(2)}, u32[]{:S(2)}) async-start(bf16[16,32,512]{2,1,0:T(8,128)(2,1)} %get-tuple-element.32), calls=%async_computation.1 | async-start | bytes 1048576 | tf_op jit(solution)/shard_map/all_to_all | solution.py:688
  38.3 7.8 %gelu_slopes.1 = (bf16[16,32,2048]{2,1,0:T(8,128)(2,1)}, bf16[18,32,2048]{2,1,0:T(8,128)(2,1)}) custom-call(f32[16,32,2048]{2,1,0:T(8,128)} %get-tuple-element.33.expanded_ref, f32[18,32,2048]{2,1,0:T(8,128)} %get-tuple-element.34.mixed_ref), custom_call_target="tpu_custom_call" | custom-call | flops 33423360 | bytes 13369344 | tf_op jit(solution)/shard_map/gelu_slopes/pallas_call | solution.py:336
  46.1 2.5 %attended_gradient.1.grad_attended_ref = bf16[512,512]{1,0:T(8,128)(2,1)} custom-call(bf16[8,2,32,512]{3,2,1,0:T(8,128)(2,1)} %bitcast.24, bf16[512,512]{1,0:T(8,128)(2,1)} %out_ref.3), custom_call_target="tpu_custom_call" | custom-call | flops 268435456 | bytes 2097152 | tf_op jit(solution)/shard_map/attended_gradient/pallas_call | solution.py:405
  48.6 4.1 %all-to-all-done.1 = bf16[16,32,512]{2,1,0:T(8,128)(2,1)S(1)} async-done(((bf16[16,32,512]{2,1,0:T(8,128)(2,1)}), bf16[16,32,512]{2,1,0:T(8,128)(2,1)S(1)}, u32[]{:S(2)}, u32[]{:S(2)}) %all-to-all-start.1) | async-done | bytes 524320 | tf_op jit(solution)/shard_map/all_to_all | solution.py:688
  52.7 0.8 copy-done.5
  53.5 12.9 %window_attention.1 = (bf16[8,2,32,512]{3,2,1,0:T(8,128)(2,1)}, bf16[8,64,1024]{2,1,0:T(8,128)(2,1)}, bf16[512,512]{1,0:T(8,128)(2,1)}) custom-call(bf16[8,2,32,512]{3,2,1,0:T(8,128)(2,1)} %bitcast.26, bf16[512,512]{1,0:T(8,128)(2,1)} %attended_gradient.1.grad_attended_ref, bf16[256,128]{1,0:T(8,128)(2,1)} %constant.29.clone.mask_ref, bf16[512,1536]{1,0:T(8,128)(2,1)} %qkv_ref.1), custom_call_target="tpu_custom_call" | custom-call | flops 2147483648 | bytes 4194304 | tf_op jit(solution)/shard_map/window_attention/pallas_call | solution.py:477
  66.4 3.6 %all-to-all-start.2 = ((bf16[16,32,512]{2,1,0:T(8,128)(2,1)}), bf16[16,32,512]{2,1,0:T(8,128)(2,1)S(1)}, u32[]{:S(2)}, u32[]{:S(2)}) async-start(bf16[16,32,512]{2,1,0:T(8,128)(2,1)} %bitcast.25), calls=%async_computation.2 | async-start | bytes 1048576 | tf_op jit(solution)/shard_map/all_to_all | solution.py:688
  70.1 3.8 %attended_output.1 = bf16[8,2,32,512]{3,2,1,0:T(8,128)(2,1)} custom-call(bf16[8,64,1024]{2,1,0:T(8,128)(2,1)} %get-tuple-element.41.weights_ref, bf16[512,512]{1,0:T(8,128)(2,1)} %get-tuple-element.42.values_ref, bf16[512,512]{1,0:T(8,128)(2,1)} %out_ref.3), custom_call_target="tpu_custom_call" | custom-call | flops 536870912 | bytes 3145728 | tf_op jit(solution)/shard_map/attended_output/pallas_call | solution.py:517
  73.9 10.8 %all-to-all-done.2.grad_ref = bf16[16,32,512]{2,1,0:T(8,128)(2,1)S(1)} async-done(((bf16[16,32,512]{2,1,0:T(8,128)(2,1)}), bf16[16,32,512]{2,1,0:T(8,128)(2,1)S(1)}, u32[]{:S(2)}, u32[]{:S(2)}) %all-to-all-start.2) | async-done | bytes 524320 | tf_op jit(solution)/shard_map/all_to_all | solution.py:688
  84.8 0.7 collective-permute-start.4
  86.0 7.7 %all-to-all-start.3 = ((bf16[16,32,512]{2,1,0:T(8,128)(2,1)}), bf16[16,32,512]{2,1,0:T(8,128)(2,1)S(1)}, u32[]{:S(2)}, u32[]{:S(2)}) async-start(bf16[16,32,512]{2,1,0:T(8,128)(2,1)} %bitcast.23), calls=%async_computation.3 | async-start | bytes 1048576 | tf_op jit(solution)/shard_map/all_to_all | solution.py:688
  93.8 14.4 %bottleneck_backward.1 = bf16[16,32,512]{2,1,0:T(8,128)(2,1)} custom-call(s32[16]{0:T(128)} %bands_ref.7, bf16[24,32,512]{2,1,0:T(8,128)(2,1)} %cotangent_ref.3, bf16[24,32,512]{2,1,0:T(8,128)(2,1)} %copy-done.2, bf16[3,32,512]{2,1,0:T(8,128)(2,1)} %copy-done.6, bf16[16,32,512]{2,1,0:T(8,128)(2,1)} %get-tuple-element.29.slab_ref, ...), custom_call_target="tpu_custom_call" | custom-call | flops 2415919104 | bytes 12582912 | tf_op jit(solution)/shard_map/bottleneck_backward/pallas_call | solution.py:645
  108.2 0.7 all-to-all-done.3
  109.4 0.6 collective-permute-start.5
  110.0 0.6 dynamic_slice.3
  111.6 1.0 pad_maximum_fusion.1
  112.6 1.0 pad_maximum_fusion
  (35 shorter events, 2.2 us)
Async XLA Ops:
  0.6 3.5 %collective-permute-start.2 = (bf16[24,32,512]{2,1,0:T(8,128)(2,1)}, bf16[24,32,512]{2,1,0:T(8,128)(2,1)S(1)}, u32[]{:S(2)}, u32[]{:S(2)}) collective-permute-start(bf16[24,32,512]{2,1,0:T(8,128)(2,1)} %cotangent_ref.3), channel_id=1, source_target_pairs={{0,1},{1,0},{2,3},{3,2},{4,5},{5,4},{6,7},{7,6},{8,9},{9,8},{10,11... | collective-permute-start | bytes 2359304 | tf_op jit(solution)/shard_map/ppermute | solution.py:695
  1.1 15.7 %collective-permute-start = (bf16[24,32,512]{2,1,0:T(8,128)(2,1)}, bf16[24,32,512]{2,1,0:T(8,128)(2,1)S(1)}, u32[]{:S(2)}, u32[]{:S(2)}) collective-permute-start(bf16[24,32,512]{2,1,0:T(8,128)(2,1)} %features_ref.3), channel_id=1, source_target_pairs={{0,1},{1,0},{2,3},{3,2},{4,5},{5,4},{6,7},{7,6},{8,9},{9,8},{10,11... | collective-permute-start | bytes 2359304 | tf_op jit(solution)/shard_map/ppermute | solution.py:695
  3.4 4.5 %collective-permute-start.1 = (bf16[3,32,512]{2,1,0:T(8,128)(2,1)}, bf16[3,32,512]{2,1,0:T(8,128)(2,1)S(1)}, u32[]{:S(2)}, u32[]{:S(2)}) collective-permute-start(bf16[3,32,512]{2,1,0:T(8,128)(2,1)} %rim_rows.1), channel_id=1, source_target_pairs={{1,2},{3,4},{5,6},{7,8},{9,10},{11,12},{13,14},{2,1},{4,3},{6,5},{... | collective-permute-start | bytes 294920 | tf_op jit(solution)/shard_map/ppermute | solution.py:701
  4.1 0.9 copy-start.2
  7.9 8.9 %copy-start.6 = (bf16[3,32,512]{2,1,0:T(8,128)(2,1)}, bf16[3,32,512]{2,1,0:T(8,128)(2,1)S(1)}, u32[]{:S(2)}) copy-start(bf16[3,32,512]{2,1,0:T(8,128)(2,1)S(1)} %collective-permute-done.1.rim_ref) | copy-start | bytes 294916
  7.9 24.4 %all-to-all-start = ((bf16[16,32,512]{2,1,0:T(8,128)(2,1)}), bf16[16,32,512]{2,1,0:T(8,128)(2,1)S(1)}, u32[]{:S(2)}, u32[]{:S(2)}) async-start(bf16[16,32,512]{2,1,0:T(8,128)(2,1)} %even_rows.1.grad_slab_ref), calls=%async_computation | async-start | bytes 1048576 | tf_op jit(solution)/shard_map/all_to_all | solution.py:688
  16.9 0.9 copy-start.10
  32.3 13.8 %copy-start.4 = (bf16[16,32,512]{2,1,0:T(8,128)(2,1)}, bf16[16,32,512]{2,1,0:T(8,128)(2,1)S(1)}, u32[]{:S(2)}) copy-start(bf16[16,32,512]{2,1,0:T(8,128)(2,1)S(1)} %all-to-all-done) | copy-start | bytes 1572868
  32.3 20.4 %all-to-all-start.1 = ((bf16[16,32,512]{2,1,0:T(8,128)(2,1)}), bf16[16,32,512]{2,1,0:T(8,128)(2,1)S(1)}, u32[]{:S(2)}, u32[]{:S(2)}) async-start(bf16[16,32,512]{2,1,0:T(8,128)(2,1)} %get-tuple-element.32), calls=%async_computation.1 | async-start | bytes 1048576 | tf_op jit(solution)/shard_map/all_to_all | solution.py:688
  52.7 0.8 copy-start.5
  66.4 18.3 %all-to-all-start.2 = ((bf16[16,32,512]{2,1,0:T(8,128)(2,1)}), bf16[16,32,512]{2,1,0:T(8,128)(2,1)S(1)}, u32[]{:S(2)}, u32[]{:S(2)}) async-start(bf16[16,32,512]{2,1,0:T(8,128)(2,1)} %bitcast.25), calls=%async_computation.2 | async-start | bytes 1048576 | tf_op jit(solution)/shard_map/all_to_all | solution.py:688
  70.1 23.6 %copy-start.1 = (f32[576,512]{1,0:T(8,128)S(1)}, f32[576,512]{1,0:T(8,128)}, u32[]{:S(2)}) copy-start(f32[576,512]{1,0:T(8,128)} %get-tuple-element.28.first_ref) | copy-start | bytes 3538948
  84.7 9.1 %copy-start.3 = (bf16[16,32,512]{2,1,0:T(8,128)(2,1)}, bf16[16,32,512]{2,1,0:T(8,128)(2,1)S(1)}, u32[]{:S(2)}) copy-start(bf16[16,32,512]{2,1,0:T(8,128)(2,1)S(1)} %all-to-all-done.2.grad_ref) | copy-start | bytes 1572868
  84.7 1.3 %collective-permute-start.3 = (bf16[1,32,512]{2,1,0:T(8,128)(2,1)S(1)}, bf16[1,32,512]{2,1,0:T(8,128)(2,1)S(1)}, u32[]{:S(2)}, u32[]{:S(2)}) collective-permute-start(bf16[1,32,512]{2,1,0:T(8,128)(2,1)S(1)} %get-tuple-element.61), channel_id=1, source_target_pairs={{0,1},{1,0},{2,3},{3,2},{4,5},{5,4},{6,7},{7,6},{8,9},{9,8},{10,11... | collective-permute-start | bytes 98312 | tf_op jit(solution)/shard_map/ppermute | solution.py:695
  84.8 1.2 %collective-permute-start.4 = (bf16[1,32,512]{2,1,0:T(8,128)(2,1)S(1)}, bf16[1,32,512]{2,1,0:T(8,128)(2,1)S(1)}, u32[]{:S(2)}, u32[]{:S(2)}) collective-permute-start(bf16[1,32,512]{2,1,0:T(8,128)(2,1)S(1)} %get-tuple-element.60), channel_id=1, source_target_pairs={{1,2},{3,4},{5,6},{7,8},{9,10},{11,12},{13,14},{2,1},{4,3},{6,5},{... | collective-permute-start | bytes 98312 | tf_op jit(solution)/shard_map/ppermute | solution.py:701
  86.0 7.8 %copy-start.7 = (bf16[1,32,512]{2,1,0:T(8,128)(2,1)}, bf16[1,32,512]{2,1,0:T(8,128)(2,1)S(1)}, u32[]{:S(2)}) copy-start(bf16[1,32,512]{2,1,0:T(8,128)(2,1)S(1)} %collective-permute-done.3.pair_ref) | copy-start | bytes 98308
  86.0 7.8 %copy-start.8 = (bf16[1,32,512]{2,1,0:T(8,128)(2,1)}, bf16[1,32,512]{2,1,0:T(8,128)(2,1)S(1)}, u32[]{:S(2)}) copy-start(bf16[1,32,512]{2,1,0:T(8,128)(2,1)S(1)} %collective-permute-done.4.next_ref) | copy-start | bytes 98308
  86.0 22.9 %all-to-all-start.3 = ((bf16[16,32,512]{2,1,0:T(8,128)(2,1)}), bf16[16,32,512]{2,1,0:T(8,128)(2,1)S(1)}, u32[]{:S(2)}, u32[]{:S(2)}) async-start(bf16[16,32,512]{2,1,0:T(8,128)(2,1)} %bitcast.23), calls=%async_computation.3 | async-start | bytes 1048576 | tf_op jit(solution)/shard_map/all_to_all | solution.py:688
  108.2 1.0 copy-start
  108.9 1.1 copy-start.9
  109.4 2.2 %collective-permute-start.5 = (bf16[2,8,32,512]{3,2,1,0:T(8,128)(2,1)S(1)}, bf16[2,8,32,512]{3,2,1,0:T(8,128)(2,1)S(1)}, u32[]{:S(2)}, u32[]{:S(2)}) collective-permute-start(bf16[2,8,32,512]{3,2,1,0:T(8,128)(2,1)S(1)} %pad_maximum_fusion.2), channel_id=1, source_target_pairs={{0,1},{1,0},{2,3},{3,2},{4,5},{5,4},{6,7},{7,6},{8,9},{9,8},{10,11... | collective-permute-start | bytes 1572872 | tf_op jit(solution)/shard_map/ppermute | solution.py:695

commit v8 on v6

--- a/solution.py
+++ b/solution.py
@@ -2,7 +2,6 @@
 
 import jax
 import jax.numpy as jnp
-import numpy as np
 from jax import lax
 from jax.experimental import pallas as pl
 from jax.experimental.pallas import tpu as pltpu
@@ -19,7 +18,7 @@
 CUBIC = 0.044715
 F32 = jnp.float32
 BF16 = jnp.bfloat16
-VMEM_LIMIT = 20 * 1024 * 1024
+MIB = 1024 * 1024
 
 
 def nt_dot(left, right):
@@ -53,12 +52,29 @@
     return cdf + (value - value * cdf) * (2.0 * ROOT + (6.0 * ROOT * CUBIC) * square)
 
 
+def whole(shape, space=None):
+    zeros = (0,) * len(shape)
+    return pl.BlockSpec(shape, lambda *_: zeros)
+
+
+def params(mebibytes=56):
+    return pltpu.CompilerParams(vmem_limit_bytes=mebibytes * MIB)
+
+
 def in_vmem():
     return pl.BlockSpec(memory_space=pltpu.VMEM)
 
 
-def params():
-    return pltpu.CompilerParams(vmem_limit_bytes=VMEM_LIMIT)
+def in_hbm():
+    return pl.BlockSpec(memory_space=pltpu.HBM)
+
+
+def held(array):
+    return pltpu.with_memory_space_constraint(array, pltpu.HBM)
+
+
+def near(array):
+    return pltpu.with_memory_space_constraint(array, pltpu.VMEM)
 
 
 def in_scalars():
@@ -81,19 +97,28 @@
     return source, jnp.where(beyond, 0, jnp.where(in_leader, row, row - leader_share))
 
 
-def pull(bands_ref, first, sources, rows, target, at, rim_row=0):
+def start_pull(bands_ref, first, sources, rows, target, sem, rim_row=0):
     where, row = place(bands_ref, first)
     row = jnp.where(where == 2, rim_row, row)
     for number, source in enumerate(sources):
 
         @pl.when(where == number)
         def _():
-            target[at : at + rows] = source[pl.ds(row, rows)]
+            pltpu.make_async_copy(source.at[pl.ds(row, rows)], target, sem).start()
+
+
+def wait_pull(sources, rows, target, sem):
+    pltpu.make_async_copy(sources[0].at[pl.ds(0, rows)], target, sem).wait()
 
 
 def even_body(bands_ref, own_ref, other_ref, out_ref):
     for half in range(2):
-        pull(bands_ref, BAND * half, (own_ref, other_ref), BAND, out_ref, BAND * half)
+        where, row = place(bands_ref, BAND * half)
+        for number, source in enumerate((own_ref, other_ref)):
+
+            @pl.when(where == number)
+            def _():
+                out_ref[BAND * half : BAND * half + BAND] = source[pl.ds(row, BAND)]
 
 
 def even_rows(bands, own, other):
@@ -103,28 +128,39 @@
         in_specs=[in_scalars(), in_vmem(), in_vmem()],
         out_specs=in_vmem(),
         out_shape=jax.ShapeDtypeStruct(shape, own.dtype),
-        compiler_params=params(),
+        compiler_params=params(8),
         name="even_rows",
-    )(bands, own, other)
-
-
-def rim_body(bands_ref, features_ref, cotangent_ref, out_ref):
+    )(bands, near(own), near(other))
+
+
+def rim_body(bands_ref, features_ref, cotangent_ref, out_ref, sems):
     parity, _, share = shares(bands_ref)
     leads = parity == 0
-    out_ref[0:RIM] = features_ref[pl.ds(jnp.where(leads, 0, share - RIM), RIM)]
-    out_ref[RIM : RIM + 1] = cotangent_ref[pl.ds(jnp.where(leads, 0, share - 1), 1)]
+    copies = [
+        pltpu.make_async_copy(
+            features_ref.at[pl.ds(jnp.where(leads, 0, share - RIM), RIM)], out_ref.at[pl.ds(0, RIM)], sems.at[0]
+        ),
+        pltpu.make_async_copy(
+            cotangent_ref.at[pl.ds(jnp.where(leads, 0, share - 1), 1)], out_ref.at[pl.ds(RIM, 1)], sems.at[1]
+        ),
+    ]
+    for copy in copies:
+        copy.start()
+    for copy in copies:
+        copy.wait()
 
 
 def rim_rows(bands, features, cotangent):
     shape = (RIM + 1,) + features.shape[1:]
     return pl.pallas_call(
         rim_body,
-        in_specs=[in_scalars(), in_vmem(), in_vmem()],
+        in_specs=[in_scalars(), in_hbm(), in_hbm()],
         out_specs=in_vmem(),
         out_shape=jax.ShapeDtypeStruct(shape, features.dtype),
-        compiler_params=params(),
+        scratch_shapes=[pltpu.SemaphoreType.DMA((2,))],
+        compiler_params=params(8),
         name="rim_rows",
-    )(bands, features, cotangent)
+    )(bands, held(features), held(cotangent))
 
 
 def column_sums(left, mid, right, column, last):
@@ -138,19 +174,47 @@
     return [jnp.broadcast_to(taps[i : i + 1], (cols, LANES)) for i in range(9)]
 
 
-def hidden_lanes(step, lane=0, count=CHUNK):
-    return pl.ds(pl.multiple_of(step * CHUNK + lane, LANES), count)
+def chunk_lanes(index, lane=0, count=CHUNK):
+    return pl.ds(pl.multiple_of(index * CHUNK + lane, LANES), count)
 
 
 def forward_body(bands_ref, features_ref, other_ref, rim_ref, expand_ref, taps_ref, project_ref, first_ref,
-                 normed_ref, slab_ref, expanded_ref, mixed_ref, slab, normed_one, hidden, hidden_two, total):
+                 normed_ref, slab_ref, expanded_ref, mixed_ref, slab, normed_one, expand, project, expanded,
+                 hidden, mixed, hidden_two, total, normed, row_sems, weight_sems, chunk_sems, out_sems):
     rows, cols, width = slab.shape
     own = rows - 2 * RIM
+    chunks = expand_ref.shape[1] // CHUNK
 
     sources = (features_ref, other_ref, rim_ref)
-    for first, count in ((0, RIM), (RIM, BAND), (RIM + BAND, BAND), (RIM + 2 * BAND, RIM)):
-        pull(bands_ref, first - RIM, sources, count, slab, first)
-    slab_ref[...] = slab[RIM : RIM + own]
+    pieces = [(0, RIM), (RIM, BAND), (RIM + BAND, BAND), (RIM + 2 * BAND, RIM)]
+    for index, (first, count) in enumerate(pieces):
+        start_pull(bands_ref, first - RIM, sources, count, slab.at[pl.ds(first, count)], row_sems.at[index])
+
+    def fetch_expand(index):
+        lanes = chunk_lanes(index)
+        return pltpu.make_async_copy(expand_ref.at[:, lanes], expand.at[:, lanes], weight_sems.at[0, index])
+
+    def fetch_project(index):
+        lanes = chunk_lanes(index)
+        return pltpu.make_async_copy(project_ref.at[lanes], project.at[lanes], weight_sems.at[1, index])
+
+    def store_expanded(index):
+        lanes = chunk_lanes(index)
+        return pltpu.make_async_copy(
+            expanded.at[:, :, lanes], expanded_ref.at[:, :, lanes], chunk_sems.at[0, index]
+        )
+
+    def store_mixed(index):
+        lanes = chunk_lanes(index)
+        return pltpu.make_async_copy(mixed.at[:, :, lanes], mixed_ref.at[:, :, lanes], chunk_sems.at[1, index])
+
+    for index in range(chunks):
+        fetch_expand(index).start()
+        fetch_project(index).start()
+    for index, (first, count) in enumerate(pieces):
+        wait_pull(sources, count, slab.at[pl.ds(first, count)], row_sems.at[index])
+    store_slab = pltpu.make_async_copy(slab.at[pl.ds(RIM, own)], slab_ref, out_sems.at[0])
+    store_slab.start()
     for row in range(0, rows, 2):
         at = slice(row * cols, (row + 2) * cols)
         values = slab[row : row + 2].astype(F32).reshape(2 * cols, width)
@@ -159,88 +223,112 @@
     column = lax.broadcasted_iota(jnp.int32, (cols, LANES), 0)
 
     def step(index, carry):
-        weights = expand_ref[:, hidden_lanes(index)]
+        fetch_expand(index).wait()
+        weights = expand[:, chunk_lanes(index)]
         for row in range(0, rows, 4):
-            expanded = nn_dot(normed_one[row * cols : (row + 4) * cols, :], weights)
+            product = nn_dot(normed_one[row * cols : (row + 4) * cols, :], weights)
             for inner in range(4):
                 for lane in range(0, CHUNK, LANES):
                     lanes = slice(lane, lane + LANES)
-                    values = expanded[inner * cols : (inner + 1) * cols, lanes]
+                    values = product[inner * cols : (inner + 1) * cols, lanes]
                     hidden[row + inner, :, lanes] = gelu(values).astype(BF16).astype(F32)
                     if RIM <= row + inner < RIM + own:
-                        expanded_ref[row + inner - RIM, :, hidden_lanes(index, lane, LANES)] = values
+                        expanded[row + inner - RIM, :, chunk_lanes(index, lane, LANES)] = values
+        store_expanded(index).start()
 
         for lane in range(0, CHUNK, LANES):
             lanes = slice(lane, lane + LANES)
-            taps = spread_taps(taps_ref, hidden_lanes(index, lane, LANES), cols)
+            taps = spread_taps(taps_ref, chunk_lanes(index, lane, LANES), cols)
             for row in range(rows - 2):
-                near = [hidden[row + a, :, lanes] for a in range(3)]
+                rows_near = [hidden[row + a, :, lanes] for a in range(3)]
                 sums = [
-                    taps[b] * near[0] + taps[3 + b] * near[1] + taps[6 + b] * near[2] for b in range(3)
+                    taps[b] * rows_near[0] + taps[3 + b] * rows_near[1] + taps[6 + b] * rows_near[2] for b in range(3)
                 ]
-                mixed = column_sums(sums[0], sums[1], sums[2], column, cols - 1)
-                hidden_two[row * cols : (row + 1) * cols, lanes] = gelu(mixed).astype(BF16)
-                mixed_ref[row, :, hidden_lanes(index, lane, LANES)] = mixed
-        total[...] += nn_dot(hidden_two[...], project_ref[hidden_lanes(index), :])
+                values = column_sums(sums[0], sums[1], sums[2], column, cols - 1)
+                hidden_two[row * cols : (row + 1) * cols, lanes] = gelu(values).astype(BF16)
+                mixed[row, :, chunk_lanes(index, lane, LANES)] = values
+        store_mixed(index).start()
+        fetch_project(index).wait()
+        total[...] += nn_dot(hidden_two[...], project[chunk_lanes(index), :])
         return carry
 
-    lax.fori_loop(0, expand_ref.shape[1] // CHUNK, step, 0)
-    for row in range(rows - 2):
+    lax.fori_loop(0, chunks, step, 0)
+    for row in range(1, own + 1):
         first = total[row * cols : (row + 1) * cols]
-        first_ref[row] = first
-        if 1 <= row <= own:
-            normed_ref[row - 1] = (first * rms_scale(first)).astype(BF16)
+        normed[row - 1] = (first * rms_scale(first)).astype(BF16)
+    store_normed = pltpu.make_async_copy(normed, normed_ref, out_sems.at[1])
+    store_first = pltpu.make_async_copy(total, first_ref, out_sems.at[2])
+    store_normed.start()
+    store_first.start()
+    for index in range(chunks):
+        store_expanded(index).wait()
+        store_mixed(index).wait()
+    store_slab.wait()
+    store_normed.wait()
+    store_first.wait()
 
 
 def forward(bands, features, other, rim, w_expand, kernel, w_project):
     capacity, cols, width = features.shape
     own, rows = GRID_ROWS, GRID_ROWS + 2 * RIM
     hidden_width = w_expand.shape[1]
+    chunks = hidden_width // CHUNK
     return pl.pallas_call(
         forward_body,
-        in_specs=[in_scalars()] + [in_vmem()] * 6,
-        out_specs=[in_vmem()] * 5,
+        in_specs=[in_scalars(), in_hbm(), in_vmem(), in_vmem(), in_hbm(), in_vmem(), in_hbm()],
+        out_specs=[in_hbm()] * 5,
         out_shape=[
-            jax.ShapeDtypeStruct((rows - 2, cols, width), F32),
-            jax.ShapeDtypeStruct((own, cols, width), BF16),
-            jax.ShapeDtypeStruct((own, cols, width), BF16),
-            jax.ShapeDtypeStruct((own, cols, hidden_width), F32),
-            jax.ShapeDtypeStruct((rows - 2, cols, hidden_width), F32),
+            pltpu.HBM(((rows - 2) * cols, width), F32),
+            pltpu.HBM((own, cols, width), BF16),
+            pltpu.HBM((own, cols, width), BF16),
+            pltpu.HBM((own, cols, hidden_width), F32),
+            pltpu.HBM((rows - 2, cols, hidden_width), F32),
         ],
         scratch_shapes=[
             pltpu.VMEM((rows, cols, width), BF16),
             pltpu.VMEM((rows * cols, width), BF16),
+            pltpu.VMEM((width, hidden_width), BF16),
+            pltpu.VMEM((hidden_width, width), BF16),
+            pltpu.VMEM((own, cols, hidden_width), F32),
             pltpu.VMEM((rows, cols, CHUNK), F32),
+            pltpu.VMEM((rows - 2, cols, hidden_width), F32),
             pltpu.VMEM(((rows - 2) * cols, CHUNK), BF16),
             pltpu.VMEM(((rows - 2) * cols, width), F32),
+            pltpu.VMEM((own, cols, width), BF16),
+            pltpu.SemaphoreType.DMA((4,)),
+            pltpu.SemaphoreType.DMA((2, chunks)),
+            pltpu.SemaphoreType.DMA((2, chunks)),
+            pltpu.SemaphoreType.DMA((3,)),
         ],
-        compiler_params=params(),
+        compiler_params=params(26),
         cost_estimate=pl.CostEstimate(
             flops=4 * rows * cols * width * hidden_width,
             bytes_accessed=12 * 1024 * 1024,
             transcendentals=2 * rows * cols * hidden_width,
         ),
         name="bottleneck_forward",
-    )(bands, features, other, rim, w_expand, kernel, w_project)
+    )(bands, held(features), near(other), near(rim), held(w_expand), near(kernel), held(w_project))
 
 
 def slopes_body(expanded_ref, mixed_ref, slope_one_ref, slope_two_ref):
     for source, target in ((expanded_ref, slope_one_ref), (mixed_ref, slope_two_ref)):
-
-        def step(row, carry):
-            for lane in range(0, source.shape[2], LANES):
+        rows, _, chunk = source.shape
+        for row in range(rows):
+            for lane in range(0, chunk, LANES):
                 lanes = slice(lane, lane + LANES)
                 target[row, :, lanes] = gelu_slope(source[row, :, lanes]).astype(BF16)
-            return carry
-
-        lax.fori_loop(0, source.shape[0], step, 0)
 
 
 def slopes(expanded, mixed):
+    hidden_width = expanded.shape[2]
+    blocks = [
+        pl.BlockSpec(values.shape[:2] + (CHUNK,), lambda j: (0, 0, j)) for values in (expanded, mixed)
+    ]
     return pl.pallas_call(
         slopes_body,
-        in_specs=[in_vmem()] * 2,
-        out_specs=[in_vmem()] * 2,
+        grid=(hidden_width // CHUNK,),
+        in_specs=blocks,
+        out_specs=blocks,
         out_shape=[jax.ShapeDtypeStruct(values.shape, BF16) for values in (expanded, mixed)],
         compiler_params=params(),
         cost_estimate=pl.CostEstimate(
@@ -250,12 +338,6 @@
         ),
         name="gelu_slopes",
     )(expanded, mixed)
-
-
-def head_mask(span, head_dim):
-    heads = LANES // head_dim
-    row_head = np.arange(heads * span)[:, None] // span
-    return (row_head == np.arange(LANES)[None, :] // head_dim).astype(np.float32)
 
 
 def lane_tiles(width):
@@ -307,8 +389,9 @@
     shape = (groups * own * cols, width)
     return pl.pallas_call(
         grad_attended_body,
-        in_specs=[in_vmem()] * 2,
-        out_specs=in_vmem(),
+        grid=(1,),
+        in_specs=[whole(cotangent.shape), whole(w_out.shape)],
+        out_specs=whole(shape),
         out_shape=jax.ShapeDtypeStruct(shape, BF16),
         scratch_shapes=[wide_scratch(cotangent.shape), pltpu.VMEM(shape, BF16)],
         compiler_params=params(),
@@ -327,21 +410,33 @@
     return jnp.where(lane_head % 2 == 0, own[:span], own[span:])
 
 
-def attention_body(normed_ref, grad_attended_ref, mask_ref, qkv_ref, grad_ref, weights_ref, values_ref,
-                   rows_wide, in_windows, projected, grad_projected):
+def attention_body(normed_ref, grad_attended_ref, qkv_ref, grad_ref, weights_ref, values_ref, rows_wide,
+                   in_windows, projected, grad_projected, grad_attended, qkv, grad, weights, in_sems, out_sems):
     groups, own, cols, width = normed_ref.shape
     span = groups * 8
+    windows = own * cols // 8
     head_dim = width // HEADS
     heads = LANES // head_dim
     scale = 1.0 / math.sqrt(head_dim)
     steepness = scale * math.log2(math.e)
 
+    fetch_qkv = pltpu.make_async_copy(qkv_ref, qkv, in_sems.at[0])
+    fetch_grad = pltpu.make_async_copy(grad_attended_ref, grad_attended, in_sems.at[1])
+    fetch_qkv.start()
+    fetch_grad.start()
     to_windows(normed_ref, rows_wide, in_windows)
-    projected[...] = nn_dot(in_windows[...], qkv_ref[...]).astype(BF16)
-    values_ref[...] = projected[:, 2 * width :]
+    fetch_qkv.wait()
+    projected[...] = nn_dot(in_windows[...], qkv[...]).astype(BF16)
+    store_values = pltpu.make_async_copy(projected.at[:, pl.ds(2 * width, width)], values_ref, out_sems.at[0])
+    store_values.start()
+    fetch_grad.wait()
+
+    row_head = lax.broadcasted_iota(jnp.int32, (heads * span, LANES), 0) // span
+    lane_head = lax.broadcasted_iota(jnp.int32, (heads * span, LANES), 1) // head_dim
+    mask = (row_head == lane_head).astype(F32).astype(BF16)
 
     def spread(values):
-        return jnp.concatenate([values] * heads, axis=0) * mask_ref[...]
+        return jnp.concatenate([values] * heads, axis=0) * mask
 
     def window(index, carry):
         rows = pl.ds(pl.multiple_of(index * span, span), span)
@@ -351,50 +446,61 @@
             )
             q, k, v = projected[rows, q_at], projected[rows, k_at], projected[rows, v_at]
             q_wide = spread(q)
-            g_wide = spread(grad_attended_ref[rows, q_at])
+            g_wide = spread(grad_attended[rows, q_at])
             scores = nt_dot(k, q_wide)
             powers = jnp.exp2((scores - jnp.max(scores, axis=0, keepdims=True)) * steepness)
-            weights = powers * (1.0 / jnp.sum(powers, axis=0, keepdims=True))
-            half = weights.astype(BF16)
-            weights_ref[index, :, part * heads * span : (part + 1) * heads * span] = half
+            shares = powers * (1.0 / jnp.sum(powers, axis=0, keepdims=True))
+            half = shares.astype(BF16)
+            weights[index, :, part * heads * span : (part + 1) * heads * span] = half
             grad_weights = nt_dot(v, g_wide)
-            row_dot = jnp.sum(weights * grad_weights, axis=0, keepdims=True)
-            grad_scores = (weights * (grad_weights - row_dot)).astype(BF16)
+            row_dot = jnp.sum(shares * grad_weights, axis=0, keepdims=True)
+            grad_scores = (shares * (grad_weights - row_dot)).astype(BF16)
             grad_projected[rows, q_at] = (per_query(k, grad_scores, span, head_dim) * scale).astype(BF16)
             grad_projected[rows, k_at] = (nn_dot(grad_scores, q_wide) * scale).astype(BF16)
             grad_projected[rows, v_at] = nn_dot(half, g_wide).astype(BF16)
         return carry
 
-    lax.fori_loop(0, own * cols // 8, window, 0, unroll=4)
-    to_rows(nt_dot(grad_projected[...], qkv_ref[...]), rows_wide, grad_ref)
+    lax.fori_loop(0, windows, window, 0, unroll=4)
+    store_weights = pltpu.make_async_copy(weights, weights_ref, out_sems.at[1])
+    store_weights.start()
+    to_rows(nt_dot(grad_projected[...], qkv[...]), rows_wide, grad)
+    store_grad = pltpu.make_async_copy(grad, grad_ref, out_sems.at[2])
+    store_grad.start()
+    store_values.wait()
+    store_weights.wait()
+    store_grad.wait()
 
 
 def attention(normed, grad_attended, w_qkv):
     groups, own, cols, width = normed.shape
     span = groups * 8
     tokens = groups * own * cols
-    windows = tokens // span
-    mask = head_mask(span, width // HEADS)
-    out_shapes = [normed.shape, (windows, span, HEADS * span), (tokens, width)]
+    out_shapes = [normed.shape, (tokens // span, span, HEADS * span), (tokens, width)]
     return pl.pallas_call(
         attention_body,
-        in_specs=[in_vmem()] * 4,
-        out_specs=[in_vmem()] * 3,
-        out_shape=[jax.ShapeDtypeStruct(shape, BF16) for shape in out_shapes],
+        in_specs=[in_vmem(), in_hbm(), in_hbm()],
+        out_specs=[in_hbm()] * 3,
+        out_shape=[pltpu.HBM(shape, BF16) for shape in out_shapes],
         scratch_shapes=[
             wide_scratch(normed.shape),
             pltpu.VMEM((tokens, width), BF16),
             pltpu.VMEM((tokens, 3 * width), BF16),
             pltpu.VMEM((tokens, 3 * width), BF16),
+            pltpu.VMEM((tokens, width), BF16),
+            pltpu.VMEM(w_qkv.shape, BF16),
+            pltpu.VMEM(normed.shape, BF16),
+            pltpu.VMEM(out_shapes[1], BF16),
+            pltpu.SemaphoreType.DMA((2,)),
+            pltpu.SemaphoreType.DMA((3,)),
         ],
-        compiler_params=params(),
+        compiler_params=params(18),
         cost_estimate=pl.CostEstimate(
             flops=16 * tokens * width * width,
             bytes_accessed=4 * 1024 * 1024,
             transcendentals=tokens * span * HEADS,
         ),
         name="window_attention",
-    )(normed, grad_attended, jnp.asarray(mask, BF16), w_qkv)
+    )(near(normed), held(grad_attended), held(w_qkv))
 
 
 def attended_body(weights_ref, values_ref, out_ref, added_ref, rows_wide, attended):
@@ -412,8 +518,9 @@
 def attend(weights, values, w_out, shape):
     return pl.pallas_call(
         attended_body,
-        in_specs=[in_vmem()] * 3,
-        out_specs=in_vmem(),
+        grid=(1,),
+        in_specs=[whole(weights.shape), whole(values.shape), whole(w_out.shape)],
+        out_specs=whole(shape),
         out_shape=jax.ShapeDtypeStruct(shape, BF16),
         scratch_shapes=[wide_scratch(shape), pltpu.VMEM(values.shape, BF16)],
         compiler_params=params(),
@@ -426,8 +533,40 @@
 
 def backward_body(bands_ref, cotangent_ref, other_ref, rim_ref, slab_ref, first_ref, grad_slab_ref, grad_ref,
                   pair_ref, next_ref, slope_one_ref, slope_two_ref, expand_ref, taps_ref, project_ref,
-                  out_ref, rims, grad_first, grad_rows, mixed, expanded, total):
-    own, cols, width = slab_ref.shape
+                  out_ref, rims, slab, first, grad_slab, grad_in, slope_one, slope_two, expand, project,
+                  grad_first, grad_rows, mixed, expanded, total, row_sems, in_sems, chunk_sems):
+    own, cols, width = slab.shape
+    chunks = expand_ref.shape[1] // CHUNK
+
+    sources = (cotangent_ref, other_ref, rim_ref)
+    sides = list(enumerate((-1, own)))
+    for side, place_first in sides:
+        start_pull(bands_ref, place_first, sources, 1, rims.at[pl.ds(side, 1)], row_sems.at[side], RIM)
+    inputs = [
+        pltpu.make_async_copy(source, target, in_sems.at[index])
+        for index, (source, target) in enumerate(
+            ((first_ref, first), (grad_ref, grad_in), (grad_slab_ref, grad_slab), (slab_ref, slab))
+        )
+    ]
+    for copy in inputs:
+        copy.start()
+
+    def fetches(index):
+        lanes = chunk_lanes(index)
+        pairs = (
+            (project_ref.at[lanes], project.at[lanes]),
+            (slope_two_ref.at[:, :, lanes], slope_two.at[:, :, lanes]),
+            (slope_one_ref.at[:, :, lanes], slope_one.at[:, :, lanes]),
+            (expand_ref.at[:, lanes], expand.at[:, lanes]),
+        )
+        return [
+            pltpu.make_async_copy(source, target, chunk_sems.at[number, index])
+            for number, (source, target) in enumerate(pairs)
+        ]
+
+    for index in range(chunks):
+        for copy in fetches(index):
+            copy.start()
 
     def through_norm(cotangent, grad, first):
         rms = rms_scale(first)
@@ -436,49 +575,57 @@
         inner = jnp.mean(grad * normed, -1, keepdims=True)
         return cotangent.astype(F32) + rms * (grad - normed * inner)
 
-    for side, first in enumerate((-1, own)):
-        pull(bands_ref, first, (cotangent_ref, other_ref, rim_ref), 1, rims, side, RIM)
+    for copy in inputs[:3]:
+        copy.wait()
     for row in range(own):
-        result = through_norm(grad_slab_ref[row], grad_ref[row], first_ref[row + 1])
+        below = first[(row + 1) * cols : (row + 2) * cols]
+        result = through_norm(grad_slab[row], grad_in[row], below)
         grad_first[row * cols : (row + 1) * cols] = result
         grad_rows[(row + 1) * cols : (row + 2) * cols] = result.astype(BF16)
+    for side, place_first in sides:
+        wait_pull(sources, 1, rims.at[pl.ds(side, 1)], row_sems.at[side])
     leads = lax.rem(lax.axis_index("row"), 2) == 0
     above = jnp.where(leads, next_ref[0].astype(F32), pair_ref[0].astype(F32))
     below = jnp.where(leads, pair_ref[0].astype(F32), next_ref[0].astype(F32))
-    grad_rows[0:cols] = through_norm(rims[0], above, first_ref[0]).astype(BF16)
-    grad_rows[(own + 1) * cols :] = through_norm(rims[1], below, first_ref[own + 1]).astype(BF16)
+    last = (own + 1) * cols
+    grad_rows[0:cols] = through_norm(rims[0], above, first[0:cols]).astype(BF16)
+    grad_rows[last:] = through_norm(rims[1], below, first[last:]).astype(BF16)
+    column = lax.broadcasted_iota(jnp.int32, (cols, LANES), 0)
+
     total[...] = jnp.zeros_like(total)
-    column = lax.broadcasted_iota(jnp.int32, (cols, LANES), 0)
 
     def step(index, carry):
-        weights = project_ref[hidden_lanes(index), :]
+        for copy in fetches(index):
+            copy.wait()
+        weights = project[chunk_lanes(index), :]
         for row in range(0, own + 2, 6):
             grad = nt_dot(grad_rows[row * cols : (row + 6) * cols, :], weights)
             for inner in range(6):
                 for lane in range(0, CHUNK, LANES):
                     lanes = slice(lane, lane + LANES)
-                    slope = slope_two_ref[row + inner, :, hidden_lanes(index, lane, LANES)].astype(F32)
+                    slope = slope_two[row + inner, :, chunk_lanes(index, lane, LANES)].astype(F32)
                     value = grad[inner * cols : (inner + 1) * cols, lanes] * slope
                     mixed[row + inner, :, lanes] = value.astype(BF16).astype(F32)
 
         for lane in range(0, CHUNK, LANES):
             lanes = slice(lane, lane + LANES)
-            taps = spread_taps(taps_ref, hidden_lanes(index, lane, LANES), cols)
+            taps = spread_taps(taps_ref, chunk_lanes(index, lane, LANES), cols)
             for row in range(own):
-                near = [mixed[row + a, :, lanes] for a in range(3)]
+                rows_near = [mixed[row + a, :, lanes] for a in range(3)]
                 sums = [
-                    taps[8 - b] * near[0] + taps[5 - b] * near[1] + taps[2 - b] * near[2] for b in range(3)
+                    taps[8 - b] * rows_near[0] + taps[5 - b] * rows_near[1] + taps[2 - b] * rows_near[2] for b in range(3)
                 ]
-                grad = column_sums(sums[0], sums[1], sums[2], column, cols - 1)
-                slope = slope_one_ref[row, :, hidden_lanes(index, lane, LANES)].astype(F32)
-                expanded[row * cols : (row + 1) * cols, lanes] = (grad * slope).astype(BF16)
-        total[...] += nt_dot(expanded[...], expand_ref[:, hidden_lanes(index)])
+                value = column_sums(sums[0], sums[1], sums[2], column, cols - 1)
+                value = value * slope_one[row, :, chunk_lanes(index, lane, LANES)].astype(F32)
+                expanded[row * cols : (row + 1) * cols, lanes] = value.astype(BF16)
+        total[...] += nt_dot(expanded[...], expand[:, chunk_lanes(index)])
         return carry
 
-    lax.fori_loop(0, expand_ref.shape[1] // CHUNK, step, 0)
+    lax.fori_loop(0, chunks, step, 0)
+    inputs[3].wait()
     for row in range(own):
         at = slice(row * cols, (row + 1) * cols)
-        values = slab_ref[row].astype(F32)
+        values = slab[row].astype(F32)
         rms = rms_scale(values)
         normed = values * rms
         grad = total[at]
@@ -490,28 +637,41 @@
              slope_two, w_expand, kernel, w_project):
     own, cols, width = slab.shape
     hidden_width = w_expand.shape[1]
+    chunks = hidden_width // CHUNK
     return pl.pallas_call(
         backward_body,
-        in_specs=[in_scalars()] + [in_vmem()] * 14,
+        in_specs=[in_scalars()] + [in_hbm()] * 7 + [in_vmem()] * 2 + [in_hbm()] * 3 + [in_vmem(), in_hbm()],
         out_specs=in_vmem(),
         out_shape=jax.ShapeDtypeStruct((own, cols, width), BF16),
         scratch_shapes=[
             pltpu.VMEM((2, cols, width), BF16),
+            pltpu.VMEM((own, cols, width), BF16),
+            pltpu.VMEM(((own + 2) * cols, width), F32),
+            pltpu.VMEM((own, cols, width), BF16),
+            pltpu.VMEM((own, cols, width), BF16),
+            pltpu.VMEM((own, cols, hidden_width), BF16),
+            pltpu.VMEM((own + 2, cols, hidden_width), BF16),
+            pltpu.VMEM((width, hidden_width), BF16),
+            pltpu.VMEM((hidden_width, width), BF16),
             pltpu.VMEM((own * cols, width), F32),
             pltpu.VMEM(((own + 2) * cols, width), BF16),
             pltpu.VMEM((own + 2, cols, CHUNK), F32),
             pltpu.VMEM((own * cols, CHUNK), BF16),
             pltpu.VMEM((own * cols, width), F32),
+            pltpu.SemaphoreType.DMA((2,)),
+            pltpu.SemaphoreType.DMA((4,)),
+            pltpu.SemaphoreType.DMA((4, chunks)),
         ],
-        compiler_params=params(),
+        compiler_params=params(26),
         cost_estimate=pl.CostEstimate(
             flops=4 * (own + 2) * cols * width * hidden_width,
             bytes_accessed=12 * 1024 * 1024,
             transcendentals=0,
         ),
         name="bottleneck_backward",
-    )(bands, cotangent, other, rim, slab, first, grad_slab, grad, pair_row, next_row, slope_one,
-      slope_two, w_expand, kernel, w_project)
+    )(bands, held(cotangent), held(other), held(rim), held(slab), held(first), held(grad_slab), held(grad),
+      near(pair_row), near(next_row), held(slope_one), held(slope_two), held(w_expand), near(kernel),
+      held(w_project))
 
 
 def window_groups(size):
@@ -586,7 +746,8 @@
         slope_one, slope_two, w_expand, kernel, w_project,
     )
     grad_input, added_rows = lax.optimization_barrier((grad_input, added_rows))
-    final = (first[1 : GRID_ROWS + 1] + added_rows.astype(F32)).astype(BF16)
+    first = first.reshape(GRID_ROWS + 2, cols, width)[1 : GRID_ROWS + 1]
+    final = (first + added_rows.astype(F32)).astype(BF16)
     sent = [jnp.where(leads, rows[BAND:], rows[:BAND]) for rows in (final, grad_input)]
     swapped = swap_pair(jnp.stack(sent))
     leader_share = BAND * row_bands[device - parity]

time: 129 us -> 110 us (0.85)
  local copies, waits for them, and re-layouts: 39.4 us -> 2.34 us
  Pallas kernels: 40.9 us -> 56.4 us
  waiting for transfers between devices: 10 us -> 17.7 us
  starting transfers between devices: 32.9 us -> 29.5 us
    unnamed x72 -> x20, local copies, waits for them, and re-layouts: 38.8 us -> 0.69 us
    pallas_call x7, Pallas kernels: 39.4 us -> 55 us  [the longest x1 13.7 us: forward(): pl.pallas_call(forward_body, in_specs=[in_scalars(), in_hbm(), in_vmem(),...]
    all_to_all x4, waiting for transfers between devices: 9.19 us -> 16.6 us  [exchange_windows(): lax.all_to_all(rows, 'row', split_axis=0, concat_axis=0, tiled=True, axis...]
    all_to_all x4, starting transfers between devices: 29.8 us -> 27.4 us  [exchange_windows(): lax.all_to_all(rows, 'row', split_axis=0, concat_axis=0, tiled=True, axis...]
  transfers between devices with their start and end apart: 10 -> 10, of which waited for: 4 -> 6; matrix products, arithmetic and copies ran while one was open for 0% -> 1% of each run, Pallas kernels for 23% -> 40%
where the time goes in v8:
time: 110 us
  Pallas kernels  56.4 us (51%)
  starting transfers between devices  29.5 us (27%)
  waiting for transfers between devices  17.7 us (16%)
  local copies, waits for them, and re-layouts  2.34 us (2%)
  other arithmetic  2.33 us (2%)
  between operations  1.5 us (1%)
    all_to_all x4, starting transfers between devices, exchange_windows(): lax.all_to_all(rows, 'row', split_axis=0, concat_axis=0, tiled=True, axis...  27.4 us
    all_to_all x4, waiting for transfers between devices, exchange_windows(): lax.all_to_all(rows, 'row', split_axis=0, concat_axis=0, tiled=True, axis...  16.6 us
    pallas_call x1, Pallas kernels, forward(): pl.pallas_call(forward_body, in_specs=[in_scalars(), in_hbm(), in_vmem(),...  13.7 us
    pallas_call x1, Pallas kernels, backward(): pl.pallas_call(backward_body, in_specs=[in_scalars()] + [in_hbm()] * 7 +...  13.2 us
    pallas_call x1, Pallas kernels, attention(): pl.pallas_call(attention_body, in_specs=[in_vmem(), in_hbm(), in_hbm()],...  12.7 us
    pallas_call x1, Pallas kernels, slopes(): pl.pallas_call(slopes_body, grid=(hidden_width // CHUNK,), in_specs=block...  7.71 us
    pallas_call x1, Pallas kernels, attend(): pl.pallas_call(attended_body, grid=(1,), in_specs=[whole(weights.shape),...  3.8 us
    pallas_call x1, Pallas kernels, attended_gradient(): pl.pallas_call(grad_attended_body, grid=(1,), in_specs=[whole(cotangent.s...  2.52 us
  transfers between devices with their start and end apart: 10, of which 6 were waited for; matrix products, arithmetic and copies ran while one was open for 1% of the time, Pallas kernels for 40%

profile of v8, /device:TPU:0, one launch (start us, length us, event | category | flops | bytes accessed | tf_op | source)
XLA Modules:
  0.0 109.8 jit_solution(18054210337381710397)
XLA Ops:
  1.3 0.7 copy-done.4
  1.9 1.4 %rim_rows.1 = bf16[3,32,512]{2,1,0:T(8,128)(2,1)S(1)} custom-call(s32[16]{0:T(128)S(1)} %copy-done.4, bf16[24,32,512]{2,1,0:T(8,128)(2,1)} %features_ref.3, bf16[24,32,512]{2,1,0:T(8,128)(2,1)} %cotangent_ref.3), custom_call_target="tpu_custom_call" | custom-call | tf_op jit(solution)/shard_map/rim_rows/pallas_call | solution.py:155
  3.3 0.7 collective-permute-start.1
  4.0 1.4 %even_rows.1.grad_slab_ref = bf16[16,32,512]{2,1,0:T(8,128)(2,1)} custom-call(s32[16]{0:T(128)S(1)} %copy-done.4, bf16[24,32,512]{2,1,0:T(8,128)(2,1)S(1)} %copy-done, bf16[24,32,512]{2,1,0:T(8,128)(2,1)S(1)} %collective-permute-done.2.other_ref), custom_call_target="tpu_custom_call" | custom-call | tf_op jit(solution)/shard_map/even_rows/pallas_call | solution.py:126
  5.5 11.1 %all-to-all-start = ((bf16[16,32,512]{2,1,0:T(8,128)(2,1)}), bf16[16,32,512]{2,1,0:T(8,128)(2,1)S(1)}, u32[]{:S(2)}, u32[]{:S(2)}) async-start(bf16[16,32,512]{2,1,0:T(8,128)(2,1)} %even_rows.1.grad_slab_ref), calls=%async_computation | async-start | bytes 1048576 | tf_op jit(solution)/shard_map/all_to_all | solution.py:684
  16.6 13.7 %bottleneck_forward.1 = (f32[576,512]{1,0:T(8,128)}, bf16[16,32,512]{2,1,0:T(8,128)(2,1)}, bf16[16,32,512]{2,1,0:T(8,128)(2,1)}, f32[16,32,2048]{2,1,0:T(8,128)}, f32[18,32,2048]{2,1,0:T(8,128)}) custom-call(s32[16]{0:T(128)S(1)} %copy-done.5, bf16[24,32,512]{2,1,0:T(8,128)(2,1)} %features_ref.3, bf16[24,32,512]{2,1,0:T(8,128)(2,1)S(1)} %collective-permute-done.other_ref, ...), custom_call_target="tpu_custom_call" | custom-call | flops 2684354560 | bytes 12582912 | tf_op jit(solution)/shard_map/bottleneck_forward/pallas_call | solution.py:276
  30.3 1.0 all-to-all-done
  31.4 5.0 %all-to-all-start.1 = ((bf16[16,32,512]{2,1,0:T(8,128)(2,1)}), bf16[16,32,512]{2,1,0:T(8,128)(2,1)S(1)}, u32[]{:S(2)}, u32[]{:S(2)}) async-start(bf16[16,32,512]{2,1,0:T(8,128)(2,1)} %get-tuple-element.32), calls=%async_computation.1 | async-start | bytes 1048576 | tf_op jit(solution)/shard_map/all_to_all | solution.py:684
  36.3 7.7 %gelu_slopes.1 = (bf16[16,32,2048]{2,1,0:T(8,128)(2,1)}, bf16[18,32,2048]{2,1,0:T(8,128)(2,1)}) custom-call(f32[16,32,2048]{2,1,0:T(8,128)} %get-tuple-element.33.expanded_ref, f32[18,32,2048]{2,1,0:T(8,128)} %get-tuple-element.34.mixed_ref), custom_call_target="tpu_custom_call" | custom-call | flops 33423360 | bytes 13369344 | tf_op jit(solution)/shard_map/gelu_slopes/pallas_call | solution.py:327
  44.0 2.5 %attended_gradient.1.grad_attended_ref = bf16[512,512]{1,0:T(8,128)(2,1)} custom-call(bf16[8,2,32,512]{3,2,1,0:T(8,128)(2,1)} %bitcast.25, bf16[512,512]{1,0:T(8,128)(2,1)} %out_ref.3), custom_call_target="tpu_custom_call" | custom-call | flops 268435456 | bytes 2097152 | tf_op jit(solution)/shard_map/attended_gradient/pallas_call | solution.py:390
  46.6 4.0 %all-to-all-done.1 = bf16[16,32,512]{2,1,0:T(8,128)(2,1)S(1)} async-done(((bf16[16,32,512]{2,1,0:T(8,128)(2,1)}), bf16[16,32,512]{2,1,0:T(8,128)(2,1)S(1)}, u32[]{:S(2)}, u32[]{:S(2)}) %all-to-all-start.1) | async-done | bytes 524320 | tf_op jit(solution)/shard_map/all_to_all | solution.py:684
  50.5 12.7 %window_attention.1 = (bf16[8,2,32,512]{3,2,1,0:T(8,128)(2,1)}, bf16[8,64,1024]{2,1,0:T(8,128)(2,1)}, bf16[512,512]{1,0:T(8,128)(2,1)}) custom-call(bf16[8,2,32,512]{3,2,1,0:T(8,128)(2,1)S(1)} %bitcast.22, bf16[512,512]{1,0:T(8,128)(2,1)} %attended_gradient.1.grad_attended_ref, bf16[512,1536]{1,0:T(8,128)(2,1)} %qkv_ref.1), custom_call_target="tpu_custom_call" | custom-call | flops 2147483648 | bytes 4194304 | tf_op jit(solution)/shard_map/window_attention/pallas_call | solution.py:479
  63.2 3.6 %all-to-all-start.2 = ((bf16[16,32,512]{2,1,0:T(8,128)(2,1)}), bf16[16,32,512]{2,1,0:T(8,128)(2,1)S(1)}, u32[]{:S(2)}, u32[]{:S(2)}) async-start(bf16[16,32,512]{2,1,0:T(8,128)(2,1)} %bitcast.26), calls=%async_computation.2 | async-start | bytes 1048576 | tf_op jit(solution)/shard_map/all_to_all | solution.py:684
  66.9 3.8 %attended_output.1 = bf16[8,2,32,512]{3,2,1,0:T(8,128)(2,1)} custom-call(bf16[8,64,1024]{2,1,0:T(8,128)(2,1)} %get-tuple-element.41.weights_ref, bf16[512,512]{1,0:T(8,128)(2,1)} %get-tuple-element.42.values_ref, bf16[512,512]{1,0:T(8,128)(2,1)} %out_ref.3), custom_call_target="tpu_custom_call" | custom-call | flops 536870912 | bytes 3145728 | tf_op jit(solution)/shard_map/attended_output/pallas_call | solution.py:519
  70.7 10.6 %all-to-all-done.2.grad_ref = bf16[16,32,512]{2,1,0:T(8,128)(2,1)S(1)} async-done(((bf16[16,32,512]{2,1,0:T(8,128)(2,1)}), bf16[16,32,512]{2,1,0:T(8,128)(2,1)S(1)}, u32[]{:S(2)}, u32[]{:S(2)}) %all-to-all-start.2) | async-done | bytes 524320 | tf_op jit(solution)/shard_map/all_to_all | solution.py:684
  81.4 0.7 collective-permute-start.4
  82.6 7.7 %all-to-all-start.3 = ((bf16[16,32,512]{2,1,0:T(8,128)(2,1)}), bf16[16,32,512]{2,1,0:T(8,128)(2,1)S(1)}, u32[]{:S(2)}, u32[]{:S(2)}) async-start(bf16[16,32,512]{2,1,0:T(8,128)(2,1)} %bitcast.24), calls=%async_computation.3 | async-start | bytes 1048576 | tf_op jit(solution)/shard_map/all_to_all | solution.py:684
  90.3 1.1 slice.34
  91.4 13.2 %bottleneck_backward.1 = bf16[16,32,512]{2,1,0:T(8,128)(2,1)S(1)} custom-call(s32[16]{0:T(128)S(1)} %copy-done.5, bf16[24,32,512]{2,1,0:T(8,128)(2,1)} %cotangent_ref.3, bf16[24,32,512]{2,1,0:T(8,128)(2,1)} %copy-done.1, bf16[3,32,512]{2,1,0:T(8,128)(2,1)} %copy-done.2, bf16[16,32,512]{2,1,0:T(8,128)(2,1)} %get-tuple-element.29.slab_ref, ...), custom_call_target="tpu_custom_call" | custom-call | flops 2415919104 | bytes 12582912 | tf_op jit(solution)/shard_map/bottleneck_backward/pallas_call | solution.py:641
  104.6 0.9 all-to-all-done.3
  105.9 0.6 dynamic_slice.3
  107.1 0.6 collective-permute-done.5
  107.9 1.0 pad_maximum_fusion.1
  108.8 1.0 pad_maximum_fusion
  (33 shorter events, 1.7 us)
Async XLA Ops:
  0.6 3.4 %copy-start = (bf16[24,32,512]{2,1,0:T(8,128)(2,1)S(1)}, bf16[24,32,512]{2,1,0:T(8,128)(2,1)}, u32[]{:S(2)}) copy-start(bf16[24,32,512]{2,1,0:T(8,128)(2,1)} %cotangent_ref.3) | copy-start | bytes 2359300
  0.6 15.9 %copy-start.3 = (bf16[9,2048]{1,0:T(8,128)(2,1)S(1)}, bf16[9,2048]{1,0:T(8,128)(2,1)}, u32[]{:S(2)}) copy-start(bf16[9,2048]{1,0:T(8,128)(2,1)} %taps_ref.3) | copy-start | bytes 110596
  0.7 3.4 %collective-permute-start.2 = (bf16[24,32,512]{2,1,0:T(8,128)(2,1)}, bf16[24,32,512]{2,1,0:T(8,128)(2,1)S(1)}, u32[]{:S(2)}, u32[]{:S(2)}) collective-permute-start(bf16[24,32,512]{2,1,0:T(8,128)(2,1)} %cotangent_ref.3), channel_id=1, source_target_pairs={{0,1},{1,0},{2,3},{3,2},{4,5},{5,4},{6,7},{7,6},{8,9},{9,8},{10,11... | collective-permute-start | bytes 2359304 | tf_op jit(solution)/shard_map/ppermute | solution.py:691
  1.2 15.4 %collective-permute-start = (bf16[24,32,512]{2,1,0:T(8,128)(2,1)}, bf16[24,32,512]{2,1,0:T(8,128)(2,1)S(1)}, u32[]{:S(2)}, u32[]{:S(2)}) collective-permute-start(bf16[24,32,512]{2,1,0:T(8,128)(2,1)} %features_ref.3), channel_id=1, source_target_pairs={{0,1},{1,0},{2,3},{3,2},{4,5},{5,4},{6,7},{7,6},{8,9},{9,8},{10,11... | collective-permute-start | bytes 2359304 | tf_op jit(solution)/shard_map/ppermute | solution.py:691
  1.2 0.7 copy-start.4
  1.9 14.7 %copy-start.5 = (s32[16]{0:T(128)S(1)}, s32[16]{0:T(128)}, u32[]{:S(2)}) copy-start(s32[16]{0:T(128)} %bands_ref.7) | copy-start | bytes 196
  3.3 2.1 %collective-permute-start.1 = (bf16[3,32,512]{2,1,0:T(8,128)(2,1)S(1)}, bf16[3,32,512]{2,1,0:T(8,128)(2,1)S(1)}, u32[]{:S(2)}, u32[]{:S(2)}) collective-permute-start(bf16[3,32,512]{2,1,0:T(8,128)(2,1)S(1)} %rim_rows.1), channel_id=1, source_target_pairs={{1,2},{3,4},{5,6},{7,8},{9,10},{11,12},{13,14},{2,1},{4,3},{6,5},{... | collective-permute-start | bytes 294920 | tf_op jit(solution)/shard_map/ppermute | solution.py:697
  4.0 26.3 %copy-start.1 = (bf16[24,32,512]{2,1,0:T(8,128)(2,1)}, bf16[24,32,512]{2,1,0:T(8,128)(2,1)S(1)}, u32[]{:S(2)}) copy-start(bf16[24,32,512]{2,1,0:T(8,128)(2,1)S(1)} %collective-permute-done.2.other_ref) | copy-start | bytes 2359300
  5.5 24.9 %copy-start.2 = (bf16[3,32,512]{2,1,0:T(8,128)(2,1)}, bf16[3,32,512]{2,1,0:T(8,128)(2,1)S(1)}, u32[]{:S(2)}) copy-start(bf16[3,32,512]{2,1,0:T(8,128)(2,1)S(1)} %collective-permute-done.1.rim_ref) | copy-start | bytes 294916
  5.5 25.9 %all-to-all-start = ((bf16[16,32,512]{2,1,0:T(8,128)(2,1)}), bf16[16,32,512]{2,1,0:T(8,128)(2,1)S(1)}, u32[]{:S(2)}, u32[]{:S(2)}) async-start(bf16[16,32,512]{2,1,0:T(8,128)(2,1)} %even_rows.1.grad_slab_ref), calls=%async_computation | async-start | bytes 1048576 | tf_op jit(solution)/shard_map/all_to_all | solution.py:684
  31.4 12.7 %copy-start.9 = (bf16[16,32,512]{2,1,0:T(8,128)(2,1)}, bf16[16,32,512]{2,1,0:T(8,128)(2,1)S(1)}, u32[]{:S(2)}) copy-start(bf16[16,32,512]{2,1,0:T(8,128)(2,1)S(1)} %all-to-all-done) | copy-start | bytes 1572868
  31.4 19.2 %all-to-all-start.1 = ((bf16[16,32,512]{2,1,0:T(8,128)(2,1)}), bf16[16,32,512]{2,1,0:T(8,128)(2,1)S(1)}, u32[]{:S(2)}, u32[]{:S(2)}) async-start(bf16[16,32,512]{2,1,0:T(8,128)(2,1)} %get-tuple-element.32), calls=%async_computation.1 | async-start | bytes 1048576 | tf_op jit(solution)/shard_map/all_to_all | solution.py:684
  63.2 18.1 %all-to-all-start.2 = ((bf16[16,32,512]{2,1,0:T(8,128)(2,1)}), bf16[16,32,512]{2,1,0:T(8,128)(2,1)S(1)}, u32[]{:S(2)}, u32[]{:S(2)}) async-start(bf16[16,32,512]{2,1,0:T(8,128)(2,1)} %bitcast.26), calls=%async_computation.2 | async-start | bytes 1048576 | tf_op jit(solution)/shard_map/all_to_all | solution.py:684
  66.9 23.4 %copy-start.6 = (f32[576,512]{1,0:T(8,128)S(1)}, f32[576,512]{1,0:T(8,128)}, u32[]{:S(2)}) copy-start(f32[576,512]{1,0:T(8,128)} %get-tuple-element.28.first_ref) | copy-start | bytes 3538948
  81.3 10.0 %copy-start.8 = (bf16[16,32,512]{2,1,0:T(8,128)(2,1)}, bf16[16,32,512]{2,1,0:T(8,128)(2,1)S(1)}, u32[]{:S(2)}) copy-start(bf16[16,32,512]{2,1,0:T(8,128)(2,1)S(1)} %all-to-all-done.2.grad_ref) | copy-start | bytes 1572868
  81.3 1.3 %collective-permute-start.3 = (bf16[1,32,512]{2,1,0:T(8,128)(2,1)S(1)}, bf16[1,32,512]{2,1,0:T(8,128)(2,1)S(1)}, u32[]{:S(2)}, u32[]{:S(2)}) collective-permute-start(bf16[1,32,512]{2,1,0:T(8,128)(2,1)S(1)} %get-tuple-element.61), channel_id=1, source_target_pairs={{0,1},{1,0},{2,3},{3,2},{4,5},{5,4},{6,7},{7,6},{8,9},{9,8},{10,11... | collective-permute-start | bytes 98312 | tf_op jit(solution)/shard_map/ppermute | solution.py:691
  81.4 1.2 %collective-permute-start.4 = (bf16[1,32,512]{2,1,0:T(8,128)(2,1)S(1)}, bf16[1,32,512]{2,1,0:T(8,128)(2,1)S(1)}, u32[]{:S(2)}, u32[]{:S(2)}) collective-permute-start(bf16[1,32,512]{2,1,0:T(8,128)(2,1)S(1)} %get-tuple-element.60), channel_id=1, source_target_pairs={{1,2},{3,4},{5,6},{7,8},{9,10},{11,12},{13,14},{2,1},{4,3},{6,5},{... | collective-permute-start | bytes 98312 | tf_op jit(solution)/shard_map/ppermute | solution.py:697
  82.6 22.9 %all-to-all-start.3 = ((bf16[16,32,512]{2,1,0:T(8,128)(2,1)}), bf16[16,32,512]{2,1,0:T(8,128)(2,1)S(1)}, u32[]{:S(2)}, u32[]{:S(2)}) async-start(bf16[16,32,512]{2,1,0:T(8,128)(2,1)} %bitcast.24), calls=%async_computation.3 | async-start | bytes 1048576 | tf_op jit(solution)/shard_map/all_to_all | solution.py:684
  91.3 14.1 %copy-start.7 = (f32[512,512]{1,0:T(8,128)S(1)}, f32[512,512]{1,0:T(8,128)}, u32[]{:S(2)}) copy-start(f32[512,512]{1,0:T(8,128)} %slice.34) | copy-start | bytes 3145732
  105.8 2.0 %collective-permute-start.5 = (bf16[2,8,32,512]{3,2,1,0:T(8,128)(2,1)S(1)}, bf16[2,8,32,512]{3,2,1,0:T(8,128)(2,1)S(1)}, u32[]{:S(2)}, u32[]{:S(2)}) collective-permute-start(bf16[2,8,32,512]{3,2,1,0:T(8,128)(2,1)S(1)} %pad_maximum_fusion.2), channel_id=1, source_target_pairs={{0,1},{1,0},{2,3},{3,2},{4,5},{5,4},{6,7},{7,6},{8,9},{9,8},{10,11... | collective-permute-start | bytes 1572872 | tf_op jit(solution)/shard_map/ppermute | solution.py:691

commit v9 on v8

--- a/solution.py
+++ b/solution.py
@@ -13,6 +13,7 @@
 RIM = 2
 EPSILON = 1e-06
 CHUNK = 512
+HALF = 256
 LANES = 128
 ROOT = math.sqrt(2.0 / math.pi)
 CUBIC = 0.044715
@@ -179,8 +180,9 @@
 
 
 def forward_body(bands_ref, features_ref, other_ref, rim_ref, expand_ref, taps_ref, project_ref, first_ref,
-                 normed_ref, slab_ref, expanded_ref, mixed_ref, slab, normed_one, expand, project, expanded,
-                 hidden, mixed, hidden_two, total, normed, row_sems, weight_sems, chunk_sems, out_sems):
+                 own_first_ref, normed_ref, slab_ref, expanded_ref, mixed_ref, slab, normed_one, expand, project,
+                 expanded, hidden, mixed, product_a, product_b, hidden_a, hidden_b, total, normed, row_sems,
+                 weight_sems, chunk_sems, out_sems):
     rows, cols, width = slab.shape
     own = rows - 2 * RIM
     chunks = expand_ref.shape[1] // CHUNK
@@ -208,9 +210,8 @@
         lanes = chunk_lanes(index)
         return pltpu.make_async_copy(mixed.at[:, :, lanes], mixed_ref.at[:, :, lanes], chunk_sems.at[1, index])
 
-    for index in range(chunks):
-        fetch_expand(index).start()
-        fetch_project(index).start()
+    fetch_expand(0).start()
+    fetch_project(0).start()
     for index, (first, count) in enumerate(pieces):
         wait_pull(sources, count, slab.at[pl.ds(first, count)], row_sems.at[index])
     store_slab = pltpu.make_async_copy(slab.at[pl.ds(RIM, own)], slab_ref, out_sems.at[0])
@@ -223,33 +224,48 @@
     column = lax.broadcasted_iota(jnp.int32, (cols, LANES), 0)
 
     def step(index, carry):
+        @pl.when(index + 1 < chunks)
+        def _():
+            fetch_expand(index + 1).start()
+            fetch_project(index + 1).start()
+
+        def expand_half(half, product):
+            weights = expand[:, chunk_lanes(index, half * HALF, HALF)]
+            product[...] = nn_dot(normed_one[...], weights).reshape(rows, cols, HALF)
+
+        def project_half(half, hidden_two):
+            total[...] += nn_dot(hidden_two[...], project[chunk_lanes(index, half * HALF, HALF), :])
+
+        def mix_half(half, product, hidden_two):
+            for lane in range(0, HALF, LANES):
+                lanes = slice(lane, lane + LANES)
+                at = chunk_lanes(index, half * HALF + lane, LANES)
+                for row in range(rows):
+                    values = product[row, :, lanes]
+                    hidden[row, :, lanes] = gelu(values).astype(BF16).astype(F32)
+                    if RIM <= row < RIM + own:
+                        expanded[row - RIM, :, at] = values
+                taps = spread_taps(taps_ref, at, cols)
+                for row in range(rows - 2):
+                    rows_near = [hidden[row + a, :, lanes] for a in range(3)]
+                    sums = [
+                        taps[b] * rows_near[0] + taps[3 + b] * rows_near[1] + taps[6 + b] * rows_near[2]
+                        for b in range(3)
+                    ]
+                    values = column_sums(sums[0], sums[1], sums[2], column, cols - 1)
+                    hidden_two[row * cols : (row + 1) * cols, lanes] = gelu(values).astype(BF16)
+                    mixed[row, :, at] = values
+
         fetch_expand(index).wait()
-        weights = expand[:, chunk_lanes(index)]
-        for row in range(0, rows, 4):
-            product = nn_dot(normed_one[row * cols : (row + 4) * cols, :], weights)
-            for inner in range(4):
-                for lane in range(0, CHUNK, LANES):
-                    lanes = slice(lane, lane + LANES)
-                    values = product[inner * cols : (inner + 1) * cols, lanes]
-                    hidden[row + inner, :, lanes] = gelu(values).astype(BF16).astype(F32)
-                    if RIM <= row + inner < RIM + own:
-                        expanded[row + inner - RIM, :, chunk_lanes(index, lane, LANES)] = values
+        expand_half(0, product_a)
+        expand_half(1, product_b)
+        mix_half(0, product_a, hidden_a)
+        fetch_project(index).wait()
+        project_half(0, hidden_a)
+        mix_half(1, product_b, hidden_b)
+        project_half(1, hidden_b)
         store_expanded(index).start()
-
-        for lane in range(0, CHUNK, LANES):
-            lanes = slice(lane, lane + LANES)
-            taps = spread_taps(taps_ref, chunk_lanes(index, lane, LANES), cols)
-            for row in range(rows - 2):
-                rows_near = [hidden[row + a, :, lanes] for a in range(3)]
-                sums = [
-                    taps[b] * rows_near[0] + taps[3 + b] * rows_near[1] + taps[6 + b] * rows_near[2] for b in range(3)
-                ]
-                values = column_sums(sums[0], sums[1], sums[2], column, cols - 1)
-                hidden_two[row * cols : (row + 1) * cols, lanes] = gelu(values).astype(BF16)
-                mixed[row, :, chunk_lanes(index, lane, LANES)] = values
         store_mixed(index).start()
-        fetch_project(index).wait()
-        total[...] += nn_dot(hidden_two[...], project[chunk_lanes(index), :])
         return carry
 
     lax.fori_loop(0, chunks, step, 0)
@@ -258,14 +274,17 @@
         normed[row - 1] = (first * rms_scale(first)).astype(BF16)
     store_normed = pltpu.make_async_copy(normed, normed_ref, out_sems.at[1])
     store_first = pltpu.make_async_copy(total, first_ref, out_sems.at[2])
+    store_own = pltpu.make_async_copy(total.at[pl.ds(cols, own * cols)], own_first_ref, out_sems.at[3])
     store_normed.start()
     store_first.start()
+    store_own.start()
     for index in range(chunks):
         store_expanded(index).wait()
         store_mixed(index).wait()
     store_slab.wait()
     store_normed.wait()
     store_first.wait()
+    store_own.wait()
 
 
 def forward(bands, features, other, rim, w_expand, kernel, w_project):
@@ -276,9 +295,10 @@
     return pl.pallas_call(
         forward_body,
         in_specs=[in_scalars(), in_hbm(), in_vmem(), in_vmem(), in_hbm(), in_vmem(), in_hbm()],
-        out_specs=[in_hbm()] * 5,
+        out_specs=[in_hbm()] * 6,
         out_shape=[
             pltpu.HBM(((rows - 2) * cols, width), F32),
+            pltpu.HBM((own * cols, width), F32),
             pltpu.HBM((own, cols, width), BF16),
             pltpu.HBM((own, cols, width), BF16),
             pltpu.HBM((own, cols, hidden_width), F32),
@@ -290,17 +310,20 @@
             pltpu.VMEM((width, hidden_width), BF16),
             pltpu.VMEM((hidden_width, width), BF16),
             pltpu.VMEM((own, cols, hidden_width), F32),
-            pltpu.VMEM((rows, cols, CHUNK), F32),
+            pltpu.VMEM((rows, cols, HALF), F32),
             pltpu.VMEM((rows - 2, cols, hidden_width), F32),
-            pltpu.VMEM(((rows - 2) * cols, CHUNK), BF16),
+            pltpu.VMEM((rows, cols, HALF), F32),
+            pltpu.VMEM((rows, cols, HALF), F32),
+            pltpu.VMEM(((rows - 2) * cols, HALF), BF16),
+            pltpu.VMEM(((rows - 2) * cols, HALF), BF16),
             pltpu.VMEM(((rows - 2) * cols, width), F32),
             pltpu.VMEM((own, cols, width), BF16),
             pltpu.SemaphoreType.DMA((4,)),
             pltpu.SemaphoreType.DMA((2, chunks)),
             pltpu.SemaphoreType.DMA((2, chunks)),
-            pltpu.SemaphoreType.DMA((3,)),
+            pltpu.SemaphoreType.DMA((4,)),
         ],
-        compiler_params=params(26),
+        compiler_params=params(28),
         cost_estimate=pl.CostEstimate(
             flops=4 * rows * cols * width * hidden_width,
             bytes_accessed=12 * 1024 * 1024,
@@ -534,7 +557,8 @@
 def backward_body(bands_ref, cotangent_ref, other_ref, rim_ref, slab_ref, first_ref, grad_slab_ref, grad_ref,
                   pair_ref, next_ref, slope_one_ref, slope_two_ref, expand_ref, taps_ref, project_ref,
                   out_ref, rims, slab, first, grad_slab, grad_in, slope_one, slope_two, expand, project,
-                  grad_first, grad_rows, mixed, expanded, total, row_sems, in_sems, chunk_sems):
+                  grad_first, grad_rows, mixed, product_a, product_b, expanded_a, expanded_b, total, row_sems,
+                  in_sems, chunk_sems):
     own, cols, width = slab.shape
     chunks = expand_ref.shape[1] // CHUNK
 
@@ -564,9 +588,8 @@
             for number, (source, target) in enumerate(pairs)
         ]
 
-    for index in range(chunks):
-        for copy in fetches(index):
-            copy.start()
+    for copy in fetches(0):
+        copy.start()
 
     def through_norm(cotangent, grad, first):
         rms = rms_scale(first)
@@ -595,30 +618,44 @@
     total[...] = jnp.zeros_like(total)
 
     def step(index, carry):
+        @pl.when(index + 1 < chunks)
+        def _():
+            for copy in fetches(index + 1):
+                copy.start()
+
+        def project_half(half, product):
+            weights = project[chunk_lanes(index, half * HALF, HALF), :]
+            product[...] = nt_dot(grad_rows[...], weights).reshape(own + 2, cols, HALF)
+
+        def expand_half(half, expanded):
+            total[...] += nt_dot(expanded[...], expand[:, chunk_lanes(index, half * HALF, HALF)])
+
+        def unmix_half(half, product, expanded):
+            for lane in range(0, HALF, LANES):
+                lanes = slice(lane, lane + LANES)
+                at = chunk_lanes(index, half * HALF + lane, LANES)
+                for row in range(own + 2):
+                    value = product[row, :, lanes] * slope_two[row, :, at].astype(F32)
+                    mixed[row, :, lanes] = value.astype(BF16).astype(F32)
+                taps = spread_taps(taps_ref, at, cols)
+                for row in range(own):
+                    rows_near = [mixed[row + a, :, lanes] for a in range(3)]
+                    sums = [
+                        taps[8 - b] * rows_near[0] + taps[5 - b] * rows_near[1] + taps[2 - b] * rows_near[2]
+                        for b in range(3)
+                    ]
+                    value = column_sums(sums[0], sums[1], sums[2], column, cols - 1)
+                    value = value * slope_one[row, :, at].astype(F32)
+                    expanded[row * cols : (row + 1) * cols, lanes] = value.astype(BF16)
+
         for copy in fetches(index):
             copy.wait()
-        weights = project[chunk_lanes(index), :]
-        for row in range(0, own + 2, 6):
-            grad = nt_dot(grad_rows[row * cols : (row + 6) * cols, :], weights)
-            for inner in range(6):
-                for lane in range(0, CHUNK, LANES):
-                    lanes = slice(lane, lane + LANES)
-                    slope = slope_two[row + inner, :, chunk_lanes(index, lane, LANES)].astype(F32)
-                    value = grad[inner * cols : (inner + 1) * cols, lanes] * slope
-                    mixed[row + inner, :, lanes] = value.astype(BF16).astype(F32)
-
-        for lane in range(0, CHUNK, LANES):
-            lanes = slice(lane, lane + LANES)
-            taps = spread_taps(taps_ref, chunk_lanes(index, lane, LANES), cols)
-            for row in range(own):
-                rows_near = [mixed[row + a, :, lanes] for a in range(3)]
-                sums = [
-                    taps[8 - b] * rows_near[0] + taps[5 - b] * rows_near[1] + taps[2 - b] * rows_near[2] for b in range(3)
-                ]
-                value = column_sums(sums[0], sums[1], sums[2], column, cols - 1)
-                value = value * slope_one[row, :, chunk_lanes(index, lane, LANES)].astype(F32)
-                expanded[row * cols : (row + 1) * cols, lanes] = value.astype(BF16)
-        total[...] += nt_dot(expanded[...], expand[:, chunk_lanes(index)])
+        project_half(0, product_a)
+        project_half(1, product_b)
+        unmix_half(0, product_a, expanded_a)
+        expand_half(0, expanded_a)
+        unmix_half(1, product_b, expanded_b)
+        expand_half(1, expanded_b)
         return carry
 
     lax.fori_loop(0, chunks, step, 0)
@@ -655,8 +692,11 @@
             pltpu.VMEM((hidden_width, width), BF16),
             pltpu.VMEM((own * cols, width), F32),
             pltpu.VMEM(((own + 2) * cols, width), BF16),
-            pltpu.VMEM((own + 2, cols, CHUNK), F32),
-            pltpu.VMEM((own * cols, CHUNK), BF16),
+            pltpu.VMEM((own + 2, cols, HALF), F32),
+            pltpu.VMEM((own + 2, cols, HALF), F32),
+            pltpu.VMEM((own + 2, cols, HALF), F32),
+            pltpu.VMEM((own * cols, HALF), BF16),
+            pltpu.VMEM((own * cols, HALF), BF16),
             pltpu.VMEM((own * cols, width), F32),
             pltpu.SemaphoreType.DMA((2,)),
             pltpu.SemaphoreType.DMA((4,)),
@@ -721,7 +761,7 @@
     rim, grad_slab = lax.optimization_barrier((rim, grad_slab))
 
     grad_windows = exchange_windows(grad_slab)
-    first, normed, slab, expanded, mixed = forward(
+    first, own_first, normed, slab, expanded, mixed = forward(
         row_bands, features, other_features, rim, w_expand, kernel, w_project
     )
     normed, grad_windows = lax.optimization_barrier((normed, grad_windows))
@@ -746,8 +786,7 @@
         slope_one, slope_two, w_expand, kernel, w_project,
     )
     grad_input, added_rows = lax.optimization_barrier((grad_input, added_rows))
-    first = first.reshape(GRID_ROWS + 2, cols, width)[1 : GRID_ROWS + 1]
-    final = (first + added_rows.astype(F32)).astype(BF16)
+    final = (own_first.reshape(GRID_ROWS, cols, width) + added_rows.astype(F32)).astype(BF16)
     sent = [jnp.where(leads, rows[BAND:], rows[:BAND]) for rows in (final, grad_input)]
     swapped = swap_pair(jnp.stack(sent))
     leader_share = BAND * row_bands[device - parity]

time: 110 us -> 112 us (1.018)
  waiting for transfers between devices: 17.7 us -> 19.8 us
    all_to_all x4, waiting for transfers between devices: 16.6 us -> 18.6 us  [exchange_windows(): lax.all_to_all(rows, 'row', split_axis=0, concat_axis=0, tiled=True, axis...]
    pallas_call x1, Pallas kernels: 13.2 us -> 11.3 us  [backward(): pl.pallas_call(backward_body, in_specs=[in_scalars()] + [in_hbm()] * 7 +...]
    pallas_call x1, Pallas kernels: 13.7 us -> 14.8 us  [forward(): pl.pallas_call(forward_body, in_specs=[in_scalars(), in_hbm(), in_vmem(),...]
  transfers between devices with their start and end apart: 10 -> 10, of which waited for: 6 -> 5; matrix products, arithmetic and copies ran while one was open for 1% -> 1% of each run, Pallas kernels for 40% -> 39%
where the time goes in v9:
time: 112 us; the launch traced here: 111 us
  Pallas kernels  55.6 us (50%)
  starting transfers between devices  30.5 us (27%)
  waiting for transfers between devices  19.8 us (18%)
  other arithmetic  2.33 us (2%)
  between operations  1.51 us (1%)
  local copies, waits for them, and re-layouts  1.28 us (1%)
    all_to_all x4, starting transfers between devices, exchange_windows(): lax.all_to_all(rows, 'row', split_axis=0, concat_axis=0, tiled=True, axis...  28.4 us
    all_to_all x4, waiting for transfers between devices, exchange_windows(): lax.all_to_all(rows, 'row', split_axis=0, concat_axis=0, tiled=True, axis...  18.6 us
    pallas_call x1, Pallas kernels, forward(): pl.pallas_call(forward_body, in_specs=[in_scalars(), in_hbm(), in_vmem(),...  14.8 us
    pallas_call x1, Pallas kernels, attention(): pl.pallas_call(attention_body, in_specs=[in_vmem(), in_hbm(), in_hbm()],...  12.7 us
    pallas_call x1, Pallas kernels, backward(): pl.pallas_call(backward_body, in_specs=[in_scalars()] + [in_hbm()] * 7 +...  11.3 us
    pallas_call x1, Pallas kernels, slopes(): pl.pallas_call(slopes_body, grid=(hidden_width // CHUNK,), in_specs=block...  7.76 us
    pallas_call x1, Pallas kernels, attend(): pl.pallas_call(attended_body, grid=(1,), in_specs=[whole(weights.shape),...  3.69 us
    pallas_call x1, Pallas kernels, attended_gradient(): pl.pallas_call(grad_attended_body, grid=(1,), in_specs=[whole(cotangent.s...  2.51 us
  transfers between devices with their start and end apart: 10, of which 5 were waited for; matrix products, arithmetic and copies ran while one was open for 1% of the time, Pallas kernels for 39%

profile of v9, /device:TPU:0, one launch (start us, length us, event | category | flops | bytes accessed | tf_op | source)
XLA Modules:
  0.0 111.0 jit_solution(10858401027216474614)
XLA Ops:
  0.7 0.5 collective-permute-start.2
  1.3 0.7 copy-done.4
  1.9 1.4 %rim_rows.1 = bf16[3,32,512]{2,1,0:T(8,128)(2,1)S(1)} custom-call(s32[16]{0:T(128)S(1)} %copy-done.4, bf16[24,32,512]{2,1,0:T(8,128)(2,1)} %features_ref.3, bf16[24,32,512]{2,1,0:T(8,128)(2,1)} %cotangent_ref.3), custom_call_target="tpu_custom_call" | custom-call | tf_op jit(solution)/shard_map/rim_rows/pallas_call | solution.py:156
  3.3 0.7 collective-permute-start.1
  4.0 1.4 %even_rows.1.grad_slab_ref = bf16[16,32,512]{2,1,0:T(8,128)(2,1)} custom-call(s32[16]{0:T(128)S(1)} %copy-done.4, bf16[24,32,512]{2,1,0:T(8,128)(2,1)S(1)} %copy-done, bf16[24,32,512]{2,1,0:T(8,128)(2,1)S(1)} %collective-permute-done.2.other_ref), custom_call_target="tpu_custom_call" | custom-call | tf_op jit(solution)/shard_map/even_rows/pallas_call | solution.py:127
  5.5 11.1 %all-to-all-start = ((bf16[16,32,512]{2,1,0:T(8,128)(2,1)}), bf16[16,32,512]{2,1,0:T(8,128)(2,1)S(1)}, u32[]{:S(2)}, u32[]{:S(2)}) async-start(bf16[16,32,512]{2,1,0:T(8,128)(2,1)} %even_rows.1.grad_slab_ref), calls=%async_computation | async-start | bytes 1048576 | tf_op jit(solution)/shard_map/all_to_all | solution.py:724
  16.6 14.8 %bottleneck_forward.1 = (f32[576,512]{1,0:T(8,128)}, f32[512,512]{1,0:T(8,128)}, bf16[16,32,512]{2,1,0:T(8,128)(2,1)}, bf16[16,32,512]{2,1,0:T(8,128)(2,1)}, f32...) custom-call(s32[16]{0:T(128)S(1)} %copy-done.5, bf16[24,32,512]{2,1,0:T(8,128)(2,1)} %features_ref.3, ...), custom_call_target="tpu_custom_call" | custom-call | flops 2684354560 | bytes 12582912 | tf_op jit(solution)/shard_map/bottleneck_forward/pallas_call | solution.py:295
  31.5 6.0 %all-to-all-start.1 = ((bf16[16,32,512]{2,1,0:T(8,128)(2,1)}), bf16[16,32,512]{2,1,0:T(8,128)(2,1)S(1)}, u32[]{:S(2)}, u32[]{:S(2)}) async-start(bf16[16,32,512]{2,1,0:T(8,128)(2,1)} %get-tuple-element.34), calls=%async_computation.1 | async-start | bytes 1048576 | tf_op jit(solution)/shard_map/all_to_all | solution.py:724
  37.5 7.8 %gelu_slopes.1 = (bf16[16,32,2048]{2,1,0:T(8,128)(2,1)}, bf16[18,32,2048]{2,1,0:T(8,128)(2,1)}) custom-call(f32[16,32,2048]{2,1,0:T(8,128)} %get-tuple-element.35.expanded_ref, f32[18,32,2048]{2,1,0:T(8,128)} %get-tuple-element.36.mixed_ref), custom_call_target="tpu_custom_call" | custom-call | flops 33423360 | bytes 13369344 | tf_op jit(solution)/shard_map/gelu_slopes/pallas_call | solution.py:350
  45.2 2.5 %attended_gradient.1.grad_attended_ref = bf16[512,512]{1,0:T(8,128)(2,1)} custom-call(bf16[8,2,32,512]{3,2,1,0:T(8,128)(2,1)} %bitcast.24, bf16[512,512]{1,0:T(8,128)(2,1)} %out_ref.3), custom_call_target="tpu_custom_call" | custom-call | flops 268435456 | bytes 2097152 | tf_op jit(solution)/shard_map/attended_gradient/pallas_call | solution.py:413
  47.8 4.0 %all-to-all-done.1 = bf16[16,32,512]{2,1,0:T(8,128)(2,1)S(1)} async-done(((bf16[16,32,512]{2,1,0:T(8,128)(2,1)}), bf16[16,32,512]{2,1,0:T(8,128)(2,1)S(1)}, u32[]{:S(2)}, u32[]{:S(2)}) %all-to-all-start.1) | async-done | bytes 524320 | tf_op jit(solution)/shard_map/all_to_all | solution.py:724
  51.7 12.7 %window_attention.1 = (bf16[8,2,32,512]{3,2,1,0:T(8,128)(2,1)}, bf16[8,64,1024]{2,1,0:T(8,128)(2,1)}, bf16[512,512]{1,0:T(8,128)(2,1)}) custom-call(bf16[8,2,32,512]{3,2,1,0:T(8,128)(2,1)S(1)} %bitcast.22, bf16[512,512]{1,0:T(8,128)(2,1)} %attended_gradient.1.grad_attended_ref, bf16[512,1536]{1,0:T(8,128)(2,1)} %qkv_ref.1), custom_call_target="tpu_custom_call" | custom-call | flops 2147483648 | bytes 4194304 | tf_op jit(solution)/shard_map/window_attention/pallas_call | solution.py:502
  64.4 3.6 %all-to-all-start.2 = ((bf16[16,32,512]{2,1,0:T(8,128)(2,1)}), bf16[16,32,512]{2,1,0:T(8,128)(2,1)S(1)}, u32[]{:S(2)}, u32[]{:S(2)}) async-start(bf16[16,32,512]{2,1,0:T(8,128)(2,1)} %bitcast.26), calls=%async_computation.2 | async-start | bytes 1048576 | tf_op jit(solution)/shard_map/all_to_all | solution.py:724
  68.1 3.7 %attended_output.1 = bf16[8,2,32,512]{3,2,1,0:T(8,128)(2,1)} custom-call(bf16[8,64,1024]{2,1,0:T(8,128)(2,1)} %get-tuple-element.43.weights_ref, bf16[512,512]{1,0:T(8,128)(2,1)} %get-tuple-element.44.values_ref, bf16[512,512]{1,0:T(8,128)(2,1)} %out_ref.3), custom_call_target="tpu_custom_call" | custom-call | flops 536870912 | bytes 3145728 | tf_op jit(solution)/shard_map/attended_output/pallas_call | solution.py:542
  71.8 10.8 %all-to-all-done.2.grad_ref = bf16[16,32,512]{2,1,0:T(8,128)(2,1)S(1)} async-done(((bf16[16,32,512]{2,1,0:T(8,128)(2,1)}), bf16[16,32,512]{2,1,0:T(8,128)(2,1)S(1)}, u32[]{:S(2)}, u32[]{:S(2)}) %all-to-all-start.2) | async-done | bytes 524320 | tf_op jit(solution)/shard_map/all_to_all | solution.py:724
  82.6 0.7 collective-permute-start.4
  83.3 0.5 collective-permute-done.3.pair_ref
  83.8 7.7 %all-to-all-start.3 = ((bf16[16,32,512]{2,1,0:T(8,128)(2,1)}), bf16[16,32,512]{2,1,0:T(8,128)(2,1)S(1)}, u32[]{:S(2)}, u32[]{:S(2)}) async-start(bf16[16,32,512]{2,1,0:T(8,128)(2,1)} %bitcast.23), calls=%async_computation.3 | async-start | bytes 1048576 | tf_op jit(solution)/shard_map/all_to_all | solution.py:724
  91.5 11.3 %bottleneck_backward.1 = bf16[16,32,512]{2,1,0:T(8,128)(2,1)S(1)} custom-call(s32[16]{0:T(128)S(1)} %copy-done.5, bf16[24,32,512]{2,1,0:T(8,128)(2,1)} %cotangent_ref.3, bf16[24,32,512]{2,1,0:T(8,128)(2,1)} %copy-done.1, bf16[3,32,512]{2,1,0:T(8,128)(2,1)} %copy-done.2, bf16[16,32,512]{2,1,0:T(8,128)(2,1)} %get-tuple-element.30.slab_ref, ...), custom_call_target="tpu_custom_call" | custom-call | flops 2415919104 | bytes 12582912 | tf_op jit(solution)/shard_map/bottleneck_backward/pallas_call | solution.py:678
  102.9 3.8 %all-to-all-done.3 = bf16[16,32,512]{2,1,0:T(8,128)(2,1)S(1)} async-done(((bf16[16,32,512]{2,1,0:T(8,128)(2,1)}), bf16[16,32,512]{2,1,0:T(8,128)(2,1)S(1)}, u32[]{:S(2)}, u32[]{:S(2)}) %all-to-all-start.3) | async-done | bytes 524320 | tf_op jit(solution)/shard_map/all_to_all | solution.py:724
  107.1 0.6 dynamic_slice.3
  108.3 0.6 collective-permute-done.5
  109.1 1.0 pad_maximum_fusion.1
  110.1 1.0 pad_maximum_fusion
  (30 shorter events, 0.7 us)
Async XLA Ops:
  0.6 3.4 %copy-start = (bf16[24,32,512]{2,1,0:T(8,128)(2,1)S(1)}, bf16[24,32,512]{2,1,0:T(8,128)(2,1)}, u32[]{:S(2)}) copy-start(bf16[24,32,512]{2,1,0:T(8,128)(2,1)} %cotangent_ref.3) | copy-start | bytes 2359300
  0.6 15.9 %copy-start.3 = (bf16[9,2048]{1,0:T(8,128)(2,1)S(1)}, bf16[9,2048]{1,0:T(8,128)(2,1)}, u32[]{:S(2)}) copy-start(bf16[9,2048]{1,0:T(8,128)(2,1)} %taps_ref.3) | copy-start | bytes 110596
  0.7 3.4 %collective-permute-start.2 = (bf16[24,32,512]{2,1,0:T(8,128)(2,1)}, bf16[24,32,512]{2,1,0:T(8,128)(2,1)S(1)}, u32[]{:S(2)}, u32[]{:S(2)}) collective-permute-start(bf16[24,32,512]{2,1,0:T(8,128)(2,1)} %cotangent_ref.3), channel_id=1, source_target_pairs={{0,1},{1,0},{2,3},{3,2},{4,5},{5,4},{6,7},{7,6},{8,9},{9,8},{10,11... | collective-permute-start | bytes 2359304 | tf_op jit(solution)/shard_map/ppermute | solution.py:731
  1.2 15.4 %collective-permute-start = (bf16[24,32,512]{2,1,0:T(8,128)(2,1)}, bf16[24,32,512]{2,1,0:T(8,128)(2,1)S(1)}, u32[]{:S(2)}, u32[]{:S(2)}) collective-permute-start(bf16[24,32,512]{2,1,0:T(8,128)(2,1)} %features_ref.3), channel_id=1, source_target_pairs={{0,1},{1,0},{2,3},{3,2},{4,5},{5,4},{6,7},{7,6},{8,9},{9,8},{10,11... | collective-permute-start | bytes 2359304 | tf_op jit(solution)/shard_map/ppermute | solution.py:731
  1.2 0.7 copy-start.4
  1.9 14.7 %copy-start.5 = (s32[16]{0:T(128)S(1)}, s32[16]{0:T(128)}, u32[]{:S(2)}) copy-start(s32[16]{0:T(128)} %bands_ref.7) | copy-start | bytes 196
  3.3 2.1 %collective-permute-start.1 = (bf16[3,32,512]{2,1,0:T(8,128)(2,1)S(1)}, bf16[3,32,512]{2,1,0:T(8,128)(2,1)S(1)}, u32[]{:S(2)}, u32[]{:S(2)}) collective-permute-start(bf16[3,32,512]{2,1,0:T(8,128)(2,1)S(1)} %rim_rows.1), channel_id=1, source_target_pairs={{1,2},{3,4},{5,6},{7,8},{9,10},{11,12},{13,14},{2,1},{4,3},{6,5},{... | collective-permute-start | bytes 294920 | tf_op jit(solution)/shard_map/ppermute | solution.py:737
  4.0 27.4 %copy-start.1 = (bf16[24,32,512]{2,1,0:T(8,128)(2,1)}, bf16[24,32,512]{2,1,0:T(8,128)(2,1)S(1)}, u32[]{:S(2)}) copy-start(bf16[24,32,512]{2,1,0:T(8,128)(2,1)S(1)} %collective-permute-done.2.other_ref) | copy-start | bytes 2359300
  5.4 26.0 %copy-start.2 = (bf16[3,32,512]{2,1,0:T(8,128)(2,1)}, bf16[3,32,512]{2,1,0:T(8,128)(2,1)S(1)}, u32[]{:S(2)}) copy-start(bf16[3,32,512]{2,1,0:T(8,128)(2,1)S(1)} %collective-permute-done.1.rim_ref) | copy-start | bytes 294916
  5.5 26.0 %all-to-all-start = ((bf16[16,32,512]{2,1,0:T(8,128)(2,1)}), bf16[16,32,512]{2,1,0:T(8,128)(2,1)S(1)}, u32[]{:S(2)}, u32[]{:S(2)}) async-start(bf16[16,32,512]{2,1,0:T(8,128)(2,1)} %even_rows.1.grad_slab_ref), calls=%async_computation | async-start | bytes 1048576 | tf_op jit(solution)/shard_map/all_to_all | solution.py:724
  31.5 13.8 %copy-start.7 = (bf16[16,32,512]{2,1,0:T(8,128)(2,1)}, bf16[16,32,512]{2,1,0:T(8,128)(2,1)S(1)}, u32[]{:S(2)}) copy-start(bf16[16,32,512]{2,1,0:T(8,128)(2,1)S(1)} %all-to-all-done) | copy-start | bytes 1572868
  31.5 20.3 %all-to-all-start.1 = ((bf16[16,32,512]{2,1,0:T(8,128)(2,1)}), bf16[16,32,512]{2,1,0:T(8,128)(2,1)S(1)}, u32[]{:S(2)}, u32[]{:S(2)}) async-start(bf16[16,32,512]{2,1,0:T(8,128)(2,1)} %get-tuple-element.34), calls=%async_computation.1 | async-start | bytes 1048576 | tf_op jit(solution)/shard_map/all_to_all | solution.py:724
  64.4 18.1 %all-to-all-start.2 = ((bf16[16,32,512]{2,1,0:T(8,128)(2,1)}), bf16[16,32,512]{2,1,0:T(8,128)(2,1)S(1)}, u32[]{:S(2)}, u32[]{:S(2)}) async-start(bf16[16,32,512]{2,1,0:T(8,128)(2,1)} %bitcast.26), calls=%async_computation.2 | async-start | bytes 1048576 | tf_op jit(solution)/shard_map/all_to_all | solution.py:724
  82.5 9.0 %copy-start.6 = (bf16[16,32,512]{2,1,0:T(8,128)(2,1)}, bf16[16,32,512]{2,1,0:T(8,128)(2,1)S(1)}, u32[]{:S(2)}) copy-start(bf16[16,32,512]{2,1,0:T(8,128)(2,1)S(1)} %all-to-all-done.2.grad_ref) | copy-start | bytes 1572868
  82.6 1.3 %collective-permute-start.3 = (bf16[1,32,512]{2,1,0:T(8,128)(2,1)S(1)}, bf16[1,32,512]{2,1,0:T(8,128)(2,1)S(1)}, u32[]{:S(2)}, u32[]{:S(2)}) collective-permute-start(bf16[1,32,512]{2,1,0:T(8,128)(2,1)S(1)} %get-tuple-element.63), channel_id=1, source_target_pairs={{0,1},{1,0},{2,3},{3,2},{4,5},{5,4},{6,7},{7,6},{8,9},{9,8},{10,11... | collective-permute-start | bytes 98312 | tf_op jit(solution)/shard_map/ppermute | solution.py:731
  82.6 1.2 %collective-permute-start.4 = (bf16[1,32,512]{2,1,0:T(8,128)(2,1)S(1)}, bf16[1,32,512]{2,1,0:T(8,128)(2,1)S(1)}, u32[]{:S(2)}, u32[]{:S(2)}) collective-permute-start(bf16[1,32,512]{2,1,0:T(8,128)(2,1)S(1)} %get-tuple-element.62), channel_id=1, source_target_pairs={{1,2},{3,4},{5,6},{7,8},{9,10},{11,12},{13,14},{2,1},{4,3},{6,5},{... | collective-permute-start | bytes 98312 | tf_op jit(solution)/shard_map/ppermute | solution.py:737
  83.8 22.9 %all-to-all-start.3 = ((bf16[16,32,512]{2,1,0:T(8,128)(2,1)}), bf16[16,32,512]{2,1,0:T(8,128)(2,1)S(1)}, u32[]{:S(2)}, u32[]{:S(2)}) async-start(bf16[16,32,512]{2,1,0:T(8,128)(2,1)} %bitcast.23), calls=%async_computation.3 | async-start | bytes 1048576 | tf_op jit(solution)/shard_map/all_to_all | solution.py:724
  91.5 15.2 %copy-start.8 = (f32[512,512]{1,0:T(8,128)S(1)}, f32[512,512]{1,0:T(8,128)}, u32[]{:S(2)}) copy-start(f32[512,512]{1,0:T(8,128)} %get-tuple-element.29) | copy-start | bytes 3145732
  107.0 2.0 %collective-permute-start.5 = (bf16[2,8,32,512]{3,2,1,0:T(8,128)(2,1)S(1)}, bf16[2,8,32,512]{3,2,1,0:T(8,128)(2,1)S(1)}, u32[]{:S(2)}, u32[]{:S(2)}) collective-permute-start(bf16[2,8,32,512]{3,2,1,0:T(8,128)(2,1)S(1)} %pad_maximum_fusion.2), channel_id=1, source_target_pairs={{0,1},{1,0},{2,3},{3,2},{4,5},{5,4},{6,7},{7,6},{8,9},{9,8},{10,11... | collective-permute-start | bytes 1572872 | tf_op jit(solution)/shard_map/ppermute | solution.py:731

commit v10 on v9

--- a/solution.py
+++ b/solution.py
@@ -181,7 +181,7 @@
 
 def forward_body(bands_ref, features_ref, other_ref, rim_ref, expand_ref, taps_ref, project_ref, first_ref,
                  own_first_ref, normed_ref, slab_ref, expanded_ref, mixed_ref, slab, normed_one, expand, project,
-                 expanded, hidden, mixed, product_a, product_b, hidden_a, hidden_b, total, normed, row_sems,
+                 expanded, hidden, mixed, hidden_two, total, normed, row_sems,
                  weight_sems, chunk_sems, out_sems):
     rows, cols, width = slab.shape
     own = rows - 2 * RIM
@@ -229,43 +229,33 @@
             fetch_expand(index + 1).start()
             fetch_project(index + 1).start()
 
-        def expand_half(half, product):
-            weights = expand[:, chunk_lanes(index, half * HALF, HALF)]
-            product[...] = nn_dot(normed_one[...], weights).reshape(rows, cols, HALF)
-
-        def project_half(half, hidden_two):
-            total[...] += nn_dot(hidden_two[...], project[chunk_lanes(index, half * HALF, HALF), :])
-
-        def mix_half(half, product, hidden_two):
-            for lane in range(0, HALF, LANES):
-                lanes = slice(lane, lane + LANES)
-                at = chunk_lanes(index, half * HALF + lane, LANES)
-                for row in range(rows):
-                    values = product[row, :, lanes]
-                    hidden[row, :, lanes] = gelu(values).astype(BF16).astype(F32)
-                    if RIM <= row < RIM + own:
-                        expanded[row - RIM, :, at] = values
-                taps = spread_taps(taps_ref, at, cols)
-                for row in range(rows - 2):
-                    rows_near = [hidden[row + a, :, lanes] for a in range(3)]
-                    sums = [
-                        taps[b] * rows_near[0] + taps[3 + b] * rows_near[1] + taps[6 + b] * rows_near[2]
-                        for b in range(3)
-                    ]
-                    values = column_sums(sums[0], sums[1], sums[2], column, cols - 1)
-                    hidden_two[row * cols : (row + 1) * cols, lanes] = gelu(values).astype(BF16)
-                    mixed[row, :, at] = values
-
         fetch_expand(index).wait()
-        expand_half(0, product_a)
-        expand_half(1, product_b)
-        mix_half(0, product_a, hidden_a)
+        weights = expand[:, chunk_lanes(index)]
+        for row in range(0, rows, 4):
+            product = nn_dot(normed_one[row * cols : (row + 4) * cols, :], weights)
+            for inner in range(4):
+                for lane in range(0, CHUNK, LANES):
+                    lanes = slice(lane, lane + LANES)
+                    values = product[inner * cols : (inner + 1) * cols, lanes]
+                    hidden[row + inner, :, lanes] = gelu(values).astype(BF16).astype(F32)
+                    if RIM <= row + inner < RIM + own:
+                        expanded[row + inner - RIM, :, chunk_lanes(index, lane, LANES)] = values
+        store_expanded(index).start()
+
+        for lane in range(0, CHUNK, LANES):
+            lanes = slice(lane, lane + LANES)
+            taps = spread_taps(taps_ref, chunk_lanes(index, lane, LANES), cols)
+            for row in range(rows - 2):
+                rows_near = [hidden[row + a, :, lanes] for a in range(3)]
+                sums = [
+                    taps[b] * rows_near[0] + taps[3 + b] * rows_near[1] + taps[6 + b] * rows_near[2] for b in range(3)
+                ]
+                values = column_sums(sums[0], sums[1], sums[2], column, cols - 1)
+                hidden_two[row * cols : (row + 1) * cols, lanes] = gelu(values).astype(BF16)
+                mixed[row, :, chunk_lanes(index, lane, LANES)] = values
+        store_mixed(index).start()
         fetch_project(index).wait()
-        project_half(0, hidden_a)
-        mix_half(1, product_b, hidden_b)
-        project_half(1, hidden_b)
-        store_expanded(index).start()
-        store_mixed(index).start()
+        total[...] += nn_dot(hidden_two[...], project[chunk_lanes(index), :])
         return carry
 
     lax.fori_loop(0, chunks, step, 0)
@@ -310,12 +300,9 @@
             pltpu.VMEM((width, hidden_width), BF16),
             pltpu.VMEM((hidden_width, width), BF16),
             pltpu.VMEM((own, cols, hidden_width), F32),
-            pltpu.VMEM((rows, cols, HALF), F32),
+            pltpu.VMEM((rows, cols, CHUNK), F32),
             pltpu.VMEM((rows - 2, cols, hidden_width), F32),
-            pltpu.VMEM((rows, cols, HALF), F32),
-            pltpu.VMEM((rows, cols, HALF), F32),
-            pltpu.VMEM(((rows - 2) * cols, HALF), BF16),
-            pltpu.VMEM(((rows - 2) * cols, HALF), BF16),
+            pltpu.VMEM(((rows - 2) * cols, CHUNK), BF16),
             pltpu.VMEM(((rows - 2) * cols, width), F32),
             pltpu.VMEM((own, cols, width), BF16),
             pltpu.SemaphoreType.DMA((4,)),

time: 112 us -> 111 us (level)
  transfers between devices with their start and end apart: 10 -> 10, of which waited for: 5 -> 6; matrix products, arithmetic and copies ran while one was open for 1% -> 1% of each run, Pallas kernels for 39% -> 38%
where the time goes in v10:
time: 111 us; the launch traced here: 110 us
  Pallas kernels  54.9 us (49%)
  starting transfers between devices  29.9 us (27%)
  waiting for transfers between devices  20.4 us (18%)
  other arithmetic  2.33 us (2%)
  between operations  1.49 us (1%)
  local copies, waits for them, and re-layouts  1.28 us (1%)
    all_to_all x4, starting transfers between devices, exchange_windows(): lax.all_to_all(rows, 'row', split_axis=0, concat_axis=0, tiled=True, axis...  27.8 us
    all_to_all x4, waiting for transfers between devices, exchange_windows(): lax.all_to_all(rows, 'row', split_axis=0, concat_axis=0, tiled=True, axis...  19.2 us
    pallas_call x1, Pallas kernels, forward(): pl.pallas_call(forward_body, in_specs=[in_scalars(), in_hbm(), in_vmem(),...  14.1 us
    pallas_call x1, Pallas kernels, attention(): pl.pallas_call(attention_body, in_specs=[in_vmem(), in_hbm(), in_hbm()],...  12.7 us
    pallas_call x1, Pallas kernels, backward(): pl.pallas_call(backward_body, in_specs=[in_scalars()] + [in_hbm()] * 7 +...  11.3 us
    pallas_call x1, Pallas kernels, slopes(): pl.pallas_call(slopes_body, grid=(hidden_width // CHUNK,), in_specs=block...  7.76 us
    pallas_call x1, Pallas kernels, attend(): pl.pallas_call(attended_body, grid=(1,), in_specs=[whole(weights.shape),...  3.69 us
    pallas_call x1, Pallas kernels, attended_gradient(): pl.pallas_call(grad_attended_body, grid=(1,), in_specs=[whole(cotangent.s...  2.51 us
  transfers between devices with their start and end apart: 10, of which 6 were waited for; matrix products, arithmetic and copies ran while one was open for 1% of the time, Pallas kernels for 38%

profile of v10, /device:TPU:0, one launch (start us, length us, event | category | flops | bytes accessed | tf_op | source)
XLA Modules:
  0.0 110.2 jit_solution(7841624685242245968)
XLA Ops:
  1.3 0.7 copy-done.4
  1.9 1.4 %rim_rows.1 = bf16[3,32,512]{2,1,0:T(8,128)(2,1)S(1)} custom-call(s32[16]{0:T(128)S(1)} %copy-done.4, bf16[24,32,512]{2,1,0:T(8,128)(2,1)} %features_ref.3, bf16[24,32,512]{2,1,0:T(8,128)(2,1)} %cotangent_ref.3), custom_call_target="tpu_custom_call" | custom-call | tf_op jit(solution)/shard_map/rim_rows/pallas_call | solution.py:156
  3.3 0.7 collective-permute-start.1
  4.0 1.4 %even_rows.1.grad_slab_ref = bf16[16,32,512]{2,1,0:T(8,128)(2,1)} custom-call(s32[16]{0:T(128)S(1)} %copy-done.4, bf16[24,32,512]{2,1,0:T(8,128)(2,1)S(1)} %copy-done, bf16[24,32,512]{2,1,0:T(8,128)(2,1)S(1)} %collective-permute-done.2.other_ref), custom_call_target="tpu_custom_call" | custom-call | tf_op jit(solution)/shard_map/even_rows/pallas_call | solution.py:127
  5.5 11.1 %all-to-all-start = ((bf16[16,32,512]{2,1,0:T(8,128)(2,1)}), bf16[16,32,512]{2,1,0:T(8,128)(2,1)S(1)}, u32[]{:S(2)}, u32[]{:S(2)}) async-start(bf16[16,32,512]{2,1,0:T(8,128)(2,1)} %even_rows.1.grad_slab_ref), calls=%async_computation | async-start | bytes 1048576 | tf_op jit(solution)/shard_map/all_to_all | solution.py:711
  16.6 14.1 %bottleneck_forward.1 = (f32[576,512]{1,0:T(8,128)}, f32[512,512]{1,0:T(8,128)}, bf16[16,32,512]{2,1,0:T(8,128)(2,1)}, bf16[16,32,512]{2,1,0:T(8,128)(2,1)}, f32...) custom-call(s32[16]{0:T(128)S(1)} %copy-done.5, bf16[24,32,512]{2,1,0:T(8,128)(2,1)} %features_ref.3, ...), custom_call_target="tpu_custom_call" | custom-call | flops 2684354560 | bytes 12582912 | tf_op jit(solution)/shard_map/bottleneck_forward/pallas_call | solution.py:285
  30.7 0.7 all-to-all-done
  31.4 5.4 %all-to-all-start.1 = ((bf16[16,32,512]{2,1,0:T(8,128)(2,1)}), bf16[16,32,512]{2,1,0:T(8,128)(2,1)S(1)}, u32[]{:S(2)}, u32[]{:S(2)}) async-start(bf16[16,32,512]{2,1,0:T(8,128)(2,1)} %get-tuple-element.34), calls=%async_computation.1 | async-start | bytes 1048576 | tf_op jit(solution)/shard_map/all_to_all | solution.py:711
  36.7 7.8 %gelu_slopes.1 = (bf16[16,32,2048]{2,1,0:T(8,128)(2,1)}, bf16[18,32,2048]{2,1,0:T(8,128)(2,1)}) custom-call(f32[16,32,2048]{2,1,0:T(8,128)} %get-tuple-element.35.expanded_ref, f32[18,32,2048]{2,1,0:T(8,128)} %get-tuple-element.36.mixed_ref), custom_call_target="tpu_custom_call" | custom-call | flops 33423360 | bytes 13369344 | tf_op jit(solution)/shard_map/gelu_slopes/pallas_call | solution.py:337
  44.5 2.5 %attended_gradient.1.grad_attended_ref = bf16[512,512]{1,0:T(8,128)(2,1)} custom-call(bf16[8,2,32,512]{3,2,1,0:T(8,128)(2,1)} %bitcast.24, bf16[512,512]{1,0:T(8,128)(2,1)} %out_ref.3), custom_call_target="tpu_custom_call" | custom-call | flops 268435456 | bytes 2097152 | tf_op jit(solution)/shard_map/attended_gradient/pallas_call | solution.py:400
  47.0 3.9 %all-to-all-done.1 = bf16[16,32,512]{2,1,0:T(8,128)(2,1)S(1)} async-done(((bf16[16,32,512]{2,1,0:T(8,128)(2,1)}), bf16[16,32,512]{2,1,0:T(8,128)(2,1)S(1)}, u32[]{:S(2)}, u32[]{:S(2)}) %all-to-all-start.1) | async-done | bytes 524320 | tf_op jit(solution)/shard_map/all_to_all | solution.py:711
  50.9 12.7 %window_attention.1 = (bf16[8,2,32,512]{3,2,1,0:T(8,128)(2,1)}, bf16[8,64,1024]{2,1,0:T(8,128)(2,1)}, bf16[512,512]{1,0:T(8,128)(2,1)}) custom-call(bf16[8,2,32,512]{3,2,1,0:T(8,128)(2,1)S(1)} %bitcast.22, bf16[512,512]{1,0:T(8,128)(2,1)} %attended_gradient.1.grad_attended_ref, bf16[512,1536]{1,0:T(8,128)(2,1)} %qkv_ref.1), custom_call_target="tpu_custom_call" | custom-call | flops 2147483648 | bytes 4194304 | tf_op jit(solution)/shard_map/window_attention/pallas_call | solution.py:489
  63.6 3.6 %all-to-all-start.2 = ((bf16[16,32,512]{2,1,0:T(8,128)(2,1)}), bf16[16,32,512]{2,1,0:T(8,128)(2,1)S(1)}, u32[]{:S(2)}, u32[]{:S(2)}) async-start(bf16[16,32,512]{2,1,0:T(8,128)(2,1)} %bitcast.26), calls=%async_computation.2 | async-start | bytes 1048576 | tf_op jit(solution)/shard_map/all_to_all | solution.py:711
  67.3 3.7 %attended_output.1 = bf16[8,2,32,512]{3,2,1,0:T(8,128)(2,1)} custom-call(bf16[8,64,1024]{2,1,0:T(8,128)(2,1)} %get-tuple-element.43.weights_ref, bf16[512,512]{1,0:T(8,128)(2,1)} %get-tuple-element.44.values_ref, bf16[512,512]{1,0:T(8,128)(2,1)} %out_ref.3), custom_call_target="tpu_custom_call" | custom-call | flops 536870912 | bytes 3145728 | tf_op jit(solution)/shard_map/attended_output/pallas_call | solution.py:529
  71.0 10.7 %all-to-all-done.2.grad_ref = bf16[16,32,512]{2,1,0:T(8,128)(2,1)S(1)} async-done(((bf16[16,32,512]{2,1,0:T(8,128)(2,1)}), bf16[16,32,512]{2,1,0:T(8,128)(2,1)S(1)}, u32[]{:S(2)}, u32[]{:S(2)}) %all-to-all-start.2) | async-done | bytes 524320 | tf_op jit(solution)/shard_map/all_to_all | solution.py:711
  81.8 0.7 collective-permute-start.4
  82.5 0.5 collective-permute-done.3.pair_ref
  83.0 7.7 %all-to-all-start.3 = ((bf16[16,32,512]{2,1,0:T(8,128)(2,1)}), bf16[16,32,512]{2,1,0:T(8,128)(2,1)S(1)}, u32[]{:S(2)}, u32[]{:S(2)}) async-start(bf16[16,32,512]{2,1,0:T(8,128)(2,1)} %bitcast.23), calls=%async_computation.3 | async-start | bytes 1048576 | tf_op jit(solution)/shard_map/all_to_all | solution.py:711
  90.7 11.3 %bottleneck_backward.1 = bf16[16,32,512]{2,1,0:T(8,128)(2,1)S(1)} custom-call(s32[16]{0:T(128)S(1)} %copy-done.5, bf16[24,32,512]{2,1,0:T(8,128)(2,1)} %cotangent_ref.3, bf16[24,32,512]{2,1,0:T(8,128)(2,1)} %copy-done.1, bf16[3,32,512]{2,1,0:T(8,128)(2,1)} %copy-done.2, bf16[16,32,512]{2,1,0:T(8,128)(2,1)} %get-tuple-element.30.slab_ref, ...), custom_call_target="tpu_custom_call" | custom-call | flops 2415919104 | bytes 12582912 | tf_op jit(solution)/shard_map/bottleneck_backward/pallas_call | solution.py:665
  102.0 3.8 %all-to-all-done.3 = bf16[16,32,512]{2,1,0:T(8,128)(2,1)S(1)} async-done(((bf16[16,32,512]{2,1,0:T(8,128)(2,1)}), bf16[16,32,512]{2,1,0:T(8,128)(2,1)S(1)}, u32[]{:S(2)}, u32[]{:S(2)}) %all-to-all-start.3) | async-done | bytes 524320 | tf_op jit(solution)/shard_map/all_to_all | solution.py:711
  106.3 0.6 dynamic_slice.3
  107.5 0.6 collective-permute-done.5
  108.3 1.0 pad_maximum_fusion.1
  109.2 1.0 pad_maximum_fusion
  (30 shorter events, 1.2 us)
Async XLA Ops:
  0.6 3.4 %copy-start = (bf16[24,32,512]{2,1,0:T(8,128)(2,1)S(1)}, bf16[24,32,512]{2,1,0:T(8,128)(2,1)}, u32[]{:S(2)}) copy-start(bf16[24,32,512]{2,1,0:T(8,128)(2,1)} %cotangent_ref.3) | copy-start | bytes 2359300
  0.6 15.9 %copy-start.3 = (bf16[9,2048]{1,0:T(8,128)(2,1)S(1)}, bf16[9,2048]{1,0:T(8,128)(2,1)}, u32[]{:S(2)}) copy-start(bf16[9,2048]{1,0:T(8,128)(2,1)} %taps_ref.3) | copy-start | bytes 110596
  0.7 3.4 %collective-permute-start.2 = (bf16[24,32,512]{2,1,0:T(8,128)(2,1)}, bf16[24,32,512]{2,1,0:T(8,128)(2,1)S(1)}, u32[]{:S(2)}, u32[]{:S(2)}) collective-permute-start(bf16[24,32,512]{2,1,0:T(8,128)(2,1)} %cotangent_ref.3), channel_id=1, source_target_pairs={{0,1},{1,0},{2,3},{3,2},{4,5},{5,4},{6,7},{7,6},{8,9},{9,8},{10,11... | collective-permute-start | bytes 2359304 | tf_op jit(solution)/shard_map/ppermute | solution.py:718
  1.2 15.4 %collective-permute-start = (bf16[24,32,512]{2,1,0:T(8,128)(2,1)}, bf16[24,32,512]{2,1,0:T(8,128)(2,1)S(1)}, u32[]{:S(2)}, u32[]{:S(2)}) collective-permute-start(bf16[24,32,512]{2,1,0:T(8,128)(2,1)} %features_ref.3), channel_id=1, source_target_pairs={{0,1},{1,0},{2,3},{3,2},{4,5},{5,4},{6,7},{7,6},{8,9},{9,8},{10,11... | collective-permute-start | bytes 2359304 | tf_op jit(solution)/shard_map/ppermute | solution.py:718
  1.2 0.7 copy-start.4
  1.9 14.7 %copy-start.5 = (s32[16]{0:T(128)S(1)}, s32[16]{0:T(128)}, u32[]{:S(2)}) copy-start(s32[16]{0:T(128)} %bands_ref.7) | copy-start | bytes 196
  3.3 2.1 %collective-permute-start.1 = (bf16[3,32,512]{2,1,0:T(8,128)(2,1)S(1)}, bf16[3,32,512]{2,1,0:T(8,128)(2,1)S(1)}, u32[]{:S(2)}, u32[]{:S(2)}) collective-permute-start(bf16[3,32,512]{2,1,0:T(8,128)(2,1)S(1)} %rim_rows.1), channel_id=1, source_target_pairs={{1,2},{3,4},{5,6},{7,8},{9,10},{11,12},{13,14},{2,1},{4,3},{6,5},{... | collective-permute-start | bytes 294920 | tf_op jit(solution)/shard_map/ppermute | solution.py:724
  4.0 26.7 %copy-start.1 = (bf16[24,32,512]{2,1,0:T(8,128)(2,1)}, bf16[24,32,512]{2,1,0:T(8,128)(2,1)S(1)}, u32[]{:S(2)}) copy-start(bf16[24,32,512]{2,1,0:T(8,128)(2,1)S(1)} %collective-permute-done.2.other_ref) | copy-start | bytes 2359300
  5.4 25.2 %copy-start.2 = (bf16[3,32,512]{2,1,0:T(8,128)(2,1)}, bf16[3,32,512]{2,1,0:T(8,128)(2,1)S(1)}, u32[]{:S(2)}) copy-start(bf16[3,32,512]{2,1,0:T(8,128)(2,1)S(1)} %collective-permute-done.1.rim_ref) | copy-start | bytes 294916
  5.5 25.9 %all-to-all-start = ((bf16[16,32,512]{2,1,0:T(8,128)(2,1)}), bf16[16,32,512]{2,1,0:T(8,128)(2,1)S(1)}, u32[]{:S(2)}, u32[]{:S(2)}) async-start(bf16[16,32,512]{2,1,0:T(8,128)(2,1)} %even_rows.1.grad_slab_ref), calls=%async_computation | async-start | bytes 1048576 | tf_op jit(solution)/shard_map/all_to_all | solution.py:711
  31.4 13.1 %copy-start.7 = (bf16[16,32,512]{2,1,0:T(8,128)(2,1)}, bf16[16,32,512]{2,1,0:T(8,128)(2,1)S(1)}, u32[]{:S(2)}) copy-start(bf16[16,32,512]{2,1,0:T(8,128)(2,1)S(1)} %all-to-all-done) | copy-start | bytes 1572868
  31.4 19.6 %all-to-all-start.1 = ((bf16[16,32,512]{2,1,0:T(8,128)(2,1)}), bf16[16,32,512]{2,1,0:T(8,128)(2,1)S(1)}, u32[]{:S(2)}, u32[]{:S(2)}) async-start(bf16[16,32,512]{2,1,0:T(8,128)(2,1)} %get-tuple-element.34), calls=%async_computation.1 | async-start | bytes 1048576 | tf_op jit(solution)/shard_map/all_to_all | solution.py:711
  63.6 18.1 %all-to-all-start.2 = ((bf16[16,32,512]{2,1,0:T(8,128)(2,1)}), bf16[16,32,512]{2,1,0:T(8,128)(2,1)S(1)}, u32[]{:S(2)}, u32[]{:S(2)}) async-start(bf16[16,32,512]{2,1,0:T(8,128)(2,1)} %bitcast.26), calls=%async_computation.2 | async-start | bytes 1048576 | tf_op jit(solution)/shard_map/all_to_all | solution.py:711
  81.7 9.0 %copy-start.6 = (bf16[16,32,512]{2,1,0:T(8,128)(2,1)}, bf16[16,32,512]{2,1,0:T(8,128)(2,1)S(1)}, u32[]{:S(2)}) copy-start(bf16[16,32,512]{2,1,0:T(8,128)(2,1)S(1)} %all-to-all-done.2.grad_ref) | copy-start | bytes 1572868
  81.7 1.3 %collective-permute-start.3 = (bf16[1,32,512]{2,1,0:T(8,128)(2,1)S(1)}, bf16[1,32,512]{2,1,0:T(8,128)(2,1)S(1)}, u32[]{:S(2)}, u32[]{:S(2)}) collective-permute-start(bf16[1,32,512]{2,1,0:T(8,128)(2,1)S(1)} %get-tuple-element.63), channel_id=1, source_target_pairs={{0,1},{1,0},{2,3},{3,2},{4,5},{5,4},{6,7},{7,6},{8,9},{9,8},{10,11... | collective-permute-start | bytes 98312 | tf_op jit(solution)/shard_map/ppermute | solution.py:718
  81.8 1.2 %collective-permute-start.4 = (bf16[1,32,512]{2,1,0:T(8,128)(2,1)S(1)}, bf16[1,32,512]{2,1,0:T(8,128)(2,1)S(1)}, u32[]{:S(2)}, u32[]{:S(2)}) collective-permute-start(bf16[1,32,512]{2,1,0:T(8,128)(2,1)S(1)} %get-tuple-element.62), channel_id=1, source_target_pairs={{1,2},{3,4},{5,6},{7,8},{9,10},{11,12},{13,14},{2,1},{4,3},{6,5},{... | collective-permute-start | bytes 98312 | tf_op jit(solution)/shard_map/ppermute | solution.py:724
  83.0 22.9 %all-to-all-start.3 = ((bf16[16,32,512]{2,1,0:T(8,128)(2,1)}), bf16[16,32,512]{2,1,0:T(8,128)(2,1)S(1)}, u32[]{:S(2)}, u32[]{:S(2)}) async-start(bf16[16,32,512]{2,1,0:T(8,128)(2,1)} %bitcast.23), calls=%async_computation.3 | async-start | bytes 1048576 | tf_op jit(solution)/shard_map/all_to_all | solution.py:711
  90.7 15.2 %copy-start.8 = (f32[512,512]{1,0:T(8,128)S(1)}, f32[512,512]{1,0:T(8,128)}, u32[]{:S(2)}) copy-start(f32[512,512]{1,0:T(8,128)} %get-tuple-element.29) | copy-start | bytes 3145732
  106.2 2.0 %collective-permute-start.5 = (bf16[2,8,32,512]{3,2,1,0:T(8,128)(2,1)S(1)}, bf16[2,8,32,512]{3,2,1,0:T(8,128)(2,1)S(1)}, u32[]{:S(2)}, u32[]{:S(2)}) collective-permute-start(bf16[2,8,32,512]{3,2,1,0:T(8,128)(2,1)S(1)} %pad_maximum_fusion.2), channel_id=1, source_target_pairs={{0,1},{1,0},{2,3},{3,2},{4,5},{5,4},{6,7},{7,6},{8,9},{9,8},{10,11... | collective-permute-start | bytes 1572872 | tf_op jit(solution)/shard_map/ppermute | solution.py:718

commit v11 on v10

--- a/solution.py
+++ b/solution.py
@@ -14,6 +14,8 @@
 EPSILON = 1e-06
 CHUNK = 512
 HALF = 256
+GROUP_FORWARD = 10
+GROUP_BACKWARD = 9
 LANES = 128
 ROOT = math.sqrt(2.0 / math.pi)
 CUBIC = 0.044715
@@ -230,16 +232,17 @@
             fetch_project(index + 1).start()
 
         fetch_expand(index).wait()
-        weights = expand[:, chunk_lanes(index)]
-        for row in range(0, rows, 4):
-            product = nn_dot(normed_one[row * cols : (row + 4) * cols, :], weights)
-            for inner in range(4):
-                for lane in range(0, CHUNK, LANES):
-                    lanes = slice(lane, lane + LANES)
-                    values = product[inner * cols : (inner + 1) * cols, lanes]
-                    hidden[row + inner, :, lanes] = gelu(values).astype(BF16).astype(F32)
-                    if RIM <= row + inner < RIM + own:
-                        expanded[row + inner - RIM, :, chunk_lanes(index, lane, LANES)] = values
+        for start in range(0, CHUNK, HALF):
+            weights = expand[:, chunk_lanes(index, start, HALF)]
+            for row in range(0, rows, GROUP_FORWARD):
+                product = nn_dot(normed_one[row * cols : (row + GROUP_FORWARD) * cols, :], weights)
+                for inner in range(GROUP_FORWARD):
+                    for lane in range(0, HALF, LANES):
+                        values = product[inner * cols : (inner + 1) * cols, lane : lane + LANES]
+                        at = slice(start + lane, start + lane + LANES)
+                        hidden[row + inner, :, at] = gelu(values).astype(BF16).astype(F32)
+                        if RIM <= row + inner < RIM + own:
+                            expanded[row + inner - RIM, :, chunk_lanes(index, start + lane, LANES)] = values
         store_expanded(index).start()
 
         for lane in range(0, CHUNK, LANES):
@@ -544,7 +547,7 @@
 def backward_body(bands_ref, cotangent_ref, other_ref, rim_ref, slab_ref, first_ref, grad_slab_ref, grad_ref,
                   pair_ref, next_ref, slope_one_ref, slope_two_ref, expand_ref, taps_ref, project_ref,
                   out_ref, rims, slab, first, grad_slab, grad_in, slope_one, slope_two, expand, project,
-                  grad_first, grad_rows, mixed, product_a, product_b, expanded_a, expanded_b, total, row_sems,
+                  grad_first, grad_rows, mixed, expanded, total, row_sems,
                   in_sems, chunk_sems):
     own, cols, width = slab.shape
     chunks = expand_ref.shape[1] // CHUNK
@@ -610,39 +613,32 @@
             for copy in fetches(index + 1):
                 copy.start()
 
-        def project_half(half, product):
-            weights = project[chunk_lanes(index, half * HALF, HALF), :]
-            product[...] = nt_dot(grad_rows[...], weights).reshape(own + 2, cols, HALF)
-
-        def expand_half(half, expanded):
-            total[...] += nt_dot(expanded[...], expand[:, chunk_lanes(index, half * HALF, HALF)])
-
-        def unmix_half(half, product, expanded):
-            for lane in range(0, HALF, LANES):
-                lanes = slice(lane, lane + LANES)
-                at = chunk_lanes(index, half * HALF + lane, LANES)
-                for row in range(own + 2):
-                    value = product[row, :, lanes] * slope_two[row, :, at].astype(F32)
-                    mixed[row, :, lanes] = value.astype(BF16).astype(F32)
-                taps = spread_taps(taps_ref, at, cols)
-                for row in range(own):
-                    rows_near = [mixed[row + a, :, lanes] for a in range(3)]
-                    sums = [
-                        taps[8 - b] * rows_near[0] + taps[5 - b] * rows_near[1] + taps[2 - b] * rows_near[2]
-                        for b in range(3)
-                    ]
-                    value = column_sums(sums[0], sums[1], sums[2], column, cols - 1)
-                    value = value * slope_one[row, :, at].astype(F32)
-                    expanded[row * cols : (row + 1) * cols, lanes] = value.astype(BF16)
-
         for copy in fetches(index):
             copy.wait()
-        project_half(0, product_a)
-        project_half(1, product_b)
-        unmix_half(0, product_a, expanded_a)
-        expand_half(0, expanded_a)
-        unmix_half(1, product_b, expanded_b)
-        expand_half(1, expanded_b)
+        for start in range(0, CHUNK, HALF):
+            weights = project[chunk_lanes(index, start, HALF), :]
+            for row in range(0, own + 2, GROUP_BACKWARD):
+                product = nt_dot(grad_rows[row * cols : (row + GROUP_BACKWARD) * cols, :], weights)
+                for inner in range(GROUP_BACKWARD):
+                    for lane in range(0, HALF, LANES):
+                        slope = slope_two[row + inner, :, chunk_lanes(index, start + lane, LANES)].astype(F32)
+                        value = product[inner * cols : (inner + 1) * cols, lane : lane + LANES] * slope
+                        at = slice(start + lane, start + lane + LANES)
+                        mixed[row + inner, :, at] = value.astype(BF16).astype(F32)
+
+        for lane in range(0, CHUNK, LANES):
+            lanes = slice(lane, lane + LANES)
+            taps = spread_taps(taps_ref, chunk_lanes(index, lane, LANES), cols)
+            for row in range(own):
+                rows_near = [mixed[row + a, :, lanes] for a in range(3)]
+                sums = [
+                    taps[8 - b] * rows_near[0] + taps[5 - b] * rows_near[1] + taps[2 - b] * rows_near[2]
+                    for b in range(3)
+                ]
+                value = column_sums(sums[0], sums[1], sums[2], column, cols - 1)
+                value = value * slope_one[row, :, chunk_lanes(index, lane, LANES)].astype(F32)
+                expanded[row * cols : (row + 1) * cols, lanes] = value.astype(BF16)
+        total[...] += nt_dot(expanded[...], expand[:, chunk_lanes(index)])
         return carry
 
     lax.fori_loop(0, chunks, step, 0)
@@ -679,11 +675,8 @@
             pltpu.VMEM((hidden_width, width), BF16),
             pltpu.VMEM((own * cols, width), F32),
             pltpu.VMEM(((own + 2) * cols, width), BF16),
-            pltpu.VMEM((own + 2, cols, HALF), F32),
-            pltpu.VMEM((own + 2, cols, HALF), F32),
-            pltpu.VMEM((own + 2, cols, HALF), F32),
-            pltpu.VMEM((own * cols, HALF), BF16),
-            pltpu.VMEM((own * cols, HALF), BF16),
+            pltpu.VMEM((own + 2, cols, CHUNK), F32),
+            pltpu.VMEM((own * cols, CHUNK), BF16),
             pltpu.VMEM((own * cols, width), F32),
             pltpu.SemaphoreType.DMA((2,)),
             pltpu.SemaphoreType.DMA((4,)),
@@ -772,14 +765,17 @@
         row_bands, cotangent, other_cotangent, rim, slab, first, grad_slab, grad_rows, pair_row, next_row,
         slope_one, slope_two, w_expand, kernel, w_project,
     )
+    def sent(rows):
+        return jnp.where(leads, rows[BAND:], rows[:BAND])
+
+    other_grad = swap_pair(sent(grad_input))
     grad_input, added_rows = lax.optimization_barrier((grad_input, added_rows))
     final = (own_first.reshape(GRID_ROWS, cols, width) + added_rows.astype(F32)).astype(BF16)
-    sent = [jnp.where(leads, rows[BAND:], rows[:BAND]) for rows in (final, grad_input)]
-    swapped = swap_pair(jnp.stack(sent))
+    other_final = swap_pair(sent(final))
     leader_share = BAND * row_bands[device - parity]
     return (
-        place_rows(final, swapped[0], leads, leader_share),
-        place_rows(grad_input, swapped[1], leads, leader_share),
+        place_rows(final, other_final, leads, leader_share),
+        place_rows(grad_input, other_grad, leads, leader_share),
     )
 
 

time: 111 us -> 109 us (0.982)
  waiting for transfers between devices: 20.4 us -> 19 us
    all_to_all x4, waiting for transfers between devices: 19.2 us -> 18 us  [exchange_windows(): lax.all_to_all(rows, 'row', split_axis=0, concat_axis=0, tiled=True, axis...]
  transfers between devices with their start and end apart: 10 -> 11, of which waited for: 6 -> 6; matrix products, arithmetic and copies ran while one was open for 1% -> 2% of each run, Pallas kernels for 38% -> 38%
where the time goes in v11:
time: 109 us
  Pallas kernels  54.2 us (50%)
  starting transfers between devices  30.4 us (28%)
  waiting for transfers between devices  19 us (17%)
  other arithmetic  2.29 us (2%)
  between operations  1.48 us (1%)
  local copies, waits for them, and re-layouts  1.33 us (1%)
    all_to_all x4, starting transfers between devices, exchange_windows(): lax.all_to_all(rows, 'row', split_axis=0, concat_axis=0, tiled=True, axis...  27.7 us
    all_to_all x4, waiting for transfers between devices, exchange_windows(): lax.all_to_all(rows, 'row', split_axis=0, concat_axis=0, tiled=True, axis...  18 us
    pallas_call x1, Pallas kernels, forward(): pl.pallas_call(forward_body, in_specs=[in_scalars(), in_hbm(), in_vmem(),...  14 us
    pallas_call x1, Pallas kernels, attention(): pl.pallas_call(attention_body, in_specs=[in_vmem(), in_hbm(), in_hbm()],...  12.7 us
    pallas_call x1, Pallas kernels, backward(): pl.pallas_call(backward_body, in_specs=[in_scalars()] + [in_hbm()] * 7 +...  10.8 us
    pallas_call x1, Pallas kernels, slopes(): pl.pallas_call(slopes_body, grid=(hidden_width // CHUNK,), in_specs=block...  7.71 us
    pallas_call x1, Pallas kernels, attend(): pl.pallas_call(attended_body, grid=(1,), in_specs=[whole(weights.shape),...  3.7 us
    pallas_call x1, Pallas kernels, attended_gradient(): pl.pallas_call(grad_attended_body, grid=(1,), in_specs=[whole(cotangent.s...  2.52 us
  transfers between devices with their start and end apart: 11, of which 6 were waited for; matrix products, arithmetic and copies ran while one was open for 2% of the time, Pallas kernels for 38%

profile of v11, /device:TPU:0, one launch (start us, length us, event | category | flops | bytes accessed | tf_op | source)
XLA Modules:
  0.0 108.7 jit_solution(10605830198678833611)
XLA Ops:
  1.3 0.7 copy-done.4
  1.9 1.4 %rim_rows.1 = bf16[3,32,512]{2,1,0:T(8,128)(2,1)S(1)} custom-call(s32[16]{0:T(128)S(1)} %copy-done.4, bf16[24,32,512]{2,1,0:T(8,128)(2,1)} %features_ref.3, bf16[24,32,512]{2,1,0:T(8,128)(2,1)} %cotangent_ref.3), custom_call_target="tpu_custom_call" | custom-call | tf_op jit(solution)/shard_map/rim_rows/pallas_call | solution.py:158
  3.3 0.7 collective-permute-start.1
  4.0 1.4 %even_rows.1.grad_slab_ref = bf16[16,32,512]{2,1,0:T(8,128)(2,1)} custom-call(s32[16]{0:T(128)S(1)} %copy-done.4, bf16[24,32,512]{2,1,0:T(8,128)(2,1)S(1)} %copy-done, bf16[24,32,512]{2,1,0:T(8,128)(2,1)S(1)} %collective-permute-done.2.other_ref), custom_call_target="tpu_custom_call" | custom-call | tf_op jit(solution)/shard_map/even_rows/pallas_call | solution.py:129
  5.4 11.1 %all-to-all-start = ((bf16[16,32,512]{2,1,0:T(8,128)(2,1)}), bf16[16,32,512]{2,1,0:T(8,128)(2,1)S(1)}, u32[]{:S(2)}, u32[]{:S(2)}) async-start(bf16[16,32,512]{2,1,0:T(8,128)(2,1)} %even_rows.1.grad_slab_ref), calls=%async_computation | async-start | bytes 1048576 | tf_op jit(solution)/shard_map/all_to_all | solution.py:704
  16.6 14.0 %bottleneck_forward.1 = (f32[576,512]{1,0:T(8,128)}, f32[512,512]{1,0:T(8,128)}, bf16[16,32,512]{2,1,0:T(8,128)(2,1)}, bf16[16,32,512]{2,1,0:T(8,128)(2,1)}, f32...) custom-call(s32[16]{0:T(128)S(1)} %copy-done.5, bf16[24,32,512]{2,1,0:T(8,128)(2,1)} %features_ref.3, ...), custom_call_target="tpu_custom_call" | custom-call | flops 2684354560 | bytes 12582912 | tf_op jit(solution)/shard_map/bottleneck_forward/pallas_call | solution.py:288
  30.6 0.7 all-to-all-done
  31.4 5.3 %all-to-all-start.1 = ((bf16[16,32,512]{2,1,0:T(8,128)(2,1)}), bf16[16,32,512]{2,1,0:T(8,128)(2,1)S(1)}, u32[]{:S(2)}, u32[]{:S(2)}) async-start(bf16[16,32,512]{2,1,0:T(8,128)(2,1)} %get-tuple-element.34), calls=%async_computation.1 | async-start | bytes 1048576 | tf_op jit(solution)/shard_map/all_to_all | solution.py:704
  36.6 7.7 %gelu_slopes.1 = (bf16[16,32,2048]{2,1,0:T(8,128)(2,1)}, bf16[18,32,2048]{2,1,0:T(8,128)(2,1)}) custom-call(f32[16,32,2048]{2,1,0:T(8,128)} %get-tuple-element.35.expanded_ref, f32[18,32,2048]{2,1,0:T(8,128)} %get-tuple-element.36.mixed_ref), custom_call_target="tpu_custom_call" | custom-call | flops 33423360 | bytes 13369344 | tf_op jit(solution)/shard_map/gelu_slopes/pallas_call | solution.py:340
  44.3 2.5 %attended_gradient.1.grad_attended_ref = bf16[512,512]{1,0:T(8,128)(2,1)} custom-call(bf16[8,2,32,512]{3,2,1,0:T(8,128)(2,1)} %bitcast.8, bf16[512,512]{1,0:T(8,128)(2,1)} %out_ref.3), custom_call_target="tpu_custom_call" | custom-call | flops 268435456 | bytes 2097152 | tf_op jit(solution)/shard_map/attended_gradient/pallas_call | solution.py:403
  46.9 4.0 %all-to-all-done.1 = bf16[16,32,512]{2,1,0:T(8,128)(2,1)S(1)} async-done(((bf16[16,32,512]{2,1,0:T(8,128)(2,1)}), bf16[16,32,512]{2,1,0:T(8,128)(2,1)S(1)}, u32[]{:S(2)}, u32[]{:S(2)}) %all-to-all-start.1) | async-done | bytes 524320 | tf_op jit(solution)/shard_map/all_to_all | solution.py:704
  50.9 12.7 %window_attention.1 = (bf16[8,2,32,512]{3,2,1,0:T(8,128)(2,1)}, bf16[8,64,1024]{2,1,0:T(8,128)(2,1)}, bf16[512,512]{1,0:T(8,128)(2,1)}) custom-call(bf16[8,2,32,512]{3,2,1,0:T(8,128)(2,1)S(1)} %bitcast.6, bf16[512,512]{1,0:T(8,128)(2,1)} %attended_gradient.1.grad_attended_ref, bf16[512,1536]{1,0:T(8,128)(2,1)} %qkv_ref.1), custom_call_target="tpu_custom_call" | custom-call | flops 2147483648 | bytes 4194304 | tf_op jit(solution)/shard_map/window_attention/pallas_call | solution.py:492
  63.6 3.6 %all-to-all-start.2 = ((bf16[16,32,512]{2,1,0:T(8,128)(2,1)}), bf16[16,32,512]{2,1,0:T(8,128)(2,1)S(1)}, u32[]{:S(2)}, u32[]{:S(2)}) async-start(bf16[16,32,512]{2,1,0:T(8,128)(2,1)} %bitcast.10), calls=%async_computation.2 | async-start | bytes 1048576 | tf_op jit(solution)/shard_map/all_to_all | solution.py:704
  67.2 3.7 %attended_output.1 = bf16[8,2,32,512]{3,2,1,0:T(8,128)(2,1)} custom-call(bf16[8,64,1024]{2,1,0:T(8,128)(2,1)} %get-tuple-element.43.weights_ref, bf16[512,512]{1,0:T(8,128)(2,1)} %get-tuple-element.44.values_ref, bf16[512,512]{1,0:T(8,128)(2,1)} %out_ref.3), custom_call_target="tpu_custom_call" | custom-call | flops 536870912 | bytes 3145728 | tf_op jit(solution)/shard_map/attended_output/pallas_call | solution.py:532
  70.9 10.8 %all-to-all-done.2.grad_ref = bf16[16,32,512]{2,1,0:T(8,128)(2,1)S(1)} async-done(((bf16[16,32,512]{2,1,0:T(8,128)(2,1)}), bf16[16,32,512]{2,1,0:T(8,128)(2,1)S(1)}, u32[]{:S(2)}, u32[]{:S(2)}) %all-to-all-start.2) | async-done | bytes 524320 | tf_op jit(solution)/shard_map/all_to_all | solution.py:704
  81.8 0.7 collective-permute-start.4
  82.5 0.5 collective-permute-done.3.pair_ref
  83.0 7.7 %all-to-all-start.3 = ((bf16[16,32,512]{2,1,0:T(8,128)(2,1)}), bf16[16,32,512]{2,1,0:T(8,128)(2,1)S(1)}, u32[]{:S(2)}, u32[]{:S(2)}) async-start(bf16[16,32,512]{2,1,0:T(8,128)(2,1)} %bitcast.7), calls=%async_computation.3 | async-start | bytes 1048576 | tf_op jit(solution)/shard_map/all_to_all | solution.py:704
  90.7 0.6 dynamic_slice.3
  92.0 10.8 %bottleneck_backward.1 = bf16[16,32,512]{2,1,0:T(8,128)(2,1)S(1)} custom-call(s32[16]{0:T(128)S(1)} %copy-done.5, bf16[24,32,512]{2,1,0:T(8,128)(2,1)} %cotangent_ref.3, bf16[24,32,512]{2,1,0:T(8,128)(2,1)} %copy-done.1, bf16[3,32,512]{2,1,0:T(8,128)(2,1)} %copy-done.2, bf16[16,32,512]{2,1,0:T(8,128)(2,1)} %get-tuple-element.30.slab_ref, ...), custom_call_target="tpu_custom_call" | custom-call | flops 2415919104 | bytes 12582912 | tf_op jit(solution)/shard_map/bottleneck_backward/pallas_call | solution.py:661
  102.8 0.6 collective-permute-start.6
  103.4 2.4 %all-to-all-done.3 = bf16[16,32,512]{2,1,0:T(8,128)(2,1)S(1)} async-done(((bf16[16,32,512]{2,1,0:T(8,128)(2,1)}), bf16[16,32,512]{2,1,0:T(8,128)(2,1)S(1)}, u32[]{:S(2)}, u32[]{:S(2)}) %all-to-all-start.3) | async-done | bytes 524320 | tf_op jit(solution)/shard_map/all_to_all | solution.py:704
  106.2 1.0 pad_maximum_fusion.1
  107.7 1.0 pad_maximum_fusion
  (33 shorter events, 1.6 us)
Async XLA Ops:
  0.6 3.4 %copy-start = (bf16[24,32,512]{2,1,0:T(8,128)(2,1)S(1)}, bf16[24,32,512]{2,1,0:T(8,128)(2,1)}, u32[]{:S(2)}) copy-start(bf16[24,32,512]{2,1,0:T(8,128)(2,1)} %cotangent_ref.3) | copy-start | bytes 2359300
  0.6 15.9 %copy-start.3 = (bf16[9,2048]{1,0:T(8,128)(2,1)S(1)}, bf16[9,2048]{1,0:T(8,128)(2,1)}, u32[]{:S(2)}) copy-start(bf16[9,2048]{1,0:T(8,128)(2,1)} %taps_ref.3) | copy-start | bytes 110596
  0.7 3.4 %collective-permute-start.2 = (bf16[24,32,512]{2,1,0:T(8,128)(2,1)}, bf16[24,32,512]{2,1,0:T(8,128)(2,1)S(1)}, u32[]{:S(2)}, u32[]{:S(2)}) collective-permute-start(bf16[24,32,512]{2,1,0:T(8,128)(2,1)} %cotangent_ref.3), channel_id=1, source_target_pairs={{0,1},{1,0},{2,3},{3,2},{4,5},{5,4},{6,7},{7,6},{8,9},{9,8},{10,11... | collective-permute-start | bytes 2359304 | tf_op jit(solution)/shard_map/ppermute | solution.py:711
  1.2 15.4 %collective-permute-start = (bf16[24,32,512]{2,1,0:T(8,128)(2,1)}, bf16[24,32,512]{2,1,0:T(8,128)(2,1)S(1)}, u32[]{:S(2)}, u32[]{:S(2)}) collective-permute-start(bf16[24,32,512]{2,1,0:T(8,128)(2,1)} %features_ref.3), channel_id=1, source_target_pairs={{0,1},{1,0},{2,3},{3,2},{4,5},{5,4},{6,7},{7,6},{8,9},{9,8},{10,11... | collective-permute-start | bytes 2359304 | tf_op jit(solution)/shard_map/ppermute | solution.py:711
  1.2 0.7 copy-start.4
  1.9 14.7 %copy-start.5 = (s32[16]{0:T(128)S(1)}, s32[16]{0:T(128)}, u32[]{:S(2)}) copy-start(s32[16]{0:T(128)} %bands_ref.7) | copy-start | bytes 196
  3.3 2.1 %collective-permute-start.1 = (bf16[3,32,512]{2,1,0:T(8,128)(2,1)S(1)}, bf16[3,32,512]{2,1,0:T(8,128)(2,1)S(1)}, u32[]{:S(2)}, u32[]{:S(2)}) collective-permute-start(bf16[3,32,512]{2,1,0:T(8,128)(2,1)S(1)} %rim_rows.1), channel_id=1, source_target_pairs={{1,2},{3,4},{5,6},{7,8},{9,10},{11,12},{13,14},{2,1},{4,3},{6,5},{... | collective-permute-start | bytes 294920 | tf_op jit(solution)/shard_map/ppermute | solution.py:717
  4.0 26.6 %copy-start.1 = (bf16[24,32,512]{2,1,0:T(8,128)(2,1)}, bf16[24,32,512]{2,1,0:T(8,128)(2,1)S(1)}, u32[]{:S(2)}) copy-start(bf16[24,32,512]{2,1,0:T(8,128)(2,1)S(1)} %collective-permute-done.2.other_ref) | copy-start | bytes 2359300
  5.4 25.2 %copy-start.2 = (bf16[3,32,512]{2,1,0:T(8,128)(2,1)}, bf16[3,32,512]{2,1,0:T(8,128)(2,1)S(1)}, u32[]{:S(2)}) copy-start(bf16[3,32,512]{2,1,0:T(8,128)(2,1)S(1)} %collective-permute-done.1.rim_ref) | copy-start | bytes 294916
  5.4 25.9 %all-to-all-start = ((bf16[16,32,512]{2,1,0:T(8,128)(2,1)}), bf16[16,32,512]{2,1,0:T(8,128)(2,1)S(1)}, u32[]{:S(2)}, u32[]{:S(2)}) async-start(bf16[16,32,512]{2,1,0:T(8,128)(2,1)} %even_rows.1.grad_slab_ref), calls=%async_computation | async-start | bytes 1048576 | tf_op jit(solution)/shard_map/all_to_all | solution.py:704
  31.4 13.0 %copy-start.7 = (bf16[16,32,512]{2,1,0:T(8,128)(2,1)}, bf16[16,32,512]{2,1,0:T(8,128)(2,1)S(1)}, u32[]{:S(2)}) copy-start(bf16[16,32,512]{2,1,0:T(8,128)(2,1)S(1)} %all-to-all-done) | copy-start | bytes 1572868
  31.4 19.5 %all-to-all-start.1 = ((bf16[16,32,512]{2,1,0:T(8,128)(2,1)}), bf16[16,32,512]{2,1,0:T(8,128)(2,1)S(1)}, u32[]{:S(2)}, u32[]{:S(2)}) async-start(bf16[16,32,512]{2,1,0:T(8,128)(2,1)} %get-tuple-element.34), calls=%async_computation.1 | async-start | bytes 1048576 | tf_op jit(solution)/shard_map/all_to_all | solution.py:704
  63.6 18.1 %all-to-all-start.2 = ((bf16[16,32,512]{2,1,0:T(8,128)(2,1)}), bf16[16,32,512]{2,1,0:T(8,128)(2,1)S(1)}, u32[]{:S(2)}, u32[]{:S(2)}) async-start(bf16[16,32,512]{2,1,0:T(8,128)(2,1)} %bitcast.10), calls=%async_computation.2 | async-start | bytes 1048576 | tf_op jit(solution)/shard_map/all_to_all | solution.py:704
  81.7 10.2 %copy-start.6 = (bf16[16,32,512]{2,1,0:T(8,128)(2,1)}, bf16[16,32,512]{2,1,0:T(8,128)(2,1)S(1)}, u32[]{:S(2)}) copy-start(bf16[16,32,512]{2,1,0:T(8,128)(2,1)S(1)} %all-to-all-done.2.grad_ref) | copy-start | bytes 1572868
  81.7 1.3 %collective-permute-start.3 = (bf16[1,32,512]{2,1,0:T(8,128)(2,1)S(1)}, bf16[1,32,512]{2,1,0:T(8,128)(2,1)S(1)}, u32[]{:S(2)}, u32[]{:S(2)}) collective-permute-start(bf16[1,32,512]{2,1,0:T(8,128)(2,1)S(1)} %get-tuple-element.61), channel_id=1, source_target_pairs={{0,1},{1,0},{2,3},{3,2},{4,5},{5,4},{6,7},{7,6},{8,9},{9,8},{10,11... | collective-permute-start | bytes 98312 | tf_op jit(solution)/shard_map/ppermute | solution.py:711
  81.8 1.2 %collective-permute-start.4 = (bf16[1,32,512]{2,1,0:T(8,128)(2,1)S(1)}, bf16[1,32,512]{2,1,0:T(8,128)(2,1)S(1)}, u32[]{:S(2)}, u32[]{:S(2)}) collective-permute-start(bf16[1,32,512]{2,1,0:T(8,128)(2,1)S(1)} %get-tuple-element.60), channel_id=1, source_target_pairs={{1,2},{3,4},{5,6},{7,8},{9,10},{11,12},{13,14},{2,1},{4,3},{6,5},{... | collective-permute-start | bytes 98312 | tf_op jit(solution)/shard_map/ppermute | solution.py:717
  83.0 22.9 %all-to-all-start.3 = ((bf16[16,32,512]{2,1,0:T(8,128)(2,1)}), bf16[16,32,512]{2,1,0:T(8,128)(2,1)S(1)}, u32[]{:S(2)}, u32[]{:S(2)}) async-start(bf16[16,32,512]{2,1,0:T(8,128)(2,1)} %bitcast.7), calls=%async_computation.3 | async-start | bytes 1048576 | tf_op jit(solution)/shard_map/all_to_all | solution.py:704
  91.9 13.9 %copy-start.8 = (f32[512,512]{1,0:T(8,128)S(1)}, f32[512,512]{1,0:T(8,128)}, u32[]{:S(2)}) copy-start(f32[512,512]{1,0:T(8,128)} %get-tuple-element.29) | copy-start | bytes 3145732
  102.8 3.3 %collective-permute-start.6 = (bf16[8,32,512]{2,1,0:T(8,128)(2,1)S(1)}, bf16[8,32,512]{2,1,0:T(8,128)(2,1)S(1)}, u32[]{:S(2)}, u32[]{:S(2)}) collective-permute-start(bf16[8,32,512]{2,1,0:T(8,128)(2,1)S(1)} %slice_select_fusion), channel_id=1, source_target_pairs={{0,1},{1,0},{2,3},{3,2},{4,5},{5,4},{6,7},{7,6},{8,9},{9,8},{10,11... | collective-permute-start | bytes 786440 | tf_op jit(solution)/shard_map/ppermute | solution.py:711
  106.1 1.6 %collective-permute-start.5 = (bf16[8,32,512]{2,1,0:T(8,128)(2,1)S(1)}, bf16[8,32,512]{2,1,0:T(8,128)(2,1)S(1)}, u32[]{:S(2)}, u32[]{:S(2)}) collective-permute-start(bf16[8,32,512]{2,1,0:T(8,128)(2,1)S(1)} %broadcast_select_fusion), channel_id=1, source_target_pairs={{0,1},{1,0},{2,3},{3,2},{4,5},{5,4},{6,7},{7,6},{8,9},{9,8},{10,11... | collective-permute-start | bytes 786440 | tf_op jit(solution)/shard_map/ppermute | solution.py:711

commit v12 on v11

--- a/solution.py
+++ b/solution.py
@@ -242,7 +242,7 @@
                         at = slice(start + lane, start + lane + LANES)
                         hidden[row + inner, :, at] = gelu(values).astype(BF16).astype(F32)
                         if RIM <= row + inner < RIM + own:
-                            expanded[row + inner - RIM, :, chunk_lanes(index, start + lane, LANES)] = values
+                            expanded[row + inner - RIM, :, chunk_lanes(index, start + lane, LANES)] = values.astype(BF16)
         store_expanded(index).start()
 
         for lane in range(0, CHUNK, LANES):
@@ -255,7 +255,7 @@
                 ]
                 values = column_sums(sums[0], sums[1], sums[2], column, cols - 1)
                 hidden_two[row * cols : (row + 1) * cols, lanes] = gelu(values).astype(BF16)
-                mixed[row, :, chunk_lanes(index, lane, LANES)] = values
+                mixed[row, :, chunk_lanes(index, lane, LANES)] = values.astype(BF16)
         store_mixed(index).start()
         fetch_project(index).wait()
         total[...] += nn_dot(hidden_two[...], project[chunk_lanes(index), :])
@@ -266,17 +266,22 @@
         first = total[row * cols : (row + 1) * cols]
         normed[row - 1] = (first * rms_scale(first)).astype(BF16)
     store_normed = pltpu.make_async_copy(normed, normed_ref, out_sems.at[1])
-    store_first = pltpu.make_async_copy(total, first_ref, out_sems.at[2])
-    store_own = pltpu.make_async_copy(total.at[pl.ds(cols, own * cols)], own_first_ref, out_sems.at[3])
+    store_above = pltpu.make_async_copy(total.at[pl.ds(0, cols)], first_ref.at[pl.ds(0, cols)], out_sems.at[2])
+    store_below = pltpu.make_async_copy(
+        total.at[pl.ds((own + 1) * cols, cols)], first_ref.at[pl.ds(cols, cols)], out_sems.at[3]
+    )
+    store_own = pltpu.make_async_copy(total.at[pl.ds(cols, own * cols)], own_first_ref, out_sems.at[4])
     store_normed.start()
-    store_first.start()
+    store_above.start()
+    store_below.start()
     store_own.start()
     for index in range(chunks):
         store_expanded(index).wait()
         store_mixed(index).wait()
     store_slab.wait()
     store_normed.wait()
-    store_first.wait()
+    store_above.wait()
+    store_below.wait()
     store_own.wait()
 
 
@@ -290,30 +295,30 @@
         in_specs=[in_scalars(), in_hbm(), in_vmem(), in_vmem(), in_hbm(), in_vmem(), in_hbm()],
         out_specs=[in_hbm()] * 6,
         out_shape=[
-            pltpu.HBM(((rows - 2) * cols, width), F32),
+            pltpu.HBM((2 * cols, width), F32),
             pltpu.HBM((own * cols, width), F32),
             pltpu.HBM((own, cols, width), BF16),
             pltpu.HBM((own, cols, width), BF16),
-            pltpu.HBM((own, cols, hidden_width), F32),
-            pltpu.HBM((rows - 2, cols, hidden_width), F32),
+            pltpu.HBM((own, cols, hidden_width), BF16),
+            pltpu.HBM((rows - 2, cols, hidden_width), BF16),
         ],
         scratch_shapes=[
             pltpu.VMEM((rows, cols, width), BF16),
             pltpu.VMEM((rows * cols, width), BF16),
             pltpu.VMEM((width, hidden_width), BF16),
             pltpu.VMEM((hidden_width, width), BF16),
-            pltpu.VMEM((own, cols, hidden_width), F32),
+            pltpu.VMEM((own, cols, hidden_width), BF16),
             pltpu.VMEM((rows, cols, CHUNK), F32),
-            pltpu.VMEM((rows - 2, cols, hidden_width), F32),
+            pltpu.VMEM((rows - 2, cols, hidden_width), BF16),
             pltpu.VMEM(((rows - 2) * cols, CHUNK), BF16),
             pltpu.VMEM(((rows - 2) * cols, width), F32),
             pltpu.VMEM((own, cols, width), BF16),
             pltpu.SemaphoreType.DMA((4,)),
             pltpu.SemaphoreType.DMA((2, chunks)),
             pltpu.SemaphoreType.DMA((2, chunks)),
-            pltpu.SemaphoreType.DMA((4,)),
+            pltpu.SemaphoreType.DMA((5,)),
         ],
-        compiler_params=params(28),
+        compiler_params=params(24),
         cost_estimate=pl.CostEstimate(
             flops=4 * rows * cols * width * hidden_width,
             bytes_accessed=12 * 1024 * 1024,
@@ -329,7 +334,7 @@
         for row in range(rows):
             for lane in range(0, chunk, LANES):
                 lanes = slice(lane, lane + LANES)
-                target[row, :, lanes] = gelu_slope(source[row, :, lanes]).astype(BF16)
+                target[row, :, lanes] = gelu_slope(source[row, :, lanes].astype(F32)).astype(BF16)
 
 
 def slopes(expanded, mixed):
@@ -415,12 +420,13 @@
     )(cotangent, w_out)
 
 
-def per_query(values, weights, span, head_dim):
+def per_query(values, weights, span, head_dim, scale=1.0):
     wide = nn_dot(values.T, weights)
     half = LANES // 2
-    own = jnp.concatenate([wide[:half, :LANES], wide[half:, LANES:]], axis=0).T
+    own = jnp.concatenate([wide[:half, :LANES], wide[half:, LANES:]], axis=0) * scale
+    own = own.astype(BF16).T
     lane_head = lax.broadcasted_iota(jnp.int32, (span, LANES), 1) // head_dim
-    return jnp.where(lane_head % 2 == 0, own[:span], own[span:])
+    return jnp.where(lane_head % 2 == 0, own[:span].astype(F32), own[span:].astype(F32)).astype(BF16)
 
 
 def attention_body(normed_ref, grad_attended_ref, qkv_ref, grad_ref, weights_ref, values_ref, rows_wide,
@@ -468,7 +474,7 @@
             grad_weights = nt_dot(v, g_wide)
             row_dot = jnp.sum(shares * grad_weights, axis=0, keepdims=True)
             grad_scores = (shares * (grad_weights - row_dot)).astype(BF16)
-            grad_projected[rows, q_at] = (per_query(k, grad_scores, span, head_dim) * scale).astype(BF16)
+            grad_projected[rows, q_at] = per_query(k, grad_scores, span, head_dim, scale)
             grad_projected[rows, k_at] = (nn_dot(grad_scores, q_wide) * scale).astype(BF16)
             grad_projected[rows, v_at] = nn_dot(half, g_wide).astype(BF16)
         return carry
@@ -524,7 +530,7 @@
         rows = slice(index * span, (index + 1) * span)
         for part, lanes in enumerate(lane_tiles(width)):
             weights = weights_ref[index, :, part * heads * span : (part + 1) * heads * span]
-            attended[rows, lanes] = per_query(values_ref[rows, lanes], weights, span, width // HEADS).astype(BF16)
+            attended[rows, lanes] = per_query(values_ref[rows, lanes], weights, span, width // HEADS)
     to_rows(nn_dot(attended[...], out_ref[...]), rows_wide, added_ref)
 
 
@@ -544,9 +550,9 @@
     )(weights, values, w_out)
 
 
-def backward_body(bands_ref, cotangent_ref, other_ref, rim_ref, slab_ref, first_ref, grad_slab_ref, grad_ref,
-                  pair_ref, next_ref, slope_one_ref, slope_two_ref, expand_ref, taps_ref, project_ref,
-                  out_ref, rims, slab, first, grad_slab, grad_in, slope_one, slope_two, expand, project,
+def backward_body(bands_ref, cotangent_ref, other_ref, rim_ref, slab_ref, first_ref, edges_ref, grad_slab_ref,
+                  grad_ref, pair_ref, next_ref, slope_one_ref, slope_two_ref, expand_ref, taps_ref, project_ref,
+                  out_ref, rims, slab, first, edges, grad_slab, grad_in, slope_one, slope_two, expand, project,
                   grad_first, grad_rows, mixed, expanded, total, row_sems,
                   in_sems, chunk_sems):
     own, cols, width = slab.shape
@@ -559,7 +565,7 @@
     inputs = [
         pltpu.make_async_copy(source, target, in_sems.at[index])
         for index, (source, target) in enumerate(
-            ((first_ref, first), (grad_ref, grad_in), (grad_slab_ref, grad_slab), (slab_ref, slab))
+            ((first_ref, first), (grad_ref, grad_in), (grad_slab_ref, grad_slab), (edges_ref, edges), (slab_ref, slab))
         )
     ]
     for copy in inputs:
@@ -588,12 +594,12 @@
         inner = jnp.mean(grad * normed, -1, keepdims=True)
         return cotangent.astype(F32) + rms * (grad - normed * inner)
 
-    for copy in inputs[:3]:
+    for copy in inputs[:4]:
         copy.wait()
     for row in range(own):
-        below = first[(row + 1) * cols : (row + 2) * cols]
-        result = through_norm(grad_slab[row], grad_in[row], below)
-        grad_first[row * cols : (row + 1) * cols] = result
+        at = slice(row * cols, (row + 1) * cols)
+        result = through_norm(grad_slab[row], grad_in[row], first[at])
+        grad_first[at] = result
         grad_rows[(row + 1) * cols : (row + 2) * cols] = result.astype(BF16)
     for side, place_first in sides:
         wait_pull(sources, 1, rims.at[pl.ds(side, 1)], row_sems.at[side])
@@ -601,8 +607,8 @@
     above = jnp.where(leads, next_ref[0].astype(F32), pair_ref[0].astype(F32))
     below = jnp.where(leads, pair_ref[0].astype(F32), next_ref[0].astype(F32))
     last = (own + 1) * cols
-    grad_rows[0:cols] = through_norm(rims[0], above, first[0:cols]).astype(BF16)
-    grad_rows[last:] = through_norm(rims[1], below, first[last:]).astype(BF16)
+    grad_rows[0:cols] = through_norm(rims[0], above, edges[:cols]).astype(BF16)
+    grad_rows[last:] = through_norm(rims[1], below, edges[cols:]).astype(BF16)
     column = lax.broadcasted_iota(jnp.int32, (cols, LANES), 0)
 
     total[...] = jnp.zeros_like(total)
@@ -642,7 +648,7 @@
         return carry
 
     lax.fori_loop(0, chunks, step, 0)
-    inputs[3].wait()
+    inputs[4].wait()
     for row in range(own):
         at = slice(row * cols, (row + 1) * cols)
         values = slab[row].astype(F32)
@@ -653,20 +659,21 @@
         out_ref[row] = (grad_first[at] + rms * (grad - normed * inner)).astype(BF16)
 
 
-def backward(bands, cotangent, other, rim, slab, first, grad_slab, grad, pair_row, next_row, slope_one,
+def backward(bands, cotangent, other, rim, slab, first, edges, grad_slab, grad, pair_row, next_row, slope_one,
              slope_two, w_expand, kernel, w_project):
     own, cols, width = slab.shape
     hidden_width = w_expand.shape[1]
     chunks = hidden_width // CHUNK
     return pl.pallas_call(
         backward_body,
-        in_specs=[in_scalars()] + [in_hbm()] * 7 + [in_vmem()] * 2 + [in_hbm()] * 3 + [in_vmem(), in_hbm()],
+        in_specs=[in_scalars()] + [in_hbm()] * 8 + [in_vmem()] * 2 + [in_hbm()] * 3 + [in_vmem(), in_hbm()],
         out_specs=in_vmem(),
         out_shape=jax.ShapeDtypeStruct((own, cols, width), BF16),
         scratch_shapes=[
             pltpu.VMEM((2, cols, width), BF16),
             pltpu.VMEM((own, cols, width), BF16),
-            pltpu.VMEM(((own + 2) * cols, width), F32),
+            pltpu.VMEM((own * cols, width), F32),
+            pltpu.VMEM((2 * cols, width), F32),
             pltpu.VMEM((own, cols, width), BF16),
             pltpu.VMEM((own, cols, width), BF16),
             pltpu.VMEM((own, cols, hidden_width), BF16),
@@ -679,7 +686,7 @@
             pltpu.VMEM((own * cols, CHUNK), BF16),
             pltpu.VMEM((own * cols, width), F32),
             pltpu.SemaphoreType.DMA((2,)),
-            pltpu.SemaphoreType.DMA((4,)),
+            pltpu.SemaphoreType.DMA((5,)),
             pltpu.SemaphoreType.DMA((4, chunks)),
         ],
         compiler_params=params(26),
@@ -689,7 +696,7 @@
             transcendentals=0,
         ),
         name="bottleneck_backward",
-    )(bands, held(cotangent), held(other), held(rim), held(slab), held(first), held(grad_slab), held(grad),
+    )(bands, held(cotangent), held(other), held(rim), held(slab), held(first), held(edges), held(grad_slab), held(grad),
       near(pair_row), near(next_row), held(slope_one), held(slope_two), held(w_expand), near(kernel),
       held(w_project))
 
@@ -741,7 +748,7 @@
     rim, grad_slab = lax.optimization_barrier((rim, grad_slab))
 
     grad_windows = exchange_windows(grad_slab)
-    first, own_first, normed, slab, expanded, mixed = forward(
+    edges, first, normed, slab, expanded, mixed = forward(
         row_bands, features, other_features, rim, w_expand, kernel, w_project
     )
     normed, grad_windows = lax.optimization_barrier((normed, grad_windows))
@@ -755,14 +762,15 @@
     grad_normed, weights, values = attention(normed_windows.reshape(shape), grad_attended, w_qkv)
     grad_rows = exchange_windows(grad_normed.reshape(GRID_ROWS, cols, width))
     added = attend(weights, values, w_out, shape)
-    grad_rows, added = lax.optimization_barrier((grad_rows, added))
+    leader_share = BAND * row_bands[device - parity]
+    grad_rows, added, leader_share = lax.optimization_barrier((grad_rows, added, leader_share))
     top, bottom = grad_rows[:1], grad_rows[GRID_ROWS - 1 :]
     pair_row = swap_pair(jnp.where(leads, bottom, top))
     next_row = swap_next(jnp.where(leads, top, bottom))
     added, pair_row, next_row = lax.optimization_barrier((added, pair_row, next_row))
     added_rows = exchange_windows(added.reshape(GRID_ROWS, cols, width))
     grad_input = backward(
-        row_bands, cotangent, other_cotangent, rim, slab, first, grad_slab, grad_rows, pair_row, next_row,
+        row_bands, cotangent, other_cotangent, rim, slab, first, edges, grad_slab, grad_rows, pair_row, next_row,
         slope_one, slope_two, w_expand, kernel, w_project,
     )
     def sent(rows):
@@ -770,9 +778,8 @@
 
     other_grad = swap_pair(sent(grad_input))
     grad_input, added_rows = lax.optimization_barrier((grad_input, added_rows))
-    final = (own_first.reshape(GRID_ROWS, cols, width) + added_rows.astype(F32)).astype(BF16)
+    final = (first.reshape(GRID_ROWS, cols, width) + added_rows.astype(F32)).astype(BF16)
     other_final = swap_pair(sent(final))
-    leader_share = BAND * row_bands[device - parity]
     return (
         place_rows(final, other_final, leads, leader_share),
         place_rows(grad_input, other_grad, leads, leader_share),

time: 109 us -> 109 us (level)
  no operation moved by 1% of the time
where the time goes in v12:
time: 109 us
  Pallas kernels  53.4 us (49%)
  starting transfers between devices  30.2 us (28%)
  waiting for transfers between devices  19.9 us (18%)
  other arithmetic  2.29 us (2%)
  between operations  1.47 us (1%)
  local copies, waits for them, and re-layouts  1.29 us (1%)
    all_to_all x4, starting transfers between devices, exchange_windows(): lax.all_to_all(rows, 'row', split_axis=0, concat_axis=0, tiled=True, axis...  27.5 us
    all_to_all x4, waiting for transfers between devices, exchange_windows(): lax.all_to_all(rows, 'row', split_axis=0, concat_axis=0, tiled=True, axis...  18.9 us
    pallas_call x1, Pallas kernels, forward(): pl.pallas_call(forward_body, in_specs=[in_scalars(), in_hbm(), in_vmem(),...  13.9 us
    pallas_call x1, Pallas kernels, attention(): pl.pallas_call(attention_body, in_specs=[in_vmem(), in_hbm(), in_hbm()],...  12.6 us
    pallas_call x1, Pallas kernels, backward(): pl.pallas_call(backward_body, in_specs=[in_scalars()] + [in_hbm()] * 8 +...  10.8 us
    pallas_call x1, Pallas kernels, slopes(): pl.pallas_call(slopes_body, grid=(hidden_width // CHUNK,), in_specs=block...  7.1 us
    pallas_call x1, Pallas kernels, attend(): pl.pallas_call(attended_body, grid=(1,), in_specs=[whole(weights.shape),...  3.52 us
    pallas_call x1, Pallas kernels, attended_gradient(): pl.pallas_call(grad_attended_body, grid=(1,), in_specs=[whole(cotangent.s...  2.57 us
  transfers between devices with their start and end apart: 11, of which 6 were waited for; matrix products, arithmetic and copies ran while one was open for 2% of the time, Pallas kernels for 38%

profile of v12, /device:TPU:0, one launch (start us, length us, event | category | flops | bytes accessed | tf_op | source)
XLA Modules:
  0.0 108.5 jit_solution(16823807852266872920)
XLA Ops:
  1.3 0.7 copy-done.4
  1.9 1.4 %rim_rows.1 = bf16[3,32,512]{2,1,0:T(8,128)(2,1)S(1)} custom-call(s32[16]{0:T(128)S(1)} %copy-done.4, bf16[24,32,512]{2,1,0:T(8,128)(2,1)} %features_ref.3, bf16[24,32,512]{2,1,0:T(8,128)(2,1)} %cotangent_ref.3), custom_call_target="tpu_custom_call" | custom-call | tf_op jit(solution)/shard_map/rim_rows/pallas_call | solution.py:158
  3.3 0.7 collective-permute-start.1
  4.0 1.4 %even_rows.1.grad_slab_ref = bf16[16,32,512]{2,1,0:T(8,128)(2,1)} custom-call(s32[16]{0:T(128)S(1)} %copy-done.4, bf16[24,32,512]{2,1,0:T(8,128)(2,1)S(1)} %copy-done, bf16[24,32,512]{2,1,0:T(8,128)(2,1)S(1)} %collective-permute-done.2.other_ref), custom_call_target="tpu_custom_call" | custom-call | tf_op jit(solution)/shard_map/even_rows/pallas_call | solution.py:129
  5.5 11.1 %all-to-all-start = ((bf16[16,32,512]{2,1,0:T(8,128)(2,1)}), bf16[16,32,512]{2,1,0:T(8,128)(2,1)S(1)}, u32[]{:S(2)}, u32[]{:S(2)}) async-start(bf16[16,32,512]{2,1,0:T(8,128)(2,1)} %even_rows.1.grad_slab_ref), calls=%async_computation | async-start | bytes 1048576 | tf_op jit(solution)/shard_map/all_to_all | solution.py:711
  16.6 13.9 %bottleneck_forward.1 = (f32[64,512]{1,0:T(8,128)}, f32[512,512]{1,0:T(8,128)}, bf16[16,32,512]{2,1,0:T(8,128)(2,1)}, bf16[16,32,512]{2,1,0:T(8,128)(2,1)}, bf16...) custom-call(s32[16]{0:T(128)S(1)} %copy-done.5, bf16[24,32,512]{2,1,0:T(8,128)(2,1)} %features_ref.3, ...), custom_call_target="tpu_custom_call" | custom-call | flops 2684354560 | bytes 12582912 | tf_op jit(solution)/shard_map/bottleneck_forward/pallas_call | solution.py:293
  30.6 0.8 all-to-all-done
  31.4 5.1 %all-to-all-start.1 = ((bf16[16,32,512]{2,1,0:T(8,128)(2,1)}), bf16[16,32,512]{2,1,0:T(8,128)(2,1)S(1)}, u32[]{:S(2)}, u32[]{:S(2)}) async-start(bf16[16,32,512]{2,1,0:T(8,128)(2,1)} %get-tuple-element.32), calls=%async_computation.1 | async-start | bytes 1048576 | tf_op jit(solution)/shard_map/all_to_all | solution.py:711
  36.5 7.1 %gelu_slopes.1 = (bf16[16,32,2048]{2,1,0:T(8,128)(2,1)}, bf16[18,32,2048]{2,1,0:T(8,128)(2,1)}) custom-call(bf16[16,32,2048]{2,1,0:T(8,128)(2,1)} %get-tuple-element.33.expanded_ref, bf16[18,32,2048]{2,1,0:T(8,128)(2,1)} %get-tuple-element.34.mixed_ref), custom_call_target="tpu_custom_call" | custom-call | flops 33423360 | bytes 13369344 | tf_op jit(solution)/shard_map/gelu_slopes/pallas_call | solution.py:345
  43.6 2.6 %attended_gradient.1.grad_attended_ref = bf16[512,512]{1,0:T(8,128)(2,1)} custom-call(bf16[8,2,32,512]{3,2,1,0:T(8,128)(2,1)} %bitcast.9, bf16[512,512]{1,0:T(8,128)(2,1)} %out_ref.3), custom_call_target="tpu_custom_call" | custom-call | flops 268435456 | bytes 2097152 | tf_op jit(solution)/shard_map/attended_gradient/pallas_call | solution.py:408
  46.2 4.6 %all-to-all-done.1 = bf16[16,32,512]{2,1,0:T(8,128)(2,1)S(1)} async-done(((bf16[16,32,512]{2,1,0:T(8,128)(2,1)}), bf16[16,32,512]{2,1,0:T(8,128)(2,1)S(1)}, u32[]{:S(2)}, u32[]{:S(2)}) %all-to-all-start.1) | async-done | bytes 524320 | tf_op jit(solution)/shard_map/all_to_all | solution.py:711
  50.8 12.6 %window_attention.1 = (bf16[8,2,32,512]{3,2,1,0:T(8,128)(2,1)}, bf16[8,64,1024]{2,1,0:T(8,128)(2,1)}, bf16[512,512]{1,0:T(8,128)(2,1)}) custom-call(bf16[8,2,32,512]{3,2,1,0:T(8,128)(2,1)S(1)} %bitcast.6, bf16[512,512]{1,0:T(8,128)(2,1)} %attended_gradient.1.grad_attended_ref, bf16[512,1536]{1,0:T(8,128)(2,1)} %qkv_ref.1), custom_call_target="tpu_custom_call" | custom-call | flops 2147483648 | bytes 4194304 | tf_op jit(solution)/shard_map/window_attention/pallas_call | solution.py:498
  63.4 3.6 %all-to-all-start.2 = ((bf16[16,32,512]{2,1,0:T(8,128)(2,1)}), bf16[16,32,512]{2,1,0:T(8,128)(2,1)S(1)}, u32[]{:S(2)}, u32[]{:S(2)}) async-start(bf16[16,32,512]{2,1,0:T(8,128)(2,1)} %bitcast.10), calls=%async_computation.2 | async-start | bytes 1048576 | tf_op jit(solution)/shard_map/all_to_all | solution.py:711
  67.0 0.6 dynamic_slice.3
  68.3 3.5 %attended_output.1 = bf16[8,2,32,512]{3,2,1,0:T(8,128)(2,1)} custom-call(bf16[8,64,1024]{2,1,0:T(8,128)(2,1)} %get-tuple-element.41.weights_ref, bf16[512,512]{1,0:T(8,128)(2,1)} %get-tuple-element.42.values_ref, bf16[512,512]{1,0:T(8,128)(2,1)} %out_ref.3), custom_call_target="tpu_custom_call" | custom-call | flops 536870912 | bytes 3145728 | tf_op jit(solution)/shard_map/attended_output/pallas_call | solution.py:538
  71.8 9.7 %all-to-all-done.2.grad_ref = bf16[16,32,512]{2,1,0:T(8,128)(2,1)S(1)} async-done(((bf16[16,32,512]{2,1,0:T(8,128)(2,1)}), bf16[16,32,512]{2,1,0:T(8,128)(2,1)S(1)}, u32[]{:S(2)}, u32[]{:S(2)}) %all-to-all-start.2) | async-done | bytes 524320 | tf_op jit(solution)/shard_map/all_to_all | solution.py:711
  81.6 0.7 collective-permute-start.4
  82.3 0.5 collective-permute-done.3.pair_ref
  82.8 7.7 %all-to-all-start.3 = ((bf16[16,32,512]{2,1,0:T(8,128)(2,1)}), bf16[16,32,512]{2,1,0:T(8,128)(2,1)S(1)}, u32[]{:S(2)}, u32[]{:S(2)}) async-start(bf16[16,32,512]{2,1,0:T(8,128)(2,1)} %bitcast.8), calls=%async_computation.3 | async-start | bytes 1048576 | tf_op jit(solution)/shard_map/all_to_all | solution.py:711
  90.5 10.8 %bottleneck_backward.1 = bf16[16,32,512]{2,1,0:T(8,128)(2,1)S(1)} custom-call(s32[16]{0:T(128)S(1)} %copy-done.5, bf16[24,32,512]{2,1,0:T(8,128)(2,1)} %cotangent_ref.3, bf16[24,32,512]{2,1,0:T(8,128)(2,1)} %copy-done.1, bf16[3,32,512]{2,1,0:T(8,128)(2,1)} %copy-done.2, bf16[16,32,512]{2,1,0:T(8,128)(2,1)} %get-tuple-element.45.slab_ref, ...), custom_call_target="tpu_custom_call" | custom-call | flops 2415919104 | bytes 12582912 | tf_op jit(solution)/shard_map/bottleneck_backward/pallas_call | solution.py:667
  101.4 0.6 collective-permute-start.6
  102.0 3.7 %all-to-all-done.3 = bf16[16,32,512]{2,1,0:T(8,128)(2,1)S(1)} async-done(((bf16[16,32,512]{2,1,0:T(8,128)(2,1)}), bf16[16,32,512]{2,1,0:T(8,128)(2,1)S(1)}, u32[]{:S(2)}, u32[]{:S(2)}) %all-to-all-start.3) | async-done | bytes 524320 | tf_op jit(solution)/shard_map/all_to_all | solution.py:711
  106.1 1.0 pad_maximum_fusion.1
  107.6 1.0 pad_maximum_fusion
  (33 shorter events, 1.6 us)
Async XLA Ops:
  0.6 3.4 %copy-start = (bf16[24,32,512]{2,1,0:T(8,128)(2,1)S(1)}, bf16[24,32,512]{2,1,0:T(8,128)(2,1)}, u32[]{:S(2)}) copy-start(bf16[24,32,512]{2,1,0:T(8,128)(2,1)} %cotangent_ref.3) | copy-start | bytes 2359300
  0.6 15.9 %copy-start.3 = (bf16[9,2048]{1,0:T(8,128)(2,1)S(1)}, bf16[9,2048]{1,0:T(8,128)(2,1)}, u32[]{:S(2)}) copy-start(bf16[9,2048]{1,0:T(8,128)(2,1)} %taps_ref.3) | copy-start | bytes 110596
  0.7 3.4 %collective-permute-start.2 = (bf16[24,32,512]{2,1,0:T(8,128)(2,1)}, bf16[24,32,512]{2,1,0:T(8,128)(2,1)S(1)}, u32[]{:S(2)}, u32[]{:S(2)}) collective-permute-start(bf16[24,32,512]{2,1,0:T(8,128)(2,1)} %cotangent_ref.3), channel_id=1, source_target_pairs={{0,1},{1,0},{2,3},{3,2},{4,5},{5,4},{6,7},{7,6},{8,9},{9,8},{10,11... | collective-permute-start | bytes 2359304 | tf_op jit(solution)/shard_map/ppermute | solution.py:718
  1.2 15.4 %collective-permute-start = (bf16[24,32,512]{2,1,0:T(8,128)(2,1)}, bf16[24,32,512]{2,1,0:T(8,128)(2,1)S(1)}, u32[]{:S(2)}, u32[]{:S(2)}) collective-permute-start(bf16[24,32,512]{2,1,0:T(8,128)(2,1)} %features_ref.3), channel_id=1, source_target_pairs={{0,1},{1,0},{2,3},{3,2},{4,5},{5,4},{6,7},{7,6},{8,9},{9,8},{10,11... | collective-permute-start | bytes 2359304 | tf_op jit(solution)/shard_map/ppermute | solution.py:718
  1.2 0.7 copy-start.4
  1.9 14.7 %copy-start.5 = (s32[16]{0:T(128)S(1)}, s32[16]{0:T(128)}, u32[]{:S(2)}) copy-start(s32[16]{0:T(128)} %bands_ref.7) | copy-start | bytes 196
  3.3 2.2 %collective-permute-start.1 = (bf16[3,32,512]{2,1,0:T(8,128)(2,1)S(1)}, bf16[3,32,512]{2,1,0:T(8,128)(2,1)S(1)}, u32[]{:S(2)}, u32[]{:S(2)}) collective-permute-start(bf16[3,32,512]{2,1,0:T(8,128)(2,1)S(1)} %rim_rows.1), channel_id=1, source_target_pairs={{1,2},{3,4},{5,6},{7,8},{9,10},{11,12},{13,14},{2,1},{4,3},{6,5},{... | collective-permute-start | bytes 294920 | tf_op jit(solution)/shard_map/ppermute | solution.py:724
  4.0 26.5 %copy-start.1 = (bf16[24,32,512]{2,1,0:T(8,128)(2,1)}, bf16[24,32,512]{2,1,0:T(8,128)(2,1)S(1)}, u32[]{:S(2)}) copy-start(bf16[24,32,512]{2,1,0:T(8,128)(2,1)S(1)} %collective-permute-done.2.other_ref) | copy-start | bytes 2359300
  5.5 25.1 %copy-start.2 = (bf16[3,32,512]{2,1,0:T(8,128)(2,1)}, bf16[3,32,512]{2,1,0:T(8,128)(2,1)S(1)}, u32[]{:S(2)}) copy-start(bf16[3,32,512]{2,1,0:T(8,128)(2,1)S(1)} %collective-permute-done.1.rim_ref) | copy-start | bytes 294916
  5.5 25.9 %all-to-all-start = ((bf16[16,32,512]{2,1,0:T(8,128)(2,1)}), bf16[16,32,512]{2,1,0:T(8,128)(2,1)S(1)}, u32[]{:S(2)}, u32[]{:S(2)}) async-start(bf16[16,32,512]{2,1,0:T(8,128)(2,1)} %even_rows.1.grad_slab_ref), calls=%async_computation | async-start | bytes 1048576 | tf_op jit(solution)/shard_map/all_to_all | solution.py:711
  31.4 12.2 %copy-start.8 = (bf16[16,32,512]{2,1,0:T(8,128)(2,1)}, bf16[16,32,512]{2,1,0:T(8,128)(2,1)S(1)}, u32[]{:S(2)}) copy-start(bf16[16,32,512]{2,1,0:T(8,128)(2,1)S(1)} %all-to-all-done) | copy-start | bytes 1572868
  31.4 19.4 %all-to-all-start.1 = ((bf16[16,32,512]{2,1,0:T(8,128)(2,1)}), bf16[16,32,512]{2,1,0:T(8,128)(2,1)S(1)}, u32[]{:S(2)}, u32[]{:S(2)}) async-start(bf16[16,32,512]{2,1,0:T(8,128)(2,1)} %get-tuple-element.32), calls=%async_computation.1 | async-start | bytes 1048576 | tf_op jit(solution)/shard_map/all_to_all | solution.py:711
  63.4 18.1 %all-to-all-start.2 = ((bf16[16,32,512]{2,1,0:T(8,128)(2,1)}), bf16[16,32,512]{2,1,0:T(8,128)(2,1)S(1)}, u32[]{:S(2)}, u32[]{:S(2)}) async-start(bf16[16,32,512]{2,1,0:T(8,128)(2,1)} %bitcast.10), calls=%async_computation.2 | async-start | bytes 1048576 | tf_op jit(solution)/shard_map/all_to_all | solution.py:711
  81.5 9.0 %copy-start.7 = (bf16[16,32,512]{2,1,0:T(8,128)(2,1)}, bf16[16,32,512]{2,1,0:T(8,128)(2,1)S(1)}, u32[]{:S(2)}) copy-start(bf16[16,32,512]{2,1,0:T(8,128)(2,1)S(1)} %all-to-all-done.2.grad_ref) | copy-start | bytes 1572868
  81.5 1.3 %collective-permute-start.3 = (bf16[1,32,512]{2,1,0:T(8,128)(2,1)S(1)}, bf16[1,32,512]{2,1,0:T(8,128)(2,1)S(1)}, u32[]{:S(2)}, u32[]{:S(2)}) collective-permute-start(bf16[1,32,512]{2,1,0:T(8,128)(2,1)S(1)} %get-tuple-element.63), channel_id=1, source_target_pairs={{0,1},{1,0},{2,3},{3,2},{4,5},{5,4},{6,7},{7,6},{8,9},{9,8},{10,11... | collective-permute-start | bytes 98312 | tf_op jit(solution)/shard_map/ppermute | solution.py:718
  81.6 1.2 %collective-permute-start.4 = (bf16[1,32,512]{2,1,0:T(8,128)(2,1)S(1)}, bf16[1,32,512]{2,1,0:T(8,128)(2,1)S(1)}, u32[]{:S(2)}, u32[]{:S(2)}) collective-permute-start(bf16[1,32,512]{2,1,0:T(8,128)(2,1)S(1)} %get-tuple-element.62), channel_id=1, source_target_pairs={{1,2},{3,4},{5,6},{7,8},{9,10},{11,12},{13,14},{2,1},{4,3},{6,5},{... | collective-permute-start | bytes 98312 | tf_op jit(solution)/shard_map/ppermute | solution.py:724
  82.8 22.9 %all-to-all-start.3 = ((bf16[16,32,512]{2,1,0:T(8,128)(2,1)}), bf16[16,32,512]{2,1,0:T(8,128)(2,1)S(1)}, u32[]{:S(2)}, u32[]{:S(2)}) async-start(bf16[16,32,512]{2,1,0:T(8,128)(2,1)} %bitcast.8), calls=%async_computation.3 | async-start | bytes 1048576 | tf_op jit(solution)/shard_map/all_to_all | solution.py:711
  90.5 15.2 %copy-start.6 = (f32[512,512]{1,0:T(8,128)S(1)}, f32[512,512]{1,0:T(8,128)}, u32[]{:S(2)}) copy-start(f32[512,512]{1,0:T(8,128)} %get-tuple-element.44.first_ref) | copy-start | bytes 3145732
  101.4 4.6 %collective-permute-start.6 = (bf16[8,32,512]{2,1,0:T(8,128)(2,1)S(1)}, bf16[8,32,512]{2,1,0:T(8,128)(2,1)S(1)}, u32[]{:S(2)}, u32[]{:S(2)}) collective-permute-start(bf16[8,32,512]{2,1,0:T(8,128)(2,1)S(1)} %slice_select_fusion), channel_id=1, source_target_pairs={{0,1},{1,0},{2,3},{3,2},{4,5},{5,4},{6,7},{7,6},{8,9},{9,8},{10,11... | collective-permute-start | bytes 786440 | tf_op jit(solution)/shard_map/ppermute | solution.py:718
  105.9 1.6 %collective-permute-start.5 = (bf16[8,32,512]{2,1,0:T(8,128)(2,1)S(1)}, bf16[8,32,512]{2,1,0:T(8,128)(2,1)S(1)}, u32[]{:S(2)}, u32[]{:S(2)}) collective-permute-start(bf16[8,32,512]{2,1,0:T(8,128)(2,1)S(1)} %broadcast_select_fusion), channel_id=1, source_target_pairs={{0,1},{1,0},{2,3},{3,2},{4,5},{5,4},{6,7},{7,6},{8,9},{9,8},{10,11... | collective-permute-start | bytes 786440 | tf_op jit(solution)/shard_map/ppermute | solution.py:718

commit v13 on v12

--- a/solution.py
+++ b/solution.py
@@ -320,8 +320,8 @@
         ],
         compiler_params=params(24),
         cost_estimate=pl.CostEstimate(
-            flops=4 * rows * cols * width * hidden_width,
-            bytes_accessed=12 * 1024 * 1024,
+            flops=16 * 10**9,
+            bytes_accessed=48 * MIB,
             transcendentals=2 * rows * cols * hidden_width,
         ),
         name="bottleneck_forward",
@@ -691,8 +691,8 @@
         ],
         compiler_params=params(26),
         cost_estimate=pl.CostEstimate(
-            flops=4 * (own + 2) * cols * width * hidden_width,
-            bytes_accessed=12 * 1024 * 1024,
+            flops=16 * 10**9,
+            bytes_accessed=48 * MIB,
             transcendentals=0,
         ),
         name="bottleneck_backward",
@@ -745,7 +745,6 @@
     other_cotangent = swap_pair(cotangent)
     other_features = swap_pair(features)
     grad_slab = even_rows(row_bands, cotangent, other_cotangent)
-    rim, grad_slab = lax.optimization_barrier((rim, grad_slab))
 
     grad_windows = exchange_windows(grad_slab)
     edges, first, normed, slab, expanded, mixed = forward(
@@ -765,9 +764,9 @@
     leader_share = BAND * row_bands[device - parity]
     grad_rows, added, leader_share = lax.optimization_barrier((grad_rows, added, leader_share))
     top, bottom = grad_rows[:1], grad_rows[GRID_ROWS - 1 :]
-    pair_row = swap_pair(jnp.where(leads, bottom, top))
-    next_row = swap_next(jnp.where(leads, top, bottom))
-    added, pair_row, next_row = lax.optimization_barrier((added, pair_row, next_row))
+    sent_next, sent_pair = jnp.where(leads, top, bottom), jnp.where(leads, bottom, top)
+    added, sent_next, sent_pair = lax.optimization_barrier((added, sent_next, sent_pair))
+    next_row, pair_row = swap_next(sent_next), swap_pair(sent_pair)
     added_rows = exchange_windows(added.reshape(GRID_ROWS, cols, width))
     grad_input = backward(
         row_bands, cotangent, other_cotangent, rim, slab, first, edges, grad_slab, grad_rows, pair_row, next_row,

time: 109 us -> 105 us (0.963)
  starting transfers between devices: 30.2 us -> 25.9 us
    all_to_all x4, starting transfers between devices: 27.5 us -> 22.8 us  [exchange_windows(): lax.all_to_all(rows, 'row', split_axis=0, concat_axis=0, tiled=True, axis...]
  transfers between devices with their start and end apart: 11 -> 11, of which waited for: 6 -> 5; matrix products, arithmetic and copies ran while one was open for 2% -> 2% of each run, Pallas kernels for 38% -> 39%
where the time goes in v13:
time: 105 us
  Pallas kernels  53.4 us (51%)
  starting transfers between devices  25.9 us (25%)
  waiting for transfers between devices  20.3 us (19%)
  other arithmetic  2.29 us (2%)
  between operations  1.51 us (1%)
  local copies, waits for them, and re-layouts  1.29 us (1%)
    all_to_all x4, starting transfers between devices, exchange_windows(): lax.all_to_all(rows, 'row', split_axis=0, concat_axis=0, tiled=True, axis...  22.8 us
    all_to_all x4, waiting for transfers between devices, exchange_windows(): lax.all_to_all(rows, 'row', split_axis=0, concat_axis=0, tiled=True, axis...  19.8 us
    pallas_call x1, Pallas kernels, forward(): pl.pallas_call(forward_body, in_specs=[in_scalars(), in_hbm(), in_vmem(),...  13.9 us
    pallas_call x1, Pallas kernels, attention(): pl.pallas_call(attention_body, in_specs=[in_vmem(), in_hbm(), in_hbm()],...  12.6 us
    pallas_call x1, Pallas kernels, backward(): pl.pallas_call(backward_body, in_specs=[in_scalars()] + [in_hbm()] * 8 +...  10.8 us
    pallas_call x1, Pallas kernels, slopes(): pl.pallas_call(slopes_body, grid=(hidden_width // CHUNK,), in_specs=block...  7.1 us
    pallas_call x1, Pallas kernels, attend(): pl.pallas_call(attended_body, grid=(1,), in_specs=[whole(weights.shape),...  3.52 us
    pallas_call x1, Pallas kernels, attended_gradient(): pl.pallas_call(grad_attended_body, grid=(1,), in_specs=[whole(cotangent.s...  2.57 us
  transfers between devices with their start and end apart: 11, of which 5 were waited for; matrix products, arithmetic and copies ran while one was open for 2% of the time, Pallas kernels for 39%

profile of v13, /device:TPU:0, one launch (start us, length us, event | category | flops | bytes accessed | tf_op | source)
XLA Modules:
  0.0 104.6 jit_solution(8210447333966866970)
XLA Ops:
  0.6 0.5 collective-permute-start.2
  1.2 0.7 copy-done.2
  1.9 1.4 %rim_rows.1 = bf16[3,32,512]{2,1,0:T(8,128)(2,1)S(1)} custom-call(s32[16]{0:T(128)S(1)} %copy-done.2, bf16[24,32,512]{2,1,0:T(8,128)(2,1)} %features_ref.3, bf16[24,32,512]{2,1,0:T(8,128)(2,1)} %cotangent_ref.3), custom_call_target="tpu_custom_call" | custom-call | tf_op jit(solution)/shard_map/rim_rows/pallas_call | solution.py:158
  3.3 0.7 collective-permute-start.1
  4.0 1.4 %even_rows.1.grad_slab_ref = bf16[16,32,512]{2,1,0:T(8,128)(2,1)} custom-call(s32[16]{0:T(128)S(1)} %copy-done.2, bf16[24,32,512]{2,1,0:T(8,128)(2,1)S(1)} %copy-done, bf16[24,32,512]{2,1,0:T(8,128)(2,1)S(1)} %collective-permute-done.2.other_ref), custom_call_target="tpu_custom_call" | custom-call | tf_op jit(solution)/shard_map/even_rows/pallas_call | solution.py:129
  5.5 8.7 %all-to-all-start = ((bf16[16,32,512]{2,1,0:T(8,128)(2,1)}), bf16[16,32,512]{2,1,0:T(8,128)(2,1)S(1)}, u32[]{:S(2)}, u32[]{:S(2)}) async-start(bf16[16,32,512]{2,1,0:T(8,128)(2,1)} %even_rows.1.grad_slab_ref), calls=%async_computation | async-start | bytes 1048576 | tf_op jit(solution)/shard_map/all_to_all | solution.py:711
  14.2 13.9 %bottleneck_forward.1 = (f32[64,512]{1,0:T(8,128)}, f32[512,512]{1,0:T(8,128)}, bf16[16,32,512]{2,1,0:T(8,128)(2,1)}, bf16[16,32,512]{2,1,0:T(8,128)(2,1)}, bf16...) custom-call(s32[16]{0:T(128)S(1)} %copy-done.3, bf16[24,32,512]{2,1,0:T(8,128)(2,1)} %features_ref.3, ...), custom_call_target="tpu_custom_call" | custom-call | flops 16000000000 | bytes 50331648 | tf_op jit(solution)/shard_map/bottleneck_forward/pallas_call | solution.py:293
  28.2 1.1 %all-to-all-done = bf16[16,32,512]{2,1,0:T(8,128)(2,1)S(1)} async-done(((bf16[16,32,512]{2,1,0:T(8,128)(2,1)}), bf16[16,32,512]{2,1,0:T(8,128)(2,1)S(1)}, u32[]{:S(2)}, u32[]{:S(2)}) %all-to-all-start) | async-done | bytes 524320 | tf_op jit(solution)/shard_map/all_to_all | solution.py:711
  29.3 4.9 %all-to-all-start.1 = ((bf16[16,32,512]{2,1,0:T(8,128)(2,1)}), bf16[16,32,512]{2,1,0:T(8,128)(2,1)S(1)}, u32[]{:S(2)}, u32[]{:S(2)}) async-start(bf16[16,32,512]{2,1,0:T(8,128)(2,1)} %get-tuple-element.28), calls=%async_computation.1 | async-start | bytes 1048576 | tf_op jit(solution)/shard_map/all_to_all | solution.py:711
  34.2 7.1 %gelu_slopes.1 = (bf16[16,32,2048]{2,1,0:T(8,128)(2,1)}, bf16[18,32,2048]{2,1,0:T(8,128)(2,1)}) custom-call(bf16[16,32,2048]{2,1,0:T(8,128)(2,1)} %get-tuple-element.29.expanded_ref, bf16[18,32,2048]{2,1,0:T(8,128)(2,1)} %get-tuple-element.30.mixed_ref), custom_call_target="tpu_custom_call" | custom-call | flops 33423360 | bytes 13369344 | tf_op jit(solution)/shard_map/gelu_slopes/pallas_call | solution.py:345
  41.3 2.6 %attended_gradient.1.grad_attended_ref = bf16[512,512]{1,0:T(8,128)(2,1)} custom-call(bf16[8,2,32,512]{3,2,1,0:T(8,128)(2,1)} %bitcast.8, bf16[512,512]{1,0:T(8,128)(2,1)} %out_ref.3), custom_call_target="tpu_custom_call" | custom-call | flops 268435456 | bytes 2097152 | tf_op jit(solution)/shard_map/attended_gradient/pallas_call | solution.py:408
  43.9 4.9 %all-to-all-done.1 = bf16[16,32,512]{2,1,0:T(8,128)(2,1)S(1)} async-done(((bf16[16,32,512]{2,1,0:T(8,128)(2,1)}), bf16[16,32,512]{2,1,0:T(8,128)(2,1)S(1)}, u32[]{:S(2)}, u32[]{:S(2)}) %all-to-all-start.1) | async-done | bytes 524320 | tf_op jit(solution)/shard_map/all_to_all | solution.py:711
  48.7 12.6 %window_attention.1 = (bf16[8,2,32,512]{3,2,1,0:T(8,128)(2,1)}, bf16[8,64,1024]{2,1,0:T(8,128)(2,1)}, bf16[512,512]{1,0:T(8,128)(2,1)}) custom-call(bf16[8,2,32,512]{3,2,1,0:T(8,128)(2,1)S(1)} %bitcast.6, bf16[512,512]{1,0:T(8,128)(2,1)} %attended_gradient.1.grad_attended_ref, bf16[512,1536]{1,0:T(8,128)(2,1)} %qkv_ref.1), custom_call_target="tpu_custom_call" | custom-call | flops 2147483648 | bytes 4194304 | tf_op jit(solution)/shard_map/window_attention/pallas_call | solution.py:498
  61.4 3.6 %all-to-all-start.2 = ((bf16[16,32,512]{2,1,0:T(8,128)(2,1)}), bf16[16,32,512]{2,1,0:T(8,128)(2,1)S(1)}, u32[]{:S(2)}, u32[]{:S(2)}) async-start(bf16[16,32,512]{2,1,0:T(8,128)(2,1)} %bitcast.10), calls=%async_computation.2 | async-start | bytes 1048576 | tf_op jit(solution)/shard_map/all_to_all | solution.py:711
  65.0 0.6 dynamic_slice.3
  66.2 3.5 %attended_output.1 = bf16[8,2,32,512]{3,2,1,0:T(8,128)(2,1)} custom-call(bf16[8,64,1024]{2,1,0:T(8,128)(2,1)} %get-tuple-element.37.weights_ref, bf16[512,512]{1,0:T(8,128)(2,1)} %get-tuple-element.38.values_ref, bf16[512,512]{1,0:T(8,128)(2,1)} %out_ref.3), custom_call_target="tpu_custom_call" | custom-call | flops 536870912 | bytes 3145728 | tf_op jit(solution)/shard_map/attended_output/pallas_call | solution.py:538
  69.8 9.9 %all-to-all-done.2.grad_ref = bf16[16,32,512]{2,1,0:T(8,128)(2,1)S(1)} async-done(((bf16[16,32,512]{2,1,0:T(8,128)(2,1)}), bf16[16,32,512]{2,1,0:T(8,128)(2,1)S(1)}, u32[]{:S(2)}, u32[]{:S(2)}) %all-to-all-start.2) | async-done | bytes 524320 | tf_op jit(solution)/shard_map/all_to_all | solution.py:711
  79.8 0.7 collective-permute-start.4
  80.4 5.5 %all-to-all-start.3 = ((bf16[16,32,512]{2,1,0:T(8,128)(2,1)}), bf16[16,32,512]{2,1,0:T(8,128)(2,1)S(1)}, u32[]{:S(2)}, u32[]{:S(2)}) async-start(bf16[16,32,512]{2,1,0:T(8,128)(2,1)} %bitcast.7), calls=%async_computation.3 | async-start | bytes 1048576 | tf_op jit(solution)/shard_map/all_to_all | solution.py:711
  86.0 10.8 %bottleneck_backward.1 = bf16[16,32,512]{2,1,0:T(8,128)(2,1)S(1)} custom-call(s32[16]{0:T(128)S(1)} %copy-done.3, bf16[24,32,512]{2,1,0:T(8,128)(2,1)} %cotangent_ref.3, bf16[24,32,512]{2,1,0:T(8,128)(2,1)} %copy-done.1, bf16[3,32,512]{2,1,0:T(8,128)(2,1)} %copy-done.4, bf16[16,32,512]{2,1,0:T(8,128)(2,1)} %get-tuple-element.41.slab_ref, ...), custom_call_target="tpu_custom_call" | custom-call | flops 16000000000 | bytes 50331648 | tf_op jit(solution)/shard_map/bottleneck_backward/pallas_call | solution.py:667
  96.9 1.0 collective-permute-start.6
  97.9 3.8 %all-to-all-done.3 = bf16[16,32,512]{2,1,0:T(8,128)(2,1)S(1)} async-done(((bf16[16,32,512]{2,1,0:T(8,128)(2,1)}), bf16[16,32,512]{2,1,0:T(8,128)(2,1)S(1)}, u32[]{:S(2)}, u32[]{:S(2)}) %all-to-all-start.3) | async-done | bytes 524320 | tf_op jit(solution)/shard_map/all_to_all | solution.py:711
  102.1 1.0 pad_maximum_fusion.1
  103.6 1.0 pad_maximum_fusion
  (33 shorter events, 1.1 us)
Async XLA Ops:
  0.6 3.4 %copy-start = (bf16[24,32,512]{2,1,0:T(8,128)(2,1)S(1)}, bf16[24,32,512]{2,1,0:T(8,128)(2,1)}, u32[]{:S(2)}) copy-start(bf16[24,32,512]{2,1,0:T(8,128)(2,1)} %cotangent_ref.3) | copy-start | bytes 2359300
  0.6 3.4 %collective-permute-start.2 = (bf16[24,32,512]{2,1,0:T(8,128)(2,1)}, bf16[24,32,512]{2,1,0:T(8,128)(2,1)S(1)}, u32[]{:S(2)}, u32[]{:S(2)}) collective-permute-start(bf16[24,32,512]{2,1,0:T(8,128)(2,1)} %cotangent_ref.3), channel_id=1, source_target_pairs={{0,1},{1,0},{2,3},{3,2},{4,5},{5,4},{6,7},{7,6},{8,9},{9,8},{10,11... | collective-permute-start | bytes 2359304 | tf_op jit(solution)/shard_map/ppermute | solution.py:718
  1.2 13.0 %collective-permute-start = (bf16[24,32,512]{2,1,0:T(8,128)(2,1)}, bf16[24,32,512]{2,1,0:T(8,128)(2,1)S(1)}, u32[]{:S(2)}, u32[]{:S(2)}) collective-permute-start(bf16[24,32,512]{2,1,0:T(8,128)(2,1)} %features_ref.3), channel_id=1, source_target_pairs={{0,1},{1,0},{2,3},{3,2},{4,5},{5,4},{6,7},{7,6},{8,9},{9,8},{10,11... | collective-permute-start | bytes 2359304 | tf_op jit(solution)/shard_map/ppermute | solution.py:718
  1.2 0.7 copy-start.2
  1.9 12.3 %copy-start.3 = (s32[16]{0:T(128)S(1)}, s32[16]{0:T(128)}, u32[]{:S(2)}) copy-start(s32[16]{0:T(128)} %bands_ref.7) | copy-start | bytes 196
  1.9 12.3 %copy-start.5 = (bf16[9,2048]{1,0:T(8,128)(2,1)S(1)}, bf16[9,2048]{1,0:T(8,128)(2,1)}, u32[]{:S(2)}) copy-start(bf16[9,2048]{1,0:T(8,128)(2,1)} %taps_ref.3) | copy-start | bytes 110596
  3.3 10.8 %collective-permute-start.1 = (bf16[3,32,512]{2,1,0:T(8,128)(2,1)S(1)}, bf16[3,32,512]{2,1,0:T(8,128)(2,1)S(1)}, u32[]{:S(2)}, u32[]{:S(2)}) collective-permute-start(bf16[3,32,512]{2,1,0:T(8,128)(2,1)S(1)} %rim_rows.1), channel_id=1, source_target_pairs={{1,2},{3,4},{5,6},{7,8},{9,10},{11,12},{13,14},{2,1},{4,3},{6,5},{... | collective-permute-start | bytes 294920 | tf_op jit(solution)/shard_map/ppermute | solution.py:724
  4.0 24.1 %copy-start.1 = (bf16[24,32,512]{2,1,0:T(8,128)(2,1)}, bf16[24,32,512]{2,1,0:T(8,128)(2,1)S(1)}, u32[]{:S(2)}) copy-start(bf16[24,32,512]{2,1,0:T(8,128)(2,1)S(1)} %collective-permute-done.2.other_ref) | copy-start | bytes 2359300
  5.5 23.8 %all-to-all-start = ((bf16[16,32,512]{2,1,0:T(8,128)(2,1)}), bf16[16,32,512]{2,1,0:T(8,128)(2,1)S(1)}, u32[]{:S(2)}, u32[]{:S(2)}) async-start(bf16[16,32,512]{2,1,0:T(8,128)(2,1)} %even_rows.1.grad_slab_ref), calls=%async_computation | async-start | bytes 1048576 | tf_op jit(solution)/shard_map/all_to_all | solution.py:711
  14.2 14.0 %copy-start.4 = (bf16[3,32,512]{2,1,0:T(8,128)(2,1)}, bf16[3,32,512]{2,1,0:T(8,128)(2,1)S(1)}, u32[]{:S(2)}) copy-start(bf16[3,32,512]{2,1,0:T(8,128)(2,1)S(1)} %collective-permute-done.1.rim_ref) | copy-start | bytes 294916
  29.3 12.0 %copy-start.6 = (bf16[16,32,512]{2,1,0:T(8,128)(2,1)}, bf16[16,32,512]{2,1,0:T(8,128)(2,1)S(1)}, u32[]{:S(2)}) copy-start(bf16[16,32,512]{2,1,0:T(8,128)(2,1)S(1)} %all-to-all-done) | copy-start | bytes 1572868
  29.3 19.4 %all-to-all-start.1 = ((bf16[16,32,512]{2,1,0:T(8,128)(2,1)}), bf16[16,32,512]{2,1,0:T(8,128)(2,1)S(1)}, u32[]{:S(2)}, u32[]{:S(2)}) async-start(bf16[16,32,512]{2,1,0:T(8,128)(2,1)} %get-tuple-element.28), calls=%async_computation.1 | async-start | bytes 1048576 | tf_op jit(solution)/shard_map/all_to_all | solution.py:711
  61.4 18.3 %all-to-all-start.2 = ((bf16[16,32,512]{2,1,0:T(8,128)(2,1)}), bf16[16,32,512]{2,1,0:T(8,128)(2,1)S(1)}, u32[]{:S(2)}, u32[]{:S(2)}) async-start(bf16[16,32,512]{2,1,0:T(8,128)(2,1)} %bitcast.10), calls=%async_computation.2 | async-start | bytes 1048576 | tf_op jit(solution)/shard_map/all_to_all | solution.py:711
  79.7 6.3 %copy-start.8 = (bf16[16,32,512]{2,1,0:T(8,128)(2,1)}, bf16[16,32,512]{2,1,0:T(8,128)(2,1)S(1)}, u32[]{:S(2)}) copy-start(bf16[16,32,512]{2,1,0:T(8,128)(2,1)S(1)} %all-to-all-done.2.grad_ref) | copy-start | bytes 1572868
  79.7 6.3 %collective-permute-start.3 = (bf16[1,32,512]{2,1,0:T(8,128)(2,1)S(1)}, bf16[1,32,512]{2,1,0:T(8,128)(2,1)S(1)}, u32[]{:S(2)}, u32[]{:S(2)}) collective-permute-start(bf16[1,32,512]{2,1,0:T(8,128)(2,1)S(1)} %get-tuple-element.45), channel_id=1, source_target_pairs={{0,1},{1,0},{2,3},{3,2},{4,5},{5,4},{6,7},{7,6},{8,9},{9,8},{10,11... | collective-permute-start | bytes 98312 | tf_op jit(solution)/shard_map/ppermute | solution.py:718
  79.8 6.2 %collective-permute-start.4 = (bf16[1,32,512]{2,1,0:T(8,128)(2,1)S(1)}, bf16[1,32,512]{2,1,0:T(8,128)(2,1)S(1)}, u32[]{:S(2)}, u32[]{:S(2)}) collective-permute-start(bf16[1,32,512]{2,1,0:T(8,128)(2,1)S(1)} %get-tuple-element.46), channel_id=1, source_target_pairs={{1,2},{3,4},{5,6},{7,8},{9,10},{11,12},{13,14},{2,1},{4,3},{6,5},{... | collective-permute-start | bytes 98312 | tf_op jit(solution)/shard_map/ppermute | solution.py:724
  80.4 21.3 %all-to-all-start.3 = ((bf16[16,32,512]{2,1,0:T(8,128)(2,1)}), bf16[16,32,512]{2,1,0:T(8,128)(2,1)S(1)}, u32[]{:S(2)}, u32[]{:S(2)}) async-start(bf16[16,32,512]{2,1,0:T(8,128)(2,1)} %bitcast.7), calls=%async_computation.3 | async-start | bytes 1048576 | tf_op jit(solution)/shard_map/all_to_all | solution.py:711
  86.0 15.7 %copy-start.7 = (f32[512,512]{1,0:T(8,128)S(1)}, f32[512,512]{1,0:T(8,128)}, u32[]{:S(2)}) copy-start(f32[512,512]{1,0:T(8,128)} %get-tuple-element.40.first_ref) | copy-start | bytes 3145732
  96.9 5.2 %collective-permute-start.6 = (bf16[8,32,512]{2,1,0:T(8,128)(2,1)S(1)}, bf16[8,32,512]{2,1,0:T(8,128)(2,1)S(1)}, u32[]{:S(2)}, u32[]{:S(2)}) collective-permute-start(bf16[8,32,512]{2,1,0:T(8,128)(2,1)S(1)} %slice_select_fusion), channel_id=1, source_target_pairs={{0,1},{1,0},{2,3},{3,2},{4,5},{5,4},{6,7},{7,6},{8,9},{9,8},{10,11... | collective-permute-start | bytes 786440 | tf_op jit(solution)/shard_map/ppermute | solution.py:718
  102.0 1.6 %collective-permute-start.5 = (bf16[8,32,512]{2,1,0:T(8,128)(2,1)S(1)}, bf16[8,32,512]{2,1,0:T(8,128)(2,1)S(1)}, u32[]{:S(2)}, u32[]{:S(2)}) collective-permute-start(bf16[8,32,512]{2,1,0:T(8,128)(2,1)S(1)} %broadcast_select_fusion), channel_id=1, source_target_pairs={{0,1},{1,0},{2,3},{3,2},{4,5},{5,4},{6,7},{7,6},{8,9},{9,8},{10,11... | collective-permute-start | bytes 786440 | tf_op jit(solution)/shard_map/ppermute | solution.py:718

commit v14 on v13

--- a/solution.py
+++ b/solution.py
@@ -13,7 +13,6 @@
 RIM = 2
 EPSILON = 1e-06
 CHUNK = 512
-HALF = 256
 GROUP_FORWARD = 10
 GROUP_BACKWARD = 9
 LANES = 128
@@ -136,34 +135,48 @@
     )(bands, near(own), near(other))
 
 
-def rim_body(bands_ref, features_ref, cotangent_ref, out_ref, sems):
-    parity, _, share = shares(bands_ref)
-    leads = parity == 0
-    copies = [
-        pltpu.make_async_copy(
-            features_ref.at[pl.ds(jnp.where(leads, 0, share - RIM), RIM)], out_ref.at[pl.ds(0, RIM)], sems.at[0]
-        ),
-        pltpu.make_async_copy(
-            cotangent_ref.at[pl.ds(jnp.where(leads, 0, share - 1), 1)], out_ref.at[pl.ds(RIM, 1)], sems.at[1]
-        ),
-    ]
+def rim_body(bands_ref, features_ref, cotangent_ref, out_ref, bands, choices, sems):
+    fetch_bands = pltpu.make_async_copy(bands_ref, bands, sems.at[0])
+    fetch_bands.start()
+    copies = []
+    for choice in range(4):
+        first = max(0, BAND * choice - RIM)
+        second = max(0, BAND * choice - 1)
+        copies.append(
+            pltpu.make_async_copy(
+                features_ref.at[pl.ds(first, RIM)], choices.at[choice, pl.ds(0, RIM)], sems.at[1 + choice]
+            )
+        )
+        copies.append(
+            pltpu.make_async_copy(
+                cotangent_ref.at[pl.ds(second, 1)], choices.at[choice, pl.ds(RIM, 1)], sems.at[5 + choice]
+            )
+        )
     for copy in copies:
         copy.start()
+    fetch_bands.wait()
+    device = lax.axis_index("row")
+    choice = jnp.where(lax.rem(device, 2) == 0, 0, bands[device])
     for copy in copies:
         copy.wait()
+    out_ref[...] = choices[choice]
 
 
 def rim_rows(bands, features, cotangent):
     shape = (RIM + 1,) + features.shape[1:]
     return pl.pallas_call(
         rim_body,
-        in_specs=[in_scalars(), in_hbm(), in_hbm()],
+        in_specs=[in_hbm(), in_hbm(), in_hbm()],
         out_specs=in_vmem(),
         out_shape=jax.ShapeDtypeStruct(shape, features.dtype),
-        scratch_shapes=[pltpu.SemaphoreType.DMA((2,))],
+        scratch_shapes=[
+            pltpu.SMEM(bands.shape, bands.dtype),
+            pltpu.VMEM((4,) + shape, features.dtype),
+            pltpu.SemaphoreType.DMA((9,)),
+        ],
         compiler_params=params(8),
         name="rim_rows",
-    )(bands, held(features), held(cotangent))
+    )(held(bands), held(features), held(cotangent))
 
 
 def column_sums(left, mid, right, column, last):
@@ -232,17 +245,16 @@
             fetch_project(index + 1).start()
 
         fetch_expand(index).wait()
-        for start in range(0, CHUNK, HALF):
-            weights = expand[:, chunk_lanes(index, start, HALF)]
-            for row in range(0, rows, GROUP_FORWARD):
-                product = nn_dot(normed_one[row * cols : (row + GROUP_FORWARD) * cols, :], weights)
-                for inner in range(GROUP_FORWARD):
-                    for lane in range(0, HALF, LANES):
-                        values = product[inner * cols : (inner + 1) * cols, lane : lane + LANES]
-                        at = slice(start + lane, start + lane + LANES)
-                        hidden[row + inner, :, at] = gelu(values).astype(BF16).astype(F32)
-                        if RIM <= row + inner < RIM + own:
-                            expanded[row + inner - RIM, :, chunk_lanes(index, start + lane, LANES)] = values.astype(BF16)
+        weights = expand[:, chunk_lanes(index)]
+        for row in range(0, rows, GROUP_FORWARD):
+            product = nn_dot(normed_one[row * cols : (row + GROUP_FORWARD) * cols, :], weights)
+            for inner in range(GROUP_FORWARD):
+                for lane in range(0, CHUNK, LANES):
+                    lanes = slice(lane, lane + LANES)
+                    values = product[inner * cols : (inner + 1) * cols, lanes]
+                    hidden[row + inner, :, lanes] = gelu(values).astype(BF16).astype(F32)
+                    if RIM <= row + inner < RIM + own:
+                        expanded[row + inner - RIM, :, chunk_lanes(index, lane, LANES)] = values.astype(BF16)
         store_expanded(index).start()
 
         for lane in range(0, CHUNK, LANES):
@@ -621,16 +633,15 @@
 
         for copy in fetches(index):
             copy.wait()
-        for start in range(0, CHUNK, HALF):
-            weights = project[chunk_lanes(index, start, HALF), :]
-            for row in range(0, own + 2, GROUP_BACKWARD):
-                product = nt_dot(grad_rows[row * cols : (row + GROUP_BACKWARD) * cols, :], weights)
-                for inner in range(GROUP_BACKWARD):
-                    for lane in range(0, HALF, LANES):
-                        slope = slope_two[row + inner, :, chunk_lanes(index, start + lane, LANES)].astype(F32)
-                        value = product[inner * cols : (inner + 1) * cols, lane : lane + LANES] * slope
-                        at = slice(start + lane, start + lane + LANES)
-                        mixed[row + inner, :, at] = value.astype(BF16).astype(F32)
+        weights = project[chunk_lanes(index), :]
+        for row in range(0, own + 2, GROUP_BACKWARD):
+            product = nt_dot(grad_rows[row * cols : (row + GROUP_BACKWARD) * cols, :], weights)
+            for inner in range(GROUP_BACKWARD):
+                for lane in range(0, CHUNK, LANES):
+                    lanes = slice(lane, lane + LANES)
+                    slope = slope_two[row + inner, :, chunk_lanes(index, lane, LANES)].astype(F32)
+                    value = product[inner * cols : (inner + 1) * cols, lanes] * slope
+                    mixed[row + inner, :, lanes] = value.astype(BF16).astype(F32)
 
         for lane in range(0, CHUNK, LANES):
             lanes = slice(lane, lane + LANES)

time: 105 us -> 105 us (level)
  transfers between devices with their start and end apart: 11 -> 11, of which waited for: 5 -> 6; matrix products, arithmetic and copies ran while one was open for 2% -> 2% of each run, Pallas kernels for 39% -> 39%
where the time goes in v14:
time: 105 us; the launch traced here: 104 us
  Pallas kernels  53.4 us (51%)
  starting transfers between devices  25.6 us (24%)
  waiting for transfers between devices  20.3 us (19%)
  other arithmetic  2.29 us (2%)
  between operations  1.5 us (1%)
  local copies, waits for them, and re-layouts  1.29 us (1%)
    all_to_all x4, starting transfers between devices, exchange_windows(): lax.all_to_all(rows, 'row', split_axis=0, concat_axis=0, tiled=True, axis...  22.5 us
    all_to_all x4, waiting for transfers between devices, exchange_windows(): lax.all_to_all(rows, 'row', split_axis=0, concat_axis=0, tiled=True, axis...  19.5 us
    pallas_call x1, Pallas kernels, forward(): pl.pallas_call(forward_body, in_specs=[in_scalars(), in_hbm(), in_vmem(),...  14 us
    pallas_call x1, Pallas kernels, attention(): pl.pallas_call(attention_body, in_specs=[in_vmem(), in_hbm(), in_hbm()],...  12.6 us
    pallas_call x1, Pallas kernels, backward(): pl.pallas_call(backward_body, in_specs=[in_scalars()] + [in_hbm()] * 8 +...  11.1 us
    pallas_call x1, Pallas kernels, slopes(): pl.pallas_call(slopes_body, grid=(hidden_width // CHUNK,), in_specs=block...  7.1 us
    pallas_call x1, Pallas kernels, attend(): pl.pallas_call(attended_body, grid=(1,), in_specs=[whole(weights.shape),...  3.52 us
    pallas_call x1, Pallas kernels, attended_gradient(): pl.pallas_call(grad_attended_body, grid=(1,), in_specs=[whole(cotangent.s...  2.57 us
  transfers between devices with their start and end apart: 11, of which 6 were waited for; matrix products, arithmetic and copies ran while one was open for 2% of the time, Pallas kernels for 39%

profile of v14, /device:TPU:0, one launch (start us, length us, event | category | flops | bytes accessed | tf_op | source)
XLA Modules:
  0.0 104.4 jit_solution(3012330924105267733)
XLA Ops:
  0.7 0.5 collective-permute-start.2
  1.3 1.1 %rim_rows.1 = bf16[3,32,512]{2,1,0:T(8,128)(2,1)S(1)} custom-call(s32[16]{0:T(128)} %bands_ref.7, bf16[24,32,512]{2,1,0:T(8,128)(2,1)} %features_ref.3, bf16[24,32,512]{2,1,0:T(8,128)(2,1)} %cotangent_ref.3), custom_call_target="tpu_custom_call" | custom-call | tf_op jit(solution)/shard_map/rim_rows/pallas_call | solution.py:167
  2.3 0.7 collective-permute-start.1
  3.3 0.7 copy-done.2
  4.0 1.4 %even_rows.1.grad_slab_ref = bf16[16,32,512]{2,1,0:T(8,128)(2,1)} custom-call(s32[16]{0:T(128)S(1)} %copy-done.2, bf16[24,32,512]{2,1,0:T(8,128)(2,1)S(1)} %copy-done, bf16[24,32,512]{2,1,0:T(8,128)(2,1)S(1)} %collective-permute-done.2.other_ref), custom_call_target="tpu_custom_call" | custom-call | tf_op jit(solution)/shard_map/even_rows/pallas_call | solution.py:128
  5.4 8.4 %all-to-all-start = ((bf16[16,32,512]{2,1,0:T(8,128)(2,1)}), bf16[16,32,512]{2,1,0:T(8,128)(2,1)S(1)}, u32[]{:S(2)}, u32[]{:S(2)}) async-start(bf16[16,32,512]{2,1,0:T(8,128)(2,1)} %even_rows.1.grad_slab_ref), calls=%async_computation | async-start | bytes 1048576 | tf_op jit(solution)/shard_map/all_to_all | solution.py:722
  13.9 14.0 %bottleneck_forward.1 = (f32[64,512]{1,0:T(8,128)}, f32[512,512]{1,0:T(8,128)}, bf16[16,32,512]{2,1,0:T(8,128)(2,1)}, bf16[16,32,512]{2,1,0:T(8,128)(2,1)}, bf16...) custom-call(s32[16]{0:T(128)S(1)} %copy-done.3, bf16[24,32,512]{2,1,0:T(8,128)(2,1)} %features_ref.3, ...), custom_call_target="tpu_custom_call" | custom-call | flops 16000000000 | bytes 50331648 | tf_op jit(solution)/shard_map/bottleneck_forward/pallas_call | solution.py:305
  27.9 1.1 %all-to-all-done = bf16[16,32,512]{2,1,0:T(8,128)(2,1)S(1)} async-done(((bf16[16,32,512]{2,1,0:T(8,128)(2,1)}), bf16[16,32,512]{2,1,0:T(8,128)(2,1)S(1)}, u32[]{:S(2)}, u32[]{:S(2)}) %all-to-all-start) | async-done | bytes 524320 | tf_op jit(solution)/shard_map/all_to_all | solution.py:722
  29.0 4.9 %all-to-all-start.1 = ((bf16[16,32,512]{2,1,0:T(8,128)(2,1)}), bf16[16,32,512]{2,1,0:T(8,128)(2,1)S(1)}, u32[]{:S(2)}, u32[]{:S(2)}) async-start(bf16[16,32,512]{2,1,0:T(8,128)(2,1)} %get-tuple-element.28), calls=%async_computation.1 | async-start | bytes 1048576 | tf_op jit(solution)/shard_map/all_to_all | solution.py:722
  33.9 7.1 %gelu_slopes.1 = (bf16[16,32,2048]{2,1,0:T(8,128)(2,1)}, bf16[18,32,2048]{2,1,0:T(8,128)(2,1)}) custom-call(bf16[16,32,2048]{2,1,0:T(8,128)(2,1)} %get-tuple-element.29.expanded_ref, bf16[18,32,2048]{2,1,0:T(8,128)(2,1)} %get-tuple-element.30.mixed_ref), custom_call_target="tpu_custom_call" | custom-call | flops 33423360 | bytes 13369344 | tf_op jit(solution)/shard_map/gelu_slopes/pallas_call | solution.py:357
  41.0 2.6 %attended_gradient.1.grad_attended_ref = bf16[512,512]{1,0:T(8,128)(2,1)} custom-call(bf16[8,2,32,512]{3,2,1,0:T(8,128)(2,1)} %bitcast.8, bf16[512,512]{1,0:T(8,128)(2,1)} %out_ref.3), custom_call_target="tpu_custom_call" | custom-call | flops 268435456 | bytes 2097152 | tf_op jit(solution)/shard_map/attended_gradient/pallas_call | solution.py:420
  43.6 4.9 %all-to-all-done.1 = bf16[16,32,512]{2,1,0:T(8,128)(2,1)S(1)} async-done(((bf16[16,32,512]{2,1,0:T(8,128)(2,1)}), bf16[16,32,512]{2,1,0:T(8,128)(2,1)S(1)}, u32[]{:S(2)}, u32[]{:S(2)}) %all-to-all-start.1) | async-done | bytes 524320 | tf_op jit(solution)/shard_map/all_to_all | solution.py:722
  48.5 12.6 %window_attention.1 = (bf16[8,2,32,512]{3,2,1,0:T(8,128)(2,1)}, bf16[8,64,1024]{2,1,0:T(8,128)(2,1)}, bf16[512,512]{1,0:T(8,128)(2,1)}) custom-call(bf16[8,2,32,512]{3,2,1,0:T(8,128)(2,1)S(1)} %bitcast.6, bf16[512,512]{1,0:T(8,128)(2,1)} %attended_gradient.1.grad_attended_ref, bf16[512,1536]{1,0:T(8,128)(2,1)} %qkv_ref.1), custom_call_target="tpu_custom_call" | custom-call | flops 2147483648 | bytes 4194304 | tf_op jit(solution)/shard_map/window_attention/pallas_call | solution.py:510
  61.1 3.6 %all-to-all-start.2 = ((bf16[16,32,512]{2,1,0:T(8,128)(2,1)}), bf16[16,32,512]{2,1,0:T(8,128)(2,1)S(1)}, u32[]{:S(2)}, u32[]{:S(2)}) async-start(bf16[16,32,512]{2,1,0:T(8,128)(2,1)} %bitcast.10), calls=%async_computation.2 | async-start | bytes 1048576 | tf_op jit(solution)/shard_map/all_to_all | solution.py:722
  64.8 0.6 dynamic_slice.3
  66.0 3.5 %attended_output.1 = bf16[8,2,32,512]{3,2,1,0:T(8,128)(2,1)} custom-call(bf16[8,64,1024]{2,1,0:T(8,128)(2,1)} %get-tuple-element.37.weights_ref, bf16[512,512]{1,0:T(8,128)(2,1)} %get-tuple-element.38.values_ref, bf16[512,512]{1,0:T(8,128)(2,1)} %out_ref.3), custom_call_target="tpu_custom_call" | custom-call | flops 536870912 | bytes 3145728 | tf_op jit(solution)/shard_map/attended_output/pallas_call | solution.py:550
  69.5 9.9 %all-to-all-done.2.grad_ref = bf16[16,32,512]{2,1,0:T(8,128)(2,1)S(1)} async-done(((bf16[16,32,512]{2,1,0:T(8,128)(2,1)}), bf16[16,32,512]{2,1,0:T(8,128)(2,1)S(1)}, u32[]{:S(2)}, u32[]{:S(2)}) %all-to-all-start.2) | async-done | bytes 524320 | tf_op jit(solution)/shard_map/all_to_all | solution.py:722
  79.5 0.7 collective-permute-start.4
  80.2 5.5 %all-to-all-start.3 = ((bf16[16,32,512]{2,1,0:T(8,128)(2,1)}), bf16[16,32,512]{2,1,0:T(8,128)(2,1)S(1)}, u32[]{:S(2)}, u32[]{:S(2)}) async-start(bf16[16,32,512]{2,1,0:T(8,128)(2,1)} %bitcast.7), calls=%async_computation.3 | async-start | bytes 1048576 | tf_op jit(solution)/shard_map/all_to_all | solution.py:722
  85.8 11.1 %bottleneck_backward.1 = bf16[16,32,512]{2,1,0:T(8,128)(2,1)S(1)} custom-call(s32[16]{0:T(128)S(1)} %copy-done.3, bf16[24,32,512]{2,1,0:T(8,128)(2,1)} %cotangent_ref.3, bf16[24,32,512]{2,1,0:T(8,128)(2,1)} %copy-done.1, bf16[3,32,512]{2,1,0:T(8,128)(2,1)} %copy-done.4, bf16[16,32,512]{2,1,0:T(8,128)(2,1)} %get-tuple-element.41.slab_ref, ...), custom_call_target="tpu_custom_call" | custom-call | flops 16000000000 | bytes 50331648 | tf_op jit(solution)/shard_map/bottleneck_backward/pallas_call | solution.py:678
  96.9 1.0 collective-permute-start.6
  98.0 3.6 %all-to-all-done.3 = bf16[16,32,512]{2,1,0:T(8,128)(2,1)S(1)} async-done(((bf16[16,32,512]{2,1,0:T(8,128)(2,1)}), bf16[16,32,512]{2,1,0:T(8,128)(2,1)S(1)}, u32[]{:S(2)}, u32[]{:S(2)}) %all-to-all-start.3) | async-done | bytes 524320 | tf_op jit(solution)/shard_map/all_to_all | solution.py:722
  101.9 1.0 pad_maximum_fusion.1
  103.4 1.0 pad_maximum_fusion
  (33 shorter events, 1.4 us)
Async XLA Ops:
  0.6 2.7 %copy-start = (bf16[24,32,512]{2,1,0:T(8,128)(2,1)S(1)}, bf16[24,32,512]{2,1,0:T(8,128)(2,1)}, u32[]{:S(2)}) copy-start(bf16[24,32,512]{2,1,0:T(8,128)(2,1)} %cotangent_ref.3) | copy-start | bytes 2359300
  0.6 13.2 %copy-start.3 = (s32[16]{0:T(128)S(1)}, s32[16]{0:T(128)}, u32[]{:S(2)}) copy-start(s32[16]{0:T(128)} %bands_ref.7) | copy-start | bytes 196
  0.7 13.2 %copy-start.5 = (bf16[9,2048]{1,0:T(8,128)(2,1)S(1)}, bf16[9,2048]{1,0:T(8,128)(2,1)}, u32[]{:S(2)}) copy-start(bf16[9,2048]{1,0:T(8,128)(2,1)} %taps_ref.3) | copy-start | bytes 110596
  0.7 2.6 %collective-permute-start.2 = (bf16[24,32,512]{2,1,0:T(8,128)(2,1)}, bf16[24,32,512]{2,1,0:T(8,128)(2,1)S(1)}, u32[]{:S(2)}, u32[]{:S(2)}) collective-permute-start(bf16[24,32,512]{2,1,0:T(8,128)(2,1)} %cotangent_ref.3), channel_id=1, source_target_pairs={{0,1},{1,0},{2,3},{3,2},{4,5},{5,4},{6,7},{7,6},{8,9},{9,8},{10,11... | collective-permute-start | bytes 2359304 | tf_op jit(solution)/shard_map/ppermute | solution.py:729
  1.2 12.7 %collective-permute-start = (bf16[24,32,512]{2,1,0:T(8,128)(2,1)}, bf16[24,32,512]{2,1,0:T(8,128)(2,1)S(1)}, u32[]{:S(2)}, u32[]{:S(2)}) collective-permute-start(bf16[24,32,512]{2,1,0:T(8,128)(2,1)} %features_ref.3), channel_id=1, source_target_pairs={{0,1},{1,0},{2,3},{3,2},{4,5},{5,4},{6,7},{7,6},{8,9},{9,8},{10,11... | collective-permute-start | bytes 2359304 | tf_op jit(solution)/shard_map/ppermute | solution.py:729
  2.3 11.5 %collective-permute-start.1 = (bf16[3,32,512]{2,1,0:T(8,128)(2,1)S(1)}, bf16[3,32,512]{2,1,0:T(8,128)(2,1)S(1)}, u32[]{:S(2)}, u32[]{:S(2)}) collective-permute-start(bf16[3,32,512]{2,1,0:T(8,128)(2,1)S(1)} %rim_rows.1), channel_id=1, source_target_pairs={{1,2},{3,4},{5,6},{7,8},{9,10},{11,12},{13,14},{2,1},{4,3},{6,5},{... | collective-permute-start | bytes 294920 | tf_op jit(solution)/shard_map/ppermute | solution.py:735
  3.3 0.7 copy-start.2
  4.0 23.9 %copy-start.1 = (bf16[24,32,512]{2,1,0:T(8,128)(2,1)}, bf16[24,32,512]{2,1,0:T(8,128)(2,1)S(1)}, u32[]{:S(2)}) copy-start(bf16[24,32,512]{2,1,0:T(8,128)(2,1)S(1)} %collective-permute-done.2.other_ref) | copy-start | bytes 2359300
  5.4 23.6 %all-to-all-start = ((bf16[16,32,512]{2,1,0:T(8,128)(2,1)}), bf16[16,32,512]{2,1,0:T(8,128)(2,1)S(1)}, u32[]{:S(2)}, u32[]{:S(2)}) async-start(bf16[16,32,512]{2,1,0:T(8,128)(2,1)} %even_rows.1.grad_slab_ref), calls=%async_computation | async-start | bytes 1048576 | tf_op jit(solution)/shard_map/all_to_all | solution.py:722
  13.8 14.0 %copy-start.4 = (bf16[3,32,512]{2,1,0:T(8,128)(2,1)}, bf16[3,32,512]{2,1,0:T(8,128)(2,1)S(1)}, u32[]{:S(2)}) copy-start(bf16[3,32,512]{2,1,0:T(8,128)(2,1)S(1)} %collective-permute-done.1.rim_ref) | copy-start | bytes 294916
  29.0 12.0 %copy-start.6 = (bf16[16,32,512]{2,1,0:T(8,128)(2,1)}, bf16[16,32,512]{2,1,0:T(8,128)(2,1)S(1)}, u32[]{:S(2)}) copy-start(bf16[16,32,512]{2,1,0:T(8,128)(2,1)S(1)} %all-to-all-done) | copy-start | bytes 1572868
  29.0 19.5 %all-to-all-start.1 = ((bf16[16,32,512]{2,1,0:T(8,128)(2,1)}), bf16[16,32,512]{2,1,0:T(8,128)(2,1)S(1)}, u32[]{:S(2)}, u32[]{:S(2)}) async-start(bf16[16,32,512]{2,1,0:T(8,128)(2,1)} %get-tuple-element.28), calls=%async_computation.1 | async-start | bytes 1048576 | tf_op jit(solution)/shard_map/all_to_all | solution.py:722
  61.1 18.3 %all-to-all-start.2 = ((bf16[16,32,512]{2,1,0:T(8,128)(2,1)}), bf16[16,32,512]{2,1,0:T(8,128)(2,1)S(1)}, u32[]{:S(2)}, u32[]{:S(2)}) async-start(bf16[16,32,512]{2,1,0:T(8,128)(2,1)} %bitcast.10), calls=%async_computation.2 | async-start | bytes 1048576 | tf_op jit(solution)/shard_map/all_to_all | solution.py:722
  79.4 6.3 %copy-start.8 = (bf16[16,32,512]{2,1,0:T(8,128)(2,1)}, bf16[16,32,512]{2,1,0:T(8,128)(2,1)S(1)}, u32[]{:S(2)}) copy-start(bf16[16,32,512]{2,1,0:T(8,128)(2,1)S(1)} %all-to-all-done.2.grad_ref) | copy-start | bytes 1572868
  79.5 6.3 %collective-permute-start.3 = (bf16[1,32,512]{2,1,0:T(8,128)(2,1)S(1)}, bf16[1,32,512]{2,1,0:T(8,128)(2,1)S(1)}, u32[]{:S(2)}, u32[]{:S(2)}) collective-permute-start(bf16[1,32,512]{2,1,0:T(8,128)(2,1)S(1)} %get-tuple-element.45), channel_id=1, source_target_pairs={{0,1},{1,0},{2,3},{3,2},{4,5},{5,4},{6,7},{7,6},{8,9},{9,8},{10,11... | collective-permute-start | bytes 98312 | tf_op jit(solution)/shard_map/ppermute | solution.py:729
  79.5 6.2 %collective-permute-start.4 = (bf16[1,32,512]{2,1,0:T(8,128)(2,1)S(1)}, bf16[1,32,512]{2,1,0:T(8,128)(2,1)S(1)}, u32[]{:S(2)}, u32[]{:S(2)}) collective-permute-start(bf16[1,32,512]{2,1,0:T(8,128)(2,1)S(1)} %get-tuple-element.46), channel_id=1, source_target_pairs={{1,2},{3,4},{5,6},{7,8},{9,10},{11,12},{13,14},{2,1},{4,3},{6,5},{... | collective-permute-start | bytes 98312 | tf_op jit(solution)/shard_map/ppermute | solution.py:735
  80.2 21.3 %all-to-all-start.3 = ((bf16[16,32,512]{2,1,0:T(8,128)(2,1)}), bf16[16,32,512]{2,1,0:T(8,128)(2,1)S(1)}, u32[]{:S(2)}, u32[]{:S(2)}) async-start(bf16[16,32,512]{2,1,0:T(8,128)(2,1)} %bitcast.7), calls=%async_computation.3 | async-start | bytes 1048576 | tf_op jit(solution)/shard_map/all_to_all | solution.py:722
  85.8 15.7 %copy-start.7 = (f32[512,512]{1,0:T(8,128)S(1)}, f32[512,512]{1,0:T(8,128)}, u32[]{:S(2)}) copy-start(f32[512,512]{1,0:T(8,128)} %get-tuple-element.40.first_ref) | copy-start | bytes 3145732
  96.9 4.9 %collective-permute-start.6 = (bf16[8,32,512]{2,1,0:T(8,128)(2,1)S(1)}, bf16[8,32,512]{2,1,0:T(8,128)(2,1)S(1)}, u32[]{:S(2)}, u32[]{:S(2)}) collective-permute-start(bf16[8,32,512]{2,1,0:T(8,128)(2,1)S(1)} %slice_select_fusion), channel_id=1, source_target_pairs={{0,1},{1,0},{2,3},{3,2},{4,5},{5,4},{6,7},{7,6},{8,9},{9,8},{10,11... | collective-permute-start | bytes 786440 | tf_op jit(solution)/shard_map/ppermute | solution.py:729
  101.8 1.6 %collective-permute-start.5 = (bf16[8,32,512]{2,1,0:T(8,128)(2,1)S(1)}, bf16[8,32,512]{2,1,0:T(8,128)(2,1)S(1)}, u32[]{:S(2)}, u32[]{:S(2)}) collective-permute-start(bf16[8,32,512]{2,1,0:T(8,128)(2,1)S(1)} %broadcast_select_fusion), channel_id=1, source_target_pairs={{0,1},{1,0},{2,3},{3,2},{4,5},{5,4},{6,7},{7,6},{8,9},{9,8},{10,11... | collective-permute-start | bytes 786440 | tf_op jit(solution)/shard_map/ppermute | solution.py:729

commit v15 on v14

--- a/solution.py
+++ b/solution.py
@@ -13,7 +13,7 @@
 RIM = 2
 EPSILON = 1e-06
 CHUNK = 512
-GROUP_FORWARD = 10
+WIDE = 256
 GROUP_BACKWARD = 9
 LANES = 128
 ROOT = math.sqrt(2.0 / math.pi)
@@ -196,7 +196,7 @@
 
 def forward_body(bands_ref, features_ref, other_ref, rim_ref, expand_ref, taps_ref, project_ref, first_ref,
                  own_first_ref, normed_ref, slab_ref, expanded_ref, mixed_ref, slab, normed_one, expand, project,
-                 expanded, hidden, mixed, hidden_two, total, normed, row_sems,
+                 expanded, hidden_a, hidden_b, mixed, two_a, two_b, total, normed, row_sems,
                  weight_sems, chunk_sems, out_sems):
     rows, cols, width = slab.shape
     own = rows - 2 * RIM
@@ -226,6 +226,7 @@
         return pltpu.make_async_copy(mixed.at[:, :, lanes], mixed_ref.at[:, :, lanes], chunk_sems.at[1, index])
 
     fetch_expand(0).start()
+    fetch_expand(1).start()
     fetch_project(0).start()
     for index, (first, count) in enumerate(pieces):
         wait_pull(sources, count, slab.at[pl.ds(first, count)], row_sems.at[index])
@@ -238,42 +239,91 @@
     total[...] = slab[1 : rows - 1].astype(F32).reshape((rows - 2) * cols, width)
     column = lax.broadcasted_iota(jnp.int32, (cols, LANES), 0)
 
+    def expand_piece(chunk, hidden, row, lane):
+        weights = expand[:, chunk_lanes(jnp.minimum(chunk, chunks - 1), lane, WIDE)]
+        product = nn_dot(normed_one[row * cols : (row + 4) * cols, :], weights)
+        for inner in range(4):
+            for at in range(0, WIDE, LANES):
+                values = product[inner * cols : (inner + 1) * cols, at : at + LANES]
+                lanes = slice(lane + at, lane + at + LANES)
+                hidden[row + inner, :, lanes] = gelu(values).astype(BF16).astype(F32)
+                if RIM <= row + inner < RIM + own:
+                    expanded[row + inner - RIM, :, chunk_lanes(chunk, lane + at, LANES)] = values.astype(BF16)
+
+    def project_piece(chunk, hidden_two, row, lane):
+        at = slice(row * cols, (row + 6) * cols)
+        weights = project[pl.ds(pl.multiple_of(chunk * CHUNK, CHUNK), CHUNK), lane : lane + WIDE]
+        total[at, lane : lane + WIDE] += nn_dot(hidden_two[at, :], weights)
+
+    def mix_piece(chunk, hidden, hidden_two, taps, row, lane):
+        lanes = slice(lane, lane + LANES)
+        rows_near = [hidden[row + a, :, lanes] for a in range(3)]
+        sums = [
+            taps[b] * rows_near[0] + taps[3 + b] * rows_near[1] + taps[6 + b] * rows_near[2] for b in range(3)
+        ]
+        values = column_sums(sums[0], sums[1], sums[2], column, cols - 1)
+        hidden_two[row * cols : (row + 1) * cols, lanes] = gelu(values).astype(BF16)
+        mixed[row, :, chunk_lanes(chunk, lane, LANES)] = values.astype(BF16)
+
+    expand_places = [(row, lane) for lane in range(0, CHUNK, WIDE) for row in range(0, rows, 4)]
+    project_places = [(row, lane) for lane in range(0, width, WIDE) for row in range(0, rows - 2, 6)]
+
+    def stage(chunk, hidden, hidden_two, next_hidden, last_two):
+        products = [lambda at=at: expand_piece(chunk + 1, next_hidden, *at) for at in expand_places]
+        for number, at in enumerate(project_places):
+            piece = lambda at=at: project_piece(jnp.maximum(chunk - 1, 0), last_two, *at)
+            products.insert(min(3 * number, len(products)), piece)
+        pieces = [(row, lane) for lane in range(0, CHUNK, LANES) for row in range(rows - 2)]
+        done = 0
+        for number, (row, lane) in enumerate(pieces):
+            if number % (rows - 2) == 0:
+                taps = spread_taps(taps_ref, chunk_lanes(chunk, lane, LANES), cols)
+            while done * len(pieces) <= number * len(products) and done < len(products):
+                products[done]()
+                done += 1
+            mix_piece(chunk, hidden, hidden_two, taps, row, lane)
+        for piece in products[done:]:
+            piece()
+
+    def store_chunk(chunk):
+        store_expanded(chunk).start()
+        store_mixed(chunk).start()
+
     def step(index, carry):
-        @pl.when(index + 1 < chunks)
+        even = 2 * index
+
+        @pl.when(index > 0)
         def _():
-            fetch_expand(index + 1).start()
-            fetch_project(index + 1).start()
-
-        fetch_expand(index).wait()
-        weights = expand[:, chunk_lanes(index)]
-        for row in range(0, rows, GROUP_FORWARD):
-            product = nn_dot(normed_one[row * cols : (row + GROUP_FORWARD) * cols, :], weights)
-            for inner in range(GROUP_FORWARD):
-                for lane in range(0, CHUNK, LANES):
-                    lanes = slice(lane, lane + LANES)
-                    values = product[inner * cols : (inner + 1) * cols, lanes]
-                    hidden[row + inner, :, lanes] = gelu(values).astype(BF16).astype(F32)
-                    if RIM <= row + inner < RIM + own:
-                        expanded[row + inner - RIM, :, chunk_lanes(index, lane, LANES)] = values.astype(BF16)
-        store_expanded(index).start()
-
-        for lane in range(0, CHUNK, LANES):
-            lanes = slice(lane, lane + LANES)
-            taps = spread_taps(taps_ref, chunk_lanes(index, lane, LANES), cols)
-            for row in range(rows - 2):
-                rows_near = [hidden[row + a, :, lanes] for a in range(3)]
-                sums = [
-                    taps[b] * rows_near[0] + taps[3 + b] * rows_near[1] + taps[6 + b] * rows_near[2] for b in range(3)
-                ]
-                values = column_sums(sums[0], sums[1], sums[2], column, cols - 1)
-                hidden_two[row * cols : (row + 1) * cols, lanes] = gelu(values).astype(BF16)
-                mixed[row, :, chunk_lanes(index, lane, LANES)] = values.astype(BF16)
-        store_mixed(index).start()
-        fetch_project(index).wait()
-        total[...] += nn_dot(hidden_two[...], project[chunk_lanes(index), :])
+            fetch_project(even - 1).wait()
+
+        fetch_expand(even + 1).wait()
+
+        @pl.when(index + 1 < chunks // 2)
+        def _():
+            fetch_expand(even + 2).start()
+
+        fetch_project(even + 1).start()
+        stage(even, hidden_a, two_a, hidden_b, two_b)
+        store_chunk(even)
+        fetch_project(even).wait()
+
+        @pl.when(index + 1 < chunks // 2)
+        def _():
+            fetch_expand(even + 2).wait()
+            fetch_expand(even + 3).start()
+            fetch_project(even + 2).start()
+
+        stage(even + 1, hidden_b, two_b, hidden_a, two_a)
+        store_chunk(even + 1)
         return carry
 
-    lax.fori_loop(0, chunks, step, 0)
+    two_b[...] = jnp.zeros_like(two_b)
+    fetch_expand(0).wait()
+    for row, lane in expand_places:
+        expand_piece(0, hidden_a, row, lane)
+    lax.fori_loop(0, chunks // 2, step, 0)
+    fetch_project(chunks - 1).wait()
+    total[...] += nn_dot(two_b[...], project[pl.ds((chunks - 1) * CHUNK, CHUNK), :])
     for row in range(1, own + 1):
         first = total[row * cols : (row + 1) * cols]
         normed[row - 1] = (first * rms_scale(first)).astype(BF16)
@@ -319,9 +369,11 @@
             pltpu.VMEM((rows * cols, width), BF16),
             pltpu.VMEM((width, hidden_width), BF16),
             pltpu.VMEM((hidden_width, width), BF16),
-            pltpu.VMEM((own, cols, hidden_width), BF16),
+            pltpu.VMEM((own, cols, hidden_width + CHUNK), BF16),
+            pltpu.VMEM((rows, cols, CHUNK), F32),
             pltpu.VMEM((rows, cols, CHUNK), F32),
             pltpu.VMEM((rows - 2, cols, hidden_width), BF16),
+            pltpu.VMEM(((rows - 2) * cols, CHUNK), BF16),
             pltpu.VMEM(((rows - 2) * cols, CHUNK), BF16),
             pltpu.VMEM(((rows - 2) * cols, width), F32),
             pltpu.VMEM((own, cols, width), BF16),
@@ -330,7 +382,7 @@
             pltpu.SemaphoreType.DMA((2, chunks)),
             pltpu.SemaphoreType.DMA((5,)),
         ],
-        compiler_params=params(24),
+        compiler_params=params(28),
         cost_estimate=pl.CostEstimate(
             flops=16 * 10**9,
             bytes_accessed=48 * MIB,

time: 105 us -> 105 us (level)
  no operation moved by 1% of the time
where the time goes in v15:
time: 105 us; the launch traced here: 104 us
  Pallas kernels  53 us (50%)
  starting transfers between devices  25 us (24%)
  waiting for transfers between devices  20.8 us (20%)
  other arithmetic  2.29 us (2%)
  between operations  1.5 us (1%)
  local copies, waits for them, and re-layouts  1.29 us (1%)
    all_to_all x4, starting transfers between devices, exchange_windows(): lax.all_to_all(rows, 'row', split_axis=0, concat_axis=0, tiled=True, axis...  22.1 us
    all_to_all x4, waiting for transfers between devices, exchange_windows(): lax.all_to_all(rows, 'row', split_axis=0, concat_axis=0, tiled=True, axis...  20 us
    pallas_call x1, Pallas kernels, forward(): pl.pallas_call(forward_body, in_specs=[in_scalars(), in_hbm(), in_vmem(),...  13.6 us
    pallas_call x1, Pallas kernels, attention(): pl.pallas_call(attention_body, in_specs=[in_vmem(), in_hbm(), in_hbm()],...  12.6 us
    pallas_call x1, Pallas kernels, backward(): pl.pallas_call(backward_body, in_specs=[in_scalars()] + [in_hbm()] * 8 +...  11.1 us
    pallas_call x1, Pallas kernels, slopes(): pl.pallas_call(slopes_body, grid=(hidden_width // CHUNK,), in_specs=block...  7.1 us
    pallas_call x1, Pallas kernels, attend(): pl.pallas_call(attended_body, grid=(1,), in_specs=[whole(weights.shape),...  3.52 us
    pallas_call x1, Pallas kernels, attended_gradient(): pl.pallas_call(grad_attended_body, grid=(1,), in_specs=[whole(cotangent.s...  2.57 us
  transfers between devices with their start and end apart: 11, of which 6 were waited for; matrix products, arithmetic and copies ran while one was open for 2% of the time, Pallas kernels for 39%

profile of v15, /device:TPU:0, one launch (start us, length us, event | category | flops | bytes accessed | tf_op | source)
XLA Modules:
  0.0 103.8 jit_solution(17167561055656907814)
XLA Ops:
  0.7 0.5 collective-permute-start.2
  1.3 1.1 %rim_rows.1 = bf16[3,32,512]{2,1,0:T(8,128)(2,1)S(1)} custom-call(s32[16]{0:T(128)} %bands_ref.7, bf16[24,32,512]{2,1,0:T(8,128)(2,1)} %features_ref.3, bf16[24,32,512]{2,1,0:T(8,128)(2,1)} %cotangent_ref.3), custom_call_target="tpu_custom_call" | custom-call | tf_op jit(solution)/shard_map/rim_rows/pallas_call | solution.py:167
  2.3 0.7 collective-permute-start.1
  3.3 0.7 copy-done.2
  4.0 1.4 %even_rows.1.grad_slab_ref = bf16[16,32,512]{2,1,0:T(8,128)(2,1)} custom-call(s32[16]{0:T(128)S(1)} %copy-done.2, bf16[24,32,512]{2,1,0:T(8,128)(2,1)S(1)} %copy-done, bf16[24,32,512]{2,1,0:T(8,128)(2,1)S(1)} %collective-permute-done.2.other_ref), custom_call_target="tpu_custom_call" | custom-call | tf_op jit(solution)/shard_map/even_rows/pallas_call | solution.py:128
  5.4 8.4 %all-to-all-start = ((bf16[16,32,512]{2,1,0:T(8,128)(2,1)}), bf16[16,32,512]{2,1,0:T(8,128)(2,1)S(1)}, u32[]{:S(2)}, u32[]{:S(2)}) async-start(bf16[16,32,512]{2,1,0:T(8,128)(2,1)} %even_rows.1.grad_slab_ref), calls=%async_computation | async-start | bytes 1048576 | tf_op jit(solution)/shard_map/all_to_all | solution.py:774
  13.9 13.6 %bottleneck_forward.1 = (f32[64,512]{1,0:T(8,128)}, f32[512,512]{1,0:T(8,128)}, bf16[16,32,512]{2,1,0:T(8,128)(2,1)}, bf16[16,32,512]{2,1,0:T(8,128)(2,1)}, bf16...) custom-call(s32[16]{0:T(128)S(1)} %copy-done.3, bf16[24,32,512]{2,1,0:T(8,128)(2,1)} %features_ref.3, ...), custom_call_target="tpu_custom_call" | custom-call | flops 16000000000 | bytes 50331648 | tf_op jit(solution)/shard_map/bottleneck_forward/pallas_call | solution.py:355
  27.5 1.5 %all-to-all-done = bf16[16,32,512]{2,1,0:T(8,128)(2,1)S(1)} async-done(((bf16[16,32,512]{2,1,0:T(8,128)(2,1)}), bf16[16,32,512]{2,1,0:T(8,128)(2,1)S(1)}, u32[]{:S(2)}, u32[]{:S(2)}) %all-to-all-start) | async-done | bytes 524320 | tf_op jit(solution)/shard_map/all_to_all | solution.py:774
  29.0 4.4 %all-to-all-start.1 = ((bf16[16,32,512]{2,1,0:T(8,128)(2,1)}), bf16[16,32,512]{2,1,0:T(8,128)(2,1)S(1)}, u32[]{:S(2)}, u32[]{:S(2)}) async-start(bf16[16,32,512]{2,1,0:T(8,128)(2,1)} %get-tuple-element.28), calls=%async_computation.1 | async-start | bytes 1048576 | tf_op jit(solution)/shard_map/all_to_all | solution.py:774
  33.4 7.1 %gelu_slopes.1 = (bf16[16,32,2048]{2,1,0:T(8,128)(2,1)}, bf16[18,32,2048]{2,1,0:T(8,128)(2,1)}) custom-call(bf16[16,32,2048]{2,1,0:T(8,128)(2,1)} %get-tuple-element.29.expanded_ref, bf16[18,32,2048]{2,1,0:T(8,128)(2,1)} %get-tuple-element.30.mixed_ref), custom_call_target="tpu_custom_call" | custom-call | flops 33423360 | bytes 13369344 | tf_op jit(solution)/shard_map/gelu_slopes/pallas_call | solution.py:409
  40.5 2.6 %attended_gradient.1.grad_attended_ref = bf16[512,512]{1,0:T(8,128)(2,1)} custom-call(bf16[8,2,32,512]{3,2,1,0:T(8,128)(2,1)} %bitcast.8, bf16[512,512]{1,0:T(8,128)(2,1)} %out_ref.3), custom_call_target="tpu_custom_call" | custom-call | flops 268435456 | bytes 2097152 | tf_op jit(solution)/shard_map/attended_gradient/pallas_call | solution.py:472
  43.1 4.9 %all-to-all-done.1 = bf16[16,32,512]{2,1,0:T(8,128)(2,1)S(1)} async-done(((bf16[16,32,512]{2,1,0:T(8,128)(2,1)}), bf16[16,32,512]{2,1,0:T(8,128)(2,1)S(1)}, u32[]{:S(2)}, u32[]{:S(2)}) %all-to-all-start.1) | async-done | bytes 524320 | tf_op jit(solution)/shard_map/all_to_all | solution.py:774
  48.0 12.6 %window_attention.1 = (bf16[8,2,32,512]{3,2,1,0:T(8,128)(2,1)}, bf16[8,64,1024]{2,1,0:T(8,128)(2,1)}, bf16[512,512]{1,0:T(8,128)(2,1)}) custom-call(bf16[8,2,32,512]{3,2,1,0:T(8,128)(2,1)S(1)} %bitcast.6, bf16[512,512]{1,0:T(8,128)(2,1)} %attended_gradient.1.grad_attended_ref, bf16[512,1536]{1,0:T(8,128)(2,1)} %qkv_ref.1), custom_call_target="tpu_custom_call" | custom-call | flops 2147483648 | bytes 4194304 | tf_op jit(solution)/shard_map/window_attention/pallas_call | solution.py:562
  60.7 3.6 %all-to-all-start.2 = ((bf16[16,32,512]{2,1,0:T(8,128)(2,1)}), bf16[16,32,512]{2,1,0:T(8,128)(2,1)S(1)}, u32[]{:S(2)}, u32[]{:S(2)}) async-start(bf16[16,32,512]{2,1,0:T(8,128)(2,1)} %bitcast.10), calls=%async_computation.2 | async-start | bytes 1048576 | tf_op jit(solution)/shard_map/all_to_all | solution.py:774
  64.3 0.6 dynamic_slice.3
  65.5 3.5 %attended_output.1 = bf16[8,2,32,512]{3,2,1,0:T(8,128)(2,1)} custom-call(bf16[8,64,1024]{2,1,0:T(8,128)(2,1)} %get-tuple-element.37.weights_ref, bf16[512,512]{1,0:T(8,128)(2,1)} %get-tuple-element.38.values_ref, bf16[512,512]{1,0:T(8,128)(2,1)} %out_ref.3), custom_call_target="tpu_custom_call" | custom-call | flops 536870912 | bytes 3145728 | tf_op jit(solution)/shard_map/attended_output/pallas_call | solution.py:602
  69.1 9.9 %all-to-all-done.2.grad_ref = bf16[16,32,512]{2,1,0:T(8,128)(2,1)S(1)} async-done(((bf16[16,32,512]{2,1,0:T(8,128)(2,1)}), bf16[16,32,512]{2,1,0:T(8,128)(2,1)S(1)}, u32[]{:S(2)}, u32[]{:S(2)}) %all-to-all-start.2) | async-done | bytes 524320 | tf_op jit(solution)/shard_map/all_to_all | solution.py:774
  79.1 0.7 collective-permute-start.4
  79.7 5.5 %all-to-all-start.3 = ((bf16[16,32,512]{2,1,0:T(8,128)(2,1)}), bf16[16,32,512]{2,1,0:T(8,128)(2,1)S(1)}, u32[]{:S(2)}, u32[]{:S(2)}) async-start(bf16[16,32,512]{2,1,0:T(8,128)(2,1)} %bitcast.7), calls=%async_computation.3 | async-start | bytes 1048576 | tf_op jit(solution)/shard_map/all_to_all | solution.py:774
  85.3 11.1 %bottleneck_backward.1 = bf16[16,32,512]{2,1,0:T(8,128)(2,1)S(1)} custom-call(s32[16]{0:T(128)S(1)} %copy-done.3, bf16[24,32,512]{2,1,0:T(8,128)(2,1)} %cotangent_ref.3, bf16[24,32,512]{2,1,0:T(8,128)(2,1)} %copy-done.1, bf16[3,32,512]{2,1,0:T(8,128)(2,1)} %copy-done.4, bf16[16,32,512]{2,1,0:T(8,128)(2,1)} %get-tuple-element.41.slab_ref, ...), custom_call_target="tpu_custom_call" | custom-call | flops 16000000000 | bytes 50331648 | tf_op jit(solution)/shard_map/bottleneck_backward/pallas_call | solution.py:730
  96.5 0.8 collective-permute-start.6
  97.3 3.7 %all-to-all-done.3 = bf16[16,32,512]{2,1,0:T(8,128)(2,1)S(1)} async-done(((bf16[16,32,512]{2,1,0:T(8,128)(2,1)}), bf16[16,32,512]{2,1,0:T(8,128)(2,1)S(1)}, u32[]{:S(2)}, u32[]{:S(2)}) %all-to-all-start.3) | async-done | bytes 524320 | tf_op jit(solution)/shard_map/all_to_all | solution.py:774
  101.4 1.0 pad_maximum_fusion.1
  102.9 1.0 pad_maximum_fusion
  (33 shorter events, 1.4 us)
Async XLA Ops:
  0.6 2.7 %copy-start = (bf16[24,32,512]{2,1,0:T(8,128)(2,1)S(1)}, bf16[24,32,512]{2,1,0:T(8,128)(2,1)}, u32[]{:S(2)}) copy-start(bf16[24,32,512]{2,1,0:T(8,128)(2,1)} %cotangent_ref.3) | copy-start | bytes 2359300
  0.6 13.2 %copy-start.3 = (s32[16]{0:T(128)S(1)}, s32[16]{0:T(128)}, u32[]{:S(2)}) copy-start(s32[16]{0:T(128)} %bands_ref.7) | copy-start | bytes 196
  0.7 13.2 %copy-start.5 = (bf16[9,2048]{1,0:T(8,128)(2,1)S(1)}, bf16[9,2048]{1,0:T(8,128)(2,1)}, u32[]{:S(2)}) copy-start(bf16[9,2048]{1,0:T(8,128)(2,1)} %taps_ref.3) | copy-start | bytes 110596
  0.7 2.6 %collective-permute-start.2 = (bf16[24,32,512]{2,1,0:T(8,128)(2,1)}, bf16[24,32,512]{2,1,0:T(8,128)(2,1)S(1)}, u32[]{:S(2)}, u32[]{:S(2)}) collective-permute-start(bf16[24,32,512]{2,1,0:T(8,128)(2,1)} %cotangent_ref.3), channel_id=1, source_target_pairs={{0,1},{1,0},{2,3},{3,2},{4,5},{5,4},{6,7},{7,6},{8,9},{9,8},{10,11... | collective-permute-start | bytes 2359304 | tf_op jit(solution)/shard_map/ppermute | solution.py:781
  1.2 12.7 %collective-permute-start = (bf16[24,32,512]{2,1,0:T(8,128)(2,1)}, bf16[24,32,512]{2,1,0:T(8,128)(2,1)S(1)}, u32[]{:S(2)}, u32[]{:S(2)}) collective-permute-start(bf16[24,32,512]{2,1,0:T(8,128)(2,1)} %features_ref.3), channel_id=1, source_target_pairs={{0,1},{1,0},{2,3},{3,2},{4,5},{5,4},{6,7},{7,6},{8,9},{9,8},{10,11... | collective-permute-start | bytes 2359304 | tf_op jit(solution)/shard_map/ppermute | solution.py:781
  2.3 11.5 %collective-permute-start.1 = (bf16[3,32,512]{2,1,0:T(8,128)(2,1)S(1)}, bf16[3,32,512]{2,1,0:T(8,128)(2,1)S(1)}, u32[]{:S(2)}, u32[]{:S(2)}) collective-permute-start(bf16[3,32,512]{2,1,0:T(8,128)(2,1)S(1)} %rim_rows.1), channel_id=1, source_target_pairs={{1,2},{3,4},{5,6},{7,8},{9,10},{11,12},{13,14},{2,1},{4,3},{6,5},{... | collective-permute-start | bytes 294920 | tf_op jit(solution)/shard_map/ppermute | solution.py:787
  3.3 0.7 copy-start.2
  4.0 23.5 %copy-start.1 = (bf16[24,32,512]{2,1,0:T(8,128)(2,1)}, bf16[24,32,512]{2,1,0:T(8,128)(2,1)S(1)}, u32[]{:S(2)}) copy-start(bf16[24,32,512]{2,1,0:T(8,128)(2,1)S(1)} %collective-permute-done.2.other_ref) | copy-start | bytes 2359300
  5.4 23.6 %all-to-all-start = ((bf16[16,32,512]{2,1,0:T(8,128)(2,1)}), bf16[16,32,512]{2,1,0:T(8,128)(2,1)S(1)}, u32[]{:S(2)}, u32[]{:S(2)}) async-start(bf16[16,32,512]{2,1,0:T(8,128)(2,1)} %even_rows.1.grad_slab_ref), calls=%async_computation | async-start | bytes 1048576 | tf_op jit(solution)/shard_map/all_to_all | solution.py:774
  13.8 13.6 %copy-start.4 = (bf16[3,32,512]{2,1,0:T(8,128)(2,1)}, bf16[3,32,512]{2,1,0:T(8,128)(2,1)S(1)}, u32[]{:S(2)}) copy-start(bf16[3,32,512]{2,1,0:T(8,128)(2,1)S(1)} %collective-permute-done.1.rim_ref) | copy-start | bytes 294916
  29.0 11.5 %copy-start.6 = (bf16[16,32,512]{2,1,0:T(8,128)(2,1)}, bf16[16,32,512]{2,1,0:T(8,128)(2,1)S(1)}, u32[]{:S(2)}) copy-start(bf16[16,32,512]{2,1,0:T(8,128)(2,1)S(1)} %all-to-all-done) | copy-start | bytes 1572868
  29.0 19.0 %all-to-all-start.1 = ((bf16[16,32,512]{2,1,0:T(8,128)(2,1)}), bf16[16,32,512]{2,1,0:T(8,128)(2,1)S(1)}, u32[]{:S(2)}, u32[]{:S(2)}) async-start(bf16[16,32,512]{2,1,0:T(8,128)(2,1)} %get-tuple-element.28), calls=%async_computation.1 | async-start | bytes 1048576 | tf_op jit(solution)/shard_map/all_to_all | solution.py:774
  60.7 18.3 %all-to-all-start.2 = ((bf16[16,32,512]{2,1,0:T(8,128)(2,1)}), bf16[16,32,512]{2,1,0:T(8,128)(2,1)S(1)}, u32[]{:S(2)}, u32[]{:S(2)}) async-start(bf16[16,32,512]{2,1,0:T(8,128)(2,1)} %bitcast.10), calls=%async_computation.2 | async-start | bytes 1048576 | tf_op jit(solution)/shard_map/all_to_all | solution.py:774
  79.0 6.3 %copy-start.8 = (bf16[16,32,512]{2,1,0:T(8,128)(2,1)}, bf16[16,32,512]{2,1,0:T(8,128)(2,1)S(1)}, u32[]{:S(2)}) copy-start(bf16[16,32,512]{2,1,0:T(8,128)(2,1)S(1)} %all-to-all-done.2.grad_ref) | copy-start | bytes 1572868
  79.0 6.3 %collective-permute-start.3 = (bf16[1,32,512]{2,1,0:T(8,128)(2,1)S(1)}, bf16[1,32,512]{2,1,0:T(8,128)(2,1)S(1)}, u32[]{:S(2)}, u32[]{:S(2)}) collective-permute-start(bf16[1,32,512]{2,1,0:T(8,128)(2,1)S(1)} %get-tuple-element.45), channel_id=1, source_target_pairs={{0,1},{1,0},{2,3},{3,2},{4,5},{5,4},{6,7},{7,6},{8,9},{9,8},{10,11... | collective-permute-start | bytes 98312 | tf_op jit(solution)/shard_map/ppermute | solution.py:781
  79.1 6.2 %collective-permute-start.4 = (bf16[1,32,512]{2,1,0:T(8,128)(2,1)S(1)}, bf16[1,32,512]{2,1,0:T(8,128)(2,1)S(1)}, u32[]{:S(2)}, u32[]{:S(2)}) collective-permute-start(bf16[1,32,512]{2,1,0:T(8,128)(2,1)S(1)} %get-tuple-element.46), channel_id=1, source_target_pairs={{1,2},{3,4},{5,6},{7,8},{9,10},{11,12},{13,14},{2,1},{4,3},{6,5},{... | collective-permute-start | bytes 98312 | tf_op jit(solution)/shard_map/ppermute | solution.py:787
  79.7 21.2 %all-to-all-start.3 = ((bf16[16,32,512]{2,1,0:T(8,128)(2,1)}), bf16[16,32,512]{2,1,0:T(8,128)(2,1)S(1)}, u32[]{:S(2)}, u32[]{:S(2)}) async-start(bf16[16,32,512]{2,1,0:T(8,128)(2,1)} %bitcast.7), calls=%async_computation.3 | async-start | bytes 1048576 | tf_op jit(solution)/shard_map/all_to_all | solution.py:774
  85.3 15.7 %copy-start.7 = (f32[512,512]{1,0:T(8,128)S(1)}, f32[512,512]{1,0:T(8,128)}, u32[]{:S(2)}) copy-start(f32[512,512]{1,0:T(8,128)} %get-tuple-element.40.first_ref) | copy-start | bytes 3145732
  96.5 4.8 %collective-permute-start.6 = (bf16[8,32,512]{2,1,0:T(8,128)(2,1)S(1)}, bf16[8,32,512]{2,1,0:T(8,128)(2,1)S(1)}, u32[]{:S(2)}, u32[]{:S(2)}) collective-permute-start(bf16[8,32,512]{2,1,0:T(8,128)(2,1)S(1)} %slice_select_fusion), channel_id=1, source_target_pairs={{0,1},{1,0},{2,3},{3,2},{4,5},{5,4},{6,7},{7,6},{8,9},{9,8},{10,11... | collective-permute-start | bytes 786440 | tf_op jit(solution)/shard_map/ppermute | solution.py:781
  101.2 1.6 %collective-permute-start.5 = (bf16[8,32,512]{2,1,0:T(8,128)(2,1)S(1)}, bf16[8,32,512]{2,1,0:T(8,128)(2,1)S(1)}, u32[]{:S(2)}, u32[]{:S(2)}) collective-permute-start(bf16[8,32,512]{2,1,0:T(8,128)(2,1)S(1)} %broadcast_select_fusion), channel_id=1, source_target_pairs={{0,1},{1,0},{2,3},{3,2},{4,5},{5,4},{6,7},{7,6},{8,9},{9,8},{10,11... | collective-permute-start | bytes 786440 | tf_op jit(solution)/shard_map/ppermute | solution.py:781

commit v16 on v13

--- a/solution.py
+++ b/solution.py
@@ -459,24 +459,31 @@
 
     def window(index, carry):
         rows = pl.ds(pl.multiple_of(index * span, span), span)
-        for part in range(width // LANES):
-            q_at, k_at, v_at = (
-                slice(t * width + part * LANES, t * width + (part + 1) * LANES) for t in range(3)
-            )
-            q, k, v = projected[rows, q_at], projected[rows, k_at], projected[rows, v_at]
-            q_wide = spread(q)
-            g_wide = spread(grad_attended[rows, q_at])
-            scores = nt_dot(k, q_wide)
-            powers = jnp.exp2((scores - jnp.max(scores, axis=0, keepdims=True)) * steepness)
-            shares = powers * (1.0 / jnp.sum(powers, axis=0, keepdims=True))
-            half = shares.astype(BF16)
-            weights[index, :, part * heads * span : (part + 1) * heads * span] = half
-            grad_weights = nt_dot(v, g_wide)
-            row_dot = jnp.sum(shares * grad_weights, axis=0, keepdims=True)
-            grad_scores = (shares * (grad_weights - row_dot)).astype(BF16)
-            grad_projected[rows, q_at] = per_query(k, grad_scores, span, head_dim, scale)
-            grad_projected[rows, k_at] = (nn_dot(grad_scores, q_wide) * scale).astype(BF16)
-            grad_projected[rows, v_at] = nn_dot(half, g_wide).astype(BF16)
+        parts = range(width // LANES)
+        places = [
+            [slice(t * width + part * LANES, t * width + (part + 1) * LANES) for t in range(3)] for part in parts
+        ]
+        keys = [projected[rows, k_at] for _, k_at, _ in places]
+        q_wide = [spread(projected[rows, q_at]) for q_at, _, _ in places]
+        scores = [nt_dot(keys[part], q_wide[part]) for part in parts]
+        g_wide = [spread(grad_attended[rows, q_at]) for q_at, _, _ in places]
+        grad_weights = [nt_dot(projected[rows, places[part][2]], g_wide[part]) for part in parts]
+        powers = [
+            jnp.exp2((score - jnp.max(score, axis=0, keepdims=True)) * steepness) for score in scores
+        ]
+        shares = [power * (1.0 / jnp.sum(power, axis=0, keepdims=True)) for power in powers]
+        halves = [share.astype(BF16) for share in shares]
+        row_dots = [jnp.sum(shares[part] * grad_weights[part], axis=0, keepdims=True) for part in parts]
+        grad_scores = [(shares[part] * (grad_weights[part] - row_dots[part])).astype(BF16) for part in parts]
+        for part in parts:
+            weights[index, :, part * heads * span : (part + 1) * heads * span] = halves[part]
+        grad_values = [nn_dot(halves[part], g_wide[part]) for part in parts]
+        grad_keys = [nn_dot(grad_scores[part], q_wide[part]) for part in parts]
+        grad_queries = [per_query(keys[part], grad_scores[part], span, head_dim, scale) for part in parts]
+        for part, (q_at, k_at, v_at) in enumerate(places):
+            grad_projected[rows, v_at] = grad_values[part].astype(BF16)
+            grad_projected[rows, k_at] = (grad_keys[part] * scale).astype(BF16)
+            grad_projected[rows, q_at] = grad_queries[part]
         return carry
 
     lax.fori_loop(0, windows, window, 0, unroll=4)

time: 105 us -> 101 us (0.962)
  Pallas kernels: 53.4 us -> 48.8 us
    pallas_call x1, Pallas kernels: 12.6 us -> 7.98 us  [attention(): pl.pallas_call(attention_body, in_specs=[in_vmem(), in_hbm(), in_hbm()],...]
  transfers between devices with their start and end apart: 11 -> 11, of which waited for: 5 -> 5; matrix products, arithmetic and copies ran while one was open for 2% -> 2% of each run, Pallas kernels for 39% -> 41%
where the time goes in v16:
time: 101 us; the launch traced here: 100 us
  Pallas kernels  48.8 us (48%)
  starting transfers between devices  25.8 us (26%)
  waiting for transfers between devices  20.3 us (20%)
  other arithmetic  2.29 us (2%)
  between operations  1.51 us (1%)
  local copies, waits for them, and re-layouts  1.29 us (1%)
    all_to_all x4, starting transfers between devices, exchange_windows(): lax.all_to_all(rows, 'row', split_axis=0, concat_axis=0, tiled=True, axis...  22.8 us
    all_to_all x4, waiting for transfers between devices, exchange_windows(): lax.all_to_all(rows, 'row', split_axis=0, concat_axis=0, tiled=True, axis...  19.8 us
    pallas_call x1, Pallas kernels, forward(): pl.pallas_call(forward_body, in_specs=[in_scalars(), in_hbm(), in_vmem(),...  13.9 us
    pallas_call x1, Pallas kernels, backward(): pl.pallas_call(backward_body, in_specs=[in_scalars()] + [in_hbm()] * 8 +...  10.8 us
    pallas_call x1, Pallas kernels, attention(): pl.pallas_call(attention_body, in_specs=[in_vmem(), in_hbm(), in_hbm()],...  7.98 us
    pallas_call x1, Pallas kernels, slopes(): pl.pallas_call(slopes_body, grid=(hidden_width // CHUNK,), in_specs=block...  7.1 us
    pallas_call x1, Pallas kernels, attend(): pl.pallas_call(attended_body, grid=(1,), in_specs=[whole(weights.shape),...  3.52 us
    pallas_call x1, Pallas kernels, attended_gradient(): pl.pallas_call(grad_attended_body, grid=(1,), in_specs=[whole(cotangent.s...  2.57 us
  transfers between devices with their start and end apart: 11, of which 5 were waited for; matrix products, arithmetic and copies ran while one was open for 2% of the time, Pallas kernels for 41%

profile of v16, /device:TPU:0, one launch (start us, length us, event | category | flops | bytes accessed | tf_op | source)
XLA Modules:
  0.0 100.0 jit_solution(17697185635199691316)
XLA Ops:
  0.6 0.5 collective-permute-start.2
  1.2 0.7 copy-done.2
  1.9 1.4 %rim_rows.1 = bf16[3,32,512]{2,1,0:T(8,128)(2,1)S(1)} custom-call(s32[16]{0:T(128)S(1)} %copy-done.2, bf16[24,32,512]{2,1,0:T(8,128)(2,1)} %features_ref.3, bf16[24,32,512]{2,1,0:T(8,128)(2,1)} %cotangent_ref.3), custom_call_target="tpu_custom_call" | custom-call | tf_op jit(solution)/shard_map/rim_rows/pallas_call | solution.py:158
  3.3 0.7 collective-permute-start.1
  4.0 1.4 %even_rows.1.grad_slab_ref = bf16[16,32,512]{2,1,0:T(8,128)(2,1)} custom-call(s32[16]{0:T(128)S(1)} %copy-done.2, bf16[24,32,512]{2,1,0:T(8,128)(2,1)S(1)} %copy-done, bf16[24,32,512]{2,1,0:T(8,128)(2,1)S(1)} %collective-permute-done.2.other_ref), custom_call_target="tpu_custom_call" | custom-call | tf_op jit(solution)/shard_map/even_rows/pallas_call | solution.py:129
  5.5 8.7 %all-to-all-start = ((bf16[16,32,512]{2,1,0:T(8,128)(2,1)}), bf16[16,32,512]{2,1,0:T(8,128)(2,1)S(1)}, u32[]{:S(2)}, u32[]{:S(2)}) async-start(bf16[16,32,512]{2,1,0:T(8,128)(2,1)} %even_rows.1.grad_slab_ref), calls=%async_computation | async-start | bytes 1048576 | tf_op jit(solution)/shard_map/all_to_all | solution.py:718
  14.2 13.9 %bottleneck_forward.1 = (f32[64,512]{1,0:T(8,128)}, f32[512,512]{1,0:T(8,128)}, bf16[16,32,512]{2,1,0:T(8,128)(2,1)}, bf16[16,32,512]{2,1,0:T(8,128)(2,1)}, bf16...) custom-call(s32[16]{0:T(128)S(1)} %copy-done.3, bf16[24,32,512]{2,1,0:T(8,128)(2,1)} %features_ref.3, ...), custom_call_target="tpu_custom_call" | custom-call | flops 16000000000 | bytes 50331648 | tf_op jit(solution)/shard_map/bottleneck_forward/pallas_call | solution.py:293
  28.2 1.1 %all-to-all-done = bf16[16,32,512]{2,1,0:T(8,128)(2,1)S(1)} async-done(((bf16[16,32,512]{2,1,0:T(8,128)(2,1)}), bf16[16,32,512]{2,1,0:T(8,128)(2,1)S(1)}, u32[]{:S(2)}, u32[]{:S(2)}) %all-to-all-start) | async-done | bytes 524320 | tf_op jit(solution)/shard_map/all_to_all | solution.py:718
  29.3 4.9 %all-to-all-start.1 = ((bf16[16,32,512]{2,1,0:T(8,128)(2,1)}), bf16[16,32,512]{2,1,0:T(8,128)(2,1)S(1)}, u32[]{:S(2)}, u32[]{:S(2)}) async-start(bf16[16,32,512]{2,1,0:T(8,128)(2,1)} %get-tuple-element.28), calls=%async_computation.1 | async-start | bytes 1048576 | tf_op jit(solution)/shard_map/all_to_all | solution.py:718
  34.2 7.1 %gelu_slopes.1 = (bf16[16,32,2048]{2,1,0:T(8,128)(2,1)}, bf16[18,32,2048]{2,1,0:T(8,128)(2,1)}) custom-call(bf16[16,32,2048]{2,1,0:T(8,128)(2,1)} %get-tuple-element.29.expanded_ref, bf16[18,32,2048]{2,1,0:T(8,128)(2,1)} %get-tuple-element.30.mixed_ref), custom_call_target="tpu_custom_call" | custom-call | flops 33423360 | bytes 13369344 | tf_op jit(solution)/shard_map/gelu_slopes/pallas_call | solution.py:345
  41.3 2.6 %attended_gradient.1.grad_attended_ref = bf16[512,512]{1,0:T(8,128)(2,1)} custom-call(bf16[8,2,32,512]{3,2,1,0:T(8,128)(2,1)} %bitcast.8, bf16[512,512]{1,0:T(8,128)(2,1)} %out_ref.3), custom_call_target="tpu_custom_call" | custom-call | flops 268435456 | bytes 2097152 | tf_op jit(solution)/shard_map/attended_gradient/pallas_call | solution.py:408
  43.9 4.9 %all-to-all-done.1 = bf16[16,32,512]{2,1,0:T(8,128)(2,1)S(1)} async-done(((bf16[16,32,512]{2,1,0:T(8,128)(2,1)}), bf16[16,32,512]{2,1,0:T(8,128)(2,1)S(1)}, u32[]{:S(2)}, u32[]{:S(2)}) %all-to-all-start.1) | async-done | bytes 524320 | tf_op jit(solution)/shard_map/all_to_all | solution.py:718
  48.8 8.0 %window_attention.1 = (bf16[8,2,32,512]{3,2,1,0:T(8,128)(2,1)}, bf16[8,64,1024]{2,1,0:T(8,128)(2,1)}, bf16[512,512]{1,0:T(8,128)(2,1)}) custom-call(bf16[8,2,32,512]{3,2,1,0:T(8,128)(2,1)S(1)} %bitcast.6, bf16[512,512]{1,0:T(8,128)(2,1)} %attended_gradient.1.grad_attended_ref, bf16[512,1536]{1,0:T(8,128)(2,1)} %qkv_ref.1), custom_call_target="tpu_custom_call" | custom-call | flops 2147483648 | bytes 4194304 | tf_op jit(solution)/shard_map/window_attention/pallas_call | solution.py:505
  56.7 3.7 %all-to-all-start.2 = ((bf16[16,32,512]{2,1,0:T(8,128)(2,1)}), bf16[16,32,512]{2,1,0:T(8,128)(2,1)S(1)}, u32[]{:S(2)}, u32[]{:S(2)}) async-start(bf16[16,32,512]{2,1,0:T(8,128)(2,1)} %bitcast.10), calls=%async_computation.2 | async-start | bytes 1048576 | tf_op jit(solution)/shard_map/all_to_all | solution.py:718
  60.4 0.6 dynamic_slice.3
  61.6 3.5 %attended_output.1 = bf16[8,2,32,512]{3,2,1,0:T(8,128)(2,1)} custom-call(bf16[8,64,1024]{2,1,0:T(8,128)(2,1)} %get-tuple-element.37.weights_ref, bf16[512,512]{1,0:T(8,128)(2,1)} %get-tuple-element.38.values_ref, bf16[512,512]{1,0:T(8,128)(2,1)} %out_ref.3), custom_call_target="tpu_custom_call" | custom-call | flops 536870912 | bytes 3145728 | tf_op jit(solution)/shard_map/attended_output/pallas_call | solution.py:545
  65.1 9.9 %all-to-all-done.2.grad_ref = bf16[16,32,512]{2,1,0:T(8,128)(2,1)S(1)} async-done(((bf16[16,32,512]{2,1,0:T(8,128)(2,1)}), bf16[16,32,512]{2,1,0:T(8,128)(2,1)S(1)}, u32[]{:S(2)}, u32[]{:S(2)}) %all-to-all-start.2) | async-done | bytes 524320 | tf_op jit(solution)/shard_map/all_to_all | solution.py:718
  75.2 0.7 collective-permute-start.4
  75.8 5.5 %all-to-all-start.3 = ((bf16[16,32,512]{2,1,0:T(8,128)(2,1)}), bf16[16,32,512]{2,1,0:T(8,128)(2,1)S(1)}, u32[]{:S(2)}, u32[]{:S(2)}) async-start(bf16[16,32,512]{2,1,0:T(8,128)(2,1)} %bitcast.7), calls=%async_computation.3 | async-start | bytes 1048576 | tf_op jit(solution)/shard_map/all_to_all | solution.py:718
  81.4 10.8 %bottleneck_backward.1 = bf16[16,32,512]{2,1,0:T(8,128)(2,1)S(1)} custom-call(s32[16]{0:T(128)S(1)} %copy-done.3, bf16[24,32,512]{2,1,0:T(8,128)(2,1)} %cotangent_ref.3, bf16[24,32,512]{2,1,0:T(8,128)(2,1)} %copy-done.1, bf16[3,32,512]{2,1,0:T(8,128)(2,1)} %copy-done.4, bf16[16,32,512]{2,1,0:T(8,128)(2,1)} %get-tuple-element.41.slab_ref, ...), custom_call_target="tpu_custom_call" | custom-call | flops 16000000000 | bytes 50331648 | tf_op jit(solution)/shard_map/bottleneck_backward/pallas_call | solution.py:674
  92.3 1.0 %collective-permute-start.6 = (bf16[8,32,512]{2,1,0:T(8,128)(2,1)S(1)}, bf16[8,32,512]{2,1,0:T(8,128)(2,1)S(1)}, u32[]{:S(2)}, u32[]{:S(2)}) collective-permute-start(bf16[8,32,512]{2,1,0:T(8,128)(2,1)S(1)} %slice_select_fusion), channel_id=1, source_target_pairs={{0,1},{1,0},{2,3},{3,2},{4,5},{5,4},{6,7},{7,6},{8,9},{9,8},{10,11... | collective-permute-start | bytes 786440 | tf_op jit(solution)/shard_map/ppermute | solution.py:725
  93.3 3.9 %all-to-all-done.3 = bf16[16,32,512]{2,1,0:T(8,128)(2,1)S(1)} async-done(((bf16[16,32,512]{2,1,0:T(8,128)(2,1)}), bf16[16,32,512]{2,1,0:T(8,128)(2,1)S(1)}, u32[]{:S(2)}, u32[]{:S(2)}) %all-to-all-start.3) | async-done | bytes 524320 | tf_op jit(solution)/shard_map/all_to_all | solution.py:718
  97.5 1.0 pad_maximum_fusion.1
  99.0 1.0 pad_maximum_fusion
  (33 shorter events, 1.1 us)
Async XLA Ops:
  0.6 3.4 %copy-start = (bf16[24,32,512]{2,1,0:T(8,128)(2,1)S(1)}, bf16[24,32,512]{2,1,0:T(8,128)(2,1)}, u32[]{:S(2)}) copy-start(bf16[24,32,512]{2,1,0:T(8,128)(2,1)} %cotangent_ref.3) | copy-start | bytes 2359300
  0.6 3.4 %collective-permute-start.2 = (bf16[24,32,512]{2,1,0:T(8,128)(2,1)}, bf16[24,32,512]{2,1,0:T(8,128)(2,1)S(1)}, u32[]{:S(2)}, u32[]{:S(2)}) collective-permute-start(bf16[24,32,512]{2,1,0:T(8,128)(2,1)} %cotangent_ref.3), channel_id=1, source_target_pairs={{0,1},{1,0},{2,3},{3,2},{4,5},{5,4},{6,7},{7,6},{8,9},{9,8},{10,11... | collective-permute-start | bytes 2359304 | tf_op jit(solution)/shard_map/ppermute | solution.py:725
  1.2 13.0 %collective-permute-start = (bf16[24,32,512]{2,1,0:T(8,128)(2,1)}, bf16[24,32,512]{2,1,0:T(8,128)(2,1)S(1)}, u32[]{:S(2)}, u32[]{:S(2)}) collective-permute-start(bf16[24,32,512]{2,1,0:T(8,128)(2,1)} %features_ref.3), channel_id=1, source_target_pairs={{0,1},{1,0},{2,3},{3,2},{4,5},{5,4},{6,7},{7,6},{8,9},{9,8},{10,11... | collective-permute-start | bytes 2359304 | tf_op jit(solution)/shard_map/ppermute | solution.py:725
  1.2 0.7 copy-start.2
  1.9 12.3 %copy-start.3 = (s32[16]{0:T(128)S(1)}, s32[16]{0:T(128)}, u32[]{:S(2)}) copy-start(s32[16]{0:T(128)} %bands_ref.7) | copy-start | bytes 196
  1.9 12.3 %copy-start.5 = (bf16[9,2048]{1,0:T(8,128)(2,1)S(1)}, bf16[9,2048]{1,0:T(8,128)(2,1)}, u32[]{:S(2)}) copy-start(bf16[9,2048]{1,0:T(8,128)(2,1)} %taps_ref.3) | copy-start | bytes 110596
  3.3 10.8 %collective-permute-start.1 = (bf16[3,32,512]{2,1,0:T(8,128)(2,1)S(1)}, bf16[3,32,512]{2,1,0:T(8,128)(2,1)S(1)}, u32[]{:S(2)}, u32[]{:S(2)}) collective-permute-start(bf16[3,32,512]{2,1,0:T(8,128)(2,1)S(1)} %rim_rows.1), channel_id=1, source_target_pairs={{1,2},{3,4},{5,6},{7,8},{9,10},{11,12},{13,14},{2,1},{4,3},{6,5},{... | collective-permute-start | bytes 294920 | tf_op jit(solution)/shard_map/ppermute | solution.py:731
  4.0 24.1 %copy-start.1 = (bf16[24,32,512]{2,1,0:T(8,128)(2,1)}, bf16[24,32,512]{2,1,0:T(8,128)(2,1)S(1)}, u32[]{:S(2)}) copy-start(bf16[24,32,512]{2,1,0:T(8,128)(2,1)S(1)} %collective-permute-done.2.other_ref) | copy-start | bytes 2359300
  5.5 23.8 %all-to-all-start = ((bf16[16,32,512]{2,1,0:T(8,128)(2,1)}), bf16[16,32,512]{2,1,0:T(8,128)(2,1)S(1)}, u32[]{:S(2)}, u32[]{:S(2)}) async-start(bf16[16,32,512]{2,1,0:T(8,128)(2,1)} %even_rows.1.grad_slab_ref), calls=%async_computation | async-start | bytes 1048576 | tf_op jit(solution)/shard_map/all_to_all | solution.py:718
  14.2 14.0 %copy-start.4 = (bf16[3,32,512]{2,1,0:T(8,128)(2,1)}, bf16[3,32,512]{2,1,0:T(8,128)(2,1)S(1)}, u32[]{:S(2)}) copy-start(bf16[3,32,512]{2,1,0:T(8,128)(2,1)S(1)} %collective-permute-done.1.rim_ref) | copy-start | bytes 294916
  29.3 12.0 %copy-start.6 = (bf16[16,32,512]{2,1,0:T(8,128)(2,1)}, bf16[16,32,512]{2,1,0:T(8,128)(2,1)S(1)}, u32[]{:S(2)}) copy-start(bf16[16,32,512]{2,1,0:T(8,128)(2,1)S(1)} %all-to-all-done) | copy-start | bytes 1572868
  29.3 19.5 %all-to-all-start.1 = ((bf16[16,32,512]{2,1,0:T(8,128)(2,1)}), bf16[16,32,512]{2,1,0:T(8,128)(2,1)S(1)}, u32[]{:S(2)}, u32[]{:S(2)}) async-start(bf16[16,32,512]{2,1,0:T(8,128)(2,1)} %get-tuple-element.28), calls=%async_computation.1 | async-start | bytes 1048576 | tf_op jit(solution)/shard_map/all_to_all | solution.py:718
  56.7 18.3 %all-to-all-start.2 = ((bf16[16,32,512]{2,1,0:T(8,128)(2,1)}), bf16[16,32,512]{2,1,0:T(8,128)(2,1)S(1)}, u32[]{:S(2)}, u32[]{:S(2)}) async-start(bf16[16,32,512]{2,1,0:T(8,128)(2,1)} %bitcast.10), calls=%async_computation.2 | async-start | bytes 1048576 | tf_op jit(solution)/shard_map/all_to_all | solution.py:718
  75.1 6.3 %copy-start.8 = (bf16[16,32,512]{2,1,0:T(8,128)(2,1)}, bf16[16,32,512]{2,1,0:T(8,128)(2,1)S(1)}, u32[]{:S(2)}) copy-start(bf16[16,32,512]{2,1,0:T(8,128)(2,1)S(1)} %all-to-all-done.2.grad_ref) | copy-start | bytes 1572868
  75.1 6.3 %collective-permute-start.3 = (bf16[1,32,512]{2,1,0:T(8,128)(2,1)S(1)}, bf16[1,32,512]{2,1,0:T(8,128)(2,1)S(1)}, u32[]{:S(2)}, u32[]{:S(2)}) collective-permute-start(bf16[1,32,512]{2,1,0:T(8,128)(2,1)S(1)} %get-tuple-element.45), channel_id=1, source_target_pairs={{0,1},{1,0},{2,3},{3,2},{4,5},{5,4},{6,7},{7,6},{8,9},{9,8},{10,11... | collective-permute-start | bytes 98312 | tf_op jit(solution)/shard_map/ppermute | solution.py:725
  75.2 6.2 %collective-permute-start.4 = (bf16[1,32,512]{2,1,0:T(8,128)(2,1)S(1)}, bf16[1,32,512]{2,1,0:T(8,128)(2,1)S(1)}, u32[]{:S(2)}, u32[]{:S(2)}) collective-permute-start(bf16[1,32,512]{2,1,0:T(8,128)(2,1)S(1)} %get-tuple-element.46), channel_id=1, source_target_pairs={{1,2},{3,4},{5,6},{7,8},{9,10},{11,12},{13,14},{2,1},{4,3},{6,5},{... | collective-permute-start | bytes 98312 | tf_op jit(solution)/shard_map/ppermute | solution.py:731
  75.8 21.3 %all-to-all-start.3 = ((bf16[16,32,512]{2,1,0:T(8,128)(2,1)}), bf16[16,32,512]{2,1,0:T(8,128)(2,1)S(1)}, u32[]{:S(2)}, u32[]{:S(2)}) async-start(bf16[16,32,512]{2,1,0:T(8,128)(2,1)} %bitcast.7), calls=%async_computation.3 | async-start | bytes 1048576 | tf_op jit(solution)/shard_map/all_to_all | solution.py:718
  81.4 15.7 %copy-start.7 = (f32[512,512]{1,0:T(8,128)S(1)}, f32[512,512]{1,0:T(8,128)}, u32[]{:S(2)}) copy-start(f32[512,512]{1,0:T(8,128)} %get-tuple-element.40.first_ref) | copy-start | bytes 3145732
  92.3 5.2 %collective-permute-start.6 = (bf16[8,32,512]{2,1,0:T(8,128)(2,1)S(1)}, bf16[8,32,512]{2,1,0:T(8,128)(2,1)S(1)}, u32[]{:S(2)}, u32[]{:S(2)}) collective-permute-start(bf16[8,32,512]{2,1,0:T(8,128)(2,1)S(1)} %slice_select_fusion), channel_id=1, source_target_pairs={{0,1},{1,0},{2,3},{3,2},{4,5},{5,4},{6,7},{7,6},{8,9},{9,8},{10,11... | collective-permute-start | bytes 786440 | tf_op jit(solution)/shard_map/ppermute | solution.py:725
  97.4 1.6 %collective-permute-start.5 = (bf16[8,32,512]{2,1,0:T(8,128)(2,1)S(1)}, bf16[8,32,512]{2,1,0:T(8,128)(2,1)S(1)}, u32[]{:S(2)}, u32[]{:S(2)}) collective-permute-start(bf16[8,32,512]{2,1,0:T(8,128)(2,1)S(1)} %broadcast_select_fusion), channel_id=1, source_target_pairs={{0,1},{1,0},{2,3},{3,2},{4,5},{5,4},{6,7},{7,6},{8,9},{9,8},{10,11... | collective-permute-start | bytes 786440 | tf_op jit(solution)/shard_map/ppermute | solution.py:725

commit v17 on v16

--- a/solution.py
+++ b/solution.py
@@ -114,23 +114,21 @@
     pltpu.make_async_copy(sources[0].at[pl.ds(0, rows)], target, sem).wait()
 
 
-def even_body(bands_ref, own_ref, other_ref, out_ref):
+def even_body(bands_ref, own_ref, other_ref, out_ref, sems):
+    targets = [out_ref.at[pl.ds(BAND * half, BAND)] for half in range(2)]
     for half in range(2):
-        where, row = place(bands_ref, BAND * half)
-        for number, source in enumerate((own_ref, other_ref)):
-
-            @pl.when(where == number)
-            def _():
-                out_ref[BAND * half : BAND * half + BAND] = source[pl.ds(row, BAND)]
+        start_pull(bands_ref, BAND * half, (own_ref, other_ref), BAND, targets[half], sems.at[half])
+    for half in range(2):
+        wait_pull((own_ref,), BAND, targets[half], sems.at[half])
 
 
 def even_rows(bands, own, other):
-    shape = (GRID_ROWS,) + own.shape[1:]
     return pl.pallas_call(
         even_body,
         in_specs=[in_scalars(), in_vmem(), in_vmem()],
-        out_specs=in_vmem(),
-        out_shape=jax.ShapeDtypeStruct(shape, own.dtype),
+        out_specs=in_hbm(),
+        out_shape=pltpu.HBM((GRID_ROWS,) + own.shape[1:], own.dtype),
+        scratch_shapes=[pltpu.SemaphoreType.DMA((2,))],
         compiler_params=params(8),
         name="even_rows",
     )(bands, near(own), near(other))
@@ -457,36 +455,40 @@
     def spread(values):
         return jnp.concatenate([values] * heads, axis=0) * mask
 
-    def window(index, carry):
-        rows = pl.ds(pl.multiple_of(index * span, span), span)
-        parts = range(width // LANES)
-        places = [
-            [slice(t * width + part * LANES, t * width + (part + 1) * LANES) for t in range(3)] for part in parts
-        ]
-        keys = [projected[rows, k_at] for _, k_at, _ in places]
-        q_wide = [spread(projected[rows, q_at]) for q_at, _, _ in places]
-        scores = [nt_dot(keys[part], q_wide[part]) for part in parts]
-        g_wide = [spread(grad_attended[rows, q_at]) for q_at, _, _ in places]
-        grad_weights = [nt_dot(projected[rows, places[part][2]], g_wide[part]) for part in parts]
+    parts = range(width // LANES)
+    lane_places = [
+        [slice(t * width + part * LANES, t * width + (part + 1) * LANES) for t in range(3)] for part in parts
+    ]
+
+    def two_windows(index, carry):
+        places = []
+        for number in (2 * index, 2 * index + 1):
+            rows = pl.ds(pl.multiple_of(number * span, span), span)
+            places += [(number, part, rows) + tuple(lane_places[part]) for part in parts]
+        keys = [projected[rows, k_at] for _, _, rows, _, k_at, _ in places]
+        q_wide = [spread(projected[rows, q_at]) for _, _, rows, q_at, _, _ in places]
+        scores = [nt_dot(k, q) for k, q in zip(keys, q_wide)]
+        g_wide = [spread(grad_attended[rows, q_at]) for _, _, rows, q_at, _, _ in places]
+        grad_weights = [nt_dot(projected[place[2], place[5]], g) for place, g in zip(places, g_wide)]
         powers = [
             jnp.exp2((score - jnp.max(score, axis=0, keepdims=True)) * steepness) for score in scores
         ]
         shares = [power * (1.0 / jnp.sum(power, axis=0, keepdims=True)) for power in powers]
         halves = [share.astype(BF16) for share in shares]
-        row_dots = [jnp.sum(shares[part] * grad_weights[part], axis=0, keepdims=True) for part in parts]
-        grad_scores = [(shares[part] * (grad_weights[part] - row_dots[part])).astype(BF16) for part in parts]
-        for part in parts:
-            weights[index, :, part * heads * span : (part + 1) * heads * span] = halves[part]
-        grad_values = [nn_dot(halves[part], g_wide[part]) for part in parts]
-        grad_keys = [nn_dot(grad_scores[part], q_wide[part]) for part in parts]
-        grad_queries = [per_query(keys[part], grad_scores[part], span, head_dim, scale) for part in parts]
-        for part, (q_at, k_at, v_at) in enumerate(places):
-            grad_projected[rows, v_at] = grad_values[part].astype(BF16)
-            grad_projected[rows, k_at] = (grad_keys[part] * scale).astype(BF16)
-            grad_projected[rows, q_at] = grad_queries[part]
+        row_dots = [jnp.sum(s * g, axis=0, keepdims=True) for s, g in zip(shares, grad_weights)]
+        grad_scores = [(s * (g - d)).astype(BF16) for s, g, d in zip(shares, grad_weights, row_dots)]
+        for (number, part, *_), half in zip(places, halves):
+            weights[number, :, part * heads * span : (part + 1) * heads * span] = half
+        grad_values = [nn_dot(half, g) for half, g in zip(halves, g_wide)]
+        grad_keys = [nn_dot(scored, q) for scored, q in zip(grad_scores, q_wide)]
+        grad_queries = [per_query(k, scored, span, head_dim, scale) for k, scored in zip(keys, grad_scores)]
+        for number, (_, _, rows, q_at, k_at, v_at) in enumerate(places):
+            grad_projected[rows, v_at] = grad_values[number].astype(BF16)
+            grad_projected[rows, k_at] = (grad_keys[number] * scale).astype(BF16)
+            grad_projected[rows, q_at] = grad_queries[number]
         return carry
 
-    lax.fori_loop(0, windows, window, 0, unroll=4)
+    lax.fori_loop(0, windows // 2, two_windows, 0, unroll=2)
     store_weights = pltpu.make_async_copy(weights, weights_ref, out_sems.at[1])
     store_weights.start()
     to_rows(nt_dot(grad_projected[...], qkv[...]), rows_wide, grad)

time: 101 us -> 100 us (0.990)
  no operation moved by 1% of the time
where the time goes in v17:
time: 100 us; the launch traced here: 99.5 us
  Pallas kernels  48.2 us (48%)
  starting transfers between devices  25.8 us (26%)
  waiting for transfers between devices  20.3 us (20%)
  other arithmetic  2.29 us (2%)
  between operations  1.52 us (2%)
  local copies, waits for them, and re-layouts  1.29 us (1%)
    all_to_all x4, starting transfers between devices, exchange_windows(): lax.all_to_all(rows, 'row', split_axis=0, concat_axis=0, tiled=True, axis...  22.7 us
    all_to_all x4, waiting for transfers between devices, exchange_windows(): lax.all_to_all(rows, 'row', split_axis=0, concat_axis=0, tiled=True, axis...  19.8 us
    pallas_call x1, Pallas kernels, forward(): pl.pallas_call(forward_body, in_specs=[in_scalars(), in_hbm(), in_vmem(),...  13.9 us
    pallas_call x1, Pallas kernels, backward(): pl.pallas_call(backward_body, in_specs=[in_scalars()] + [in_hbm()] * 8 +...  10.8 us
    pallas_call x1, Pallas kernels, attention(): pl.pallas_call(attention_body, in_specs=[in_vmem(), in_hbm(), in_hbm()],...  7.51 us
    pallas_call x1, Pallas kernels, slopes(): pl.pallas_call(slopes_body, grid=(hidden_width // CHUNK,), in_specs=block...  7.1 us
    pallas_call x1, Pallas kernels, attend(): pl.pallas_call(attended_body, grid=(1,), in_specs=[whole(weights.shape),...  3.52 us
    pallas_call x1, Pallas kernels, attended_gradient(): pl.pallas_call(grad_attended_body, grid=(1,), in_specs=[whole(cotangent.s...  2.57 us
  transfers between devices with their start and end apart: 11, of which 5 were waited for; matrix products, arithmetic and copies ran while one was open for 2% of the time, Pallas kernels for 41%

profile of v17, /device:TPU:0, one launch (start us, length us, event | category | flops | bytes accessed | tf_op | source)
XLA Modules:
  0.0 99.5 jit_solution(10714639165056469014)
XLA Ops:
  0.6 0.5 collective-permute-start.2
  1.2 0.7 copy-done.2
  1.9 1.4 %rim_rows.1 = bf16[3,32,512]{2,1,0:T(8,128)(2,1)S(1)} custom-call(s32[16]{0:T(128)S(1)} %copy-done.2, bf16[24,32,512]{2,1,0:T(8,128)(2,1)} %features_ref.3, bf16[24,32,512]{2,1,0:T(8,128)(2,1)} %cotangent_ref.3), custom_call_target="tpu_custom_call" | custom-call | tf_op jit(solution)/shard_map/rim_rows/pallas_call | solution.py:156
  3.3 0.7 collective-permute-start.1
  4.0 1.4 %even_rows.1.grad_slab_ref = bf16[16,32,512]{2,1,0:T(8,128)(2,1)} custom-call(s32[16]{0:T(128)S(1)} %copy-done.2, bf16[24,32,512]{2,1,0:T(8,128)(2,1)S(1)} %copy-done, bf16[24,32,512]{2,1,0:T(8,128)(2,1)S(1)} %collective-permute-done.2.other_ref), custom_call_target="tpu_custom_call" | custom-call | tf_op jit(solution)/shard_map/even_rows/pallas_call | solution.py:126
  5.4 8.7 %all-to-all-start = ((bf16[16,32,512]{2,1,0:T(8,128)(2,1)}), bf16[16,32,512]{2,1,0:T(8,128)(2,1)S(1)}, u32[]{:S(2)}, u32[]{:S(2)}) async-start(bf16[16,32,512]{2,1,0:T(8,128)(2,1)} %even_rows.1.grad_slab_ref), calls=%async_computation | async-start | bytes 1048576 | tf_op jit(solution)/shard_map/all_to_all | solution.py:720
  14.2 13.9 %bottleneck_forward.1 = (f32[64,512]{1,0:T(8,128)}, f32[512,512]{1,0:T(8,128)}, bf16[16,32,512]{2,1,0:T(8,128)(2,1)}, bf16[16,32,512]{2,1,0:T(8,128)(2,1)}, bf16...) custom-call(s32[16]{0:T(128)S(1)} %copy-done.3, bf16[24,32,512]{2,1,0:T(8,128)(2,1)} %features_ref.3, ...), custom_call_target="tpu_custom_call" | custom-call | flops 16000000000 | bytes 50331648 | tf_op jit(solution)/shard_map/bottleneck_forward/pallas_call | solution.py:291
  28.1 1.1 %all-to-all-done = bf16[16,32,512]{2,1,0:T(8,128)(2,1)S(1)} async-done(((bf16[16,32,512]{2,1,0:T(8,128)(2,1)}), bf16[16,32,512]{2,1,0:T(8,128)(2,1)S(1)}, u32[]{:S(2)}, u32[]{:S(2)}) %all-to-all-start) | async-done | bytes 524320 | tf_op jit(solution)/shard_map/all_to_all | solution.py:720
  29.3 4.8 %all-to-all-start.1 = ((bf16[16,32,512]{2,1,0:T(8,128)(2,1)}), bf16[16,32,512]{2,1,0:T(8,128)(2,1)S(1)}, u32[]{:S(2)}, u32[]{:S(2)}) async-start(bf16[16,32,512]{2,1,0:T(8,128)(2,1)} %get-tuple-element.28), calls=%async_computation.1 | async-start | bytes 1048576 | tf_op jit(solution)/shard_map/all_to_all | solution.py:720
  34.1 7.1 %gelu_slopes.1 = (bf16[16,32,2048]{2,1,0:T(8,128)(2,1)}, bf16[18,32,2048]{2,1,0:T(8,128)(2,1)}) custom-call(bf16[16,32,2048]{2,1,0:T(8,128)(2,1)} %get-tuple-element.29.expanded_ref, bf16[18,32,2048]{2,1,0:T(8,128)(2,1)} %get-tuple-element.30.mixed_ref), custom_call_target="tpu_custom_call" | custom-call | flops 33423360 | bytes 13369344 | tf_op jit(solution)/shard_map/gelu_slopes/pallas_call | solution.py:343
  41.2 2.6 %attended_gradient.1.grad_attended_ref = bf16[512,512]{1,0:T(8,128)(2,1)} custom-call(bf16[8,2,32,512]{3,2,1,0:T(8,128)(2,1)} %bitcast.8, bf16[512,512]{1,0:T(8,128)(2,1)} %out_ref.3), custom_call_target="tpu_custom_call" | custom-call | flops 268435456 | bytes 2097152 | tf_op jit(solution)/shard_map/attended_gradient/pallas_call | solution.py:406
  43.8 4.9 %all-to-all-done.1 = bf16[16,32,512]{2,1,0:T(8,128)(2,1)S(1)} async-done(((bf16[16,32,512]{2,1,0:T(8,128)(2,1)}), bf16[16,32,512]{2,1,0:T(8,128)(2,1)S(1)}, u32[]{:S(2)}, u32[]{:S(2)}) %all-to-all-start.1) | async-done | bytes 524320 | tf_op jit(solution)/shard_map/all_to_all | solution.py:720
  48.7 7.5 %window_attention.1 = (bf16[8,2,32,512]{3,2,1,0:T(8,128)(2,1)}, bf16[8,64,1024]{2,1,0:T(8,128)(2,1)}, bf16[512,512]{1,0:T(8,128)(2,1)}) custom-call(bf16[8,2,32,512]{3,2,1,0:T(8,128)(2,1)S(1)} %bitcast.6, bf16[512,512]{1,0:T(8,128)(2,1)} %attended_gradient.1.grad_attended_ref, bf16[512,1536]{1,0:T(8,128)(2,1)} %qkv_ref.1), custom_call_target="tpu_custom_call" | custom-call | flops 2147483648 | bytes 4194304 | tf_op jit(solution)/shard_map/window_attention/pallas_call | solution.py:507
  56.2 3.6 %all-to-all-start.2 = ((bf16[16,32,512]{2,1,0:T(8,128)(2,1)}), bf16[16,32,512]{2,1,0:T(8,128)(2,1)S(1)}, u32[]{:S(2)}, u32[]{:S(2)}) async-start(bf16[16,32,512]{2,1,0:T(8,128)(2,1)} %bitcast.10), calls=%async_computation.2 | async-start | bytes 1048576 | tf_op jit(solution)/shard_map/all_to_all | solution.py:720
  59.8 0.6 dynamic_slice.3
  61.1 3.5 %attended_output.1 = bf16[8,2,32,512]{3,2,1,0:T(8,128)(2,1)} custom-call(bf16[8,64,1024]{2,1,0:T(8,128)(2,1)} %get-tuple-element.37.weights_ref, bf16[512,512]{1,0:T(8,128)(2,1)} %get-tuple-element.38.values_ref, bf16[512,512]{1,0:T(8,128)(2,1)} %out_ref.3), custom_call_target="tpu_custom_call" | custom-call | flops 536870912 | bytes 3145728 | tf_op jit(solution)/shard_map/attended_output/pallas_call | solution.py:547
  64.6 9.9 %all-to-all-done.2.grad_ref = bf16[16,32,512]{2,1,0:T(8,128)(2,1)S(1)} async-done(((bf16[16,32,512]{2,1,0:T(8,128)(2,1)}), bf16[16,32,512]{2,1,0:T(8,128)(2,1)S(1)}, u32[]{:S(2)}, u32[]{:S(2)}) %all-to-all-start.2) | async-done | bytes 524320 | tf_op jit(solution)/shard_map/all_to_all | solution.py:720
  74.6 0.7 collective-permute-start.4
  75.3 5.5 %all-to-all-start.3 = ((bf16[16,32,512]{2,1,0:T(8,128)(2,1)}), bf16[16,32,512]{2,1,0:T(8,128)(2,1)S(1)}, u32[]{:S(2)}, u32[]{:S(2)}) async-start(bf16[16,32,512]{2,1,0:T(8,128)(2,1)} %bitcast.7), calls=%async_computation.3 | async-start | bytes 1048576 | tf_op jit(solution)/shard_map/all_to_all | solution.py:720
  80.9 10.8 %bottleneck_backward.1 = bf16[16,32,512]{2,1,0:T(8,128)(2,1)S(1)} custom-call(s32[16]{0:T(128)S(1)} %copy-done.3, bf16[24,32,512]{2,1,0:T(8,128)(2,1)} %cotangent_ref.3, bf16[24,32,512]{2,1,0:T(8,128)(2,1)} %copy-done.1, bf16[3,32,512]{2,1,0:T(8,128)(2,1)} %copy-done.4, bf16[16,32,512]{2,1,0:T(8,128)(2,1)} %get-tuple-element.41.slab_ref, ...), custom_call_target="tpu_custom_call" | custom-call | flops 16000000000 | bytes 50331648 | tf_op jit(solution)/shard_map/bottleneck_backward/pallas_call | solution.py:676
  91.7 1.0 %collective-permute-start.6 = (bf16[8,32,512]{2,1,0:T(8,128)(2,1)S(1)}, bf16[8,32,512]{2,1,0:T(8,128)(2,1)S(1)}, u32[]{:S(2)}, u32[]{:S(2)}) collective-permute-start(bf16[8,32,512]{2,1,0:T(8,128)(2,1)S(1)} %slice_select_fusion), channel_id=1, source_target_pairs={{0,1},{1,0},{2,3},{3,2},{4,5},{5,4},{6,7},{7,6},{8,9},{9,8},{10,11... | collective-permute-start | bytes 786440 | tf_op jit(solution)/shard_map/ppermute | solution.py:727
  92.8 3.9 %all-to-all-done.3 = bf16[16,32,512]{2,1,0:T(8,128)(2,1)S(1)} async-done(((bf16[16,32,512]{2,1,0:T(8,128)(2,1)}), bf16[16,32,512]{2,1,0:T(8,128)(2,1)S(1)}, u32[]{:S(2)}, u32[]{:S(2)}) %all-to-all-start.3) | async-done | bytes 524320 | tf_op jit(solution)/shard_map/all_to_all | solution.py:720
  97.0 1.0 pad_maximum_fusion.1
  98.5 1.0 pad_maximum_fusion
  (33 shorter events, 1.1 us)
Async XLA Ops:
  0.6 3.4 %copy-start = (bf16[24,32,512]{2,1,0:T(8,128)(2,1)S(1)}, bf16[24,32,512]{2,1,0:T(8,128)(2,1)}, u32[]{:S(2)}) copy-start(bf16[24,32,512]{2,1,0:T(8,128)(2,1)} %cotangent_ref.3) | copy-start | bytes 2359300
  0.6 3.4 %collective-permute-start.2 = (bf16[24,32,512]{2,1,0:T(8,128)(2,1)}, bf16[24,32,512]{2,1,0:T(8,128)(2,1)S(1)}, u32[]{:S(2)}, u32[]{:S(2)}) collective-permute-start(bf16[24,32,512]{2,1,0:T(8,128)(2,1)} %cotangent_ref.3), channel_id=1, source_target_pairs={{0,1},{1,0},{2,3},{3,2},{4,5},{5,4},{6,7},{7,6},{8,9},{9,8},{10,11... | collective-permute-start | bytes 2359304 | tf_op jit(solution)/shard_map/ppermute | solution.py:727
  1.2 13.0 %collective-permute-start = (bf16[24,32,512]{2,1,0:T(8,128)(2,1)}, bf16[24,32,512]{2,1,0:T(8,128)(2,1)S(1)}, u32[]{:S(2)}, u32[]{:S(2)}) collective-permute-start(bf16[24,32,512]{2,1,0:T(8,128)(2,1)} %features_ref.3), channel_id=1, source_target_pairs={{0,1},{1,0},{2,3},{3,2},{4,5},{5,4},{6,7},{7,6},{8,9},{9,8},{10,11... | collective-permute-start | bytes 2359304 | tf_op jit(solution)/shard_map/ppermute | solution.py:727
  1.2 0.7 copy-start.2
  1.9 12.3 %copy-start.3 = (s32[16]{0:T(128)S(1)}, s32[16]{0:T(128)}, u32[]{:S(2)}) copy-start(s32[16]{0:T(128)} %bands_ref.7) | copy-start | bytes 196
  1.9 12.3 %copy-start.5 = (bf16[9,2048]{1,0:T(8,128)(2,1)S(1)}, bf16[9,2048]{1,0:T(8,128)(2,1)}, u32[]{:S(2)}) copy-start(bf16[9,2048]{1,0:T(8,128)(2,1)} %taps_ref.3) | copy-start | bytes 110596
  3.3 10.8 %collective-permute-start.1 = (bf16[3,32,512]{2,1,0:T(8,128)(2,1)S(1)}, bf16[3,32,512]{2,1,0:T(8,128)(2,1)S(1)}, u32[]{:S(2)}, u32[]{:S(2)}) collective-permute-start(bf16[3,32,512]{2,1,0:T(8,128)(2,1)S(1)} %rim_rows.1), channel_id=1, source_target_pairs={{1,2},{3,4},{5,6},{7,8},{9,10},{11,12},{13,14},{2,1},{4,3},{6,5},{... | collective-permute-start | bytes 294920 | tf_op jit(solution)/shard_map/ppermute | solution.py:733
  4.0 24.1 %copy-start.1 = (bf16[24,32,512]{2,1,0:T(8,128)(2,1)}, bf16[24,32,512]{2,1,0:T(8,128)(2,1)S(1)}, u32[]{:S(2)}) copy-start(bf16[24,32,512]{2,1,0:T(8,128)(2,1)S(1)} %collective-permute-done.2.other_ref) | copy-start | bytes 2359300
  5.4 23.8 %all-to-all-start = ((bf16[16,32,512]{2,1,0:T(8,128)(2,1)}), bf16[16,32,512]{2,1,0:T(8,128)(2,1)S(1)}, u32[]{:S(2)}, u32[]{:S(2)}) async-start(bf16[16,32,512]{2,1,0:T(8,128)(2,1)} %even_rows.1.grad_slab_ref), calls=%async_computation | async-start | bytes 1048576 | tf_op jit(solution)/shard_map/all_to_all | solution.py:720
  14.1 14.0 %copy-start.4 = (bf16[3,32,512]{2,1,0:T(8,128)(2,1)}, bf16[3,32,512]{2,1,0:T(8,128)(2,1)S(1)}, u32[]{:S(2)}) copy-start(bf16[3,32,512]{2,1,0:T(8,128)(2,1)S(1)} %collective-permute-done.1.rim_ref) | copy-start | bytes 294916
  29.3 11.9 %copy-start.6 = (bf16[16,32,512]{2,1,0:T(8,128)(2,1)}, bf16[16,32,512]{2,1,0:T(8,128)(2,1)S(1)}, u32[]{:S(2)}) copy-start(bf16[16,32,512]{2,1,0:T(8,128)(2,1)S(1)} %all-to-all-done) | copy-start | bytes 1572868
  29.3 19.4 %all-to-all-start.1 = ((bf16[16,32,512]{2,1,0:T(8,128)(2,1)}), bf16[16,32,512]{2,1,0:T(8,128)(2,1)S(1)}, u32[]{:S(2)}, u32[]{:S(2)}) async-start(bf16[16,32,512]{2,1,0:T(8,128)(2,1)} %get-tuple-element.28), calls=%async_computation.1 | async-start | bytes 1048576 | tf_op jit(solution)/shard_map/all_to_all | solution.py:720
  56.2 18.3 %all-to-all-start.2 = ((bf16[16,32,512]{2,1,0:T(8,128)(2,1)}), bf16[16,32,512]{2,1,0:T(8,128)(2,1)S(1)}, u32[]{:S(2)}, u32[]{:S(2)}) async-start(bf16[16,32,512]{2,1,0:T(8,128)(2,1)} %bitcast.10), calls=%async_computation.2 | async-start | bytes 1048576 | tf_op jit(solution)/shard_map/all_to_all | solution.py:720
  74.5 6.3 %copy-start.8 = (bf16[16,32,512]{2,1,0:T(8,128)(2,1)}, bf16[16,32,512]{2,1,0:T(8,128)(2,1)S(1)}, u32[]{:S(2)}) copy-start(bf16[16,32,512]{2,1,0:T(8,128)(2,1)S(1)} %all-to-all-done.2.grad_ref) | copy-start | bytes 1572868
  74.5 6.3 %collective-permute-start.3 = (bf16[1,32,512]{2,1,0:T(8,128)(2,1)S(1)}, bf16[1,32,512]{2,1,0:T(8,128)(2,1)S(1)}, u32[]{:S(2)}, u32[]{:S(2)}) collective-permute-start(bf16[1,32,512]{2,1,0:T(8,128)(2,1)S(1)} %get-tuple-element.45), channel_id=1, source_target_pairs={{0,1},{1,0},{2,3},{3,2},{4,5},{5,4},{6,7},{7,6},{8,9},{9,8},{10,11... | collective-permute-start | bytes 98312 | tf_op jit(solution)/shard_map/ppermute | solution.py:727
  74.6 6.2 %collective-permute-start.4 = (bf16[1,32,512]{2,1,0:T(8,128)(2,1)S(1)}, bf16[1,32,512]{2,1,0:T(8,128)(2,1)S(1)}, u32[]{:S(2)}, u32[]{:S(2)}) collective-permute-start(bf16[1,32,512]{2,1,0:T(8,128)(2,1)S(1)} %get-tuple-element.46), channel_id=1, source_target_pairs={{1,2},{3,4},{5,6},{7,8},{9,10},{11,12},{13,14},{2,1},{4,3},{6,5},{... | collective-permute-start | bytes 98312 | tf_op jit(solution)/shard_map/ppermute | solution.py:733
  75.3 21.3 %all-to-all-start.3 = ((bf16[16,32,512]{2,1,0:T(8,128)(2,1)}), bf16[16,32,512]{2,1,0:T(8,128)(2,1)S(1)}, u32[]{:S(2)}, u32[]{:S(2)}) async-start(bf16[16,32,512]{2,1,0:T(8,128)(2,1)} %bitcast.7), calls=%async_computation.3 | async-start | bytes 1048576 | tf_op jit(solution)/shard_map/all_to_all | solution.py:720
  80.9 15.7 %copy-start.7 = (f32[512,512]{1,0:T(8,128)S(1)}, f32[512,512]{1,0:T(8,128)}, u32[]{:S(2)}) copy-start(f32[512,512]{1,0:T(8,128)} %get-tuple-element.40.first_ref) | copy-start | bytes 3145732
  91.7 5.2 %collective-permute-start.6 = (bf16[8,32,512]{2,1,0:T(8,128)(2,1)S(1)}, bf16[8,32,512]{2,1,0:T(8,128)(2,1)S(1)}, u32[]{:S(2)}, u32[]{:S(2)}) collective-permute-start(bf16[8,32,512]{2,1,0:T(8,128)(2,1)S(1)} %slice_select_fusion), channel_id=1, source_target_pairs={{0,1},{1,0},{2,3},{3,2},{4,5},{5,4},{6,7},{7,6},{8,9},{9,8},{10,11... | collective-permute-start | bytes 786440 | tf_op jit(solution)/shard_map/ppermute | solution.py:727
  96.8 1.6 %collective-permute-start.5 = (bf16[8,32,512]{2,1,0:T(8,128)(2,1)S(1)}, bf16[8,32,512]{2,1,0:T(8,128)(2,1)S(1)}, u32[]{:S(2)}, u32[]{:S(2)}) collective-permute-start(bf16[8,32,512]{2,1,0:T(8,128)(2,1)S(1)} %broadcast_select_fusion), channel_id=1, source_target_pairs={{0,1},{1,0},{2,3},{3,2},{4,5},{5,4},{6,7},{7,6},{8,9},{9,8},{10,11... | collective-permute-start | bytes 786440 | tf_op jit(solution)/shard_map/ppermute | solution.py:727

commit v18 on v17

--- a/solution.py
+++ b/solution.py
@@ -378,16 +378,17 @@
             target[rows, lanes] = jnp.concatenate(pieces, axis=0).astype(BF16)
 
 
-def to_rows(values, rows_wide, target_ref):
+def to_rows(values, rows_wide, target_ref, start=0):
     groups, own, cols, width = target_ref.shape
     span = groups * 8
-    for tile, lanes in enumerate(lane_tiles(width)):
+    for tile, lanes in enumerate(lane_tiles(values.shape[1])):
         for index, (r, q) in enumerate(window_places(own, cols)):
             for group in range(groups):
                 first = index * span + group * 8
                 rows_wide[tile, group, r, pl.ds(q, 8, stride=cols // 8), :] = values[first : first + 8, lanes]
         for group in range(groups):
-            target_ref[group, :, :, lanes] = rows_wide[tile, group].astype(BF16)
+            at = slice(start + lanes.start, start + lanes.stop)
+            target_ref[group, :, :, at] = rows_wide[tile, group].astype(BF16)
 
 
 def wide_scratch(shape):
@@ -491,12 +492,20 @@
     lax.fori_loop(0, windows // 2, two_windows, 0, unroll=2)
     store_weights = pltpu.make_async_copy(weights, weights_ref, out_sems.at[1])
     store_weights.start()
-    to_rows(nt_dot(grad_projected[...], qkv[...]), rows_wide, grad)
-    store_grad = pltpu.make_async_copy(grad, grad_ref, out_sems.at[2])
-    store_grad.start()
+    stores = []
+    half = width // 2
+    for number in range(2):
+        start = number * half
+        to_rows(nt_dot(grad_projected[...], qkv[start : start + half, :]), rows_wide, grad, start)
+        lanes = pl.ds(start, half)
+        stores.append(
+            pltpu.make_async_copy(grad.at[:, :, :, lanes], grad_ref.at[:, :, :, lanes], out_sems.at[2 + number])
+        )
+        stores[-1].start()
     store_values.wait()
     store_weights.wait()
-    store_grad.wait()
+    for store in stores:
+        store.wait()
 
 
 def attention(normed, grad_attended, w_qkv):
@@ -519,7 +528,7 @@
             pltpu.VMEM(normed.shape, BF16),
             pltpu.VMEM(out_shapes[1], BF16),
             pltpu.SemaphoreType.DMA((2,)),
-            pltpu.SemaphoreType.DMA((3,)),
+            pltpu.SemaphoreType.DMA((4,)),
         ],
         compiler_params=params(18),
         cost_estimate=pl.CostEstimate(

time: 100 us -> 100 us (level)
  no operation moved by 1% of the time
where the time goes in v18:
time: 100 us; the launch traced here: 99.5 us
  Pallas kernels  48.3 us (48%)
  starting transfers between devices  25.9 us (26%)
  waiting for transfers between devices  20.3 us (20%)
  other arithmetic  2.29 us (2%)
  between operations  1.52 us (2%)
  local copies, waits for them, and re-layouts  1.29 us (1%)
    all_to_all x4, starting transfers between devices, exchange_windows(): lax.all_to_all(rows, 'row', split_axis=0, concat_axis=0, tiled=True, axis...  22.8 us
    all_to_all x4, waiting for transfers between devices, exchange_windows(): lax.all_to_all(rows, 'row', split_axis=0, concat_axis=0, tiled=True, axis...  19.8 us
    pallas_call x1, Pallas kernels, forward(): pl.pallas_call(forward_body, in_specs=[in_scalars(), in_hbm(), in_vmem(),...  13.9 us
    pallas_call x1, Pallas kernels, backward(): pl.pallas_call(backward_body, in_specs=[in_scalars()] + [in_hbm()] * 8 +...  10.8 us
    pallas_call x1, Pallas kernels, attention(): pl.pallas_call(attention_body, in_specs=[in_vmem(), in_hbm(), in_hbm()],...  7.51 us
    pallas_call x1, Pallas kernels, slopes(): pl.pallas_call(slopes_body, grid=(hidden_width // CHUNK,), in_specs=block...  7.1 us
    pallas_call x1, Pallas kernels, attend(): pl.pallas_call(attended_body, grid=(1,), in_specs=[whole(weights.shape),...  3.53 us
    pallas_call x1, Pallas kernels, attended_gradient(): pl.pallas_call(grad_attended_body, grid=(1,), in_specs=[whole(cotangent.s...  2.57 us
  transfers between devices with their start and end apart: 11, of which 5 were waited for; matrix products, arithmetic and copies ran while one was open for 2% of the time, Pallas kernels for 41%

profile of v18, /device:TPU:0, one launch (start us, length us, event | category | flops | bytes accessed | tf_op | source)
XLA Modules:
  0.0 99.5 jit_solution(9621227984684184410)
XLA Ops:
  0.6 0.5 collective-permute-start.2
  1.2 0.7 copy-done.2
  1.9 1.4 %rim_rows.1 = bf16[3,32,512]{2,1,0:T(8,128)(2,1)S(1)} custom-call(s32[16]{0:T(128)S(1)} %copy-done.2, bf16[24,32,512]{2,1,0:T(8,128)(2,1)} %features_ref.3, bf16[24,32,512]{2,1,0:T(8,128)(2,1)} %cotangent_ref.3), custom_call_target="tpu_custom_call" | custom-call | tf_op jit(solution)/shard_map/rim_rows/pallas_call | solution.py:156
  3.3 0.7 collective-permute-start.1
  4.0 1.4 %even_rows.1.grad_slab_ref = bf16[16,32,512]{2,1,0:T(8,128)(2,1)} custom-call(s32[16]{0:T(128)S(1)} %copy-done.2, bf16[24,32,512]{2,1,0:T(8,128)(2,1)S(1)} %copy-done, bf16[24,32,512]{2,1,0:T(8,128)(2,1)S(1)} %collective-permute-done.2.other_ref), custom_call_target="tpu_custom_call" | custom-call | tf_op jit(solution)/shard_map/even_rows/pallas_call | solution.py:126
  5.4 8.7 %all-to-all-start = ((bf16[16,32,512]{2,1,0:T(8,128)(2,1)}), bf16[16,32,512]{2,1,0:T(8,128)(2,1)S(1)}, u32[]{:S(2)}, u32[]{:S(2)}) async-start(bf16[16,32,512]{2,1,0:T(8,128)(2,1)} %even_rows.1.grad_slab_ref), calls=%async_computation | async-start | bytes 1048576 | tf_op jit(solution)/shard_map/all_to_all | solution.py:729
  14.2 13.9 %bottleneck_forward.1 = (f32[64,512]{1,0:T(8,128)}, f32[512,512]{1,0:T(8,128)}, bf16[16,32,512]{2,1,0:T(8,128)(2,1)}, bf16[16,32,512]{2,1,0:T(8,128)(2,1)}, bf16...) custom-call(s32[16]{0:T(128)S(1)} %copy-done.3, bf16[24,32,512]{2,1,0:T(8,128)(2,1)} %features_ref.3, ...), custom_call_target="tpu_custom_call" | custom-call | flops 16000000000 | bytes 50331648 | tf_op jit(solution)/shard_map/bottleneck_forward/pallas_call | solution.py:291
  28.1 1.1 %all-to-all-done = bf16[16,32,512]{2,1,0:T(8,128)(2,1)S(1)} async-done(((bf16[16,32,512]{2,1,0:T(8,128)(2,1)}), bf16[16,32,512]{2,1,0:T(8,128)(2,1)S(1)}, u32[]{:S(2)}, u32[]{:S(2)}) %all-to-all-start) | async-done | bytes 524320 | tf_op jit(solution)/shard_map/all_to_all | solution.py:729
  29.3 4.9 %all-to-all-start.1 = ((bf16[16,32,512]{2,1,0:T(8,128)(2,1)}), bf16[16,32,512]{2,1,0:T(8,128)(2,1)S(1)}, u32[]{:S(2)}, u32[]{:S(2)}) async-start(bf16[16,32,512]{2,1,0:T(8,128)(2,1)} %get-tuple-element.28), calls=%async_computation.1 | async-start | bytes 1048576 | tf_op jit(solution)/shard_map/all_to_all | solution.py:729
  34.2 7.1 %gelu_slopes.1 = (bf16[16,32,2048]{2,1,0:T(8,128)(2,1)}, bf16[18,32,2048]{2,1,0:T(8,128)(2,1)}) custom-call(bf16[16,32,2048]{2,1,0:T(8,128)(2,1)} %get-tuple-element.29.expanded_ref, bf16[18,32,2048]{2,1,0:T(8,128)(2,1)} %get-tuple-element.30.mixed_ref), custom_call_target="tpu_custom_call" | custom-call | flops 33423360 | bytes 13369344 | tf_op jit(solution)/shard_map/gelu_slopes/pallas_call | solution.py:343
  41.3 2.6 %attended_gradient.1.grad_attended_ref = bf16[512,512]{1,0:T(8,128)(2,1)} custom-call(bf16[8,2,32,512]{3,2,1,0:T(8,128)(2,1)} %bitcast.8, bf16[512,512]{1,0:T(8,128)(2,1)} %out_ref.3), custom_call_target="tpu_custom_call" | custom-call | flops 268435456 | bytes 2097152 | tf_op jit(solution)/shard_map/attended_gradient/pallas_call | solution.py:407
  43.8 4.9 %all-to-all-done.1 = bf16[16,32,512]{2,1,0:T(8,128)(2,1)S(1)} async-done(((bf16[16,32,512]{2,1,0:T(8,128)(2,1)}), bf16[16,32,512]{2,1,0:T(8,128)(2,1)S(1)}, u32[]{:S(2)}, u32[]{:S(2)}) %all-to-all-start.1) | async-done | bytes 524320 | tf_op jit(solution)/shard_map/all_to_all | solution.py:729
  48.7 7.5 %window_attention.1 = (bf16[8,2,32,512]{3,2,1,0:T(8,128)(2,1)}, bf16[8,64,1024]{2,1,0:T(8,128)(2,1)}, bf16[512,512]{1,0:T(8,128)(2,1)}) custom-call(bf16[8,2,32,512]{3,2,1,0:T(8,128)(2,1)S(1)} %bitcast.6, bf16[512,512]{1,0:T(8,128)(2,1)} %attended_gradient.1.grad_attended_ref, bf16[512,1536]{1,0:T(8,128)(2,1)} %qkv_ref.1), custom_call_target="tpu_custom_call" | custom-call | flops 2147483648 | bytes 4194304 | tf_op jit(solution)/shard_map/window_attention/pallas_call | solution.py:516
  56.3 3.6 %all-to-all-start.2 = ((bf16[16,32,512]{2,1,0:T(8,128)(2,1)}), bf16[16,32,512]{2,1,0:T(8,128)(2,1)S(1)}, u32[]{:S(2)}, u32[]{:S(2)}) async-start(bf16[16,32,512]{2,1,0:T(8,128)(2,1)} %bitcast.10), calls=%async_computation.2 | async-start | bytes 1048576 | tf_op jit(solution)/shard_map/all_to_all | solution.py:729
  59.9 0.6 dynamic_slice.3
  61.1 3.5 %attended_output.1 = bf16[8,2,32,512]{3,2,1,0:T(8,128)(2,1)} custom-call(bf16[8,64,1024]{2,1,0:T(8,128)(2,1)} %get-tuple-element.37.weights_ref, bf16[512,512]{1,0:T(8,128)(2,1)} %get-tuple-element.38.values_ref, bf16[512,512]{1,0:T(8,128)(2,1)} %out_ref.3), custom_call_target="tpu_custom_call" | custom-call | flops 536870912 | bytes 3145728 | tf_op jit(solution)/shard_map/attended_output/pallas_call | solution.py:556
  64.7 9.9 %all-to-all-done.2.grad_ref = bf16[16,32,512]{2,1,0:T(8,128)(2,1)S(1)} async-done(((bf16[16,32,512]{2,1,0:T(8,128)(2,1)}), bf16[16,32,512]{2,1,0:T(8,128)(2,1)S(1)}, u32[]{:S(2)}, u32[]{:S(2)}) %all-to-all-start.2) | async-done | bytes 524320 | tf_op jit(solution)/shard_map/all_to_all | solution.py:729
  74.7 0.7 collective-permute-start.4
  75.4 5.5 %all-to-all-start.3 = ((bf16[16,32,512]{2,1,0:T(8,128)(2,1)}), bf16[16,32,512]{2,1,0:T(8,128)(2,1)S(1)}, u32[]{:S(2)}, u32[]{:S(2)}) async-start(bf16[16,32,512]{2,1,0:T(8,128)(2,1)} %bitcast.7), calls=%async_computation.3 | async-start | bytes 1048576 | tf_op jit(solution)/shard_map/all_to_all | solution.py:729
  80.9 10.8 %bottleneck_backward.1 = bf16[16,32,512]{2,1,0:T(8,128)(2,1)S(1)} custom-call(s32[16]{0:T(128)S(1)} %copy-done.3, bf16[24,32,512]{2,1,0:T(8,128)(2,1)} %cotangent_ref.3, bf16[24,32,512]{2,1,0:T(8,128)(2,1)} %copy-done.1, bf16[3,32,512]{2,1,0:T(8,128)(2,1)} %copy-done.4, bf16[16,32,512]{2,1,0:T(8,128)(2,1)} %get-tuple-element.41.slab_ref, ...), custom_call_target="tpu_custom_call" | custom-call | flops 16000000000 | bytes 50331648 | tf_op jit(solution)/shard_map/bottleneck_backward/pallas_call | solution.py:685
  91.8 1.0 %collective-permute-start.6 = (bf16[8,32,512]{2,1,0:T(8,128)(2,1)S(1)}, bf16[8,32,512]{2,1,0:T(8,128)(2,1)S(1)}, u32[]{:S(2)}, u32[]{:S(2)}) collective-permute-start(bf16[8,32,512]{2,1,0:T(8,128)(2,1)S(1)} %slice_select_fusion), channel_id=1, source_target_pairs={{0,1},{1,0},{2,3},{3,2},{4,5},{5,4},{6,7},{7,6},{8,9},{9,8},{10,11... | collective-permute-start | bytes 786440 | tf_op jit(solution)/shard_map/ppermute | solution.py:736
  92.8 3.9 %all-to-all-done.3 = bf16[16,32,512]{2,1,0:T(8,128)(2,1)S(1)} async-done(((bf16[16,32,512]{2,1,0:T(8,128)(2,1)}), bf16[16,32,512]{2,1,0:T(8,128)(2,1)S(1)}, u32[]{:S(2)}, u32[]{:S(2)}) %all-to-all-start.3) | async-done | bytes 524320 | tf_op jit(solution)/shard_map/all_to_all | solution.py:729
  97.1 1.0 pad_maximum_fusion.1
  98.6 1.0 pad_maximum_fusion
  (33 shorter events, 1.1 us)
Async XLA Ops:
  0.6 3.4 %copy-start = (bf16[24,32,512]{2,1,0:T(8,128)(2,1)S(1)}, bf16[24,32,512]{2,1,0:T(8,128)(2,1)}, u32[]{:S(2)}) copy-start(bf16[24,32,512]{2,1,0:T(8,128)(2,1)} %cotangent_ref.3) | copy-start | bytes 2359300
  0.6 3.4 %collective-permute-start.2 = (bf16[24,32,512]{2,1,0:T(8,128)(2,1)}, bf16[24,32,512]{2,1,0:T(8,128)(2,1)S(1)}, u32[]{:S(2)}, u32[]{:S(2)}) collective-permute-start(bf16[24,32,512]{2,1,0:T(8,128)(2,1)} %cotangent_ref.3), channel_id=1, source_target_pairs={{0,1},{1,0},{2,3},{3,2},{4,5},{5,4},{6,7},{7,6},{8,9},{9,8},{10,11... | collective-permute-start | bytes 2359304 | tf_op jit(solution)/shard_map/ppermute | solution.py:736
  1.2 13.0 %collective-permute-start = (bf16[24,32,512]{2,1,0:T(8,128)(2,1)}, bf16[24,32,512]{2,1,0:T(8,128)(2,1)S(1)}, u32[]{:S(2)}, u32[]{:S(2)}) collective-permute-start(bf16[24,32,512]{2,1,0:T(8,128)(2,1)} %features_ref.3), channel_id=1, source_target_pairs={{0,1},{1,0},{2,3},{3,2},{4,5},{5,4},{6,7},{7,6},{8,9},{9,8},{10,11... | collective-permute-start | bytes 2359304 | tf_op jit(solution)/shard_map/ppermute | solution.py:736
  1.2 0.7 copy-start.2
  1.9 12.3 %copy-start.3 = (s32[16]{0:T(128)S(1)}, s32[16]{0:T(128)}, u32[]{:S(2)}) copy-start(s32[16]{0:T(128)} %bands_ref.7) | copy-start | bytes 196
  1.9 12.3 %copy-start.5 = (bf16[9,2048]{1,0:T(8,128)(2,1)S(1)}, bf16[9,2048]{1,0:T(8,128)(2,1)}, u32[]{:S(2)}) copy-start(bf16[9,2048]{1,0:T(8,128)(2,1)} %taps_ref.3) | copy-start | bytes 110596
  3.3 10.8 %collective-permute-start.1 = (bf16[3,32,512]{2,1,0:T(8,128)(2,1)S(1)}, bf16[3,32,512]{2,1,0:T(8,128)(2,1)S(1)}, u32[]{:S(2)}, u32[]{:S(2)}) collective-permute-start(bf16[3,32,512]{2,1,0:T(8,128)(2,1)S(1)} %rim_rows.1), channel_id=1, source_target_pairs={{1,2},{3,4},{5,6},{7,8},{9,10},{11,12},{13,14},{2,1},{4,3},{6,5},{... | collective-permute-start | bytes 294920 | tf_op jit(solution)/shard_map/ppermute | solution.py:742
  4.0 24.1 %copy-start.1 = (bf16[24,32,512]{2,1,0:T(8,128)(2,1)}, bf16[24,32,512]{2,1,0:T(8,128)(2,1)S(1)}, u32[]{:S(2)}) copy-start(bf16[24,32,512]{2,1,0:T(8,128)(2,1)S(1)} %collective-permute-done.2.other_ref) | copy-start | bytes 2359300
  5.4 23.8 %all-to-all-start = ((bf16[16,32,512]{2,1,0:T(8,128)(2,1)}), bf16[16,32,512]{2,1,0:T(8,128)(2,1)S(1)}, u32[]{:S(2)}, u32[]{:S(2)}) async-start(bf16[16,32,512]{2,1,0:T(8,128)(2,1)} %even_rows.1.grad_slab_ref), calls=%async_computation | async-start | bytes 1048576 | tf_op jit(solution)/shard_map/all_to_all | solution.py:729
  14.1 14.0 %copy-start.4 = (bf16[3,32,512]{2,1,0:T(8,128)(2,1)}, bf16[3,32,512]{2,1,0:T(8,128)(2,1)S(1)}, u32[]{:S(2)}) copy-start(bf16[3,32,512]{2,1,0:T(8,128)(2,1)S(1)} %collective-permute-done.1.rim_ref) | copy-start | bytes 294916
  29.3 12.0 %copy-start.6 = (bf16[16,32,512]{2,1,0:T(8,128)(2,1)}, bf16[16,32,512]{2,1,0:T(8,128)(2,1)S(1)}, u32[]{:S(2)}) copy-start(bf16[16,32,512]{2,1,0:T(8,128)(2,1)S(1)} %all-to-all-done) | copy-start | bytes 1572868
  29.3 19.5 %all-to-all-start.1 = ((bf16[16,32,512]{2,1,0:T(8,128)(2,1)}), bf16[16,32,512]{2,1,0:T(8,128)(2,1)S(1)}, u32[]{:S(2)}, u32[]{:S(2)}) async-start(bf16[16,32,512]{2,1,0:T(8,128)(2,1)} %get-tuple-element.28), calls=%async_computation.1 | async-start | bytes 1048576 | tf_op jit(solution)/shard_map/all_to_all | solution.py:729
  56.3 18.3 %all-to-all-start.2 = ((bf16[16,32,512]{2,1,0:T(8,128)(2,1)}), bf16[16,32,512]{2,1,0:T(8,128)(2,1)S(1)}, u32[]{:S(2)}, u32[]{:S(2)}) async-start(bf16[16,32,512]{2,1,0:T(8,128)(2,1)} %bitcast.10), calls=%async_computation.2 | async-start | bytes 1048576 | tf_op jit(solution)/shard_map/all_to_all | solution.py:729
  74.6 6.3 %copy-start.8 = (bf16[16,32,512]{2,1,0:T(8,128)(2,1)}, bf16[16,32,512]{2,1,0:T(8,128)(2,1)S(1)}, u32[]{:S(2)}) copy-start(bf16[16,32,512]{2,1,0:T(8,128)(2,1)S(1)} %all-to-all-done.2.grad_ref) | copy-start | bytes 1572868
  74.6 6.3 %collective-permute-start.3 = (bf16[1,32,512]{2,1,0:T(8,128)(2,1)S(1)}, bf16[1,32,512]{2,1,0:T(8,128)(2,1)S(1)}, u32[]{:S(2)}, u32[]{:S(2)}) collective-permute-start(bf16[1,32,512]{2,1,0:T(8,128)(2,1)S(1)} %get-tuple-element.45), channel_id=1, source_target_pairs={{0,1},{1,0},{2,3},{3,2},{4,5},{5,4},{6,7},{7,6},{8,9},{9,8},{10,11... | collective-permute-start | bytes 98312 | tf_op jit(solution)/shard_map/ppermute | solution.py:736
  74.7 6.2 %collective-permute-start.4 = (bf16[1,32,512]{2,1,0:T(8,128)(2,1)S(1)}, bf16[1,32,512]{2,1,0:T(8,128)(2,1)S(1)}, u32[]{:S(2)}, u32[]{:S(2)}) collective-permute-start(bf16[1,32,512]{2,1,0:T(8,128)(2,1)S(1)} %get-tuple-element.46), channel_id=1, source_target_pairs={{1,2},{3,4},{5,6},{7,8},{9,10},{11,12},{13,14},{2,1},{4,3},{6,5},{... | collective-permute-start | bytes 98312 | tf_op jit(solution)/shard_map/ppermute | solution.py:742
  75.4 21.3 %all-to-all-start.3 = ((bf16[16,32,512]{2,1,0:T(8,128)(2,1)}), bf16[16,32,512]{2,1,0:T(8,128)(2,1)S(1)}, u32[]{:S(2)}, u32[]{:S(2)}) async-start(bf16[16,32,512]{2,1,0:T(8,128)(2,1)} %bitcast.7), calls=%async_computation.3 | async-start | bytes 1048576 | tf_op jit(solution)/shard_map/all_to_all | solution.py:729
  80.9 15.7 %copy-start.7 = (f32[512,512]{1,0:T(8,128)S(1)}, f32[512,512]{1,0:T(8,128)}, u32[]{:S(2)}) copy-start(f32[512,512]{1,0:T(8,128)} %get-tuple-element.40.first_ref) | copy-start | bytes 3145732
  91.8 5.2 %collective-permute-start.6 = (bf16[8,32,512]{2,1,0:T(8,128)(2,1)S(1)}, bf16[8,32,512]{2,1,0:T(8,128)(2,1)S(1)}, u32[]{:S(2)}, u32[]{:S(2)}) collective-permute-start(bf16[8,32,512]{2,1,0:T(8,128)(2,1)S(1)} %slice_select_fusion), channel_id=1, source_target_pairs={{0,1},{1,0},{2,3},{3,2},{4,5},{5,4},{6,7},{7,6},{8,9},{9,8},{10,11... | collective-permute-start | bytes 786440 | tf_op jit(solution)/shard_map/ppermute | solution.py:736
  96.9 1.6 %collective-permute-start.5 = (bf16[8,32,512]{2,1,0:T(8,128)(2,1)S(1)}, bf16[8,32,512]{2,1,0:T(8,128)(2,1)S(1)}, u32[]{:S(2)}, u32[]{:S(2)}) collective-permute-start(bf16[8,32,512]{2,1,0:T(8,128)(2,1)S(1)} %broadcast_select_fusion), channel_id=1, source_target_pairs={{0,1},{1,0},{2,3},{3,2},{4,5},{5,4},{6,7},{7,6},{8,9},{9,8},{10,11... | collective-permute-start | bytes 786440 | tf_op jit(solution)/shard_map/ppermute | solution.py:736
